TPU v7x, 32 devices: a whole 2x2x4 slice. The times are simulated.
32 devices in a mesh: seq: 8 (over y, x, core), pipe: 4 (over z).
Axes of the slice: x: 2, y: 2, z: 4, core: 2. Of those that a mesh axis runs over, the one named last changes fastest.
Arguments:
- section_inputs: bfloat16 [4, 1024, 1536], P('pipe', 'seq'), may hold values from -6 to 6
- cotangent: bfloat16 [1024, 1536], P('seq'), may hold values from -6 to 6
- gain: float32 [4, 1536], P('pipe'), may hold values from 0.25 to 1.75
- w_gate: bfloat16 [4, 1536, 1536], P('pipe'), may hold values from -0.15625 to 0.15625
- w_out: bfloat16 [4, 1536, 1536], P('pipe'), may hold values from -0.15625 to 0.15625
- mix_first: bfloat16 [4, 16, 64, 64], P('pipe', 'seq'), may hold values from -0.75 to 0.75
- mix_second: bfloat16 [4, 16, 64, 64], P('pipe', 'seq'), may hold values from -0.75 to 0.75
Outputs:
- grad_inputs: bfloat16 [4, 1024, 1536], P('pipe', 'seq')
- grad_first: float32 [4, 16, 64, 64], P('pipe', 'seq')
- grad_second: float32 [4, 16, 64, 64], P('pipe', 'seq')
All inputs are finite; a program needn't handle non-finite values.
Results may differ from a plain program's by a relative error of at most 0.025.
Values may be sent and summed in bfloat16 or wider, within the bound.
No kernel may reach another device: no remote copies, remote signals or barrier semaphores. Data moves between devices by JAX's collectives and lax.ppermute only.
A program may use at most 64 MiB of HBM per device.

v0:
```python
import jax
import jax.numpy as jnp
from jax import lax
from jax.sharding import PartitionSpec as P


def shifted(block, axis, distance):
    devices = range(lax.axis_size(axis))
    route = [(i - distance, i) for i in devices if i - distance in devices]
    return lax.ppermute(block, axis, route)


def to_stride(first_out):
    return lax.all_to_all(first_out, "seq", split_axis=0, concat_axis=1, tiled=True)


def from_stride(delta_moved):
    return lax.all_to_all(delta_moved, "seq", split_axis=1, concat_axis=0, tiled=True)


def per_device(section_inputs, cotangent, gain, w_gate, w_out, mix_first, mix_second):
    inputs = section_inputs[0]
    gain_row = gain[0]
    weight_gate = w_gate[0]
    weight_out = w_out[0]
    first_blocks = mix_first[0]
    second_blocks = mix_second[0]
    row_count, feature_width = inputs.shape
    local_blocks = first_blocks.shape[0]
    block_rows = first_blocks.shape[1]
    seq_count = lax.axis_size("seq")
    section_count = lax.axis_size("pipe")
    section_index = lax.axis_index("pipe")
    contract = (((1,), (1,)), ((), ()))
    features = inputs.astype(jnp.float32)
    inv_rms = lax.rsqrt(jnp.mean(features * features, axis=-1, keepdims=True) + 1e-06)
    unit_rows = features * inv_rms
    normed = (unit_rows * gain_row).astype(jnp.bfloat16)
    normed_blocks = normed.reshape(local_blocks, block_rows, feature_width)
    first_out = jnp.einsum(
        "aij,ajc->iac", first_blocks, normed_blocks, preferred_element_type=jnp.float32
    ).astype(jnp.bfloat16)
    moved_blocks = to_stride(first_out).reshape(local_blocks, block_rows, feature_width)
    mixer_out = jnp.einsum(
        "kij,kjc->kic", second_blocks, moved_blocks, preferred_element_type=jnp.float32
    ).reshape(row_count, feature_width)
    gate_pre = jnp.dot(normed, weight_gate, preferred_element_type=jnp.float32)
    sigma = jax.nn.sigmoid(gate_pre)
    mix_factor = gate_pre * sigma
    gate_factor = mixer_out * sigma * (1.0 + gate_pre * (1.0 - sigma))
    incoming = cotangent
    outgoing_kept = jnp.zeros_like(cotangent)
    mid_kept = jnp.zeros_like(first_out)
    mix_kept = jnp.zeros((local_blocks, block_rows, feature_width), jnp.bfloat16)
    for tick_index in range(section_count):
        active = section_index == section_count - 1 - tick_index
        delta_hidden = lax.dot_general(
            incoming, weight_out, contract, preferred_element_type=jnp.float32
        )
        mix_blocks = (
            (delta_hidden * mix_factor)
            .astype(jnp.bfloat16)
            .reshape(local_blocks, block_rows, feature_width)
        )
        delta_gate = (delta_hidden * gate_factor).astype(jnp.bfloat16)
        delta_moved = jnp.einsum(
            "kij,kic->kjc", second_blocks, mix_blocks, preferred_element_type=jnp.float32
        ).astype(jnp.bfloat16)
        delta_mid = from_stride(
            delta_moved.reshape(block_rows // seq_count, seq_count * local_blocks, feature_width)
        )
        first_back = jnp.einsum(
            "aij,iac->ajc", first_blocks, delta_mid, preferred_element_type=jnp.float32
        ).reshape(row_count, feature_width)
        gate_back = lax.dot_general(
            delta_gate, weight_gate, contract, preferred_element_type=jnp.float32
        )
        delta_norm = (first_back + gate_back) * gain_row
        centred = delta_norm - unit_rows * jnp.mean(delta_norm * unit_rows, axis=-1, keepdims=True)
        outgoing = (incoming.astype(jnp.float32) + inv_rms * centred).astype(jnp.bfloat16)
        outgoing_kept = jnp.where(active, outgoing, outgoing_kept)
        mid_kept = jnp.where(active, delta_mid, mid_kept)
        mix_kept = jnp.where(active, mix_blocks, mix_kept)
        if tick_index + 1 < section_count:
            incoming = shifted(outgoing, "pipe", -1)
    grad_first_kept = jnp.einsum(
        "iac,ajc->aij", mid_kept, normed_blocks, preferred_element_type=jnp.float32
    )
    grad_second_kept = jnp.einsum(
        "kic,kjc->kij", mix_kept, moved_blocks, preferred_element_type=jnp.float32
    )
    return (outgoing_kept[None], grad_first_kept[None], grad_second_kept[None])


def solution(mesh):
    placed = (
        P("pipe", "seq", None),
        P("seq", None),
        P("pipe", None),
        P("pipe", None, None),
        P("pipe", None, None),
        P("pipe", "seq", None, None),
        P("pipe", "seq", None, None),
    )
    return jax.shard_map(
        per_device,
        mesh=mesh,
        in_specs=placed,
        out_specs=(
            P("pipe", "seq", None),
            P("pipe", "seq", None, None),
            P("pipe", "seq", None, None),
        ),
        check_vma=False,
    )
```

profile of v0, /device:TPU:0, one launch (start us, length us, event | category | flops | bytes accessed | tf_op | source)
XLA Modules:
  0.0 132.2 jit_solution(365119654665889446)
XLA Ops:
  0.6 0.0 copy-start
  0.6 1.2 fusion.44
  1.8 0.1 rsqrt.13
  1.9 0.7 reduce
  2.6 1.3 %fusion.42 = bf16[64,2,1536]{2,0,1:T(8,128)(2,1)S(1)} fusion(f32[1536]{0:T(1024)S(1)} %reduce, f32[2,64]{1,0:T(2,128)S(1)} %rsqrt.13, bf16[1,2,64,64]{3,2,1,0:T(8,128)(2,1)} %param.12, bf16[2,64,1536]{2,1,0:T(8,128)(2,1)} %bitcast.208), kind=kOutput, calls=%fused_computation.31 | convolution fusion | flops 26148864 | bytes 809472 | tf_op jit(solution)/shard_map/aij,ajc->iac/dot_general | solution.py:40
  4.0 1.2 copy.40
  5.1 5.3 %all-to-all-start.1 = ((bf16[64,2,1536]{2,1,0:T(2,128)(2,1)}), bf16[64,2,1536]{2,1,0:T(2,128)(2,1)S(1)}, u32[]{:S(2)}, u32[]{:S(2)}) async-start(bf16[64,2,1536]{2,1,0:T(2,128)(2,1)} %copy.40), calls=%async_computation.1 | async-start | bytes 786432 | tf_op jit(solution)/shard_map/all_to_all | solution.py:14
  10.4 4.1 %fusion.16 = f32[128,1536]{1,0:T(8,128)S(1)} fusion(bf16[128,1536]{1,0:T(8,128)(2,1)} %param.8, bf16[1,1536,1536]{2,1,0:T(8,128)(2,1)} %param.11), kind=kOutput, calls=%fused_computation.16 | convolution fusion | flops 603979776 | bytes 5898240 | tf_op jit(solution)/shard_map/dot_general | solution.py:57
  14.5 4.2 %all-to-all-done.1 = bf16[64,2,1536]{2,1,0:T(2,128)(2,1)S(1)} async-done(((bf16[64,2,1536]{2,1,0:T(2,128)(2,1)}), bf16[64,2,1536]{2,1,0:T(2,128)(2,1)S(1)}, u32[]{:S(2)}, u32[]{:S(2)}) %all-to-all-start.1) | async-done | bytes 393248 | tf_op jit(solution)/shard_map/all_to_all | solution.py:14
  18.8 0.3 copy.95
  19.0 0.1 reshape.112
  19.2 0.0 slice-start
  19.2 0.2 fusion.97
  19.5 0.0 copy-done.1
  19.5 0.0 copy-start.5
  19.5 0.0 slice-start.1
  19.5 3.6 %fusion.43 = (f32[128,1536]{1,0:T(8,128)S(1)}, bf16[128,1536]{1,0:T(8,128)(2,1)S(1)}, f32[128,1536]{1,0:T(8,128)S(1)}) fusion(f32[2,1536,64]{1,2,0:T(8,128)S(1)} %fusion.97, f32[128,1536]{1,0:T(8,128)S(1)} %fusion.16, bf16[1,1536,1536]{2,1,0:T(8,128)(2,1)} %param.10, bf16[1,128,1536]{2,1,0:T(8,128)(2,1)S(1)} %copy-done.1, f32[1536]{0:T(1024)S(1)} %reduce, ...), kind=kOutput, calls=%fused_computation.35 | convolution fusion | flops 606928896 | bytes 8657408 | tf_op jit(solution)/shard_map/dot_general | solution.py:47
  23.1 0.3 convolution_convert_fusion.4
  23.5 0.2 copy.37
  23.7 10.7 %all_to_all.87 = bf16[8,16,1536]{2,0,1:T(8,128)(2,1)S(1)} all-to-all(bf16[8,16,1536]{2,0,1:T(8,128)(2,1)S(1)} %copy.37), channel_id=1, replica_groups=mesh['seq'=8,'pipe'=4] {'seq'}, dimensions={1} | all-to-all | bytes 786432 | tf_op jit(solution)/shard_map/all_to_all | solution.py:18
  34.4 0.3 fusion.50
  34.7 0.0 copy-done.9
  34.8 0.0 slice-done
  34.8 0.0 slice-done.1
  34.8 0.0 slice-start.3
  34.8 1.7 %multiply_reduce_fusion.3 = (f32[128]{0:T(128)S(1)}, f32[128,1536]{1,0:T(8,128)S(1)}) fusion(bf16[1,128,1536]{2,1,0:T(8,128)(2,1)S(1)} %copy-done.1, f32[128]{0:T(128)S(1)} %add_rsqrt_fusion, f32[1536]{0:T(1024)S(1)} %reduce, f32[128,1536]{1,0:T(8,128)S(1)} %bitcast.215, bf16[1,1536,1536]{2,1,0:T(8,128)(2,1)S(1)} %bitcast.207, f32[128,1536]{1,0:T(8,128)S(1)} %fusion.16, ...), kind=kOutput, calls=%fused_computation.52 | convolution fusion | flops 605552512 | bytes 8264704 | tf_op jit(solution)/shard_map/dot_general | solution.py:75
  36.6 0.0 copy-done.2
  36.6 0.3 add_convert_fusion.3
  36.9 1.3 collective-permute-start
  38.2 11.3 %collective-permute-done = bf16[128,1536]{1,0:T(8,128)(2,1)S(1)} collective-permute-done((bf16[128,1536]{1,0:T(8,128)(2,1)S(1)}, bf16[128,1536]{1,0:T(8,128)(2,1)S(1)}, u32[]{:S(2)}, u32[]{:S(2)}) %collective-permute-start) | collective-permute-done | bytes 393248 | tf_op jit(solution)/shard_map/ppermute | solution.py:10
  49.4 0.0 slice-done.3
  49.4 1.7 %multiply_convert_fusion.5 = (bf16[128,1536]{1,0:T(8,128)(2,1)S(1)}, f32[128,1536]{1,0:T(8,128)S(1)}) fusion(f32[128,1536]{1,0:T(8,128)S(1)} %get-tuple-element.5, bf16[128,1536]{1,0:T(8,128)(2,1)S(1)} %collective-permute-done, bf16[1,1536,1536]{2,1,0:T(8,128)(2,1)S(1)} %bitcast.211), kind=kOutput, calls=%fused_computation.50 | convolution fusion | flops 605159424 | bytes 7077888 | tf_op jit(solution)/shard_map/dot_general | solution.py:57
  51.1 0.3 convolution_convert_fusion.3
  51.4 0.2 copy.43
  51.7 10.7 %all_to_all.88 = bf16[8,16,1536]{2,0,1:T(8,128)(2,1)S(1)} all-to-all(bf16[8,16,1536]{2,0,1:T(8,128)(2,1)S(1)} %copy.43), channel_id=1, replica_groups=mesh['seq'=8,'pipe'=4] {'seq'}, dimensions={1} | all-to-all | bytes 786432 | tf_op jit(solution)/shard_map/all_to_all | solution.py:18
  62.4 0.3 fusion.63
  62.7 0.0 copy-done.10
  62.7 0.4 copy-done.3
  63.2 1.7 %multiply_reduce_fusion.2 = (f32[128]{0:T(128)S(1)}, f32[128,1536]{1,0:T(8,128)S(1)}) fusion(bf16[1,128,1536]{2,1,0:T(8,128)(2,1)S(1)} %copy-done.1, f32[128]{0:T(128)S(1)} %add_rsqrt_fusion, f32[1536]{0:T(1024)S(1)} %reduce, f32[128,1536]{1,0:T(8,128)S(1)} %bitcast.213, bf16[1,1536,1536]{2,1,0:T(8,128)(2,1)S(1)} %bitcast.207, ...), kind=kOutput, calls=%fused_computation.48 | convolution fusion | flops 605552512 | bytes 8264704 | tf_op jit(solution)/shard_map/dot_general | solution.py:75
  64.9 0.3 add_convert_fusion.2
  65.2 1.3 collective-permute-start.1
  66.5 11.2 %collective-permute-done.1 = bf16[128,1536]{1,0:T(8,128)(2,1)S(1)} collective-permute-done((bf16[128,1536]{1,0:T(8,128)(2,1)S(1)}, bf16[128,1536]{1,0:T(8,128)(2,1)S(1)}, u32[]{:S(2)}, u32[]{:S(2)}) %collective-permute-start.1) | collective-permute-done | bytes 393248 | tf_op jit(solution)/shard_map/ppermute | solution.py:10
  77.8 1.7 %multiply_convert_fusion.3 = (bf16[128,1536]{1,0:T(8,128)(2,1)S(1)}, f32[128,1536]{1,0:T(8,128)S(1)}) fusion(f32[128,1536]{1,0:T(8,128)S(1)} %get-tuple-element.5, bf16[128,1536]{1,0:T(8,128)(2,1)S(1)} %collective-permute-done.1, bf16[1,1536,1536]{2,1,0:T(8,128)(2,1)S(1)} %bitcast.211), kind=kOutput, calls=%fused_computation.46 | convolution fusion | flops 605159424 | bytes 7077888 | tf_op jit(solution)/shard_map/dot_general | solution.py:57
  79.5 0.0 copy-start.11
  79.5 0.3 convolution_convert_fusion.2
  79.8 0.2 copy.47
  80.0 10.7 %all_to_all.89 = bf16[8,16,1536]{2,0,1:T(8,128)(2,1)S(1)} all-to-all(bf16[8,16,1536]{2,0,1:T(8,128)(2,1)S(1)} %copy.47), channel_id=1, replica_groups=mesh['seq'=8,'pipe'=4] {'seq'}, dimensions={1} | all-to-all | bytes 786432 | tf_op jit(solution)/shard_map/all_to_all | solution.py:18
  90.7 0.3 fusion.60
  91.1 0.4 copy-done.4
  91.5 1.7 %multiply_reduce_fusion.1 = (f32[128]{0:T(128)S(1)}, f32[128,1536]{1,0:T(8,128)S(1)}) fusion(bf16[1,128,1536]{2,1,0:T(8,128)(2,1)S(1)} %copy-done.1, f32[128]{0:T(128)S(1)} %add_rsqrt_fusion, f32[1536]{0:T(1024)S(1)} %reduce, f32[128,1536]{1,0:T(8,128)S(1)} %bitcast.214, bf16[1,1536,1536]{2,1,0:T(8,128)(2,1)S(1)} %bitcast.207, ...), kind=kOutput, calls=%fused_computation.44 | convolution fusion | flops 605552512 | bytes 8264704 | tf_op jit(solution)/shard_map/dot_general | solution.py:75
  93.3 0.3 add_convert_fusion.1
  93.6 1.5 %collective-permute-start.2 = (bf16[128,1536]{1,0:T(8,128)(2,1)S(1)}, bf16[128,1536]{1,0:T(8,128)(2,1)S(1)}, u32[]{:S(2)}, u32[]{:S(2)}) collective-permute-start(bf16[128,1536]{1,0:T(8,128)(2,1)S(1)} %add_convert_fusion.1), channel_id=1, source_target_pairs={{1,0},{2,1},{3,2},{5,4},{6,5},{7,6},{9,8},{10,9},{11,10},{13,12},{... | collective-permute-start | bytes 1179656 | tf_op jit(solution)/shard_map/ppermute | solution.py:10
  95.1 11.1 %collective-permute-done.2 = bf16[128,1536]{1,0:T(8,128)(2,1)S(1)} collective-permute-done((bf16[128,1536]{1,0:T(8,128)(2,1)S(1)}, bf16[128,1536]{1,0:T(8,128)(2,1)S(1)}, u32[]{:S(2)}, u32[]{:S(2)}) %collective-permute-start.2) | collective-permute-done | bytes 393248 | tf_op jit(solution)/shard_map/ppermute | solution.py:10
  106.1 2.6 %multiply_convert_fusion.1 = (bf16[128,1536]{1,0:T(8,128)(2,1)S(1)}, f32[128,1536]{1,0:T(8,128)}) fusion(f32[128,1536]{1,0:T(8,128)S(1)} %get-tuple-element.5, bf16[128,1536]{1,0:T(8,128)(2,1)S(1)} %collective-permute-done.2, bf16[1,1536,1536]{2,1,0:T(8,128)(2,1)S(1)} %bitcast.211), kind=kOutput, calls=%fused_computation.42 | convolution fusion | flops 605159424 | bytes 7077888 | tf_op jit(solution)/shard_map/dot_general | solution.py:57
  108.7 0.7 copy-done.12
  109.5 0.3 convolution_convert_fusion.1
  109.8 1.0 copy.51
  110.7 4.1 %all-to-all-start.4 = ((bf16[8,16,1536]{2,0,1:T(8,128)(2,1)}), bf16[8,16,1536]{2,0,1:T(8,128)(2,1)}, u32[]{:S(2)}, u32[]{:S(2)}) async-start(bf16[8,16,1536]{2,0,1:T(8,128)(2,1)} %copy.51), calls=%async_computation.4 | async-start | bytes 786432 | tf_op jit(solution)/shard_map/all_to_all | solution.py:18
  114.9 1.9 %convolution_bitcast_fusion = f32[1,2,64,64]{3,2,1,0:T(8,128)} fusion(bf16[2,64,1536]{2,1,0:T(8,128)(2,1)S(1)} %reshape.112, bf16[2,64,1536]{2,1,0:T(8,128)(2,1)} %bitcast.235, bf16[2,64,1536]{2,1,0:T(8,128)(2,1)} %bitcast.233, bf16[2,64,1536]{2,1,0:T(8,128)(2,1)} %bitcast.231, bf16[2,64,1536]{2,1,0:T(8,128)(2,1)} %bitcast.229, pred[]{:T(512)S(6)} %eq.15, ...), kind=kOutput, calls=%fused_computation.32 | convolution fusion | flops 25952256 | bytes 1998852 | tf_op jit(solution)/shard_map/kic,kjc->kij/dot_general | solution.py:89
  116.8 6.4 %all-to-all-done.4 = bf16[8,16,1536]{2,0,1:T(8,128)(2,1)} async-done(((bf16[8,16,1536]{2,0,1:T(8,128)(2,1)}), bf16[8,16,1536]{2,0,1:T(8,128)(2,1)}, u32[]{:S(2)}, u32[]{:S(2)}) %all-to-all-start.4) | async-done | bytes 393248 | tf_op jit(solution)/shard_map/all_to_all | solution.py:18
  123.2 2.3 %convolution_bitcast_fusion.1 = f32[1,2,64,64]{3,2,1,0:T(8,128)} fusion(pred[]{:T(512)S(6)} %eq.15, pred[]{:T(512)S(6)} %eq.14, pred[]{:T(512)S(6)} %eq.13, pred[]{:T(512)S(6)} %eq.12, bf16[8,8,2,1536]{3,1,2,0:T(8,128)(2,1)} %bitcast.40, bf16[8,8,2,1536]{3,1,2,0:T(8,128)(2,1)} %bitcast.227, bf16[8,8,2,1536]{3,1,2,0:T(8,128)(2,1)} %bitcast.225, ...), kind=kOutput, calls=%fused_computation.33 | convolution fusion | flops 26738688 | bytes 2005508 | tf_op jit(solution)/shard_map/iac,ajc->aij/dot_general | solution.py:86
  125.5 1.3 %fusion.57 = f32[2,1536,64]{1,2,0:T(8,128)S(1)} fusion(bf16[8,8,2,1536]{3,1,2,0:T(8,128)(2,1)} %bitcast.40, bf16[1,2,64,64]{3,2,1,0:T(8,128)(2,1)S(1)} %copy-done.5), kind=kOutput, calls=%fused_computation.69 | convolution fusion | flops 25165824 | bytes 1196032 | tf_op jit(solution)/shard_map/aij,iac->ajc/dot_general | solution.py:72
  126.9 4.1 %multiply_reduce_fusion = (f32[128]{0:T(128)S(1)}, f32[128,1536]{1,0:T(8,128)S(1)}) fusion(bf16[1,128,1536]{2,1,0:T(8,128)(2,1)S(1)} %copy-done.1, f32[128]{0:T(128)S(1)} %add_rsqrt_fusion, f32[1536]{0:T(1024)S(1)} %reduce, f32[128,1536]{1,0:T(8,128)S(1)} %bitcast.212, bf16[1,1536,1536]{2,1,0:T(8,128)(2,1)} %param.10, f32[128,1536]{1,0:T(8,128)S(1)} %copy-done.6, ...), kind=kOutput, calls=%fused_computation.40 | convolution fusion | flops 605552512 | bytes 8264704 | tf_op jit(solution)/shard_map/dot_general | solution.py:75
  131.0 1.2 fusion.49
  (25 shorter events, 0.1 us)
Async XLA Ops:
  0.6 18.6 %copy-start = (bf16[1,2,64,64]{3,2,1,0:T(8,128)(2,1)S(1)}, bf16[1,2,64,64]{3,2,1,0:T(8,128)(2,1)}, u32[]{:S(2)}) copy-start(bf16[1,2,64,64]{3,2,1,0:T(8,128)(2,1)} %param.13) | copy-start | bytes 49156
  5.1 14.3 %copy-start.1 = (bf16[1,128,1536]{2,1,0:T(8,128)(2,1)S(1)}, bf16[1,128,1536]{2,1,0:T(8,128)(2,1)}, u32[]{:S(2)}) copy-start(bf16[1,128,1536]{2,1,0:T(8,128)(2,1)} %param.7) | copy-start | bytes 1179652
  5.1 13.6 %all-to-all-start.1 = ((bf16[64,2,1536]{2,1,0:T(2,128)(2,1)}), bf16[64,2,1536]{2,1,0:T(2,128)(2,1)S(1)}, u32[]{:S(2)}, u32[]{:S(2)}) async-start(bf16[64,2,1536]{2,1,0:T(2,128)(2,1)} %copy.40), calls=%async_computation.1 | async-start | bytes 786432 | tf_op jit(solution)/shard_map/all_to_all | solution.py:14
  19.2 15.5 %slice-start = ((s8[4718592]{0:T(1024)(128)(4,1)}), s8[4194304]{0:T(1024)(128)(4,1)S(1)}, s32[]{:S(2)}) async-start(s8[4718592]{0:T(1024)(128)(4,1)} %bitcast.206), calls=%async_computation.5 | async-start | bytes 8388608
  19.5 14.9 %copy-start.5 = (bf16[1,2,64,64]{3,2,1,0:T(8,128)(2,1)S(1)}, bf16[1,2,64,64]{3,2,1,0:T(8,128)(2,1)}, u32[]{:S(2)}) copy-start(bf16[1,2,64,64]{3,2,1,0:T(8,128)(2,1)} %param.12) | copy-start | bytes 49156
  19.5 15.3 %slice-start.1 = ((s8[4718592]{0:T(1024)(128)(4,1)}), s8[524288]{0:T(1024)(128)(4,1)S(1)}, s32[]{:S(2)}) async-start(s8[4718592]{0:T(1024)(128)(4,1)} %bitcast.206), calls=%async_computation.6 | async-start | bytes 1048576
  23.1 11.6 %copy-start.9 = (bf16[128,1536]{1,0:T(8,128)(2,1)}, bf16[128,1536]{1,0:T(8,128)(2,1)S(1)}, u32[]{:S(2)}) copy-start(bf16[128,1536]{1,0:T(8,128)(2,1)S(1)} %get-tuple-element.4) | copy-start | bytes 1179652
  34.4 2.1 %copy-start.2 = (bf16[128,1536]{1,0:T(8,128)(2,1)S(1)}, bf16[128,1536]{1,0:T(8,128)(2,1)}, u32[]{:S(2)}) copy-start(bf16[128,1536]{1,0:T(8,128)(2,1)} %param.8) | copy-start | bytes 1179652
  34.4 15.0 %slice-start.2 = ((s8[4718592]{0:T(1024)(128)(4,1)}), s8[4194304]{0:T(1024)(128)(4,1)S(1)}, s32[]{:S(2)}) async-start(s8[4718592]{0:T(1024)(128)(4,1)} %bitcast.210), calls=%async_computation.7 | async-start | bytes 8388608
  34.8 14.7 %slice-start.3 = ((s8[4718592]{0:T(1024)(128)(4,1)}), s8[524288]{0:T(1024)(128)(4,1)S(1)}, s32[]{:S(2)}) async-start(s8[4718592]{0:T(1024)(128)(4,1)} %bitcast.210), calls=%async_computation.8 | async-start | bytes 1048576
  36.9 12.6 %collective-permute-start = (bf16[128,1536]{1,0:T(8,128)(2,1)S(1)}, bf16[128,1536]{1,0:T(8,128)(2,1)S(1)}, u32[]{:S(2)}, u32[]{:S(2)}) collective-permute-start(bf16[128,1536]{1,0:T(8,128)(2,1)S(1)} %add_convert_fusion.3), channel_id=1, source_target_pairs={{1,0},{2,1},{3,2},{5,4},{6,5},{7,6},{9,8},{10,9},{11,10},{13,12},{... | collective-permute-start | bytes 1179656 | tf_op jit(solution)/shard_map/ppermute | solution.py:10
  51.1 11.6 %copy-start.10 = (bf16[128,1536]{1,0:T(8,128)(2,1)}, bf16[128,1536]{1,0:T(8,128)(2,1)S(1)}, u32[]{:S(2)}) copy-start(bf16[128,1536]{1,0:T(8,128)(2,1)S(1)} %get-tuple-element.8) | copy-start | bytes 1179652
  62.4 0.7 copy-start.3
  65.2 12.5 %collective-permute-start.1 = (bf16[128,1536]{1,0:T(8,128)(2,1)S(1)}, bf16[128,1536]{1,0:T(8,128)(2,1)S(1)}, u32[]{:S(2)}, u32[]{:S(2)}) collective-permute-start(bf16[128,1536]{1,0:T(8,128)(2,1)S(1)} %add_convert_fusion.2), channel_id=1, source_target_pairs={{1,0},{2,1},{3,2},{5,4},{6,5},{7,6},{9,8},{10,9},{11,10},{13,12},{... | collective-permute-start | bytes 1179656 | tf_op jit(solution)/shard_map/ppermute | solution.py:10
  79.5 13.8 %copy-start.11 = (bf16[128,1536]{1,0:T(8,128)(2,1)}, bf16[128,1536]{1,0:T(8,128)(2,1)S(1)}, u32[]{:S(2)}) copy-start(bf16[128,1536]{1,0:T(8,128)(2,1)S(1)} %get-tuple-element.12) | copy-start | bytes 1179652
  90.7 0.8 copy-start.4
  93.6 12.6 %collective-permute-start.2 = (bf16[128,1536]{1,0:T(8,128)(2,1)S(1)}, bf16[128,1536]{1,0:T(8,128)(2,1)S(1)}, u32[]{:S(2)}, u32[]{:S(2)}) collective-permute-start(bf16[128,1536]{1,0:T(8,128)(2,1)S(1)} %add_convert_fusion.1), channel_id=1, source_target_pairs={{1,0},{2,1},{3,2},{5,4},{6,5},{7,6},{9,8},{10,9},{11,10},{13,12},{... | collective-permute-start | bytes 1179656 | tf_op jit(solution)/shard_map/ppermute | solution.py:10
  106.1 2.6 %copy-start.7 = (bf16[128,1536]{1,0:T(8,128)(2,1)}, bf16[128,1536]{1,0:T(8,128)(2,1)S(1)}, u32[]{:S(2)}) copy-start(bf16[128,1536]{1,0:T(8,128)(2,1)S(1)} %collective-permute-done.2) | copy-start | bytes 1179652
  108.7 0.7 copy-start.12
  110.7 12.5 %all-to-all-start.4 = ((bf16[8,16,1536]{2,0,1:T(8,128)(2,1)}), bf16[8,16,1536]{2,0,1:T(8,128)(2,1)}, u32[]{:S(2)}, u32[]{:S(2)}) async-start(bf16[8,16,1536]{2,0,1:T(8,128)(2,1)} %copy.51), calls=%async_computation.4 | async-start | bytes 786432 | tf_op jit(solution)/shard_map/all_to_all | solution.py:18
  123.2 3.7 %copy-start.6 = (f32[128,1536]{1,0:T(8,128)S(1)}, f32[128,1536]{1,0:T(8,128)}, u32[]{:S(2)}) copy-start(f32[128,1536]{1,0:T(8,128)} %get-tuple-element.17) | copy-start | bytes 2359300
  125.5 5.5 %copy-start.8 = (bf16[128,1536]{1,0:T(8,128)(2,1)S(1)}, bf16[128,1536]{1,0:T(8,128)(2,1)}, u32[]{:S(2)}) copy-start(bf16[128,1536]{1,0:T(8,128)(2,1)} %copy-done.7) | copy-start | bytes 1179652
where the time goes:
time: 133 us; the launch traced here: 132 us
  waiting for transfers between devices  44.3 us (33%)
  matrix products  32.2 us (24%)
  blocking collectives  32.2 us (24%)
  starting transfers between devices  13.5 us (10%)
  local copies, waits for them, and re-layouts  4.98 us (4%)
  other arithmetic  4.02 us (3%)
    ppermute x3, waiting for transfers between devices, shifted(): return lax.ppermute(block, axis, route)  33.6 us
    all_to_all x3, blocking collectives, from_stride(): lax.all_to_all(delta_moved, 'seq', split_axis=1, concat_axis=0, tiled=True)  32.2 us
    dot_general x4, matrix products, per_device(): lax.dot_general(incoming, weight_out, contract, preferred_element_type=jn...  9.98 us
    dot_general x4, matrix products, per_device(): lax.dot_general(delta_gate, weight_gate, contract, preferred_element_type...  9.32 us
    all_to_all x1, waiting for transfers between devices, from_stride(): lax.all_to_all(delta_moved, 'seq', split_axis=1, concat_axis=0, tiled=True)  6.44 us
    all_to_all x1, starting transfers between devices, to_stride(): lax.all_to_all(first_out, 'seq', split_axis=0, concat_axis=1, tiled=True)  5.3 us
    all_to_all x1, waiting for transfers between devices, to_stride(): lax.all_to_all(first_out, 'seq', split_axis=0, concat_axis=1, tiled=True)  4.25 us
    all_to_all x1, starting transfers between devices, from_stride(): lax.all_to_all(delta_moved, 'seq', split_axis=1, concat_axis=0, tiled=True)  4.11 us
  transfers between devices with their start and end apart: 5, of which 5 were waited for; matrix products, arithmetic and copies ran while one was open for 5% of the time, Pallas kernels for 0%

commit v1 on v0

v1 whole, which is shorter than its diff:
```python
import jax
import jax.numpy as jnp
from jax import lax
from jax.sharding import PartitionSpec as P

ROWS_BY_ROWS = (((1,), (1,)), ((), ()))


def dot(left, right):
    return jnp.dot(left, right, preferred_element_type=jnp.float32)


def dot_rows(left, right):
    return lax.dot_general(left, right, ROWS_BY_ROWS, preferred_element_type=jnp.float32)


def swap(block, offset):
    count = lax.axis_size("seq")
    return lax.ppermute(block, "seq", [(i, i ^ offset) for i in range(count)])


def exchange(send, count):
    half = send.shape[0] // 2
    piece = half // (count // 2)
    kept = send[:half]
    got = swap(send[half:], 1)
    parts = [kept[:piece], got[:piece]]
    for chip in range(1, count // 2):
        rows = slice(chip * piece, (chip + 1) * piece)
        parts.append(swap(jnp.concatenate([kept[rows], got[rows]]), 2 * chip))
    return jnp.concatenate(parts)


def block_diagonal(blocks):
    count, rows, columns = blocks.shape
    zero = jnp.zeros((rows, columns), blocks.dtype)
    return jnp.concatenate(
        [
            jnp.concatenate([blocks[k] if k == j else zero for j in range(count)], axis=1)
            for k in range(count)
        ],
        axis=0,
    )


def diagonal_blocks(matrix, count):
    rows, columns = matrix.shape[0] // count, matrix.shape[1] // count
    return jnp.stack(
        [
            matrix[k * rows : (k + 1) * rows, k * columns : (k + 1) * columns]
            for k in range(count)
        ]
    )


def per_device(section_inputs, cotangent, gain, w_gate, w_out, mix_first, mix_second):
    inputs = section_inputs[0]
    gain_row = gain[0]
    weight_gate = w_gate[0]
    weight_out = w_out[0]
    row_count, _ = inputs.shape
    local_blocks, block_rows = mix_first.shape[1:3]
    seq_count = lax.axis_size("seq")
    section_count = lax.axis_size("pipe")
    section_index = lax.axis_index("pipe")
    me = lax.axis_index("seq")
    steps = block_rows // seq_count

    position = jnp.arange(row_count)
    partner_send = position // (row_count // 2) + 2 * (
        position // (local_blocks * steps) % (seq_count // 2)
    )
    partner_recv = position // (local_blocks * steps)
    block = position // steps % local_blocks
    step = position % steps

    def first_rows(partner):
        return block * block_rows + (me ^ partner) * steps + step

    def second_rows(partner):
        return step * (seq_count * local_blocks) + (me ^ partner) * local_blocks + block

    def one_hot(rows):
        return (rows[:, None] == position[None, :]).astype(jnp.bfloat16)

    def permuted(rows, matrix):
        return dot(one_hot(rows), matrix).astype(jnp.bfloat16)

    first_full = block_diagonal(mix_first[0])
    second_full = block_diagonal(mix_second[0])
    first_send = permuted(first_rows(partner_send), first_full)
    first_recv = permuted(first_rows(partner_recv), first_full)
    second_send = permuted(second_rows(partner_send), second_full.T)
    second_recv = permuted(second_rows(partner_recv), second_full.T)

    features = inputs.astype(jnp.float32)
    inv_rms = lax.rsqrt(jnp.mean(features * features, axis=-1, keepdims=True) + 1e-06)
    unit_rows = features * inv_rms
    normed = (unit_rows * gain_row).astype(jnp.bfloat16)
    moved = exchange(dot(first_send, normed).astype(jnp.bfloat16), seq_count)
    gate_pre = dot(normed, weight_gate)
    sigma = jax.nn.sigmoid(gate_pre)
    mix_factor = gate_pre * sigma
    mixer_out = dot(second_recv.T, moved)
    gate_factor = mixer_out * sigma * (1.0 + gate_pre * (1.0 - sigma))

    incoming = cotangent
    outgoing_kept = jnp.zeros_like(cotangent)
    first_kept = jnp.zeros((row_count, row_count), jnp.float32)
    second_kept = jnp.zeros((row_count, row_count), jnp.float32)
    for tick_index in range(section_count):
        sender = section_count - 1 - tick_index
        active = section_index == sender
        delta_hidden = dot_rows(incoming, weight_out)
        delta_mix = (delta_hidden * mix_factor).astype(jnp.bfloat16)
        delta_gate = (delta_hidden * gate_factor).astype(jnp.bfloat16)
        delta_mid = exchange(dot(second_send, delta_mix).astype(jnp.bfloat16), seq_count)
        gate_back = dot_rows(delta_gate, weight_gate)
        first_back = dot(first_recv.T, delta_mid)
        delta_norm = (first_back + gate_back) * gain_row
        centred = delta_norm - unit_rows * jnp.mean(delta_norm * unit_rows, axis=-1, keepdims=True)
        outgoing = (incoming.astype(jnp.float32) + inv_rms * centred).astype(jnp.bfloat16)
        if sender > 0:
            incoming = lax.ppermute(outgoing, "pipe", [(sender, sender - 1)])
        outgoing_kept = jnp.where(active, outgoing, outgoing_kept)
        first_kept = jnp.where(active, dot_rows(delta_mid, normed), first_kept)
        second_kept = jnp.where(active, dot_rows(delta_mix, moved), second_kept)

    def unpermuted(rows, matrix):
        return jnp.dot(
            one_hot(rows).astype(jnp.float32).T,
            matrix,
            precision=lax.Precision.HIGHEST,
            preferred_element_type=jnp.float32,
        )

    grad_first = diagonal_blocks(unpermuted(first_rows(partner_recv), first_kept), local_blocks)
    grad_second = diagonal_blocks(
        unpermuted(second_rows(partner_recv), second_kept.T).T, local_blocks
    )
    return (outgoing_kept[None], grad_first[None], grad_second[None])


def solution(mesh):
    placed = (
        P("pipe", "seq", None),
        P("seq", None),
        P("pipe", None),
        P("pipe", None, None),
        P("pipe", None, None),
        P("pipe", "seq", None, None),
        P("pipe", "seq", None, None),
    )
    return jax.shard_map(
        per_device,
        mesh=mesh,
        in_specs=placed,
        out_specs=(
            P("pipe", "seq", None),
            P("pipe", "seq", None, None),
            P("pipe", "seq", None, None),
        ),
        check_vma=False,
    )
```

time: 133 us -> 113 us (0.85)
  blocking collectives: 32.2 us -> 0 us
  starting transfers between devices: 13.5 us -> 22.5 us
  other arithmetic: 4.02 us -> 8.77 us
  matrix products: 32.2 us -> 28.3 us
  local copies, waits for them, and re-layouts: 4.98 us -> 6.71 us
    all_to_all x3 -> x0, blocking collectives: 32.2 us -> none  [from_stride(): lax.all_to_all(delta_moved, 'seq', split_axis=1, concat_axis=0, tiled=True)]
    ppermute x3 -> x23, starting transfers between devices: 4.06 us -> 22.5 us  [the longest x20 19.6 us: swap(): return lax.ppermute(block, 'seq', [(i, i ^ offset) for i in range(count)])]
    ppermute x3 -> x23, waiting for transfers between devices: 33.6 us -> 44.7 us  [the longest x3 30.1 us: per_device(): incoming = lax.ppermute(outgoing, 'pipe', [(sender, sender - 1)])]
    all_to_all x2 -> x0, waiting for transfers between devices: 10.7 us -> none  [the longest x1 6.44 us: from_stride(): lax.all_to_all(delta_moved, 'seq', split_axis=1, concat_axis=0, tiled=True)]
    all_to_all x2 -> x0, starting transfers between devices: 9.41 us -> none  [the longest x1 5.3 us: to_stride(): lax.all_to_all(first_out, 'seq', split_axis=0, concat_axis=1, tiled=True)]
    dot_general x21 -> x31, matrix products: 32.2 us -> 28.3 us  [the longest x16 18.1 us: dot_rows(): lax.dot_general(left, right, ROWS_BY_ROWS, preferred_element_type=jnp.flo...]
    concatenate x0 -> x15, other arithmetic: none -> 2.84 us  [exchange(): parts.append(swap(jnp.concatenate([kept[rows], got[rows]]), 2 * chip))]
    slice x0 -> x15, local copies, waits for them, and re-layouts: none -> 2.77 us  [the longest x10 2.01 us: exchange(): parts.append(swap(jnp.concatenate([kept[rows], got[rows]]), 2 * chip))]
  transfers between devices with their start and end apart: 5 -> 23, of which waited for: 5 -> 10; matrix products, arithmetic and copies ran while one was open for 5% -> 22% of each run, Pallas kernels for 0% -> 0%
where the time goes in v1:
time: 113 us; the launch traced here: 112 us
  waiting for transfers between devices  44.7 us (40%)
  matrix products  28.3 us (25%)
  starting transfers between devices  22.5 us (20%)
  other arithmetic  8.77 us (8%)
  local copies, waits for them, and re-layouts  6.71 us (6%)
  between operations  1.39 us (1%)
    ppermute x3, waiting for transfers between devices, per_device(): incoming = lax.ppermute(outgoing, 'pipe', [(sender, sender - 1)])  30.1 us
    ppermute x20, starting transfers between devices, swap(): return lax.ppermute(block, 'seq', [(i, i ^ offset) for i in range(count)])  19.6 us
    dot_general x16, matrix products, dot_rows(): lax.dot_general(left, right, ROWS_BY_ROWS, preferred_element_type=jnp.flo...  18.1 us
    ppermute x20, waiting for transfers between devices, swap(): return lax.ppermute(block, 'seq', [(i, i ^ offset) for i in range(count)])  14.5 us
    dot_general x13, matrix products, dot(): return jnp.dot(left, right, preferred_element_type=jnp.float32)  9.63 us
    ppermute x3, starting transfers between devices, per_device(): incoming = lax.ppermute(outgoing, 'pipe', [(sender, sender - 1)])  2.84 us
    concatenate x15, other arithmetic, exchange(): parts.append(swap(jnp.concatenate([kept[rows], got[rows]]), 2 * chip))  2.84 us
    broadcast_in_dim x3, other arithmetic, per_device(): return (outgoing_kept[None], grad_first[None], grad_second[None])  2.47 us
  transfers between devices with their start and end apart: 23, of which 10 were waited for; matrix products, arithmetic and copies ran while one was open for 22% of the time, Pallas kernels for 0%

profile of v1, /device:TPU:0, one launch (start us, length us, event | category | flops | bytes accessed | tf_op | source)
XLA Modules:
  0.0 112.3 jit_solution(12814400928234945934)
XLA Ops:
  0.6 1.2 %fusion.55 = f32[128]{0:T(128)S(1)} fusion(bf16[1,128,1536]{2,1,0:T(8,128)(2,1)} %param.7), kind=kLoop, calls=%fused_computation.79 | loop fusion | flops 589696 | bytes 393728 | tf_op jit(solution)/shard_map/reduce_sum | solution.py:97
  1.9 0.7 slice_bitcast_fusion.7
  2.6 0.7 reduce
  3.3 1.4 %convolution_convert_fusion.3 = bf16[128,1536]{1,0:T(8,128)(2,1)S(1)} fusion(s32[128]{0:T(128)S(1)} %get-tuple-element.67, bf16[64,64]{1,0:T(8,128)(2,1)S(1)} %get-tuple-element.50, bf16[64,64]{1,0:T(8,128)(2,1)S(1)} %get-tuple-element.49, bf16[1,128,1536]{2,1,0:T(8,128)(2,1)} %param.7, f32[1536]{0:T(1024)S(1)} %reduce, f32[128]{0:T(128)S(1)} %add_rsqrt_fusion), kind=kOutput, calls=%fused_computation.31 | convolution fusion | flops 55672832 | bytes 809984 | tf_op jit(solution)/shard_map/dot_general | solution.py:10
  4.8 0.7 slice.251
  5.5 0.5 collective-permute-start.4
  6.0 1.1 slice_bitcast_fusion.5
  7.0 3.3 %fusion.8 = f32[128,1536]{1,0:T(8,128)S(1)} fusion(bf16[1,1536,1536]{2,1,0:T(8,128)(2,1)} %param.10, bf16[1,128,1536]{2,1,0:T(8,128)(2,1)} %param.7, f32[1536]{0:T(1024)S(1)} %reduce, f32[128]{0:T(128)S(1)} %add_rsqrt_fusion), kind=kOutput, calls=%fused_computation.8 | convolution fusion | flops 604766208 | bytes 5904896 | tf_op jit(solution)/shard_map/dot_general | solution.py:10
  10.6 1.7 %multiply_convert_fusion.7 = (bf16[128,1536]{1,0:T(8,128)(2,1)S(1)}, f32[128,1536]{1,0:T(8,128)S(1)}) fusion(f32[128,1536]{1,0:T(8,128)S(1)} %fusion.8, bf16[128,1536]{1,0:T(8,128)(2,1)S(1)} %copy-done.2, bf16[1,1536,1536]{2,1,0:T(8,128)(2,1)S(1)} %copy-done.7), kind=kOutput, calls=%fused_computation.89 | convolution fusion | flops 605159424 | bytes 7077888 | tf_op jit(solution)/shard_map/dot_general | solution.py:14
  12.7 0.5 add_add_fusion.1
  13.3 0.6 fusion.114
  13.9 0.6 fusion.113
  14.6 0.9 convolution_convert_fusion.8
  15.5 0.8 pad_maximum_fusion.3
  16.4 2.6 %collective-permute-start.5 = (bf16[32,1536]{1,0:T(8,128)(2,1)S(1)}, bf16[32,1536]{1,0:T(8,128)(2,1)S(1)}, u32[]{:S(2)}, u32[]{:S(2)}) collective-permute-start(bf16[32,1536]{1,0:T(8,128)(2,1)S(1)} %pad_maximum_fusion.3), channel_id=1, source_target_pairs={{0,8},{4,12},{8,0},{12,4},{16,24},{20,28},{24,16},{28,20},{1,9},{5... | collective-permute-start | bytes 294920 | tf_op jit(solution)/shard_map/ppermute | solution.py:19
  19.0 1.6 %collective-permute-start.6 = (bf16[32,1536]{1,0:T(8,128)(2,1)S(1)}, bf16[32,1536]{1,0:T(8,128)(2,1)S(1)}, u32[]{:S(2)}, u32[]{:S(2)}) collective-permute-start(bf16[32,1536]{1,0:T(8,128)(2,1)S(1)} %pad_maximum_fusion.4), channel_id=1, source_target_pairs={{0,16},{4,20},{8,24},{12,28},{16,0},{20,4},{24,8},{28,12},{1,17},{... | collective-permute-start | bytes 294920 | tf_op jit(solution)/shard_map/ppermute | solution.py:19
  20.6 0.6 fusion.118
  21.3 0.6 pad_maximum_fusion
  21.9 1.9 %collective-permute-start.1 = (bf16[32,1536]{1,0:T(8,128)(2,1)}, bf16[32,1536]{1,0:T(8,128)(2,1)S(1)}, u32[]{:S(2)}, u32[]{:S(2)}) collective-permute-start(bf16[32,1536]{1,0:T(8,128)(2,1)} %pad_maximum_fusion), channel_id=1, source_target_pairs={{0,8},{4,12},{8,0},{12,4},{16,24},{20,28},{24,16},{28,20},{1,9},{5... | collective-permute-start | bytes 294920 | tf_op jit(solution)/shard_map/ppermute | solution.py:19
  23.9 0.7 pad_maximum_fusion.1
  24.5 1.5 %collective-permute-start.2 = (bf16[32,1536]{1,0:T(8,128)(2,1)}, bf16[32,1536]{1,0:T(8,128)(2,1)}, u32[]{:S(2)}, u32[]{:S(2)}) collective-permute-start(bf16[32,1536]{1,0:T(8,128)(2,1)} %pad_maximum_fusion.1), channel_id=1, source_target_pairs={{0,16},{4,20},{8,24},{12,28},{16,0},{20,4},{24,8},{28,12},{1,17},{... | collective-permute-start | bytes 294920 | tf_op jit(solution)/shard_map/ppermute | solution.py:19
  26.0 0.7 pad_maximum_fusion.2
  26.8 1.2 %fusion.21 = f32[128,1536]{1,0:T(8,128)S(1)} fusion(bf16[128,1536]{1,0:T(8,128)(2,1)S(1)} %constant_dynamic-update-slice_fusion.5, f32[128,1536]{1,0:T(8,128)S(1)} %fusion.8, s32[128]{0:T(128)} %add_add_fusion.1, bf16[64,64]{1,0:T(8,128)(2,1)S(1)} %get-tuple-element.48, bf16[64,64]{1,0:T(8,128)(2,1)S(1)} %get-tuple-element.47), kind=kOutput, calls=%fused_computation.25 | convolution fusion | flops 56262656 | bytes 1982976 | tf_op jit(solution)/shard_map/dot_general | solution.py:10
  28.1 4.1 %fusion.6 = f32[128,1536]{1,0:T(8,128)S(1)} fusion(bf16[1,1536,1536]{2,1,0:T(8,128)(2,1)} %param.10, f32[128,1536]{1,0:T(8,128)S(1)} %get-tuple-element.52, f32[128,1536]{1,0:T(8,128)S(1)} %fusion.21), kind=kOutput, calls=%fused_computation.6 | convolution fusion | flops 604372992 | bytes 7077888 | tf_op jit(solution)/shard_map/dot_general | solution.py:14
  32.3 0.9 constant_dynamic-update-slice_fusion.1
  33.2 0.9 constant_dynamic-update-slice_fusion
  34.1 0.4 fusion.35
  34.8 0.7 collective-permute-start.8
  35.8 0.3 convolution_select_fusion.4
  36.2 1.7 %multiply_convert_fusion.5 = (bf16[128,1536]{1,0:T(8,128)(2,1)S(1)}, f32[128,1536]{1,0:T(8,128)S(1)}) fusion(f32[128,1536]{1,0:T(8,128)S(1)} %fusion.8, bf16[128,1536]{1,0:T(8,128)(2,1)S(1)} %collective-permute-done.8, bf16[1,1536,1536]{2,1,0:T(8,128)(2,1)S(1)} %bitcast.168), kind=kOutput, calls=%fused_computation.87 | convolution fusion | flops 605159424 | bytes 7077888 | tf_op jit(solution)/shard_map/dot_general | solution.py:14
  38.3 1.6 %fusion.4 = f32[128,1536]{1,0:T(8,128)S(1)} fusion(bf16[1,1536,1536]{2,1,0:T(8,128)(2,1)S(1)} %bitcast.166, f32[128,1536]{1,0:T(8,128)S(1)} %get-tuple-element.56, f32[128,1536]{1,0:T(8,128)S(1)} %fusion.21), kind=kOutput, calls=%fused_computation.4 | convolution fusion | flops 604372992 | bytes 7077888 | tf_op jit(solution)/shard_map/dot_general | solution.py:14
  39.9 2.0 %collective-permute-start.10 = (bf16[32,1536]{1,0:T(8,128)(2,1)S(1)}, bf16[32,1536]{1,0:T(8,128)(2,1)S(1)}, u32[]{:S(2)}, u32[]{:S(2)}) collective-permute-start(bf16[32,1536]{1,0:T(8,128)(2,1)S(1)} %pad_maximum_fusion.6), channel_id=1, source_target_pairs={{0,8},{4,12},{8,0},{12,4},{16,24},{20,28},{24,16},{28,20},{1,9},{5... | collective-permute-start | bytes 294920 | tf_op jit(solution)/shard_map/ppermute | solution.py:19
  42.0 1.6 %collective-permute-start.11 = (bf16[32,1536]{1,0:T(8,128)(2,1)S(1)}, bf16[32,1536]{1,0:T(8,128)(2,1)S(1)}, u32[]{:S(2)}, u32[]{:S(2)}) collective-permute-start(bf16[32,1536]{1,0:T(8,128)(2,1)S(1)} %pad_maximum_fusion.7), channel_id=1, source_target_pairs={{0,16},{4,20},{8,24},{12,28},{16,0},{20,4},{24,8},{28,12},{1,17},{... | collective-permute-start | bytes 294920 | tf_op jit(solution)/shard_map/ppermute | solution.py:19
  43.6 1.8 %collective-permute-done.10 = bf16[32,1536]{1,0:T(8,128)(2,1)S(1)} collective-permute-done((bf16[32,1536]{1,0:T(8,128)(2,1)S(1)}, bf16[32,1536]{1,0:T(8,128)(2,1)S(1)}, u32[]{:S(2)}, u32[]{:S(2)}) %collective-permute-start.10) | collective-permute-done | bytes 98336 | tf_op jit(solution)/shard_map/ppermute | solution.py:19
  45.4 2.7 %collective-permute-done.11 = bf16[32,1536]{1,0:T(8,128)(2,1)S(1)} collective-permute-done((bf16[32,1536]{1,0:T(8,128)(2,1)S(1)}, bf16[32,1536]{1,0:T(8,128)(2,1)S(1)}, u32[]{:S(2)}, u32[]{:S(2)}) %collective-permute-start.11) | collective-permute-done | bytes 98336 | tf_op jit(solution)/shard_map/ppermute | solution.py:19
  48.1 1.1 collective-permute-done.12
  49.1 0.4 fusion.40
  49.9 0.7 collective-permute-start.13
  50.8 0.3 convolution_select_fusion.5
  51.2 1.7 %multiply_convert_fusion.3 = (bf16[128,1536]{1,0:T(8,128)(2,1)S(1)}, f32[128,1536]{1,0:T(8,128)S(1)}) fusion(f32[128,1536]{1,0:T(8,128)S(1)} %fusion.8, bf16[128,1536]{1,0:T(8,128)(2,1)S(1)} %collective-permute-done.13, bf16[1,1536,1536]{2,1,0:T(8,128)(2,1)S(1)} %bitcast.168), kind=kOutput, calls=%fused_computation.85 | convolution fusion | flops 605159424 | bytes 7077888 | tf_op jit(solution)/shard_map/dot_general | solution.py:14
  53.2 1.6 %fusion.2 = f32[128,1536]{1,0:T(8,128)S(1)} fusion(bf16[1,1536,1536]{2,1,0:T(8,128)(2,1)S(1)} %bitcast.166, f32[128,1536]{1,0:T(8,128)S(1)} %get-tuple-element.60, f32[128,1536]{1,0:T(8,128)S(1)} %fusion.21), kind=kOutput, calls=%fused_computation.2 | convolution fusion | flops 604372992 | bytes 7077888 | tf_op jit(solution)/shard_map/dot_general | solution.py:14
  54.9 1.1 %collective-permute-start.15 = (bf16[32,1536]{1,0:T(8,128)(2,1)S(1)}, bf16[32,1536]{1,0:T(8,128)(2,1)S(1)}, u32[]{:S(2)}, u32[]{:S(2)}) collective-permute-start(bf16[32,1536]{1,0:T(8,128)(2,1)S(1)} %pad_maximum_fusion.9), channel_id=1, source_target_pairs={{0,8},{4,12},{8,0},{12,4},{16,24},{20,28},{24,16},{28,20},{1,9},{5... | collective-permute-start | bytes 294920 | tf_op jit(solution)/shard_map/ppermute | solution.py:19
  56.1 1.0 collective-permute-start.16
  57.1 1.6 %collective-permute-start.17 = (bf16[32,1536]{1,0:T(8,128)(2,1)S(1)}, bf16[32,1536]{1,0:T(8,128)(2,1)S(1)}, u32[]{:S(2)}, u32[]{:S(2)}) collective-permute-start(bf16[32,1536]{1,0:T(8,128)(2,1)S(1)} %pad_maximum_fusion.11), channel_id=1, source_target_pairs={{0,24},{4,28},{8,16},{12,20},{16,8},{20,12},{24,0},{28,4},{1,25},{... | collective-permute-start | bytes 294920 | tf_op jit(solution)/shard_map/ppermute | solution.py:19
  58.6 1.6 %collective-permute-done.15 = bf16[32,1536]{1,0:T(8,128)(2,1)S(1)} collective-permute-done((bf16[32,1536]{1,0:T(8,128)(2,1)S(1)}, bf16[32,1536]{1,0:T(8,128)(2,1)S(1)}, u32[]{:S(2)}, u32[]{:S(2)}) %collective-permute-start.15) | collective-permute-done | bytes 98336 | tf_op jit(solution)/shard_map/ppermute | solution.py:19
  60.2 1.4 %collective-permute-done.16 = bf16[32,1536]{1,0:T(8,128)(2,1)S(1)} collective-permute-done((bf16[32,1536]{1,0:T(8,128)(2,1)S(1)}, bf16[32,1536]{1,0:T(8,128)(2,1)S(1)}, u32[]{:S(2)}, u32[]{:S(2)}) %collective-permute-start.16) | collective-permute-done | bytes 98336 | tf_op jit(solution)/shard_map/ppermute | solution.py:19
  61.6 1.6 %collective-permute-done.17 = bf16[32,1536]{1,0:T(8,128)(2,1)S(1)} collective-permute-done((bf16[32,1536]{1,0:T(8,128)(2,1)S(1)}, bf16[32,1536]{1,0:T(8,128)(2,1)S(1)}, u32[]{:S(2)}, u32[]{:S(2)}) %collective-permute-start.17) | collective-permute-done | bytes 98336 | tf_op jit(solution)/shard_map/ppermute | solution.py:19
  63.2 0.4 fusion.45
  63.9 1.5 %collective-permute-start.18 = (bf16[128,1536]{1,0:T(8,128)(2,1)S(1)}, bf16[128,1536]{1,0:T(8,128)(2,1)S(1)}, u32[]{:S(2)}, u32[]{:S(2)}) collective-permute-start(bf16[128,1536]{1,0:T(8,128)(2,1)S(1)} %fusion.49), channel_id=1, source_target_pairs={{1,0},{5,4},{9,8},{13,12},{17,16},{21,20},{25,24},{29,28}} | collective-permute-start | bytes 1179656 | tf_op jit(solution)/shard_map/ppermute | solution.py:124
  65.7 0.3 convolution_select_fusion.6
  66.0 30.1 %collective-permute-done.18 = bf16[128,1536]{1,0:T(8,128)(2,1)S(1)} collective-permute-done((bf16[128,1536]{1,0:T(8,128)(2,1)S(1)}, bf16[128,1536]{1,0:T(8,128)(2,1)S(1)}, u32[]{:S(2)}, u32[]{:S(2)}) %collective-permute-start.18) | collective-permute-done | bytes 393248 | tf_op jit(solution)/shard_map/ppermute | solution.py:124
  96.1 1.6 %multiply_convert_fusion.1 = (bf16[128,1536]{1,0:T(8,128)(2,1)S(1)}, f32[128,1536]{1,0:T(8,128)S(1)}) fusion(f32[128,1536]{1,0:T(8,128)S(1)} %fusion.8, bf16[128,1536]{1,0:T(8,128)(2,1)S(1)} %collective-permute-done.18, bf16[1,1536,1536]{2,1,0:T(8,128)(2,1)S(1)} %bitcast.168), kind=kOutput, calls=%fused_computation.83 | convolution fusion | flops 605159424 | bytes 7077888 | tf_op jit(solution)/shard_map/dot_general | solution.py:14
  98.6 1.6 %fusion = f32[128,1536]{1,0:T(8,128)S(1)} fusion(bf16[1,1536,1536]{2,1,0:T(8,128)(2,1)S(1)} %bitcast.166, f32[128,1536]{1,0:T(8,128)S(1)} %get-tuple-element.64, f32[128,1536]{1,0:T(8,128)S(1)} %fusion.21), kind=kOutput, calls=%fused_computation | convolution fusion | flops 604372992 | bytes 7077888 | tf_op jit(solution)/shard_map/dot_general | solution.py:14
  100.4 0.6 maximum_bitcast_fusion.1
  101.1 0.7 collective-permute-done.19
  101.9 1.8 %collective-permute-start.21 = (bf16[32,1536]{1,0:T(8,128)(2,1)S(1)}, bf16[32,1536]{1,0:T(8,128)(2,1)S(1)}, u32[]{:S(2)}, u32[]{:S(2)}) collective-permute-start(bf16[32,1536]{1,0:T(8,128)(2,1)S(1)} %pad_maximum_fusion.13), channel_id=1, source_target_pairs={{0,16},{4,20},{8,24},{12,28},{16,0},{20,4},{24,8},{28,12},{1,17},{... | collective-permute-start | bytes 294920 | tf_op jit(solution)/shard_map/ppermute | solution.py:19
  103.8 1.7 %collective-permute-start.22 = (bf16[32,1536]{1,0:T(8,128)(2,1)S(1)}, bf16[32,1536]{1,0:T(8,128)(2,1)S(1)}, u32[]{:S(2)}, u32[]{:S(2)}) collective-permute-start(bf16[32,1536]{1,0:T(8,128)(2,1)S(1)} %pad_maximum_fusion.14), channel_id=1, source_target_pairs={{0,24},{4,28},{8,16},{12,20},{16,8},{20,12},{24,0},{28,4},{1,25},{... | collective-permute-start | bytes 294920 | tf_op jit(solution)/shard_map/ppermute | solution.py:19
  105.5 2.0 %collective-permute-done.20 = bf16[32,1536]{1,0:T(8,128)(2,1)S(1)} collective-permute-done((bf16[32,1536]{1,0:T(8,128)(2,1)S(1)}, bf16[32,1536]{1,0:T(8,128)(2,1)S(1)}, u32[]{:S(2)}, u32[]{:S(2)}) %collective-permute-start.20) | collective-permute-done | bytes 98336 | tf_op jit(solution)/shard_map/ppermute | solution.py:19
  107.5 1.8 %collective-permute-done.22 = bf16[32,1536]{1,0:T(8,128)(2,1)S(1)} collective-permute-done((bf16[32,1536]{1,0:T(8,128)(2,1)S(1)}, bf16[32,1536]{1,0:T(8,128)(2,1)S(1)}, u32[]{:S(2)}, u32[]{:S(2)}) %collective-permute-start.22) | collective-permute-done | bytes 98336 | tf_op jit(solution)/shard_map/ppermute | solution.py:19
  109.3 0.4 fusion.50
  109.7 0.3 convolution_select_fusion.7
  110.1 0.3 fusion.70
  110.5 0.6 maximum_bitcast_fusion
  111.1 1.2 %fusion.62 = bf16[1,128,1536]{2,1,0:T(8,128)(2,1)} fusion(f32[128,1536]{1,0:T(8,128)S(1)} %get-tuple-element.66, bf16[1,128,1536]{2,1,0:T(8,128)(2,1)S(1)} %copy-done, bf16[128,1536]{1,0:T(8,128)(2,1)S(1)} %collective-permute-done.18, bf16[128,1536]{1,0:T(8,128)(2,1)S(1)} %fusion.49, bf16[128,1536]{1,0:T(8,128)(2,1)S(1)} %fusion.44, ...), kind=kLoop, calls=%fused_computation.94 | loop fusion | flops 2359296 | bytes 3146756 | tf_op jit(solution)/shard_map/broadcast_in_dim | solution.py:141
  (104 shorter events, 4.8 us)
Async XLA Ops:
  0.6 9.9 %copy-start.2 = (bf16[128,1536]{1,0:T(8,128)(2,1)S(1)}, bf16[128,1536]{1,0:T(8,128)(2,1)}, u32[]{:S(2)}) copy-start(bf16[128,1536]{1,0:T(8,128)(2,1)} %param.8) | copy-start | bytes 1179652
  2.6 2.2 %copy-start.4 = (bf16[64,64]{1,0:T(8,128)(2,1)}, bf16[64,64]{1,0:T(8,128)(2,1)S(1)}, u32[]{:S(2)}) copy-start(bf16[64,64]{1,0:T(8,128)(2,1)S(1)} %get-tuple-element.49) | copy-start | bytes 24580
  2.6 2.2 %copy-start.5 = (bf16[64,64]{1,0:T(8,128)(2,1)}, bf16[64,64]{1,0:T(8,128)(2,1)S(1)}, u32[]{:S(2)}) copy-start(bf16[64,64]{1,0:T(8,128)(2,1)S(1)} %get-tuple-element.50) | copy-start | bytes 24580
  4.8 5.8 %copy-start.7 = (bf16[1,1536,1536]{2,1,0:T(8,128)(2,1)S(1)}, bf16[1,1536,1536]{2,1,0:T(8,128)(2,1)}, u32[]{:S(2)}) copy-start(bf16[1,1536,1536]{2,1,0:T(8,128)(2,1)} %param.11) | copy-start | bytes 14155780
  5.5 10.0 %collective-permute-start.4 = (bf16[64,1536]{1,0:T(8,128)(2,1)}, bf16[64,1536]{1,0:T(8,128)(2,1)S(1)}, u32[]{:S(2)}, u32[]{:S(2)}) collective-permute-start(bf16[64,1536]{1,0:T(8,128)(2,1)} %slice.251), channel_id=1, source_target_pairs={{0,4},{4,0},{8,12},{12,8},{16,20},{20,16},{24,28},{28,24},{1,5},{5... | collective-permute-start | bytes 589832 | tf_op jit(solution)/shard_map/ppermute | solution.py:19
  12.5 8.1 %collective-permute-start = (bf16[64,1536]{1,0:T(8,128)(2,1)S(1)}, bf16[64,1536]{1,0:T(8,128)(2,1)S(1)}, u32[]{:S(2)}, u32[]{:S(2)}) collective-permute-start(bf16[64,1536]{1,0:T(8,128)(2,1)S(1)} %slice.242), channel_id=1, source_target_pairs={{0,4},{4,0},{8,12},{12,8},{16,20},{20,16},{24,28},{28,24},{1,5},{5... | collective-permute-start | bytes 589832 | tf_op jit(solution)/shard_map/ppermute | solution.py:19
  16.4 10.3 %collective-permute-start.5 = (bf16[32,1536]{1,0:T(8,128)(2,1)S(1)}, bf16[32,1536]{1,0:T(8,128)(2,1)S(1)}, u32[]{:S(2)}, u32[]{:S(2)}) collective-permute-start(bf16[32,1536]{1,0:T(8,128)(2,1)S(1)} %pad_maximum_fusion.3), channel_id=1, source_target_pairs={{0,8},{4,12},{8,0},{12,4},{16,24},{20,28},{24,16},{28,20},{1,9},{5... | collective-permute-start | bytes 294920 | tf_op jit(solution)/shard_map/ppermute | solution.py:19
  19.0 7.8 %collective-permute-start.6 = (bf16[32,1536]{1,0:T(8,128)(2,1)S(1)}, bf16[32,1536]{1,0:T(8,128)(2,1)S(1)}, u32[]{:S(2)}, u32[]{:S(2)}) collective-permute-start(bf16[32,1536]{1,0:T(8,128)(2,1)S(1)} %pad_maximum_fusion.4), channel_id=1, source_target_pairs={{0,16},{4,20},{8,24},{12,28},{16,0},{20,4},{24,8},{28,12},{1,17},{... | collective-permute-start | bytes 294920 | tf_op jit(solution)/shard_map/ppermute | solution.py:19
  20.6 6.2 %collective-permute-start.7 = (bf16[32,1536]{1,0:T(8,128)(2,1)S(1)}, bf16[32,1536]{1,0:T(8,128)(2,1)S(1)}, u32[]{:S(2)}, u32[]{:S(2)}) collective-permute-start(bf16[32,1536]{1,0:T(8,128)(2,1)S(1)} %pad_maximum_fusion.5), channel_id=1, source_target_pairs={{0,24},{4,28},{8,16},{12,20},{16,8},{20,12},{24,0},{28,4},{1,25},{... | collective-permute-start | bytes 294920 | tf_op jit(solution)/shard_map/ppermute | solution.py:19
  21.9 10.3 %collective-permute-start.1 = (bf16[32,1536]{1,0:T(8,128)(2,1)}, bf16[32,1536]{1,0:T(8,128)(2,1)S(1)}, u32[]{:S(2)}, u32[]{:S(2)}) collective-permute-start(bf16[32,1536]{1,0:T(8,128)(2,1)} %pad_maximum_fusion), channel_id=1, source_target_pairs={{0,8},{4,12},{8,0},{12,4},{16,24},{20,28},{24,16},{28,20},{1,9},{5... | collective-permute-start | bytes 294920 | tf_op jit(solution)/shard_map/ppermute | solution.py:19
  24.5 7.8 %collective-permute-start.2 = (bf16[32,1536]{1,0:T(8,128)(2,1)}, bf16[32,1536]{1,0:T(8,128)(2,1)}, u32[]{:S(2)}, u32[]{:S(2)}) collective-permute-start(bf16[32,1536]{1,0:T(8,128)(2,1)} %pad_maximum_fusion.1), channel_id=1, source_target_pairs={{0,16},{4,20},{8,24},{12,28},{16,0},{20,4},{24,8},{28,12},{1,17},{... | collective-permute-start | bytes 294920 | tf_op jit(solution)/shard_map/ppermute | solution.py:19
  26.7 6.5 %collective-permute-start.3 = (bf16[32,1536]{1,0:T(8,128)(2,1)}, bf16[32,1536]{1,0:T(8,128)(2,1)}, u32[]{:S(2)}, u32[]{:S(2)}) collective-permute-start(bf16[32,1536]{1,0:T(8,128)(2,1)} %pad_maximum_fusion.2), channel_id=1, source_target_pairs={{0,24},{4,28},{8,16},{12,20},{16,8},{20,12},{24,0},{28,4},{1,25},{... | collective-permute-start | bytes 294920 | tf_op jit(solution)/shard_map/ppermute | solution.py:19
  28.0 4.2 %copy-start.1 = (bf16[128,1536]{1,0:T(8,128)(2,1)S(1)}, bf16[128,1536]{1,0:T(8,128)(2,1)}, u32[]{:S(2)}) copy-start(bf16[128,1536]{1,0:T(8,128)(2,1)} %get-tuple-element.38) | copy-start | bytes 1179652
  28.0 6.1 %copy-start = (bf16[1,128,1536]{2,1,0:T(8,128)(2,1)S(1)}, bf16[1,128,1536]{2,1,0:T(8,128)(2,1)}, u32[]{:S(2)}) copy-start(bf16[1,128,1536]{2,1,0:T(8,128)(2,1)} %param.7) | copy-start | bytes 1179652
  28.0 8.1 %slice-start.2 = ((s8[4718592]{0:T(1024)(128)(4,1)}), s8[4194304]{0:T(1024)(128)(4,1)S(1)}, s32[]{:S(2)}) async-start(s8[4718592]{0:T(1024)(128)(4,1)} %bitcast.167), calls=%async_computation.2 | async-start | bytes 8388608
  28.0 6.4 %copy-start.3 = (bf16[128,1536]{1,0:T(8,128)(2,1)S(1)}, bf16[128,1536]{1,0:T(8,128)(2,1)}, u32[]{:S(2)}) copy-start(bf16[128,1536]{1,0:T(8,128)(2,1)} %param.8) | copy-start | bytes 1179652
  28.1 8.1 %slice-start.3 = ((s8[4718592]{0:T(1024)(128)(4,1)}), s8[524288]{0:T(1024)(128)(4,1)S(1)}, s32[]{:S(2)}) async-start(s8[4718592]{0:T(1024)(128)(4,1)} %bitcast.167), calls=%async_computation.3 | async-start | bytes 1048576
  34.8 1.3 %collective-permute-start.8 = (bf16[128,1536]{1,0:T(8,128)(2,1)S(1)}, bf16[128,1536]{1,0:T(8,128)(2,1)S(1)}, u32[]{:S(2)}, u32[]{:S(2)}) collective-permute-start(bf16[128,1536]{1,0:T(8,128)(2,1)S(1)} %fusion.39), channel_id=1, source_target_pairs={{3,2},{7,6},{11,10},{15,14},{19,18},{23,22},{27,26},{31,30}} | collective-permute-start | bytes 1179656 | tf_op jit(solution)/shard_map/ppermute | solution.py:124
  35.8 2.5 %slice-start = ((s8[4718592]{0:T(1024)(128)(4,1)}), s8[4194304]{0:T(1024)(128)(4,1)S(1)}, s32[]{:S(2)}) async-start(s8[4718592]{0:T(1024)(128)(4,1)} %bitcast.165), calls=%async_computation | async-start | bytes 8388608
  36.1 2.1 %slice-start.1 = ((s8[4718592]{0:T(1024)(128)(4,1)}), s8[524288]{0:T(1024)(128)(4,1)S(1)}, s32[]{:S(2)}) async-start(s8[4718592]{0:T(1024)(128)(4,1)} %bitcast.165), calls=%async_computation.1 | async-start | bytes 1048576
  38.2 1.7 %collective-permute-start.9 = (bf16[64,1536]{1,0:T(8,128)(2,1)S(1)}, bf16[64,1536]{1,0:T(8,128)(2,1)S(1)}, u32[]{:S(2)}, u32[]{:S(2)}) collective-permute-start(bf16[64,1536]{1,0:T(8,128)(2,1)S(1)} %slice.260), channel_id=1, source_target_pairs={{0,4},{4,0},{8,12},{12,8},{16,20},{20,16},{24,28},{28,24},{1,5},{5... | collective-permute-start | bytes 589832 | tf_op jit(solution)/shard_map/ppermute | solution.py:19
  39.9 5.4 %collective-permute-start.10 = (bf16[32,1536]{1,0:T(8,128)(2,1)S(1)}, bf16[32,1536]{1,0:T(8,128)(2,1)S(1)}, u32[]{:S(2)}, u32[]{:S(2)}) collective-permute-start(bf16[32,1536]{1,0:T(8,128)(2,1)S(1)} %pad_maximum_fusion.6), channel_id=1, source_target_pairs={{0,8},{4,12},{8,0},{12,4},{16,24},{20,28},{24,16},{28,20},{1,9},{5... | collective-permute-start | bytes 294920 | tf_op jit(solution)/shard_map/ppermute | solution.py:19
  42.0 6.1 %collective-permute-start.11 = (bf16[32,1536]{1,0:T(8,128)(2,1)S(1)}, bf16[32,1536]{1,0:T(8,128)(2,1)S(1)}, u32[]{:S(2)}, u32[]{:S(2)}) collective-permute-start(bf16[32,1536]{1,0:T(8,128)(2,1)S(1)} %pad_maximum_fusion.7), channel_id=1, source_target_pairs={{0,16},{4,20},{8,24},{12,28},{16,0},{20,4},{24,8},{28,12},{1,17},{... | collective-permute-start | bytes 294920 | tf_op jit(solution)/shard_map/ppermute | solution.py:19
  43.5 5.6 %collective-permute-start.12 = (bf16[32,1536]{1,0:T(8,128)(2,1)S(1)}, bf16[32,1536]{1,0:T(8,128)(2,1)S(1)}, u32[]{:S(2)}, u32[]{:S(2)}) collective-permute-start(bf16[32,1536]{1,0:T(8,128)(2,1)S(1)} %pad_maximum_fusion.8), channel_id=1, source_target_pairs={{0,24},{4,28},{8,16},{12,20},{16,8},{20,12},{24,0},{28,4},{1,25},{... | collective-permute-start | bytes 294920 | tf_op jit(solution)/shard_map/ppermute | solution.py:19
  49.9 1.3 %collective-permute-start.13 = (bf16[128,1536]{1,0:T(8,128)(2,1)S(1)}, bf16[128,1536]{1,0:T(8,128)(2,1)S(1)}, u32[]{:S(2)}, u32[]{:S(2)}) collective-permute-start(bf16[128,1536]{1,0:T(8,128)(2,1)S(1)} %fusion.44), channel_id=1, source_target_pairs={{2,1},{6,5},{10,9},{14,13},{18,17},{22,21},{26,25},{30,29}} | collective-permute-start | bytes 1179656 | tf_op jit(solution)/shard_map/ppermute | solution.py:124
  53.1 1.7 %collective-permute-start.14 = (bf16[64,1536]{1,0:T(8,128)(2,1)S(1)}, bf16[64,1536]{1,0:T(8,128)(2,1)S(1)}, u32[]{:S(2)}, u32[]{:S(2)}) collective-permute-start(bf16[64,1536]{1,0:T(8,128)(2,1)S(1)} %slice.269), channel_id=1, source_target_pairs={{0,4},{4,0},{8,12},{12,8},{16,20},{20,16},{24,28},{28,24},{1,5},{5... | collective-permute-start | bytes 589832 | tf_op jit(solution)/shard_map/ppermute | solution.py:19
  54.9 5.3 %collective-permute-start.15 = (bf16[32,1536]{1,0:T(8,128)(2,1)S(1)}, bf16[32,1536]{1,0:T(8,128)(2,1)S(1)}, u32[]{:S(2)}, u32[]{:S(2)}) collective-permute-start(bf16[32,1536]{1,0:T(8,128)(2,1)S(1)} %pad_maximum_fusion.9), channel_id=1, source_target_pairs={{0,8},{4,12},{8,0},{12,4},{16,24},{20,28},{24,16},{28,20},{1,9},{5... | collective-permute-start | bytes 294920 | tf_op jit(solution)/shard_map/ppermute | solution.py:19
  56.1 5.5 %collective-permute-start.16 = (bf16[32,1536]{1,0:T(8,128)(2,1)S(1)}, bf16[32,1536]{1,0:T(8,128)(2,1)S(1)}, u32[]{:S(2)}, u32[]{:S(2)}) collective-permute-start(bf16[32,1536]{1,0:T(8,128)(2,1)S(1)} %pad_maximum_fusion.10), channel_id=1, source_target_pairs={{0,16},{4,20},{8,24},{12,28},{16,0},{20,4},{24,8},{28,12},{1,17},{... | collective-permute-start | bytes 294920 | tf_op jit(solution)/shard_map/ppermute | solution.py:19
  57.1 6.1 %collective-permute-start.17 = (bf16[32,1536]{1,0:T(8,128)(2,1)S(1)}, bf16[32,1536]{1,0:T(8,128)(2,1)S(1)}, u32[]{:S(2)}, u32[]{:S(2)}) collective-permute-start(bf16[32,1536]{1,0:T(8,128)(2,1)S(1)} %pad_maximum_fusion.11), channel_id=1, source_target_pairs={{0,24},{4,28},{8,16},{12,20},{16,8},{20,12},{24,0},{28,4},{1,25},{... | collective-permute-start | bytes 294920 | tf_op jit(solution)/shard_map/ppermute | solution.py:19
  63.9 32.2 %collective-permute-start.18 = (bf16[128,1536]{1,0:T(8,128)(2,1)S(1)}, bf16[128,1536]{1,0:T(8,128)(2,1)S(1)}, u32[]{:S(2)}, u32[]{:S(2)}) collective-permute-start(bf16[128,1536]{1,0:T(8,128)(2,1)S(1)} %fusion.49), channel_id=1, source_target_pairs={{1,0},{5,4},{9,8},{13,12},{17,16},{21,20},{25,24},{29,28}} | collective-permute-start | bytes 1179656 | tf_op jit(solution)/shard_map/ppermute | solution.py:124
  66.0 32.4 %copy-start.6 = (s32[128]{0:T(128)S(1)}, s32[128]{0:T(128)}, u32[]{:S(2)}) copy-start(s32[128]{0:T(128)} %add_add_fusion.1) | copy-start | bytes 1540
  100.3 1.5 %collective-permute-start.19 = (bf16[64,1536]{1,0:T(8,128)(2,1)S(1)}, bf16[64,1536]{1,0:T(8,128)(2,1)S(1)}, u32[]{:S(2)}, u32[]{:S(2)}) collective-permute-start(bf16[64,1536]{1,0:T(8,128)(2,1)S(1)} %slice.278), channel_id=1, source_target_pairs={{0,4},{4,0},{8,12},{12,8},{16,20},{20,16},{24,28},{28,24},{1,5},{5... | collective-permute-start | bytes 589832 | tf_op jit(solution)/shard_map/ppermute | solution.py:19
  101.8 5.7 %collective-permute-start.20 = (bf16[32,1536]{1,0:T(8,128)(2,1)S(1)}, bf16[32,1536]{1,0:T(8,128)(2,1)S(1)}, u32[]{:S(2)}, u32[]{:S(2)}) collective-permute-start(bf16[32,1536]{1,0:T(8,128)(2,1)S(1)} %pad_maximum_fusion.12), channel_id=1, source_target_pairs={{0,8},{4,12},{8,0},{12,4},{16,24},{20,28},{24,16},{28,20},{1,9},{5... | collective-permute-start | bytes 294920 | tf_op jit(solution)/shard_map/ppermute | solution.py:19
  101.9 5.6 %collective-permute-start.21 = (bf16[32,1536]{1,0:T(8,128)(2,1)S(1)}, bf16[32,1536]{1,0:T(8,128)(2,1)S(1)}, u32[]{:S(2)}, u32[]{:S(2)}) collective-permute-start(bf16[32,1536]{1,0:T(8,128)(2,1)S(1)} %pad_maximum_fusion.13), channel_id=1, source_target_pairs={{0,16},{4,20},{8,24},{12,28},{16,0},{20,4},{24,8},{28,12},{1,17},{... | collective-permute-start | bytes 294920 | tf_op jit(solution)/shard_map/ppermute | solution.py:19
  103.8 5.6 %collective-permute-start.22 = (bf16[32,1536]{1,0:T(8,128)(2,1)S(1)}, bf16[32,1536]{1,0:T(8,128)(2,1)S(1)}, u32[]{:S(2)}, u32[]{:S(2)}) collective-permute-start(bf16[32,1536]{1,0:T(8,128)(2,1)S(1)} %pad_maximum_fusion.14), channel_id=1, source_target_pairs={{0,24},{4,28},{8,16},{12,20},{16,8},{20,12},{24,0},{28,4},{1,25},{... | collective-permute-start | bytes 294920 | tf_op jit(solution)/shard_map/ppermute | solution.py:19

commit v2 on v1

v2 whole, which is shorter than its diff:
```python
import functools

import jax
import jax.numpy as jnp
from jax import lax
from jax.experimental import pallas as pl
from jax.experimental.pallas import tpu as pltpu
from jax.sharding import PartitionSpec as P

ROWS_BY_ROWS = (((1,), (1,)), ((), ()))
WHOLE = pl.BlockSpec(memory_space=pltpu.VMEM)
ANYWHERE = pl.BlockSpec(memory_space=pl.ANY)
SCALAR = pl.BlockSpec(memory_space=pltpu.SMEM)
PARAMS = pltpu.CompilerParams(vmem_limit_bytes=12 << 20)


def dot(left, right):
    return jnp.dot(left, right, preferred_element_type=jnp.float32)


def dot_rows(left, right):
    return lax.dot_general(left, right, ROWS_BY_ROWS, preferred_element_type=jnp.float32)


def swap(block, offset):
    count = lax.axis_size("seq")
    return lax.ppermute(block, "seq", [(i, i ^ offset) for i in range(count)])


def chip_exchange(kept, got, count):
    piece = kept.shape[0] // (count // 2)
    parts = [kept[:piece], got[:piece]]
    for chip in range(1, count // 2):
        rows = slice(chip * piece, (chip + 1) * piece)
        parts.append(swap(jnp.concatenate([kept[rows], got[rows]]), 2 * chip))
    return jnp.concatenate(parts)


def chunks(size, count):
    return [slice(i * size // count, (i + 1) * size // count) for i in range(count)]


def block_diagonal(blocks):
    zero = jnp.zeros(blocks[0].shape, blocks[0].dtype)
    return jnp.concatenate(
        [
            jnp.concatenate([b if k == j else zero for j in range(len(blocks))], axis=1)
            for k, b in enumerate(blocks)
        ],
        axis=0,
    )


def log2(size):
    assert size & (size - 1) == 0
    return size.bit_length() - 1


class Order:
    def __init__(self, row_count, local_blocks, block_rows, seq_count):
        self.row_count = row_count
        self.local_blocks = local_blocks
        self.block_rows = block_rows
        self.seq_count = seq_count
        self.steps = block_rows // seq_count
        self.group = local_blocks * self.steps

    def recv_partner(self, position):
        return position >> log2(self.group)

    def send_partner(self, position):
        chip = (position >> log2(self.group)) & (self.seq_count // 2 - 1)
        return (position >> log2(self.row_count // 2)) + 2 * chip

    def block(self, position):
        return (position >> log2(self.steps)) & (self.local_blocks - 1)

    def first_rows(self, me, partner, position):
        step = position & (self.steps - 1)
        return self.block(position) * self.block_rows + (me ^ partner) * self.steps + step

    def second_rows(self, me, partner, position):
        step = position & (self.steps - 1)
        device = me ^ partner
        return (step * self.seq_count + device) * self.local_blocks + self.block(position)


def prepare_kernel(
    order, me_ref, x_ref, gain_ref, first_ref, second_ref, gate_ref,
    normed_ref, inv_ref, keep_ref, give_ref, first_recv_ref, second_send_ref, second_recv_ref,
    gate_held, sems,
):
    copies = [
        pltpu.make_async_copy(gate_ref.at[rows], gate_held.at[rows], sems.at[i])
        for i, rows in enumerate(chunks(gate_ref.shape[0], sems.shape[0]))
    ]
    for copy in copies:
        copy.start()
    me = me_ref[0]
    square = (order.row_count, order.row_count)
    down = lax.broadcasted_iota(jnp.int32, square, 0)
    across = lax.broadcasted_iota(jnp.int32, square, 1)

    def one_hot(matches):
        return jnp.where(matches, 1.0, 0.0).astype(jnp.bfloat16)

    def rounded(left, right):
        return dot(left, right).astype(jnp.bfloat16)

    first = block_diagonal([first_ref[k].astype(jnp.float32) for k in range(order.local_blocks)])
    second = block_diagonal([second_ref[k].astype(jnp.float32) for k in range(order.local_blocks)])
    sent, received = order.send_partner(down), order.recv_partner(across)
    first_send = rounded(
        one_hot(order.first_rows(me, sent, down) == across), first.astype(jnp.bfloat16)
    )
    second_send_ref[...] = rounded(
        one_hot(order.second_rows(me, sent, down) == across), second.T.astype(jnp.bfloat16)
    )
    first_recv_ref[...] = rounded(
        first.T.astype(jnp.bfloat16), one_hot(order.first_rows(me, received, across) == down)
    )
    second_recv_ref[...] = rounded(
        second.astype(jnp.bfloat16), one_hot(order.second_rows(me, received, across) == down)
    )
    features = x_ref[...].astype(jnp.float32)
    inv_rms = lax.rsqrt(jnp.mean(features * features, axis=-1, keepdims=True) + 1e-06)
    inv_ref[...] = inv_rms
    normed = (features * inv_rms * gain_ref[...]).astype(jnp.bfloat16)
    normed_ref[...] = normed
    send = rounded(first_send, normed)
    half = order.row_count // 2
    keep_ref[...] = send[:half]
    give_ref[...] = send[half:]
    for copy in copies:
        copy.wait()


def begin_kernel(
    normed_ref, gate_ref, incoming_ref, out_ref, second_send_ref,
    mix_factor_ref, slope_ref, hidden_ref, mix_ref, keep_ref, give_ref, out_held, sems,
):
    parts = chunks(out_ref.shape[0], sems.shape[0])
    copies = [
        pltpu.make_async_copy(out_ref.at[rows], out_held.at[rows], sems.at[i])
        for i, rows in enumerate(parts)
    ]
    for copy in copies:
        copy.start()
    half = keep_ref.shape[0]
    for columns in parts:
        gate_pre = dot(normed_ref[...], gate_ref[:, columns])
        sigma = jax.nn.sigmoid(gate_pre)
        mix_factor_ref[:, columns] = gate_pre * sigma
        slope_ref[:, columns] = sigma * (1.0 + gate_pre * (1.0 - sigma))
    for columns, copy in zip(parts, copies):
        copy.wait()
        hidden = dot_rows(incoming_ref[...], out_held[columns])
        hidden_ref[:, columns] = hidden
        mix = (hidden * mix_factor_ref[:, columns]).astype(jnp.bfloat16)
        mix_ref[:, columns] = mix
        send = dot(second_send_ref[...], mix).astype(jnp.bfloat16)
        keep_ref[:, columns] = send[:half]
        give_ref[:, columns] = send[half:]


def transpose_kernel(gate_ref, out_ref, gate_turned_ref, out_turned_ref):
    for rows in chunks(gate_ref.shape[0], 6):
        gate_turned_ref[:, rows] = gate_ref[rows].T
        out_turned_ref[:, rows] = out_ref[rows].T


def prepare(order, me, inputs, gain_row, first_blocks, second_blocks, weight_gate):
    row_count, width = inputs.shape
    square = pltpu.VMEM((row_count, row_count), jnp.bfloat16)
    half = pltpu.VMEM((row_count // 2, width), jnp.bfloat16)
    return pl.pallas_call(
        functools.partial(prepare_kernel, order),
        in_specs=[SCALAR, WHOLE, WHOLE, WHOLE, WHOLE, ANYWHERE],
        out_specs=[WHOLE] * 8,
        out_shape=[
            pltpu.VMEM((row_count, width), jnp.bfloat16),
            pltpu.VMEM((row_count, 1), jnp.float32),
            half,
            half,
            square,
            square,
            square,
            pltpu.VMEM(weight_gate.shape, jnp.bfloat16),
        ],
        scratch_shapes=[pltpu.SemaphoreType.DMA((6,))],
        compiler_params=PARAMS,
        name="prepare",
    )(me, inputs, gain_row, first_blocks, second_blocks, weight_gate)


def begin(normed, gate_held, incoming, weight_out, second_send):
    row_count, width = normed.shape
    half = pltpu.VMEM((row_count // 2, width), jnp.bfloat16)
    full = pltpu.VMEM((row_count, width), jnp.float32)
    return pl.pallas_call(
        begin_kernel,
        in_specs=[WHOLE, WHOLE, WHOLE, ANYWHERE, WHOLE],
        out_specs=[WHOLE] * 7,
        out_shape=[
            full,
            full,
            full,
            pltpu.VMEM((row_count, width), jnp.bfloat16),
            half,
            half,
            pltpu.VMEM(weight_out.shape, jnp.bfloat16),
        ],
        scratch_shapes=[pltpu.SemaphoreType.DMA((6,))],
        compiler_params=PARAMS,
        name="begin",
    )(normed, gate_held, incoming, weight_out, second_send)


def transposed(gate_held, out_held):
    return pl.pallas_call(
        transpose_kernel,
        in_specs=[WHOLE] * 2,
        out_specs=[WHOLE] * 2,
        out_shape=[
            pltpu.VMEM(gate_held.shape[::-1], jnp.bfloat16),
            pltpu.VMEM(out_held.shape[::-1], jnp.bfloat16),
        ],
        compiler_params=PARAMS,
        name="transposed",
    )(gate_held, out_held)


def diagonal_blocks(matrix, count):
    rows, columns = matrix.shape[0] // count, matrix.shape[1] // count
    return jnp.stack(
        [
            matrix[k * rows : (k + 1) * rows, k * columns : (k + 1) * columns]
            for k in range(count)
        ]
    )


def per_device(section_inputs, cotangent, gain, w_gate, w_out, mix_first, mix_second):
    inputs = section_inputs[0]
    gain_row = gain[0]
    row_count, _ = inputs.shape
    local_blocks, block_rows = mix_first.shape[1:3]
    seq_count = lax.axis_size("seq")
    section_count = lax.axis_size("pipe")
    section_index = lax.axis_index("pipe")
    me = lax.axis_index("seq")
    order = Order(row_count, local_blocks, block_rows, seq_count)

    normed, inv_rms, kept, give, first_recv, second_send, second_recv, gate_held = prepare(
        order, me[None], inputs, gain, mix_first[0], mix_second[0], w_gate[0]
    )
    got_moved = swap(give, 1)
    mix_factor, slope, delta_hidden, delta_mix, kept_mix, give_mix, out_held = begin(
        normed, gate_held, cotangent, w_out[0], second_send
    )
    got_mid = swap(give_mix, 1)
    kept, got_moved, kept_mix = lax.optimization_barrier((kept, got_moved, kept_mix))
    moved = chip_exchange(kept, got_moved, seq_count)
    delta_mid = chip_exchange(kept_mix, got_mid, seq_count)
    gate_factor = dot(second_recv, moved) * slope

    unit_rows = inputs.astype(jnp.float32) * inv_rms
    incoming = cotangent
    gate_turned = None
    out_turned = None
    outgoing_kept = jnp.zeros_like(cotangent)
    first_kept = jnp.zeros((row_count, row_count), jnp.float32)
    second_kept = jnp.zeros((row_count, row_count), jnp.float32)
    for tick_index in range(section_count):
        sender = section_count - 1 - tick_index
        active = section_index == sender
        if tick_index > 0:
            delta_hidden = dot(incoming, out_turned)
            delta_mix = (delta_hidden * mix_factor).astype(jnp.bfloat16)
            send = dot(second_send, delta_mix).astype(jnp.bfloat16)
            kept_mix = send[: row_count // 2]
            delta_mid = chip_exchange(kept_mix, swap(send[row_count // 2 :], 1), seq_count)
        delta_gate = (delta_hidden * gate_factor).astype(jnp.bfloat16)
        gate_back = dot(delta_gate, gate_turned) if tick_index else dot_rows(delta_gate, gate_held)
        first_back = dot(first_recv, delta_mid)
        delta_norm = (first_back + gate_back) * gain_row
        centred = delta_norm - unit_rows * jnp.mean(delta_norm * unit_rows, axis=-1, keepdims=True)
        outgoing = (incoming.astype(jnp.float32) + inv_rms * centred).astype(jnp.bfloat16)
        if tick_index == 0:
            outgoing, gate_held, out_held = lax.optimization_barrier(
                (outgoing, gate_held, out_held)
            )
            gate_turned, out_turned = transposed(gate_held, out_held)
        if sender > 0:
            incoming = lax.ppermute(outgoing, "pipe", [(sender, sender - 1)])
        outgoing_kept = jnp.where(active, outgoing, outgoing_kept)
        first_kept = jnp.where(active, dot_rows(delta_mid, normed), first_kept)
        second_kept = jnp.where(active, dot_rows(delta_mix, moved), second_kept)

    position = jnp.arange(row_count)
    partner = order.recv_partner(position)

    def unpermuted(rows, matrix):
        return jnp.dot(
            (rows[:, None] == position[None, :]).astype(jnp.float32).T,
            matrix,
            precision=lax.Precision.HIGHEST,
            preferred_element_type=jnp.float32,
        )

    grad_first = diagonal_blocks(
        unpermuted(order.first_rows(me, partner, position), first_kept), local_blocks
    )
    grad_second = diagonal_blocks(
        unpermuted(order.second_rows(me, partner, position), second_kept.T).T, local_blocks
    )
    return (outgoing_kept[None], grad_first[None], grad_second[None])


def solution(mesh):
    placed = (
        P("pipe", "seq", None),
        P("seq", None),
        P("pipe", None),
        P("pipe", None, None),
        P("pipe", None, None),
        P("pipe", "seq", None, None),
        P("pipe", "seq", None, None),
    )
    return jax.shard_map(
        per_device,
        mesh=mesh,
        in_specs=placed,
        out_specs=(
            P("pipe", "seq", None),
            P("pipe", "seq", None, None),
            P("pipe", "seq", None, None),
        ),
        check_vma=False,
    )
```

time: 113 us -> 111 us (0.982)
  matrix products: 28.3 us -> 11.6 us
  Pallas kernels: 0 us -> 10.2 us
  local copies, waits for them, and re-layouts: 6.71 us -> 13.2 us
  other arithmetic: 8.77 us -> 3.11 us
  starting transfers between devices: 22.5 us -> 25.2 us
  waiting for transfers between devices: 44.7 us -> 46 us
    dot_general x16 -> x9, matrix products: 18.1 us -> 3.75 us  [dot_rows(): lax.dot_general(left, right, ROWS_BY_ROWS, preferred_element_type=jnp.flo...]
    pallas_call x0 -> x3, Pallas kernels: none -> 10.2 us  [the longest x1 6.19 us: begin(): pl.pallas_call(begin_kernel, in_specs=[WHOLE, WHOLE, WHOLE, ANYWHERE, WHO...]
    unnamed x34 -> x44, local copies, waits for them, and re-layouts: 1.04 us -> 9.79 us
    ppermute x20, waiting for transfers between devices: 14.5 us -> 21.4 us  [swap(): return lax.ppermute(block, 'seq', [(i, i ^ offset) for i in range(count)])]
    ppermute x3, waiting for transfers between devices: 30.1 us -> 24.6 us  [per_device(): incoming = lax.ppermute(outgoing, 'pipe', [(sender, sender - 1)])]
    concatenate x15, other arithmetic: 2.84 us -> 0.12 us  [chip_exchange(): parts.append(swap(jnp.concatenate([kept[rows], got[rows]]), 2 * chip))]
    ppermute x20, starting transfers between devices: 19.6 us -> 22.2 us  [swap(): return lax.ppermute(block, 'seq', [(i, i ^ offset) for i in range(count)])]
    dot_general x13 -> x14, matrix products: 9.63 us -> 7.25 us  [dot(): return jnp.dot(left, right, preferred_element_type=jnp.float32)]
  transfers between devices with their start and end apart: 23 -> 23, of which waited for: 10 -> 16; matrix products, arithmetic and copies ran while one was open for 22% -> 7% of each run, Pallas kernels for 0% -> 8%
where the time goes in v2:
time: 111 us
  waiting for transfers between devices  46 us (41%)
  starting transfers between devices  25.2 us (23%)
  local copies, waits for them, and re-layouts  13.2 us (12%)
  matrix products  11.6 us (10%)
  Pallas kernels  10.2 us (9%)
  other arithmetic  3.11 us (3%)
  between operations  1.31 us (1%)
    ppermute x3, waiting for transfers between devices, per_device(): incoming = lax.ppermute(outgoing, 'pipe', [(sender, sender - 1)])  24.6 us
    ppermute x20, starting transfers between devices, swap(): return lax.ppermute(block, 'seq', [(i, i ^ offset) for i in range(count)])  22.2 us
    ppermute x20, waiting for transfers between devices, swap(): return lax.ppermute(block, 'seq', [(i, i ^ offset) for i in range(count)])  21.4 us
    unnamed x44, local copies, waits for them, and re-layouts  9.79 us
    dot_general x14, matrix products, dot(): return jnp.dot(left, right, preferred_element_type=jnp.float32)  7.25 us
    pallas_call x1, Pallas kernels, begin(): pl.pallas_call(begin_kernel, in_specs=[WHOLE, WHOLE, WHOLE, ANYWHERE, WHO...  6.19 us
    dot_general x9, matrix products, dot_rows(): lax.dot_general(left, right, ROWS_BY_ROWS, preferred_element_type=jnp.flo...  3.75 us
    slice x10, local copies, waits for them, and re-layouts, chip_exchange(): parts.append(swap(jnp.concatenate([kept[rows], got[rows]]), 2 * chip))  3.15 us
  transfers between devices with their start and end apart: 23, of which 16 were waited for; matrix products, arithmetic and copies ran while one was open for 7% of the time, Pallas kernels for 8%

profile of v2, /device:TPU:0, one launch (start us, length us, event | category | flops | bytes accessed | tf_op | source)
XLA Modules:
  0.0 110.5 jit_solution(5070622992099378513)
XLA Ops:
  0.6 1.0 copy-done.2
  1.6 2.3 %copy-done.5 = bf16[1,1536,1536]{2,1,0:T(8,128)(2,1)S(1)} copy-done((bf16[1,1536,1536]{2,1,0:T(8,128)(2,1)S(1)}, bf16[1,1536,1536]{2,1,0:T(8,128)(2,1)}, u32[]{:S(2)}) %copy-start.5) | copy-done | bytes 4718616
  4.0 0.8 copy-done.11
  4.7 0.8 copy-done.12
  5.5 0.7 copy-done.13
  6.2 1.5 %prepare.1 = (bf16[128,1536]{1,0:T(8,128)(2,1)S(1)}, f32[128,1]{1,0:T(8,128)S(1)}, bf16[64,1536]{1,0:T(8,128)(2,1)S(1)}, bf16[64,1536]{1,0:T(8,128)(2,1)}, bf16[...) custom-call(s32[1]{0:T(128)} %bitcast.me_ref, ...), custom_call_target="tpu_custom_call" | custom-call | tf_op jit(solution)/shard_map/prepare/pallas_call | solution.py:176
  7.7 0.5 collective-permute-start
  8.2 0.3 copy-done.4
  8.8 6.2 %begin.1 = (f32[128,1536]{1,0:T(8,128)S(1)}, f32[128,1536]{1,0:T(8,128)S(1)}, f32[128,1536]{1,0:T(8,128)S(1)}, bf16[128,1536]{1,0:T(8,128)(2,1)S(1)}, bf16[64,15...) custom-call(bf16[128,1536]{1,0:T(8,128)(2,1)S(1)} %get-tuple-element.30.normed_ref, ...), custom_call_target="tpu_custom_call" | custom-call | tf_op jit(solution)/shard_map/begin/pallas_call | solution.py:200
  15.0 2.2 %copy-done.6 = bf16[1536,1536]{1,0:T(8,128)(2,1)} copy-done((bf16[1536,1536]{1,0:T(8,128)(2,1)}, bf16[1536,1536]{1,0:T(8,128)(2,1)S(1)}, u32[]{:S(2)}) %copy-start.6) | copy-done | bytes 4718616
  17.2 0.7 copy-done.8
  17.9 0.7 copy-done.10
  18.6 0.5 collective-permute-start.1
  19.2 1.0 fusion.21
  20.5 1.1 %fusion.22 = (bf16[16,1536]{1,0:T(8,128)(2,1)S(1)}, bf16[16,1536]{1,0:T(8,128)(2,1)S(1)}, bf16[16,1536]{1,0:T(8,128)(2,1)S(1)}, bf16[128,1536]{1,0:T(8,128)(2,1)S(1)}) fusion(bf16[64,1536]{1,0:T(8,128)(2,1)} %collective-permute-done.1, bf16[128,1536]{1,0:T(8,128)(2,1)S(1)} %get-tuple-element.76), kind=kLoop, calls=%fused_computation.110 | loop fusion | bytes 393216 | tf_op jit(solution)/shard_map/slice | solution.py:35
  21.6 2.7 %collective-permute-start.2 = (bf16[32,1536]{1,0:T(8,128)(2,1)S(1)}, bf16[32,1536]{1,0:T(8,128)(2,1)S(1)}, u32[]{:S(2)}, u32[]{:S(2)}) collective-permute-start(bf16[32,1536]{1,0:T(8,128)(2,1)S(1)} %pad_maximum_fusion), channel_id=1, source_target_pairs={{0,8},{4,12},{8,0},{12,4},{16,24},{20,28},{24,16},{28,20},{1,9},{5... | collective-permute-start | bytes 294920 | tf_op jit(solution)/shard_map/ppermute | solution.py:27
  24.3 1.6 %collective-permute-start.3 = (bf16[32,1536]{1,0:T(8,128)(2,1)S(1)}, bf16[32,1536]{1,0:T(8,128)(2,1)S(1)}, u32[]{:S(2)}, u32[]{:S(2)}) collective-permute-start(bf16[32,1536]{1,0:T(8,128)(2,1)S(1)} %pad_maximum_fusion.1), channel_id=1, source_target_pairs={{0,16},{4,20},{8,24},{12,28},{16,0},{20,4},{24,8},{28,12},{1,17},{... | collective-permute-start | bytes 294920 | tf_op jit(solution)/shard_map/ppermute | solution.py:27
  26.0 0.9 fusion.24
  26.9 2.0 %collective-permute-start.5 = (bf16[32,1536]{1,0:T(8,128)(2,1)S(1)}, bf16[32,1536]{1,0:T(8,128)(2,1)S(1)}, u32[]{:S(2)}, u32[]{:S(2)}) collective-permute-start(bf16[32,1536]{1,0:T(8,128)(2,1)S(1)} %pad_maximum_fusion.3), channel_id=1, source_target_pairs={{0,8},{4,12},{8,0},{12,4},{16,24},{20,28},{24,16},{28,20},{1,9},{5... | collective-permute-start | bytes 294920 | tf_op jit(solution)/shard_map/ppermute | solution.py:27
  28.9 1.6 %collective-permute-start.6 = (bf16[32,1536]{1,0:T(8,128)(2,1)S(1)}, bf16[32,1536]{1,0:T(8,128)(2,1)S(1)}, u32[]{:S(2)}, u32[]{:S(2)}) collective-permute-start(bf16[32,1536]{1,0:T(8,128)(2,1)S(1)} %pad_maximum_fusion.4), channel_id=1, source_target_pairs={{0,16},{4,20},{8,24},{12,28},{16,0},{20,4},{24,8},{28,12},{1,17},{... | collective-permute-start | bytes 294920 | tf_op jit(solution)/shard_map/ppermute | solution.py:27
  30.5 2.0 %collective-permute-done.5 = bf16[32,1536]{1,0:T(8,128)(2,1)S(1)} collective-permute-done((bf16[32,1536]{1,0:T(8,128)(2,1)S(1)}, bf16[32,1536]{1,0:T(8,128)(2,1)S(1)}, u32[]{:S(2)}, u32[]{:S(2)}) %collective-permute-start.5) | collective-permute-done | bytes 98336 | tf_op jit(solution)/shard_map/ppermute | solution.py:27
  32.6 2.0 %collective-permute-start.7 = (bf16[32,1536]{1,0:T(8,128)(2,1)S(1)}, bf16[32,1536]{1,0:T(8,128)(2,1)S(1)}, u32[]{:S(2)}, u32[]{:S(2)}) collective-permute-start(bf16[32,1536]{1,0:T(8,128)(2,1)S(1)} %pad_maximum_fusion.5), channel_id=1, source_target_pairs={{0,24},{4,28},{8,16},{12,20},{16,8},{20,12},{24,0},{28,4},{1,25},{... | collective-permute-start | bytes 294920 | tf_op jit(solution)/shard_map/ppermute | solution.py:27
  34.6 3.5 %collective-permute-done.7 = bf16[32,1536]{1,0:T(8,128)(2,1)S(1)} collective-permute-done((bf16[32,1536]{1,0:T(8,128)(2,1)S(1)}, bf16[32,1536]{1,0:T(8,128)(2,1)S(1)}, u32[]{:S(2)}, u32[]{:S(2)}) %collective-permute-start.7) | collective-permute-done | bytes 98336 | tf_op jit(solution)/shard_map/ppermute | solution.py:27
  38.4 1.6 %fusion.4 = f32[128,1536]{1,0:T(8,128)S(1)} fusion(bf16[1536,1536]{1,0:T(8,128)(2,1)S(1)} %copy-done.1, f32[128,1536]{1,0:T(8,128)S(1)} %get-tuple-element.36, f32[128,1536]{1,0:T(8,128)S(1)} %convolution_multiply_fusion), kind=kOutput, calls=%fused_computation.36 | convolution fusion | flops 604372992 | bytes 7077888 | tf_op jit(solution)/shard_map/dot_general | solution.py:22
  40.1 0.4 multiply_reduce_fusion.3
  40.8 0.8 collective-permute-start.8
  41.7 2.5 %transposed.1 = (bf16[1536,1536]{1,0:T(8,128)(2,1)S(1)}, bf16[1536,1536]{1,0:T(8,128)(2,1)S(1)}) custom-call(bf16[1536,1536]{1,0:T(8,128)(2,1)S(1)} %copy-done.1, bf16[1536,1536]{1,0:T(8,128)(2,1)S(1)} %bitcast.76), custom_call_target="tpu_custom_call" | custom-call | tf_op jit(solution)/shard_map/transposed/pallas_call | solution.py:220
  44.7 0.8 multiply_convert_fusion.5
  45.9 0.8 fusion.5
  46.7 0.6 collective-permute-done.9
  47.4 1.1 %collective-permute-start.10 = (bf16[32,1536]{1,0:T(8,128)(2,1)S(1)}, bf16[32,1536]{1,0:T(8,128)(2,1)S(1)}, u32[]{:S(2)}, u32[]{:S(2)}) collective-permute-start(bf16[32,1536]{1,0:T(8,128)(2,1)S(1)} %pad_maximum_fusion.6), channel_id=1, source_target_pairs={{0,8},{4,12},{8,0},{12,4},{16,24},{20,28},{24,16},{28,20},{1,9},{5... | collective-permute-start | bytes 294920 | tf_op jit(solution)/shard_map/ppermute | solution.py:27
  48.5 1.5 %collective-permute-start.11 = (bf16[32,1536]{1,0:T(8,128)(2,1)S(1)}, bf16[32,1536]{1,0:T(8,128)(2,1)S(1)}, u32[]{:S(2)}, u32[]{:S(2)}) collective-permute-start(bf16[32,1536]{1,0:T(8,128)(2,1)S(1)} %pad_maximum_fusion.7), channel_id=1, source_target_pairs={{0,16},{4,20},{8,24},{12,28},{16,0},{20,4},{24,8},{28,12},{1,17},{... | collective-permute-start | bytes 294920 | tf_op jit(solution)/shard_map/ppermute | solution.py:27
  50.1 1.0 collective-permute-start.12
  51.1 1.2 %collective-permute-done.10 = bf16[32,1536]{1,0:T(8,128)(2,1)S(1)} collective-permute-done((bf16[32,1536]{1,0:T(8,128)(2,1)S(1)}, bf16[32,1536]{1,0:T(8,128)(2,1)S(1)}, u32[]{:S(2)}, u32[]{:S(2)}) %collective-permute-start.10) | collective-permute-done | bytes 98336 | tf_op jit(solution)/shard_map/ppermute | solution.py:27
  52.3 2.0 %collective-permute-done.11 = bf16[32,1536]{1,0:T(8,128)(2,1)S(1)} collective-permute-done((bf16[32,1536]{1,0:T(8,128)(2,1)S(1)}, bf16[32,1536]{1,0:T(8,128)(2,1)S(1)}, u32[]{:S(2)}, u32[]{:S(2)}) %collective-permute-start.11) | collective-permute-done | bytes 98336 | tf_op jit(solution)/shard_map/ppermute | solution.py:27
  54.4 1.3 %collective-permute-done.12 = bf16[32,1536]{1,0:T(8,128)(2,1)S(1)} collective-permute-done((bf16[32,1536]{1,0:T(8,128)(2,1)S(1)}, bf16[32,1536]{1,0:T(8,128)(2,1)S(1)}, u32[]{:S(2)}, u32[]{:S(2)}) %collective-permute-start.12) | collective-permute-done | bytes 98336 | tf_op jit(solution)/shard_map/ppermute | solution.py:27
  55.7 0.4 multiply_reduce_fusion.2
  56.1 0.3 add_convert_fusion.2
  56.4 0.9 collective-permute-start.13
  57.8 0.8 multiply_convert_fusion.3
  59.0 0.8 fusion.6
  59.8 0.6 collective-permute-done.14
  60.5 1.1 %collective-permute-start.15 = (bf16[32,1536]{1,0:T(8,128)(2,1)S(1)}, bf16[32,1536]{1,0:T(8,128)(2,1)S(1)}, u32[]{:S(2)}, u32[]{:S(2)}) collective-permute-start(bf16[32,1536]{1,0:T(8,128)(2,1)S(1)} %pad_maximum_fusion.9), channel_id=1, source_target_pairs={{0,8},{4,12},{8,0},{12,4},{16,24},{20,28},{24,16},{28,20},{1,9},{5... | collective-permute-start | bytes 294920 | tf_op jit(solution)/shard_map/ppermute | solution.py:27
  61.6 1.2 %collective-permute-start.16 = (bf16[32,1536]{1,0:T(8,128)(2,1)S(1)}, bf16[32,1536]{1,0:T(8,128)(2,1)S(1)}, u32[]{:S(2)}, u32[]{:S(2)}) collective-permute-start(bf16[32,1536]{1,0:T(8,128)(2,1)S(1)} %pad_maximum_fusion.10), channel_id=1, source_target_pairs={{0,16},{4,20},{8,24},{12,28},{16,0},{20,4},{24,8},{28,12},{1,17},{... | collective-permute-start | bytes 294920 | tf_op jit(solution)/shard_map/ppermute | solution.py:27
  62.9 1.3 %collective-permute-start.17 = (bf16[32,1536]{1,0:T(8,128)(2,1)S(1)}, bf16[32,1536]{1,0:T(8,128)(2,1)S(1)}, u32[]{:S(2)}, u32[]{:S(2)}) collective-permute-start(bf16[32,1536]{1,0:T(8,128)(2,1)S(1)} %pad_maximum_fusion.11), channel_id=1, source_target_pairs={{0,24},{4,28},{8,16},{12,20},{16,8},{20,12},{24,0},{28,4},{1,25},{... | collective-permute-start | bytes 294920 | tf_op jit(solution)/shard_map/ppermute | solution.py:27
  64.2 1.2 %collective-permute-done.15 = bf16[32,1536]{1,0:T(8,128)(2,1)S(1)} collective-permute-done((bf16[32,1536]{1,0:T(8,128)(2,1)S(1)}, bf16[32,1536]{1,0:T(8,128)(2,1)S(1)}, u32[]{:S(2)}, u32[]{:S(2)}) %collective-permute-start.15) | collective-permute-done | bytes 98336 | tf_op jit(solution)/shard_map/ppermute | solution.py:27
  65.4 2.0 %collective-permute-done.16 = bf16[32,1536]{1,0:T(8,128)(2,1)S(1)} collective-permute-done((bf16[32,1536]{1,0:T(8,128)(2,1)S(1)}, bf16[32,1536]{1,0:T(8,128)(2,1)S(1)}, u32[]{:S(2)}, u32[]{:S(2)}) %collective-permute-start.16) | collective-permute-done | bytes 98336 | tf_op jit(solution)/shard_map/ppermute | solution.py:27
  67.4 1.1 collective-permute-done.17
  68.5 0.4 multiply_reduce_fusion.1
  68.8 0.3 add_convert_fusion.1
  69.2 1.3 %collective-permute-start.18 = (bf16[128,1536]{1,0:T(8,128)(2,1)S(1)}, bf16[128,1536]{1,0:T(8,128)(2,1)S(1)}, u32[]{:S(2)}, u32[]{:S(2)}) collective-permute-start(bf16[128,1536]{1,0:T(8,128)(2,1)S(1)} %add_convert_fusion.1), channel_id=1, source_target_pairs={{1,0},{5,4},{9,8},{13,12},{17,16},{21,20},{25,24},{29,28}} | collective-permute-start | bytes 1179656 | tf_op jit(solution)/shard_map/ppermute | solution.py:295
  71.0 24.6 %collective-permute-done.18 = bf16[128,1536]{1,0:T(8,128)(2,1)S(1)} collective-permute-done((bf16[128,1536]{1,0:T(8,128)(2,1)S(1)}, bf16[128,1536]{1,0:T(8,128)(2,1)S(1)}, u32[]{:S(2)}, u32[]{:S(2)}) %collective-permute-start.18) | collective-permute-done | bytes 393248 | tf_op jit(solution)/shard_map/ppermute | solution.py:295
  95.6 0.8 multiply_convert_fusion.1
  96.7 0.8 fusion.7
  98.2 0.8 collective-permute-done.19
  99.1 1.1 %collective-permute-start.20 = (bf16[32,1536]{1,0:T(8,128)(2,1)S(1)}, bf16[32,1536]{1,0:T(8,128)(2,1)S(1)}, u32[]{:S(2)}, u32[]{:S(2)}) collective-permute-start(bf16[32,1536]{1,0:T(8,128)(2,1)S(1)} %pad_maximum_fusion.12), channel_id=1, source_target_pairs={{0,8},{4,12},{8,0},{12,4},{16,24},{20,28},{24,16},{28,20},{1,9},{5... | collective-permute-start | bytes 294920 | tf_op jit(solution)/shard_map/ppermute | solution.py:27
  100.2 1.7 %collective-permute-start.21 = (bf16[32,1536]{1,0:T(8,128)(2,1)S(1)}, bf16[32,1536]{1,0:T(8,128)(2,1)S(1)}, u32[]{:S(2)}, u32[]{:S(2)}) collective-permute-start(bf16[32,1536]{1,0:T(8,128)(2,1)S(1)} %pad_maximum_fusion.13), channel_id=1, source_target_pairs={{0,16},{4,20},{8,24},{12,28},{16,0},{20,4},{24,8},{28,12},{1,17},{... | collective-permute-start | bytes 294920 | tf_op jit(solution)/shard_map/ppermute | solution.py:27
  101.9 1.0 collective-permute-start.22
  102.9 1.1 %collective-permute-done.20 = bf16[32,1536]{1,0:T(8,128)(2,1)S(1)} collective-permute-done((bf16[32,1536]{1,0:T(8,128)(2,1)S(1)}, bf16[32,1536]{1,0:T(8,128)(2,1)S(1)}, u32[]{:S(2)}, u32[]{:S(2)}) %collective-permute-start.20) | collective-permute-done | bytes 98336 | tf_op jit(solution)/shard_map/ppermute | solution.py:27
  104.0 2.1 %collective-permute-done.21 = bf16[32,1536]{1,0:T(8,128)(2,1)S(1)} collective-permute-done((bf16[32,1536]{1,0:T(8,128)(2,1)S(1)}, bf16[32,1536]{1,0:T(8,128)(2,1)S(1)}, u32[]{:S(2)}, u32[]{:S(2)}) %collective-permute-start.21) | collective-permute-done | bytes 98336 | tf_op jit(solution)/shard_map/ppermute | solution.py:27
  106.1 1.5 %collective-permute-done.22 = bf16[32,1536]{1,0:T(8,128)(2,1)S(1)} collective-permute-done((bf16[32,1536]{1,0:T(8,128)(2,1)S(1)}, bf16[32,1536]{1,0:T(8,128)(2,1)S(1)}, u32[]{:S(2)}, u32[]{:S(2)}) %collective-permute-start.22) | collective-permute-done | bytes 98336 | tf_op jit(solution)/shard_map/ppermute | solution.py:27
  107.9 0.4 multiply_reduce_fusion
  108.7 0.7 maximum_bitcast_fusion
  109.4 1.2 %fusion.9 = bf16[1,128,1536]{2,1,0:T(8,128)(2,1)} fusion(f32[128,1536]{1,0:T(8,128)S(1)} %get-tuple-element.106, bf16[128,1536]{1,0:T(8,128)(2,1)S(1)} %collective-permute-done.18, bf16[128,1536]{1,0:T(8,128)(2,1)S(1)} %add_convert_fusion.1, bf16[128,1536]{1,0:T(8,128)(2,1)S(1)} %add_convert_fusion.2, bf16[128,1536]{1,0:T(8,128)(2,1)S(1)} %add_convert_fusion.3, ...), kind=kLoop, calls=%fused_computation.41 | loop fusion | flops 2359296 | bytes 3146756 | tf_op jit(solution)/shard_map/broadcast_in_dim | solution.py:317
  (103 shorter events, 5.4 us)
Async XLA Ops:
  0.6 1.0 copy-start.2
  1.6 2.3 %copy-start.5 = (bf16[1,1536,1536]{2,1,0:T(8,128)(2,1)S(1)}, bf16[1,1536,1536]{2,1,0:T(8,128)(2,1)}, u32[]{:S(2)}) copy-start(bf16[1,1536,1536]{2,1,0:T(8,128)(2,1)} %param.10) | copy-start | bytes 14155780
  4.0 0.8 copy-start.11
  4.7 0.8 copy-start.12
  5.5 0.7 copy-start.13
  6.2 2.4 %copy-start.4 = (bf16[1,1536,1536]{2,1,0:T(8,128)(2,1)S(1)}, bf16[1,1536,1536]{2,1,0:T(8,128)(2,1)}, u32[]{:S(2)}) copy-start(bf16[1,1536,1536]{2,1,0:T(8,128)(2,1)} %param.11) | copy-start | bytes 14155780
  6.2 2.6 %copy-start.7 = (bf16[128,1536]{1,0:T(8,128)(2,1)S(1)}, bf16[128,1536]{1,0:T(8,128)(2,1)}, u32[]{:S(2)}) copy-start(bf16[128,1536]{1,0:T(8,128)(2,1)} %incoming_ref.1) | copy-start | bytes 1179652
  7.7 7.3 %copy-start = (bf16[1536,1536]{1,0:T(8,128)(2,1)}, bf16[1536,1536]{1,0:T(8,128)(2,1)S(1)}, u32[]{:S(2)}) copy-start(bf16[1536,1536]{1,0:T(8,128)(2,1)S(1)} %get-tuple-element.43.gate_ref) | copy-start | bytes 14155780
  7.7 11.5 %collective-permute-start = (bf16[64,1536]{1,0:T(8,128)(2,1)}, bf16[64,1536]{1,0:T(8,128)(2,1)}, u32[]{:S(2)}, u32[]{:S(2)}) collective-permute-start(bf16[64,1536]{1,0:T(8,128)(2,1)} %get-tuple-element.29), channel_id=1, source_target_pairs={{0,4},{4,0},{8,12},{12,8},{16,20},{20,16},{24,28},{28,24},{1,5},{5... | collective-permute-start | bytes 589832 | tf_op jit(solution)/shard_map/ppermute | solution.py:27
  8.8 10.3 %copy-start.14 = (f32[1,1536]{1,0:T(1,128)S(1)}, f32[1,1536]{1,0:T(1,128)}, u32[]{:S(2)}) copy-start(f32[1,1536]{1,0:T(1,128)} %gain_ref.1) | copy-start | bytes 18436
  15.0 2.2 %copy-start.6 = (bf16[1536,1536]{1,0:T(8,128)(2,1)}, bf16[1536,1536]{1,0:T(8,128)(2,1)S(1)}, u32[]{:S(2)}) copy-start(bf16[1536,1536]{1,0:T(8,128)(2,1)S(1)} %get-tuple-element.44.out_ref) | copy-start | bytes 14155780
  17.2 0.7 copy-start.8
  17.9 0.7 copy-start.10
  18.6 1.9 %collective-permute-start.1 = (bf16[64,1536]{1,0:T(8,128)(2,1)}, bf16[64,1536]{1,0:T(8,128)(2,1)}, u32[]{:S(2)}, u32[]{:S(2)}) collective-permute-start(bf16[64,1536]{1,0:T(8,128)(2,1)} %get-tuple-element.35), channel_id=1, source_target_pairs={{0,4},{4,0},{8,12},{12,8},{16,20},{20,16},{24,28},{28,24},{1,5},{5... | collective-permute-start | bytes 589832 | tf_op jit(solution)/shard_map/ppermute | solution.py:27
  19.2 19.2 %copy-start.1 = (bf16[1536,1536]{1,0:T(8,128)(2,1)S(1)}, bf16[1536,1536]{1,0:T(8,128)(2,1)}, u32[]{:S(2)}) copy-start(bf16[1536,1536]{1,0:T(8,128)(2,1)} %copy-done) | copy-start | bytes 14155780
  21.6 18.4 %collective-permute-start.2 = (bf16[32,1536]{1,0:T(8,128)(2,1)S(1)}, bf16[32,1536]{1,0:T(8,128)(2,1)S(1)}, u32[]{:S(2)}, u32[]{:S(2)}) collective-permute-start(bf16[32,1536]{1,0:T(8,128)(2,1)S(1)} %pad_maximum_fusion), channel_id=1, source_target_pairs={{0,8},{4,12},{8,0},{12,4},{16,24},{20,28},{24,16},{28,20},{1,9},{5... | collective-permute-start | bytes 294920 | tf_op jit(solution)/shard_map/ppermute | solution.py:27
  24.3 15.7 %collective-permute-start.3 = (bf16[32,1536]{1,0:T(8,128)(2,1)S(1)}, bf16[32,1536]{1,0:T(8,128)(2,1)S(1)}, u32[]{:S(2)}, u32[]{:S(2)}) collective-permute-start(bf16[32,1536]{1,0:T(8,128)(2,1)S(1)} %pad_maximum_fusion.1), channel_id=1, source_target_pairs={{0,16},{4,20},{8,24},{12,28},{16,0},{20,4},{24,8},{28,12},{1,17},{... | collective-permute-start | bytes 294920 | tf_op jit(solution)/shard_map/ppermute | solution.py:27
  25.9 14.2 %collective-permute-start.4 = (bf16[32,1536]{1,0:T(8,128)(2,1)S(1)}, bf16[32,1536]{1,0:T(8,128)(2,1)S(1)}, u32[]{:S(2)}, u32[]{:S(2)}) collective-permute-start(bf16[32,1536]{1,0:T(8,128)(2,1)S(1)} %pad_maximum_fusion.2), channel_id=1, source_target_pairs={{0,24},{4,28},{8,16},{12,20},{16,8},{20,12},{24,0},{28,4},{1,25},{... | collective-permute-start | bytes 294920 | tf_op jit(solution)/shard_map/ppermute | solution.py:27
  26.9 5.7 %collective-permute-start.5 = (bf16[32,1536]{1,0:T(8,128)(2,1)S(1)}, bf16[32,1536]{1,0:T(8,128)(2,1)S(1)}, u32[]{:S(2)}, u32[]{:S(2)}) collective-permute-start(bf16[32,1536]{1,0:T(8,128)(2,1)S(1)} %pad_maximum_fusion.3), channel_id=1, source_target_pairs={{0,8},{4,12},{8,0},{12,4},{16,24},{20,28},{24,16},{28,20},{1,9},{5... | collective-permute-start | bytes 294920 | tf_op jit(solution)/shard_map/ppermute | solution.py:27
  28.9 5.6 %collective-permute-start.6 = (bf16[32,1536]{1,0:T(8,128)(2,1)S(1)}, bf16[32,1536]{1,0:T(8,128)(2,1)S(1)}, u32[]{:S(2)}, u32[]{:S(2)}) collective-permute-start(bf16[32,1536]{1,0:T(8,128)(2,1)S(1)} %pad_maximum_fusion.4), channel_id=1, source_target_pairs={{0,16},{4,20},{8,24},{12,28},{16,0},{20,4},{24,8},{28,12},{1,17},{... | collective-permute-start | bytes 294920 | tf_op jit(solution)/shard_map/ppermute | solution.py:27
  32.6 5.5 %collective-permute-start.7 = (bf16[32,1536]{1,0:T(8,128)(2,1)S(1)}, bf16[32,1536]{1,0:T(8,128)(2,1)S(1)}, u32[]{:S(2)}, u32[]{:S(2)}) collective-permute-start(bf16[32,1536]{1,0:T(8,128)(2,1)S(1)} %pad_maximum_fusion.5), channel_id=1, source_target_pairs={{0,24},{4,28},{8,16},{12,20},{16,8},{20,12},{24,0},{28,4},{1,25},{... | collective-permute-start | bytes 294920 | tf_op jit(solution)/shard_map/ppermute | solution.py:27
  38.1 2.0 %copy-start.3 = (bf16[1,128,1536]{2,1,0:T(8,128)(2,1)S(1)}, bf16[1,128,1536]{2,1,0:T(8,128)(2,1)}, u32[]{:S(2)}) copy-start(bf16[1,128,1536]{2,1,0:T(8,128)(2,1)} %param.7) | copy-start | bytes 1179652
  38.4 3.3 %slice-start = ((s8[4718592]{0:T(1024)(128)(4,1)}), s8[4194304]{0:T(1024)(128)(4,1)S(1)}, s32[]{:S(2)}) async-start(s8[4718592]{0:T(1024)(128)(4,1)} %bitcast.75), calls=%async_computation | async-start | bytes 8388608
  38.4 3.3 %slice-start.1 = ((s8[4718592]{0:T(1024)(128)(4,1)}), s8[524288]{0:T(1024)(128)(4,1)S(1)}, s32[]{:S(2)}) async-start(s8[4718592]{0:T(1024)(128)(4,1)} %bitcast.75), calls=%async_computation.1 | async-start | bytes 1048576
  40.8 3.6 %copy-start.9 = (bf16[128,1536]{1,0:T(8,128)(2,1)S(1)}, bf16[128,1536]{1,0:T(8,128)(2,1)}, u32[]{:S(2)}) copy-start(bf16[128,1536]{1,0:T(8,128)(2,1)} %copy-done.8) | copy-start | bytes 1179652
  40.8 3.9 %collective-permute-start.8 = (bf16[128,1536]{1,0:T(8,128)(2,1)S(1)}, bf16[128,1536]{1,0:T(8,128)(2,1)S(1)}, u32[]{:S(2)}, u32[]{:S(2)}) collective-permute-start(bf16[128,1536]{1,0:T(8,128)(2,1)S(1)} %add_convert_fusion.3), channel_id=1, source_target_pairs={{3,2},{7,6},{11,10},{15,14},{19,18},{23,22},{27,26},{31,30}} | collective-permute-start | bytes 1179656 | tf_op jit(solution)/shard_map/ppermute | solution.py:295
  45.9 1.5 %collective-permute-start.9 = (bf16[64,1536]{1,0:T(8,128)(2,1)S(1)}, bf16[64,1536]{1,0:T(8,128)(2,1)S(1)}, u32[]{:S(2)}, u32[]{:S(2)}) collective-permute-start(bf16[64,1536]{1,0:T(8,128)(2,1)S(1)} %slice.208), channel_id=1, source_target_pairs={{0,4},{4,0},{8,12},{12,8},{16,20},{20,16},{24,28},{28,24},{1,5},{5... | collective-permute-start | bytes 589832 | tf_op jit(solution)/shard_map/ppermute | solution.py:27
  47.4 4.9 %collective-permute-start.10 = (bf16[32,1536]{1,0:T(8,128)(2,1)S(1)}, bf16[32,1536]{1,0:T(8,128)(2,1)S(1)}, u32[]{:S(2)}, u32[]{:S(2)}) collective-permute-start(bf16[32,1536]{1,0:T(8,128)(2,1)S(1)} %pad_maximum_fusion.6), channel_id=1, source_target_pairs={{0,8},{4,12},{8,0},{12,4},{16,24},{20,28},{24,16},{28,20},{1,9},{5... | collective-permute-start | bytes 294920 | tf_op jit(solution)/shard_map/ppermute | solution.py:27
  48.5 5.8 %collective-permute-start.11 = (bf16[32,1536]{1,0:T(8,128)(2,1)S(1)}, bf16[32,1536]{1,0:T(8,128)(2,1)S(1)}, u32[]{:S(2)}, u32[]{:S(2)}) collective-permute-start(bf16[32,1536]{1,0:T(8,128)(2,1)S(1)} %pad_maximum_fusion.7), channel_id=1, source_target_pairs={{0,16},{4,20},{8,24},{12,28},{16,0},{20,4},{24,8},{28,12},{1,17},{... | collective-permute-start | bytes 294920 | tf_op jit(solution)/shard_map/ppermute | solution.py:27
  50.1 5.6 %collective-permute-start.12 = (bf16[32,1536]{1,0:T(8,128)(2,1)S(1)}, bf16[32,1536]{1,0:T(8,128)(2,1)S(1)}, u32[]{:S(2)}, u32[]{:S(2)}) collective-permute-start(bf16[32,1536]{1,0:T(8,128)(2,1)S(1)} %pad_maximum_fusion.8), channel_id=1, source_target_pairs={{0,24},{4,28},{8,16},{12,20},{16,8},{20,12},{24,0},{28,4},{1,25},{... | collective-permute-start | bytes 294920 | tf_op jit(solution)/shard_map/ppermute | solution.py:27
  56.4 1.4 %collective-permute-start.13 = (bf16[128,1536]{1,0:T(8,128)(2,1)S(1)}, bf16[128,1536]{1,0:T(8,128)(2,1)S(1)}, u32[]{:S(2)}, u32[]{:S(2)}) collective-permute-start(bf16[128,1536]{1,0:T(8,128)(2,1)S(1)} %add_convert_fusion.2), channel_id=1, source_target_pairs={{2,1},{6,5},{10,9},{14,13},{18,17},{22,21},{26,25},{30,29}} | collective-permute-start | bytes 1179656 | tf_op jit(solution)/shard_map/ppermute | solution.py:295
  58.9 1.5 %collective-permute-start.14 = (bf16[64,1536]{1,0:T(8,128)(2,1)S(1)}, bf16[64,1536]{1,0:T(8,128)(2,1)S(1)}, u32[]{:S(2)}, u32[]{:S(2)}) collective-permute-start(bf16[64,1536]{1,0:T(8,128)(2,1)S(1)} %slice.217), channel_id=1, source_target_pairs={{0,4},{4,0},{8,12},{12,8},{16,20},{20,16},{24,28},{28,24},{1,5},{5... | collective-permute-start | bytes 589832 | tf_op jit(solution)/shard_map/ppermute | solution.py:27
  60.5 4.9 %collective-permute-start.15 = (bf16[32,1536]{1,0:T(8,128)(2,1)S(1)}, bf16[32,1536]{1,0:T(8,128)(2,1)S(1)}, u32[]{:S(2)}, u32[]{:S(2)}) collective-permute-start(bf16[32,1536]{1,0:T(8,128)(2,1)S(1)} %pad_maximum_fusion.9), channel_id=1, source_target_pairs={{0,8},{4,12},{8,0},{12,4},{16,24},{20,28},{24,16},{28,20},{1,9},{5... | collective-permute-start | bytes 294920 | tf_op jit(solution)/shard_map/ppermute | solution.py:27
  61.6 5.7 %collective-permute-start.16 = (bf16[32,1536]{1,0:T(8,128)(2,1)S(1)}, bf16[32,1536]{1,0:T(8,128)(2,1)S(1)}, u32[]{:S(2)}, u32[]{:S(2)}) collective-permute-start(bf16[32,1536]{1,0:T(8,128)(2,1)S(1)} %pad_maximum_fusion.10), channel_id=1, source_target_pairs={{0,16},{4,20},{8,24},{12,28},{16,0},{20,4},{24,8},{28,12},{1,17},{... | collective-permute-start | bytes 294920 | tf_op jit(solution)/shard_map/ppermute | solution.py:27
  62.9 5.6 %collective-permute-start.17 = (bf16[32,1536]{1,0:T(8,128)(2,1)S(1)}, bf16[32,1536]{1,0:T(8,128)(2,1)S(1)}, u32[]{:S(2)}, u32[]{:S(2)}) collective-permute-start(bf16[32,1536]{1,0:T(8,128)(2,1)S(1)} %pad_maximum_fusion.11), channel_id=1, source_target_pairs={{0,24},{4,28},{8,16},{12,20},{16,8},{20,12},{24,0},{28,4},{1,25},{... | collective-permute-start | bytes 294920 | tf_op jit(solution)/shard_map/ppermute | solution.py:27
  69.2 26.5 %collective-permute-start.18 = (bf16[128,1536]{1,0:T(8,128)(2,1)S(1)}, bf16[128,1536]{1,0:T(8,128)(2,1)S(1)}, u32[]{:S(2)}, u32[]{:S(2)}) collective-permute-start(bf16[128,1536]{1,0:T(8,128)(2,1)S(1)} %add_convert_fusion.1), channel_id=1, source_target_pairs={{1,0},{5,4},{9,8},{13,12},{17,16},{21,20},{25,24},{29,28}} | collective-permute-start | bytes 1179656 | tf_op jit(solution)/shard_map/ppermute | solution.py:295
  97.5 1.5 %collective-permute-start.19 = (bf16[64,1536]{1,0:T(8,128)(2,1)S(1)}, bf16[64,1536]{1,0:T(8,128)(2,1)S(1)}, u32[]{:S(2)}, u32[]{:S(2)}) collective-permute-start(bf16[64,1536]{1,0:T(8,128)(2,1)S(1)} %slice.226), channel_id=1, source_target_pairs={{0,4},{4,0},{8,12},{12,8},{16,20},{20,16},{24,28},{28,24},{1,5},{5... | collective-permute-start | bytes 589832 | tf_op jit(solution)/shard_map/ppermute | solution.py:27
  99.1 4.9 %collective-permute-start.20 = (bf16[32,1536]{1,0:T(8,128)(2,1)S(1)}, bf16[32,1536]{1,0:T(8,128)(2,1)S(1)}, u32[]{:S(2)}, u32[]{:S(2)}) collective-permute-start(bf16[32,1536]{1,0:T(8,128)(2,1)S(1)} %pad_maximum_fusion.12), channel_id=1, source_target_pairs={{0,8},{4,12},{8,0},{12,4},{16,24},{20,28},{24,16},{28,20},{1,9},{5... | collective-permute-start | bytes 294920 | tf_op jit(solution)/shard_map/ppermute | solution.py:27
  100.2 5.9 %collective-permute-start.21 = (bf16[32,1536]{1,0:T(8,128)(2,1)S(1)}, bf16[32,1536]{1,0:T(8,128)(2,1)S(1)}, u32[]{:S(2)}, u32[]{:S(2)}) collective-permute-start(bf16[32,1536]{1,0:T(8,128)(2,1)S(1)} %pad_maximum_fusion.13), channel_id=1, source_target_pairs={{0,16},{4,20},{8,24},{12,28},{16,0},{20,4},{24,8},{28,12},{1,17},{... | collective-permute-start | bytes 294920 | tf_op jit(solution)/shard_map/ppermute | solution.py:27
  101.9 5.7 %collective-permute-start.22 = (bf16[32,1536]{1,0:T(8,128)(2,1)S(1)}, bf16[32,1536]{1,0:T(8,128)(2,1)S(1)}, u32[]{:S(2)}, u32[]{:S(2)}) collective-permute-start(bf16[32,1536]{1,0:T(8,128)(2,1)S(1)} %pad_maximum_fusion.14), channel_id=1, source_target_pairs={{0,24},{4,28},{8,16},{12,20},{16,8},{20,12},{24,0},{28,4},{1,25},{... | collective-permute-start | bytes 294920 | tf_op jit(solution)/shard_map/ppermute | solution.py:27

commit v3 on v2

v3 whole, which is shorter than its diff:
```python
import functools

import jax
import jax.numpy as jnp
from jax import lax
from jax.experimental import pallas as pl
from jax.experimental.pallas import tpu as pltpu
from jax.sharding import PartitionSpec as P

ROWS_BY_ROWS = (((1,), (1,)), ((), ()))
WHOLE = pl.BlockSpec(memory_space=pltpu.VMEM)
ANYWHERE = pl.BlockSpec(memory_space=pl.ANY)
SCALAR = pl.BlockSpec(memory_space=pltpu.SMEM)
PARAMS = pltpu.CompilerParams(vmem_limit_bytes=12 << 20)


def in_hbm(array):
    return pltpu.with_memory_space_constraint(array, pltpu.HBM)


def dot(left, right):
    return jnp.dot(left, right, preferred_element_type=jnp.float32)


def dot_rows(left, right):
    return lax.dot_general(left, right, ROWS_BY_ROWS, preferred_element_type=jnp.float32)


def swap(block, offset):
    count = lax.axis_size("seq")
    return lax.ppermute(block, "seq", [(i, i ^ offset) for i in range(count)])


def chip_exchange(messages):
    return jnp.concatenate([messages[0]] + [swap(m, 2 * i) for i, m in enumerate(messages) if i])


def messages_of(kept, got, count):
    piece = kept.shape[0] // count
    parts = [slice(chip * piece, (chip + 1) * piece) for chip in range(count)]
    return [jnp.concatenate([kept[rows], got[rows]]) for rows in parts]


def chunks(size, count):
    return [slice(i * size // count, (i + 1) * size // count) for i in range(count)]


def block_diagonal(blocks):
    zero = jnp.zeros(blocks[0].shape, blocks[0].dtype)
    return jnp.concatenate(
        [
            jnp.concatenate([b if k == j else zero for j in range(len(blocks))], axis=1)
            for k, b in enumerate(blocks)
        ],
        axis=0,
    )


def log2(size):
    assert size & (size - 1) == 0
    return size.bit_length() - 1


class Order:
    def __init__(self, row_count, local_blocks, block_rows, seq_count):
        self.row_count = row_count
        self.local_blocks = local_blocks
        self.block_rows = block_rows
        self.seq_count = seq_count
        self.steps = block_rows // seq_count
        self.group = local_blocks * self.steps

    def recv_partner(self, position):
        return position >> log2(self.group)

    def send_partner(self, position):
        chip = (position >> log2(self.group)) & (self.seq_count // 2 - 1)
        return (position >> log2(self.row_count // 2)) + 2 * chip

    def block(self, position):
        return (position >> log2(self.steps)) & (self.local_blocks - 1)

    def first_rows(self, me, partner, position):
        step = position & (self.steps - 1)
        return self.block(position) * self.block_rows + (me ^ partner) * self.steps + step

    def second_rows(self, me, partner, position):
        step = position & (self.steps - 1)
        device = me ^ partner
        return (step * self.seq_count + device) * self.local_blocks + self.block(position)


def begin_kernel(
    order, x_hbm, gain_hbm, first_hbm, second_hbm, gate_hbm, incoming_hbm, out_hbm,
    normed_ref, inv_ref, first_recv_ref, second_send_ref, second_recv_ref,
    mix_factor_ref, slope_ref, hidden_ref, mix_ref, keep_ref, give_ref,
    x_ref, gain_ref, first_ref, second_ref, gate_ref, incoming_ref, out_ref, sems,
):
    parts = chunks(out_hbm.shape[0], sems.shape[0] - 6)
    pairs = [(x_hbm, x_ref), (first_hbm, first_ref), (second_hbm, second_ref), (gain_hbm, gain_ref)]
    pairs += [(gate_hbm, gate_ref), (incoming_hbm, incoming_ref)]
    pairs += [(out_hbm.at[rows], out_ref.at[rows]) for rows in parts]
    copies = [pltpu.make_async_copy(*pair, sems.at[i]) for i, pair in enumerate(pairs)]
    for copy in copies:
        copy.start()
    me = lax.axis_index("seq")
    square = (order.row_count, order.row_count)
    down = lax.broadcasted_iota(jnp.int32, square, 0)
    across = lax.broadcasted_iota(jnp.int32, square, 1)

    def one_hot(matches):
        return jnp.where(matches, 1.0, 0.0).astype(jnp.bfloat16)

    def rounded(left, right):
        return dot(left, right).astype(jnp.bfloat16)

    for copy in copies[:4]:
        copy.wait()
    first = block_diagonal([first_ref[k].astype(jnp.float32) for k in range(order.local_blocks)])
    second = block_diagonal([second_ref[k].astype(jnp.float32) for k in range(order.local_blocks)])
    sent, received = order.send_partner(down), order.recv_partner(across)
    first_send = rounded(
        one_hot(order.first_rows(me, sent, down) == across), first.astype(jnp.bfloat16)
    )
    second_send_ref[...] = rounded(
        one_hot(order.second_rows(me, sent, down) == across), second.T.astype(jnp.bfloat16)
    )
    first_recv_ref[...] = rounded(
        first.T.astype(jnp.bfloat16), one_hot(order.first_rows(me, received, across) == down)
    )
    second_recv_ref[...] = rounded(
        second.astype(jnp.bfloat16), one_hot(order.second_rows(me, received, across) == down)
    )
    features = x_ref[...].astype(jnp.float32)
    inv_rms = lax.rsqrt(jnp.mean(features * features, axis=-1, keepdims=True) + 1e-06)
    inv_ref[...] = inv_rms
    normed = (features * inv_rms * gain_ref[...]).astype(jnp.bfloat16)
    normed_ref[...] = normed

    def place(send, stream, columns):
        half = order.row_count // 2
        piece = half // (order.seq_count // 2)
        for row in range(0, half, piece):
            rows = slice(2 * row + stream * piece, 2 * row + (stream + 1) * piece)
            keep_ref[rows, columns] = send[row : row + piece]
            give_ref[rows, columns] = send[half + row : half + row + piece]

    place(rounded(first_send, normed), 0, slice(None))
    copies[4].wait()
    gate_pre = dot(normed, gate_ref[...])
    sigma = jax.nn.sigmoid(gate_pre)
    mix_factor_ref[...] = gate_pre * sigma
    slope_ref[...] = sigma * (1.0 + gate_pre * (1.0 - sigma))
    copies[5].wait()
    for columns, copy in zip(parts, copies[6:]):
        copy.wait()
        hidden = dot_rows(incoming_ref[...], out_ref[columns])
        hidden_ref[:, columns] = hidden
        mix = (hidden * mix_factor_ref[:, columns]).astype(jnp.bfloat16)
        mix_ref[:, columns] = mix
        place(rounded(second_send_ref[...], mix), 1, columns)


def pack_kernel(count, *refs):
    kept_ref, got_ref, outs = refs[0], refs[1], refs[-count:]
    piece = kept_ref.shape[0] // count
    for chip, out_ref in enumerate(outs):
        rows = slice(chip * piece, (chip + 1) * piece)
        out_ref[:piece] = kept_ref[rows]
        out_ref[piece:] = got_ref[rows]


def packed(kept, got, count):
    piece = jax.ShapeDtypeStruct((2 * kept.shape[0] // count, kept.shape[1]), kept.dtype)
    return pl.pallas_call(
        functools.partial(pack_kernel, count),
        in_specs=[WHOLE] * 2,
        out_specs=[WHOLE] * count,
        out_shape=[piece] * count,
        compiler_params=PARAMS,
        name="packed",
    )(kept, got)


def finish_kernel(
    count, *refs,
):
    messages, refs = refs[:count], refs[count:]
    (
        second_recv_ref, first_recv_ref, slope_ref, hidden_ref, gate_ref, gain_ref,
        x_ref, inv_ref, incoming_ref, moved_ref, mid_ref, gate_factor_ref, outgoing_ref,
    ) = refs
    piece = messages[0].shape[0] // 4
    for chip, message in enumerate(messages):
        for core in range(2):
            rows = slice((2 * chip + core) * piece, (2 * chip + core + 1) * piece)
            moved_ref[rows] = message[2 * core * piece : (2 * core + 1) * piece]
            mid_ref[rows] = message[(2 * core + 1) * piece : (2 * core + 2) * piece]
    gate_factor = dot(second_recv_ref[...], moved_ref[...]) * slope_ref[...]
    gate_factor_ref[...] = gate_factor
    delta_gate = (hidden_ref[...] * gate_factor).astype(jnp.bfloat16)
    gate_back = dot(delta_gate, gate_ref[...])
    first_back = dot(first_recv_ref[...], mid_ref[...])
    outgoing_ref[...] = outgoing_of(
        gate_back, first_back, gain_ref[...], x_ref[...], inv_ref[...], incoming_ref[...]
    )


def outgoing_of(gate_back, first_back, gain, inputs, inv_rms, incoming):
    delta_norm = (first_back + gate_back) * gain
    unit_rows = inputs.astype(jnp.float32) * inv_rms
    centred = delta_norm - unit_rows * jnp.mean(delta_norm * unit_rows, axis=-1, keepdims=True)
    return (incoming.astype(jnp.float32) + inv_rms * centred).astype(jnp.bfloat16)


def finish(messages, *operands):
    row_count, width = operands[-1].shape
    return pl.pallas_call(
        functools.partial(finish_kernel, len(messages)),
        in_specs=[WHOLE] * (len(messages) + len(operands)),
        out_specs=[WHOLE] * 4,
        out_shape=[
            jax.ShapeDtypeStruct((row_count, width), jnp.bfloat16),
            jax.ShapeDtypeStruct((row_count, width), jnp.bfloat16),
            jax.ShapeDtypeStruct((row_count, width), jnp.float32),
            jax.ShapeDtypeStruct((row_count, width), jnp.bfloat16),
        ],
        compiler_params=PARAMS,
        name="finish",
    )(*messages, *operands)


def transpose_kernel(weight_hbm, after_ref, turned_ref, held, sems):
    parts = chunks(held.shape[0], sems.shape[0])
    copies = [
        pltpu.make_async_copy(weight_hbm.at[rows], held.at[rows], sems.at[i])
        for i, rows in enumerate(parts)
    ]
    for copy in copies:
        copy.start()
    for rows, copy in zip(parts, copies):
        copy.wait()
        turned_ref[:, rows] = held[rows].T


def begin(order, *operands):
    row_count, width = operands[0].shape
    square = jax.ShapeDtypeStruct((row_count, row_count), jnp.bfloat16)
    short = jax.ShapeDtypeStruct((row_count, width), jnp.bfloat16)
    full = jax.ShapeDtypeStruct((row_count, width), jnp.float32)
    column = jax.ShapeDtypeStruct((row_count, 1), jnp.float32)
    return pl.pallas_call(
        functools.partial(begin_kernel, order),
        in_specs=[ANYWHERE] * len(operands),
        out_specs=[WHOLE] * 11,
        out_shape=[short, column, square, square, square, full, full, full, short, short, short],
        scratch_shapes=[pltpu.VMEM(o.shape, o.dtype) for o in operands]
        + [pltpu.SemaphoreType.DMA((9,))],
        compiler_params=pltpu.CompilerParams(vmem_limit_bytes=20 << 20),
        name="begin",
    )(*[in_hbm(o) for o in operands])


def transposed(weight, after):
    return pl.pallas_call(
        transpose_kernel,
        in_specs=[ANYWHERE, ANYWHERE],
        out_specs=WHOLE,
        out_shape=pltpu.VMEM(weight.shape[::-1], jnp.bfloat16),
        scratch_shapes=[pltpu.VMEM(weight.shape, weight.dtype), pltpu.SemaphoreType.DMA((6,))],
        compiler_params=PARAMS,
        name="transposed",
    )(in_hbm(weight), after)


def diagonal_blocks(matrix, count):
    rows, columns = matrix.shape[0] // count, matrix.shape[1] // count
    return jnp.stack(
        [
            matrix[k * rows : (k + 1) * rows, k * columns : (k + 1) * columns]
            for k in range(count)
        ]
    )


def per_device(section_inputs, cotangent, gain, w_gate, w_out, mix_first, mix_second):
    inputs = section_inputs[0]
    gain_row = gain[0]
    row_count, _ = inputs.shape
    local_blocks, block_rows = mix_first.shape[1:3]
    seq_count = lax.axis_size("seq")
    section_count = lax.axis_size("pipe")
    section_index = lax.axis_index("pipe")
    me = lax.axis_index("seq")
    order = Order(row_count, local_blocks, block_rows, seq_count)

    (
        normed, inv_rms, first_recv, second_send, second_recv,
        mix_factor, slope, delta_hidden, delta_mix, kept, give,
    ) = begin(
        order, inputs, gain, mix_first[0], mix_second[0], w_gate[0], cotangent, w_out[0]
    )
    messages = packed(kept, swap(give, 1), seq_count // 2)
    gate_turned = transposed(w_gate[0], messages[-1])
    messages = [messages[0]] + [swap(m, 2 * i) for i, m in enumerate(messages) if i]
    moved, delta_mid, gate_factor, outgoing = finish(
        messages, second_recv, first_recv, slope, delta_hidden, gate_turned, gain,
        inputs, inv_rms, cotangent,
    )
    out_turned = transposed(w_out[0], outgoing)

    outgoing_kept = outgoing
    first_kept = dot_rows(delta_mid, normed)
    second_kept = dot_rows(delta_mix, moved)
    for sender in reversed(range(section_count - 1)):
        active = section_index == sender
        incoming = lax.ppermute(outgoing, "pipe", [(sender + 1, sender)])
        delta_hidden = dot(incoming, out_turned)
        delta_mix = (delta_hidden * mix_factor).astype(jnp.bfloat16)
        send = dot(second_send, delta_mix).astype(jnp.bfloat16)
        kept_mix = send[: row_count // 2]
        got_mix = swap(send[row_count // 2 :], 1)
        delta_mid = chip_exchange(messages_of(kept_mix, got_mix, seq_count // 2))
        delta_gate = (delta_hidden * gate_factor).astype(jnp.bfloat16)
        gate_back = dot(delta_gate, gate_turned)
        first_back = dot(first_recv, delta_mid)
        outgoing = outgoing_of(gate_back, first_back, gain_row, inputs, inv_rms, incoming)
        outgoing_kept = jnp.where(active, outgoing, outgoing_kept)
        first_kept = jnp.where(active, dot_rows(delta_mid, normed), first_kept)
        second_kept = jnp.where(active, dot_rows(delta_mix, moved), second_kept)

    position = jnp.arange(row_count)
    partner = order.recv_partner(position)

    def unpermuted(rows, matrix):
        return jnp.dot(
            (rows[:, None] == position[None, :]).astype(jnp.float32).T,
            matrix,
            precision=lax.Precision.HIGHEST,
            preferred_element_type=jnp.float32,
        )

    grad_first = diagonal_blocks(
        unpermuted(order.first_rows(me, partner, position), first_kept), local_blocks
    )
    grad_second = diagonal_blocks(
        unpermuted(order.second_rows(me, partner, position), second_kept.T).T, local_blocks
    )
    return (outgoing_kept[None], grad_first[None], grad_second[None])


def solution(mesh):
    placed = (
        P("pipe", "seq", None),
        P("seq", None),
        P("pipe", None),
        P("pipe", None, None),
        P("pipe", None, None),
        P("pipe", "seq", None, None),
        P("pipe", "seq", None, None),
    )
    return jax.shard_map(
        per_device,
        mesh=mesh,
        in_specs=placed,
        out_specs=(
            P("pipe", "seq", None),
            P("pipe", "seq", None, None),
            P("pipe", "seq", None, None),
        ),
        check_vma=False,
    )
```

time: 111 us -> 97.4 us (0.88)
  local copies, waits for them, and re-layouts: 13.2 us -> 1.11 us
  starting transfers between devices: 25.2 us -> 19.1 us
  Pallas kernels: 10.2 us -> 14.4 us
  waiting for transfers between devices: 46 us -> 49.4 us
  matrix products: 11.6 us -> 9.34 us
    unnamed x44 -> x16, local copies, waits for them, and re-layouts: 9.79 us -> 0.8 us
    ppermute x20 -> x16, starting transfers between devices: 22.2 us -> 16.1 us  [swap(): return lax.ppermute(block, 'seq', [(i, i ^ offset) for i in range(count)])]
    pallas_call x3 -> x5, Pallas kernels: 10.2 us -> 14.4 us  [the longest x1 6.62 us: begin(): pl.pallas_call(functools.partial(begin_kernel, order), in_specs=[ANYWHERE...]
    slice x13 -> x9, local copies, waits for them, and re-layouts: 3.2 us -> 0.13 us  [the longest x6 0.09 us: messages_of(): return [jnp.concatenate([kept[rows], got[rows]]) for rows in parts]]
    ppermute x20 -> x16, waiting for transfers between devices: 21.4 us -> 23.3 us  [swap(): return lax.ppermute(block, 'seq', [(i, i ^ offset) for i in range(count)])]
    dot_general x9 -> x8, matrix products: 3.75 us -> 2.11 us  [dot_rows(): lax.dot_general(left, right, ROWS_BY_ROWS, preferred_element_type=jnp.flo...]
    ppermute x3, waiting for transfers between devices: 24.6 us -> 26.1 us  [per_device(): incoming = lax.ppermute(outgoing, 'pipe', [(sender + 1, sender)])]
    dot_general x14 -> x12, matrix products: 7.25 us -> 6.66 us  [dot(): return jnp.dot(left, right, preferred_element_type=jnp.float32)]
  transfers between devices with their start and end apart: 23 -> 19, of which waited for: 16 -> 14; matrix products, arithmetic and copies ran while one was open for 7% -> 4% of each run, Pallas kernels for 8% -> 6%
where the time goes in v3:
time: 97.4 us; the launch traced here: 97.2 us
  waiting for transfers between devices  49.4 us (51%)
  starting transfers between devices  19.1 us (20%)
  Pallas kernels  14.4 us (15%)
  matrix products  9.34 us (10%)
  other arithmetic  2.71 us (3%)
  local copies, waits for them, and re-layouts  1.11 us (1%)
  between operations  1.11 us (1%)
    ppermute x3, waiting for transfers between devices, per_device(): incoming = lax.ppermute(outgoing, 'pipe', [(sender + 1, sender)])  26.1 us
    ppermute x16, waiting for transfers between devices, swap(): return lax.ppermute(block, 'seq', [(i, i ^ offset) for i in range(count)])  23.3 us
    ppermute x16, starting transfers between devices, swap(): return lax.ppermute(block, 'seq', [(i, i ^ offset) for i in range(count)])  16.1 us
    dot_general x12, matrix products, dot(): return jnp.dot(left, right, preferred_element_type=jnp.float32)  6.66 us
    pallas_call x1, Pallas kernels, begin(): pl.pallas_call(functools.partial(begin_kernel, order), in_specs=[ANYWHERE...  6.62 us
    pallas_call x2, Pallas kernels, transposed(): pl.pallas_call(transpose_kernel, in_specs=[ANYWHERE, ANYWHERE], out_specs...  5.54 us
    ppermute x3, starting transfers between devices, per_device(): incoming = lax.ppermute(outgoing, 'pipe', [(sender + 1, sender)])  2.98 us
    dot_general x8, matrix products, dot_rows(): lax.dot_general(left, right, ROWS_BY_ROWS, preferred_element_type=jnp.flo...  2.11 us
  transfers between devices with their start and end apart: 19, of which 14 were waited for; matrix products, arithmetic and copies ran while one was open for 4% of the time, Pallas kernels for 6%

profile of v3, /device:TPU:0, one launch (start us, length us, event | category | flops | bytes accessed | tf_op | source)
XLA Modules:
  0.0 97.2 jit_solution(8242248891014331555)
XLA Ops:
  0.6 6.6 %begin.1 = (bf16[128,1536]{1,0:T(8,128)(2,1)S(1)}, f32[128,1]{1,0:T(8,128)S(1)}, bf16[128,128]{1,0:T(8,128)(2,1)S(1)}, bf16[128,128]{1,0:T(8,128)(2,1)S(1)}, bf1...) custom-call(bf16[128,1536]{1,0:T(8,128)(2,1)} %bitcast.64, ...), custom_call_target="tpu_custom_call" | custom-call | tf_op jit(solution)/shard_map/begin/pallas_call | solution.py:252
  7.3 0.7 copy-done.2
  8.0 0.4 collective-permute-start
  8.5 0.1 reduce
  8.6 1.6 %collective-permute-done.refs_1_ = bf16[128,1536]{1,0:T(8,128)(2,1)} collective-permute-done((bf16[128,1536]{1,0:T(8,128)(2,1)}, bf16[128,1536]{1,0:T(8,128)(2,1)}, u32[]{:S(2)}, u32[]{:S(2)}) %collective-permute-start) | collective-permute-done | bytes 393248 | tf_op jit(solution)/shard_map/ppermute | solution.py:31
  10.1 1.0 %packed.1 = (bf16[64,1536]{1,0:T(8,128)(2,1)S(1)}, bf16[64,1536]{1,0:T(8,128)(2,1)S(1)}, bf16[64,1536]{1,0:T(8,128)(2,1)S(1)}, bf16[64,1536]{1,0:T(8,128)(2,1)S(1)}) custom-call(bf16[128,1536]{1,0:T(8,128)(2,1)S(1)} %get-tuple-element.22.refs_0_, bf16[128,1536]{1,0:T(8,128)(2,1)} %collective-permute-done.refs_1_), custom_call_target="tpu_custom_call" | custom-call | tf_op jit(solution)/shard_map/packed/pallas_call | solution.py:175
  11.2 3.0 %collective-permute-start.1 = (bf16[64,1536]{1,0:T(8,128)(2,1)S(1)}, bf16[64,1536]{1,0:T(8,128)(2,1)S(1)}, u32[]{:S(2)}, u32[]{:S(2)}) collective-permute-start(bf16[64,1536]{1,0:T(8,128)(2,1)S(1)} %get-tuple-element.25), channel_id=1, source_target_pairs={{0,8},{4,12},{8,0},{12,4},{16,24},{20,28},{24,16},{28,20},{1,9},{5... | collective-permute-start | bytes 589832 | tf_op jit(solution)/shard_map/ppermute | solution.py:31
  14.1 1.5 %collective-permute-start.2 = (bf16[64,1536]{1,0:T(8,128)(2,1)S(1)}, bf16[64,1536]{1,0:T(8,128)(2,1)S(1)}, u32[]{:S(2)}, u32[]{:S(2)}) collective-permute-start(bf16[64,1536]{1,0:T(8,128)(2,1)S(1)} %get-tuple-element.26), channel_id=1, source_target_pairs={{0,16},{4,20},{8,24},{12,28},{16,0},{20,4},{24,8},{28,12},{1,17},{... | collective-permute-start | bytes 589832 | tf_op jit(solution)/shard_map/ppermute | solution.py:31
  15.7 2.8 %transposed.2.refs_8_ = bf16[1536,1536]{1,0:T(8,128)(2,1)S(1)} custom-call(bf16[1536,1536]{1,0:T(8,128)(2,1)} %bitcast.67, bf16[64,1536]{1,0:T(8,128)(2,1)S(1)} %get-tuple-element.27.after_ref), custom_call_target="tpu_custom_call" | custom-call | tf_op jit(solution)/shard_map/transposed/pallas_call | solution.py:265
  18.5 1.3 %collective-permute-done.1.refs_1_ = bf16[64,1536]{1,0:T(8,128)(2,1)S(1)} collective-permute-done((bf16[64,1536]{1,0:T(8,128)(2,1)S(1)}, bf16[64,1536]{1,0:T(8,128)(2,1)S(1)}, u32[]{:S(2)}, u32[]{:S(2)}) %collective-permute-start.1) | collective-permute-done | bytes 196640 | tf_op jit(solution)/shard_map/ppermute | solution.py:31
  19.8 5.2 %collective-permute-done.2.refs_2_ = bf16[64,1536]{1,0:T(8,128)(2,1)S(1)} collective-permute-done((bf16[64,1536]{1,0:T(8,128)(2,1)S(1)}, bf16[64,1536]{1,0:T(8,128)(2,1)S(1)}, u32[]{:S(2)}, u32[]{:S(2)}) %collective-permute-start.2) | collective-permute-done | bytes 196640 | tf_op jit(solution)/shard_map/ppermute | solution.py:31
  25.0 1.2 %finish.1 = (bf16[128,1536]{1,0:T(8,128)(2,1)S(1)}, bf16[128,1536]{1,0:T(8,128)(2,1)S(1)}, f32[128,1536]{1,0:T(8,128)S(1)}, bf16[128,1536]{1,0:T(8,128)(2,1)S(1)}) custom-call(bf16[64,1536]{1,0:T(8,128)(2,1)S(1)} %get-tuple-element.24.refs_0_, bf16[64,1536]{1,0:T(8,128)(2,1)S(1)} %collective-permute-done.1.refs_1_, ...), custom_call_target="tpu_custom_call" | custom-call | tf_op jit(solution)/shard_map/finish/pallas_call | solution.py:218
  26.2 0.8 collective-permute-start.4
  27.1 2.7 %transposed.3 = bf16[1536,1536]{1,0:T(8,128)(2,1)S(1)} custom-call(bf16[1536,1536]{1,0:T(8,128)(2,1)} %bitcast.69, bf16[128,1536]{1,0:T(8,128)(2,1)S(1)} %get-tuple-element.33.after_ref), custom_call_target="tpu_custom_call" | custom-call | tf_op jit(solution)/shard_map/transposed/pallas_call | solution.py:265
  29.8 0.3 fusion.20
  30.1 0.3 fusion.19
  30.4 0.8 multiply_convert_fusion.5
  31.2 0.2 convolution_convert_fusion.2
  31.5 0.8 fusion.3
  32.4 0.6 collective-permute-done.5
  33.0 1.3 %collective-permute-start.6 = (bf16[32,1536]{1,0:T(8,128)(2,1)S(1)}, bf16[32,1536]{1,0:T(8,128)(2,1)S(1)}, u32[]{:S(2)}, u32[]{:S(2)}) collective-permute-start(bf16[32,1536]{1,0:T(8,128)(2,1)S(1)} %pad_maximum_fusion), channel_id=1, source_target_pairs={{0,8},{4,12},{8,0},{12,4},{16,24},{20,28},{24,16},{28,20},{1,9},{5... | collective-permute-start | bytes 294920 | tf_op jit(solution)/shard_map/ppermute | solution.py:31
  34.3 0.9 collective-permute-start.7
  35.2 1.5 %collective-permute-start.8 = (bf16[32,1536]{1,0:T(8,128)(2,1)S(1)}, bf16[32,1536]{1,0:T(8,128)(2,1)S(1)}, u32[]{:S(2)}, u32[]{:S(2)}) collective-permute-start(bf16[32,1536]{1,0:T(8,128)(2,1)S(1)} %pad_maximum_fusion.2), channel_id=1, source_target_pairs={{0,24},{4,28},{8,16},{12,20},{16,8},{20,12},{24,0},{28,4},{1,25},{... | collective-permute-start | bytes 294920 | tf_op jit(solution)/shard_map/ppermute | solution.py:31
  36.7 1.2 %collective-permute-done.6 = bf16[32,1536]{1,0:T(8,128)(2,1)S(1)} collective-permute-done((bf16[32,1536]{1,0:T(8,128)(2,1)S(1)}, bf16[32,1536]{1,0:T(8,128)(2,1)S(1)}, u32[]{:S(2)}, u32[]{:S(2)}) %collective-permute-start.6) | collective-permute-done | bytes 98336 | tf_op jit(solution)/shard_map/ppermute | solution.py:31
  37.9 3.2 %collective-permute-done.7 = bf16[32,1536]{1,0:T(8,128)(2,1)S(1)} collective-permute-done((bf16[32,1536]{1,0:T(8,128)(2,1)S(1)}, bf16[32,1536]{1,0:T(8,128)(2,1)S(1)}, u32[]{:S(2)}, u32[]{:S(2)}) %collective-permute-start.7) | collective-permute-done | bytes 98336 | tf_op jit(solution)/shard_map/ppermute | solution.py:31
  41.1 0.4 multiply_reduce_fusion.2
  41.5 0.3 add_convert_fusion.2
  41.9 0.7 collective-permute-start.9
  42.5 0.3 convolution_select_fusion
  42.8 0.3 convolution_select_fusion.3
  43.1 0.8 multiply_convert_fusion.3
  43.9 0.2 convolution_convert_fusion.1
  44.3 0.8 fusion.4
  45.1 0.6 collective-permute-done.10
  45.7 1.2 %collective-permute-start.11 = (bf16[32,1536]{1,0:T(8,128)(2,1)S(1)}, bf16[32,1536]{1,0:T(8,128)(2,1)S(1)}, u32[]{:S(2)}, u32[]{:S(2)}) collective-permute-start(bf16[32,1536]{1,0:T(8,128)(2,1)S(1)} %pad_maximum_fusion.3), channel_id=1, source_target_pairs={{0,8},{4,12},{8,0},{12,4},{16,24},{20,28},{24,16},{28,20},{1,9},{5... | collective-permute-start | bytes 294920 | tf_op jit(solution)/shard_map/ppermute | solution.py:31
  47.0 1.2 %collective-permute-start.12 = (bf16[32,1536]{1,0:T(8,128)(2,1)S(1)}, bf16[32,1536]{1,0:T(8,128)(2,1)S(1)}, u32[]{:S(2)}, u32[]{:S(2)}) collective-permute-start(bf16[32,1536]{1,0:T(8,128)(2,1)S(1)} %pad_maximum_fusion.4), channel_id=1, source_target_pairs={{0,16},{4,20},{8,24},{12,28},{16,0},{20,4},{24,8},{28,12},{1,17},{... | collective-permute-start | bytes 294920 | tf_op jit(solution)/shard_map/ppermute | solution.py:31
  48.2 1.2 %collective-permute-start.13 = (bf16[32,1536]{1,0:T(8,128)(2,1)S(1)}, bf16[32,1536]{1,0:T(8,128)(2,1)S(1)}, u32[]{:S(2)}, u32[]{:S(2)}) collective-permute-start(bf16[32,1536]{1,0:T(8,128)(2,1)S(1)} %pad_maximum_fusion.5), channel_id=1, source_target_pairs={{0,24},{4,28},{8,16},{12,20},{16,8},{20,12},{24,0},{28,4},{1,25},{... | collective-permute-start | bytes 294920 | tf_op jit(solution)/shard_map/ppermute | solution.py:31
  49.4 1.2 %collective-permute-done.11 = bf16[32,1536]{1,0:T(8,128)(2,1)S(1)} collective-permute-done((bf16[32,1536]{1,0:T(8,128)(2,1)S(1)}, bf16[32,1536]{1,0:T(8,128)(2,1)S(1)}, u32[]{:S(2)}, u32[]{:S(2)}) %collective-permute-start.11) | collective-permute-done | bytes 98336 | tf_op jit(solution)/shard_map/ppermute | solution.py:31
  50.7 2.0 %collective-permute-done.12 = bf16[32,1536]{1,0:T(8,128)(2,1)S(1)} collective-permute-done((bf16[32,1536]{1,0:T(8,128)(2,1)S(1)}, bf16[32,1536]{1,0:T(8,128)(2,1)S(1)}, u32[]{:S(2)}, u32[]{:S(2)}) %collective-permute-start.12) | collective-permute-done | bytes 98336 | tf_op jit(solution)/shard_map/ppermute | solution.py:31
  52.7 1.1 %collective-permute-done.13 = bf16[32,1536]{1,0:T(8,128)(2,1)S(1)} collective-permute-done((bf16[32,1536]{1,0:T(8,128)(2,1)S(1)}, bf16[32,1536]{1,0:T(8,128)(2,1)S(1)}, u32[]{:S(2)}, u32[]{:S(2)}) %collective-permute-start.13) | collective-permute-done | bytes 98336 | tf_op jit(solution)/shard_map/ppermute | solution.py:31
  53.8 0.4 multiply_reduce_fusion.1
  54.2 0.3 add_convert_fusion.1
  54.5 1.5 %collective-permute-start.14 = (bf16[128,1536]{1,0:T(8,128)(2,1)S(1)}, bf16[128,1536]{1,0:T(8,128)(2,1)S(1)}, u32[]{:S(2)}, u32[]{:S(2)}) collective-permute-start(bf16[128,1536]{1,0:T(8,128)(2,1)S(1)} %add_convert_fusion.1), channel_id=1, source_target_pairs={{1,0},{5,4},{9,8},{13,12},{17,16},{21,20},{25,24},{29,28}} | collective-permute-start | bytes 1179656 | tf_op jit(solution)/shard_map/ppermute | solution.py:317
  56.0 0.3 convolution_select_fusion.1
  56.2 0.3 convolution_select_fusion.4
  56.5 26.1 %collective-permute-done.14 = bf16[128,1536]{1,0:T(8,128)(2,1)S(1)} collective-permute-done((bf16[128,1536]{1,0:T(8,128)(2,1)S(1)}, bf16[128,1536]{1,0:T(8,128)(2,1)S(1)}, u32[]{:S(2)}, u32[]{:S(2)}) %collective-permute-start.14) | collective-permute-done | bytes 393248 | tf_op jit(solution)/shard_map/ppermute | solution.py:317
  82.7 0.8 multiply_convert_fusion.1
  83.5 0.2 convolution_convert_fusion
  83.7 0.8 fusion.5
  84.7 0.3 convolution_select_fusion.2
  84.9 0.2 fusion.9
  85.2 0.1 slice_bitcast_fusion.1
  85.3 0.8 collective-permute-done.15
  86.1 1.4 %collective-permute-start.16 = (bf16[32,1536]{1,0:T(8,128)(2,1)S(1)}, bf16[32,1536]{1,0:T(8,128)(2,1)S(1)}, u32[]{:S(2)}, u32[]{:S(2)}) collective-permute-start(bf16[32,1536]{1,0:T(8,128)(2,1)S(1)} %pad_maximum_fusion.6), channel_id=1, source_target_pairs={{0,8},{4,12},{8,0},{12,4},{16,24},{20,28},{24,16},{28,20},{1,9},{5... | collective-permute-start | bytes 294920 | tf_op jit(solution)/shard_map/ppermute | solution.py:31
  87.5 0.7 collective-permute-start.17
  88.2 1.6 %collective-permute-start.18 = (bf16[32,1536]{1,0:T(8,128)(2,1)S(1)}, bf16[32,1536]{1,0:T(8,128)(2,1)S(1)}, u32[]{:S(2)}, u32[]{:S(2)}) collective-permute-start(bf16[32,1536]{1,0:T(8,128)(2,1)S(1)} %pad_maximum_fusion.8), channel_id=1, source_target_pairs={{0,24},{4,28},{8,16},{12,20},{16,8},{20,12},{24,0},{28,4},{1,25},{... | collective-permute-start | bytes 294920 | tf_op jit(solution)/shard_map/ppermute | solution.py:31
  89.8 1.2 %collective-permute-done.16 = bf16[32,1536]{1,0:T(8,128)(2,1)S(1)} collective-permute-done((bf16[32,1536]{1,0:T(8,128)(2,1)S(1)}, bf16[32,1536]{1,0:T(8,128)(2,1)S(1)}, u32[]{:S(2)}, u32[]{:S(2)}) %collective-permute-start.16) | collective-permute-done | bytes 98336 | tf_op jit(solution)/shard_map/ppermute | solution.py:31
  91.0 3.3 %collective-permute-done.17 = bf16[32,1536]{1,0:T(8,128)(2,1)S(1)} collective-permute-done((bf16[32,1536]{1,0:T(8,128)(2,1)S(1)}, bf16[32,1536]{1,0:T(8,128)(2,1)S(1)}, u32[]{:S(2)}, u32[]{:S(2)}) %collective-permute-start.17) | collective-permute-done | bytes 98336 | tf_op jit(solution)/shard_map/ppermute | solution.py:31
  94.3 0.3 convolution_select_fusion.5
  94.6 0.4 multiply_reduce_fusion
  95.0 0.3 fusion.8
  95.3 0.1 slice_bitcast_fusion.3
  95.4 0.7 maximum_bitcast_fusion
  96.1 1.1 %fusion.7 = bf16[1,128,1536]{2,1,0:T(8,128)(2,1)} fusion(f32[128,1536]{1,0:T(8,128)S(1)} %get-tuple-element.80, bf16[128,1536]{1,0:T(8,128)(2,1)S(1)} %collective-permute-done.14, bf16[128,1536]{1,0:T(8,128)(2,1)S(1)} %add_convert_fusion.1, bf16[128,1536]{1,0:T(8,128)(2,1)S(1)} %add_convert_fusion.2, bf16[128,1536]{1,0:T(8,128)(2,1)S(1)} %get-tuple-element.33.after_ref, ...), kind=kLoop, calls=%fused_computation.32 | loop fusion | flops 2162688 | bytes 3146755 | tf_op jit(solution)/shard_map/broadcast_in_dim | solution.py:349
  (51 shorter events, 0.6 us)
Async XLA Ops:
  0.6 7.8 %copy-start.4 = (f32[1,1536]{1,0:T(1,128)S(1)}, f32[1,1536]{1,0:T(1,128)}, u32[]{:S(2)}) copy-start(f32[1,1536]{1,0:T(1,128)} %refs_9_.1) | copy-start | bytes 18436
  7.3 0.7 copy-start.2
  8.0 2.1 %collective-permute-start = (bf16[128,1536]{1,0:T(8,128)(2,1)}, bf16[128,1536]{1,0:T(8,128)(2,1)}, u32[]{:S(2)}, u32[]{:S(2)}) collective-permute-start(bf16[128,1536]{1,0:T(8,128)(2,1)} %get-tuple-element.23), channel_id=1, source_target_pairs={{0,4},{4,0},{8,12},{12,8},{16,20},{20,16},{24,28},{28,24},{1,5},{5... | collective-permute-start | bytes 1179656 | tf_op jit(solution)/shard_map/ppermute | solution.py:31
  11.2 8.6 %collective-permute-start.1 = (bf16[64,1536]{1,0:T(8,128)(2,1)S(1)}, bf16[64,1536]{1,0:T(8,128)(2,1)S(1)}, u32[]{:S(2)}, u32[]{:S(2)}) collective-permute-start(bf16[64,1536]{1,0:T(8,128)(2,1)S(1)} %get-tuple-element.25), channel_id=1, source_target_pairs={{0,8},{4,12},{8,0},{12,4},{16,24},{20,28},{24,16},{28,20},{1,9},{5... | collective-permute-start | bytes 589832 | tf_op jit(solution)/shard_map/ppermute | solution.py:31
  14.1 10.9 %collective-permute-start.2 = (bf16[64,1536]{1,0:T(8,128)(2,1)S(1)}, bf16[64,1536]{1,0:T(8,128)(2,1)S(1)}, u32[]{:S(2)}, u32[]{:S(2)}) collective-permute-start(bf16[64,1536]{1,0:T(8,128)(2,1)S(1)} %get-tuple-element.26), channel_id=1, source_target_pairs={{0,16},{4,20},{8,24},{12,28},{16,0},{20,4},{24,8},{28,12},{1,17},{... | collective-permute-start | bytes 589832 | tf_op jit(solution)/shard_map/ppermute | solution.py:31
  15.7 9.4 %collective-permute-start.3 = (bf16[64,1536]{1,0:T(8,128)(2,1)S(1)}, bf16[64,1536]{1,0:T(8,128)(2,1)S(1)}, u32[]{:S(2)}, u32[]{:S(2)}) collective-permute-start(bf16[64,1536]{1,0:T(8,128)(2,1)S(1)} %get-tuple-element.27.after_ref), channel_id=1, source_target_pairs={{0,24},{4,28},{8,16},{12,20},{16,8},{20,12},{24,0},{28,4},{1,25},{... | collective-permute-start | bytes 589832 | tf_op jit(solution)/shard_map/ppermute | solution.py:31
  15.7 9.3 %copy-start = (bf16[1,128,1536]{2,1,0:T(8,128)(2,1)S(1)}, bf16[1,128,1536]{2,1,0:T(8,128)(2,1)}, u32[]{:S(2)}) copy-start(bf16[1,128,1536]{2,1,0:T(8,128)(2,1)} %param.7) | copy-start | bytes 1179652
  15.7 9.3 %copy-start.1 = (bf16[128,1536]{1,0:T(8,128)(2,1)S(1)}, bf16[128,1536]{1,0:T(8,128)(2,1)}, u32[]{:S(2)}) copy-start(bf16[128,1536]{1,0:T(8,128)(2,1)} %refs_12_.1) | copy-start | bytes 1179652
  26.2 3.6 %copy-start.3 = (bf16[128,1536]{1,0:T(8,128)(2,1)S(1)}, bf16[128,1536]{1,0:T(8,128)(2,1)}, u32[]{:S(2)}) copy-start(bf16[128,1536]{1,0:T(8,128)(2,1)} %copy-done.2) | copy-start | bytes 1179652
  26.2 4.1 %collective-permute-start.4 = (bf16[128,1536]{1,0:T(8,128)(2,1)S(1)}, bf16[128,1536]{1,0:T(8,128)(2,1)S(1)}, u32[]{:S(2)}, u32[]{:S(2)}) collective-permute-start(bf16[128,1536]{1,0:T(8,128)(2,1)S(1)} %get-tuple-element.33.after_ref), channel_id=1, source_target_pairs={{3,2},{7,6},{11,10},{15,14},{19,18},{23,22},{27,26},{31,30}} | collective-permute-start | bytes 1179656 | tf_op jit(solution)/shard_map/ppermute | solution.py:317
  31.5 1.5 %collective-permute-start.5 = (bf16[64,1536]{1,0:T(8,128)(2,1)S(1)}, bf16[64,1536]{1,0:T(8,128)(2,1)S(1)}, u32[]{:S(2)}, u32[]{:S(2)}) collective-permute-start(bf16[64,1536]{1,0:T(8,128)(2,1)S(1)} %slice.140), channel_id=1, source_target_pairs={{0,4},{4,0},{8,12},{12,8},{16,20},{20,16},{24,28},{28,24},{1,5},{5... | collective-permute-start | bytes 589832 | tf_op jit(solution)/shard_map/ppermute | solution.py:31
  33.0 4.9 %collective-permute-start.6 = (bf16[32,1536]{1,0:T(8,128)(2,1)S(1)}, bf16[32,1536]{1,0:T(8,128)(2,1)S(1)}, u32[]{:S(2)}, u32[]{:S(2)}) collective-permute-start(bf16[32,1536]{1,0:T(8,128)(2,1)S(1)} %pad_maximum_fusion), channel_id=1, source_target_pairs={{0,8},{4,12},{8,0},{12,4},{16,24},{20,28},{24,16},{28,20},{1,9},{5... | collective-permute-start | bytes 294920 | tf_op jit(solution)/shard_map/ppermute | solution.py:31
  34.3 6.8 %collective-permute-start.7 = (bf16[32,1536]{1,0:T(8,128)(2,1)S(1)}, bf16[32,1536]{1,0:T(8,128)(2,1)S(1)}, u32[]{:S(2)}, u32[]{:S(2)}) collective-permute-start(bf16[32,1536]{1,0:T(8,128)(2,1)S(1)} %pad_maximum_fusion.1), channel_id=1, source_target_pairs={{0,16},{4,20},{8,24},{12,28},{16,0},{20,4},{24,8},{28,12},{1,17},{... | collective-permute-start | bytes 294920 | tf_op jit(solution)/shard_map/ppermute | solution.py:31
  35.2 5.9 %collective-permute-start.8 = (bf16[32,1536]{1,0:T(8,128)(2,1)S(1)}, bf16[32,1536]{1,0:T(8,128)(2,1)S(1)}, u32[]{:S(2)}, u32[]{:S(2)}) collective-permute-start(bf16[32,1536]{1,0:T(8,128)(2,1)S(1)} %pad_maximum_fusion.2), channel_id=1, source_target_pairs={{0,24},{4,28},{8,16},{12,20},{16,8},{20,12},{24,0},{28,4},{1,25},{... | collective-permute-start | bytes 294920 | tf_op jit(solution)/shard_map/ppermute | solution.py:31
  41.9 1.2 %collective-permute-start.9 = (bf16[128,1536]{1,0:T(8,128)(2,1)S(1)}, bf16[128,1536]{1,0:T(8,128)(2,1)S(1)}, u32[]{:S(2)}, u32[]{:S(2)}) collective-permute-start(bf16[128,1536]{1,0:T(8,128)(2,1)S(1)} %add_convert_fusion.2), channel_id=1, source_target_pairs={{2,1},{6,5},{10,9},{14,13},{18,17},{22,21},{26,25},{30,29}} | collective-permute-start | bytes 1179656 | tf_op jit(solution)/shard_map/ppermute | solution.py:317
  44.2 1.5 %collective-permute-start.10 = (bf16[64,1536]{1,0:T(8,128)(2,1)S(1)}, bf16[64,1536]{1,0:T(8,128)(2,1)S(1)}, u32[]{:S(2)}, u32[]{:S(2)}) collective-permute-start(bf16[64,1536]{1,0:T(8,128)(2,1)S(1)} %slice.149), channel_id=1, source_target_pairs={{0,4},{4,0},{8,12},{12,8},{16,20},{20,16},{24,28},{28,24},{1,5},{5... | collective-permute-start | bytes 589832 | tf_op jit(solution)/shard_map/ppermute | solution.py:31
  45.7 4.9 %collective-permute-start.11 = (bf16[32,1536]{1,0:T(8,128)(2,1)S(1)}, bf16[32,1536]{1,0:T(8,128)(2,1)S(1)}, u32[]{:S(2)}, u32[]{:S(2)}) collective-permute-start(bf16[32,1536]{1,0:T(8,128)(2,1)S(1)} %pad_maximum_fusion.3), channel_id=1, source_target_pairs={{0,8},{4,12},{8,0},{12,4},{16,24},{20,28},{24,16},{28,20},{1,9},{5... | collective-permute-start | bytes 294920 | tf_op jit(solution)/shard_map/ppermute | solution.py:31
  47.0 5.7 %collective-permute-start.12 = (bf16[32,1536]{1,0:T(8,128)(2,1)S(1)}, bf16[32,1536]{1,0:T(8,128)(2,1)S(1)}, u32[]{:S(2)}, u32[]{:S(2)}) collective-permute-start(bf16[32,1536]{1,0:T(8,128)(2,1)S(1)} %pad_maximum_fusion.4), channel_id=1, source_target_pairs={{0,16},{4,20},{8,24},{12,28},{16,0},{20,4},{24,8},{28,12},{1,17},{... | collective-permute-start | bytes 294920 | tf_op jit(solution)/shard_map/ppermute | solution.py:31
  48.2 5.6 %collective-permute-start.13 = (bf16[32,1536]{1,0:T(8,128)(2,1)S(1)}, bf16[32,1536]{1,0:T(8,128)(2,1)S(1)}, u32[]{:S(2)}, u32[]{:S(2)}) collective-permute-start(bf16[32,1536]{1,0:T(8,128)(2,1)S(1)} %pad_maximum_fusion.5), channel_id=1, source_target_pairs={{0,24},{4,28},{8,16},{12,20},{16,8},{20,12},{24,0},{28,4},{1,25},{... | collective-permute-start | bytes 294920 | tf_op jit(solution)/shard_map/ppermute | solution.py:31
  54.5 28.2 %collective-permute-start.14 = (bf16[128,1536]{1,0:T(8,128)(2,1)S(1)}, bf16[128,1536]{1,0:T(8,128)(2,1)S(1)}, u32[]{:S(2)}, u32[]{:S(2)}) collective-permute-start(bf16[128,1536]{1,0:T(8,128)(2,1)S(1)} %add_convert_fusion.1), channel_id=1, source_target_pairs={{1,0},{5,4},{9,8},{13,12},{17,16},{21,20},{25,24},{29,28}} | collective-permute-start | bytes 1179656 | tf_op jit(solution)/shard_map/ppermute | solution.py:317
  84.6 1.5 %collective-permute-start.15 = (bf16[64,1536]{1,0:T(8,128)(2,1)S(1)}, bf16[64,1536]{1,0:T(8,128)(2,1)S(1)}, u32[]{:S(2)}, u32[]{:S(2)}) collective-permute-start(bf16[64,1536]{1,0:T(8,128)(2,1)S(1)} %slice.158), channel_id=1, source_target_pairs={{0,4},{4,0},{8,12},{12,8},{16,20},{20,16},{24,28},{28,24},{1,5},{5... | collective-permute-start | bytes 589832 | tf_op jit(solution)/shard_map/ppermute | solution.py:31
  86.1 4.9 %collective-permute-start.16 = (bf16[32,1536]{1,0:T(8,128)(2,1)S(1)}, bf16[32,1536]{1,0:T(8,128)(2,1)S(1)}, u32[]{:S(2)}, u32[]{:S(2)}) collective-permute-start(bf16[32,1536]{1,0:T(8,128)(2,1)S(1)} %pad_maximum_fusion.6), channel_id=1, source_target_pairs={{0,8},{4,12},{8,0},{12,4},{16,24},{20,28},{24,16},{28,20},{1,9},{5... | collective-permute-start | bytes 294920 | tf_op jit(solution)/shard_map/ppermute | solution.py:31
  87.5 6.8 %collective-permute-start.17 = (bf16[32,1536]{1,0:T(8,128)(2,1)S(1)}, bf16[32,1536]{1,0:T(8,128)(2,1)S(1)}, u32[]{:S(2)}, u32[]{:S(2)}) collective-permute-start(bf16[32,1536]{1,0:T(8,128)(2,1)S(1)} %pad_maximum_fusion.7), channel_id=1, source_target_pairs={{0,16},{4,20},{8,24},{12,28},{16,0},{20,4},{24,8},{28,12},{1,17},{... | collective-permute-start | bytes 294920 | tf_op jit(solution)/shard_map/ppermute | solution.py:31
  88.2 6.1 %collective-permute-start.18 = (bf16[32,1536]{1,0:T(8,128)(2,1)S(1)}, bf16[32,1536]{1,0:T(8,128)(2,1)S(1)}, u32[]{:S(2)}, u32[]{:S(2)}) collective-permute-start(bf16[32,1536]{1,0:T(8,128)(2,1)S(1)} %pad_maximum_fusion.8), channel_id=1, source_target_pairs={{0,24},{4,28},{8,16},{12,20},{16,8},{20,12},{24,0},{28,4},{1,25},{... | collective-permute-start | bytes 294920 | tf_op jit(solution)/shard_map/ppermute | solution.py:31

commit v4 on v1

v4 whole, which is shorter than its diff:
```python
import functools

import jax
import jax.numpy as jnp
from jax import lax
from jax.experimental import pallas as pl
from jax.experimental.pallas import tpu as pltpu
from jax.sharding import PartitionSpec as P

ROWS_BY_ROWS = (((1,), (1,)), ((), ()))
WHOLE = pl.BlockSpec(memory_space=pltpu.VMEM)
ANYWHERE = pl.BlockSpec(memory_space=pl.ANY)


def granted(mebibytes):
    return pltpu.CompilerParams(vmem_limit_bytes=mebibytes << 20)


def in_hbm(array):
    return pltpu.with_memory_space_constraint(array, pltpu.HBM)


def array_of(shape, dtype):
    return jax.ShapeDtypeStruct(shape, dtype)


def dot(left, right):
    return jnp.dot(left, right, preferred_element_type=jnp.float32)


def dot_rows(left, right):
    return lax.dot_general(left, right, ROWS_BY_ROWS, preferred_element_type=jnp.float32)


def swap(block, offset):
    count = lax.axis_size("seq")
    return lax.ppermute(block, "seq", [(i, i ^ offset) for i in range(count)])


def chunks(size, count):
    return [slice(i * size // count, (i + 1) * size // count) for i in range(count)]


def log2(size):
    assert size & (size - 1) == 0
    return size.bit_length() - 1


class Order:
    def __init__(self, row_count, local_blocks, block_rows, seq_count):
        self.row_count = row_count
        self.local_blocks = local_blocks
        self.block_rows = block_rows
        self.seq_count = seq_count
        self.chips = seq_count // 2
        self.steps = block_rows // seq_count
        self.piece = local_blocks * self.steps

    def rows(self, group, count=1):
        return slice(group * self.piece, (group + count) * self.piece)

    def sent(self, position):
        group = position >> log2(self.piece)
        return (group >> log2(self.chips)) + 2 * (group & (self.chips - 1))

    def received(self, position):
        return position >> log2(self.piece)

    def first_rows(self, me, partner, position):
        block = (position >> log2(self.steps)) & (self.local_blocks - 1)
        step = position & (self.steps - 1)
        return block * self.block_rows + (me ^ partner) * self.steps + step

    def second_rows(self, me, partner, position):
        block = (position >> log2(self.steps)) & (self.local_blocks - 1)
        step = position & (self.steps - 1)
        return (step * self.seq_count + (me ^ partner)) * self.local_blocks + block

    def exchange(self, kept, give, streams=1):
        got = swap(give, 1)
        arrived = []
        for chip in range(self.chips):
            rows = self.rows(chip * streams, streams)
            message = jnp.concatenate([kept[rows], got[rows]])
            arrived.append(swap(message, 2 * chip) if chip else message)
        return arrived


def block_diagonal(blocks):
    zero = jnp.zeros(blocks[0].shape, blocks[0].dtype)
    return jnp.concatenate(
        [
            jnp.concatenate([b if k == j else zero for j in range(len(blocks))], axis=1)
            for k, b in enumerate(blocks)
        ],
        axis=0,
    )


def positions(order):
    square = (order.row_count, order.row_count)
    return lax.broadcasted_iota(jnp.int32, square, 0), lax.broadcasted_iota(jnp.int32, square, 1)


def one_hot(matches, dtype=jnp.bfloat16):
    return jnp.where(matches, 1.0, 0.0).astype(dtype)


def rounded(left, right):
    return dot(left, right).astype(jnp.bfloat16)


def begin_kernel(
    order, x_hbm, gain_hbm, first_hbm, second_hbm, gate_hbm, incoming_hbm, out_hbm,
    normed_ref, inv_ref, first_recv_ref, second_send_ref, second_recv_ref,
    mix_factor_ref, slope_ref, hidden_ref, keep_ref, give_ref,
    x_ref, gain_ref, first_ref, second_ref, gate_ref, incoming_ref, out_ref, sems,
):
    parts = chunks(out_hbm.shape[0], sems.shape[0] - 6)
    pairs = [(x_hbm, x_ref), (first_hbm, first_ref), (second_hbm, second_ref), (gain_hbm, gain_ref)]
    pairs += [(gate_hbm, gate_ref), (incoming_hbm, incoming_ref)]
    pairs += [(out_hbm.at[rows], out_ref.at[rows]) for rows in parts]
    copies = [pltpu.make_async_copy(*pair, sems.at[i]) for i, pair in enumerate(pairs)]
    for copy in copies[:5]:
        copy.start()
    active = lax.axis_index("pipe") == lax.axis_size("pipe") - 1

    @pl.when(active)
    def _():
        for copy in copies[5:]:
            copy.start()

    me = lax.axis_index("seq")
    down, across = positions(order)
    for copy in copies[:4]:
        copy.wait()
    first = block_diagonal([first_ref[k].astype(jnp.float32) for k in range(order.local_blocks)])
    second = block_diagonal([second_ref[k].astype(jnp.float32) for k in range(order.local_blocks)])
    sent, received = order.sent(down), order.received(across)
    first_send = rounded(
        one_hot(order.first_rows(me, sent, down) == across), first.astype(jnp.bfloat16)
    )
    second_send_ref[...] = rounded(
        one_hot(order.second_rows(me, sent, down) == across), second.T.astype(jnp.bfloat16)
    )
    first_recv_ref[...] = rounded(
        first.T.astype(jnp.bfloat16), one_hot(order.first_rows(me, received, across) == down)
    )
    second_recv_ref[...] = rounded(
        second.astype(jnp.bfloat16), one_hot(order.second_rows(me, received, across) == down)
    )
    features = x_ref[...].astype(jnp.float32)
    inv_rms = lax.rsqrt(jnp.mean(features * features, axis=-1, keepdims=True) + 1e-06)
    inv_ref[...] = inv_rms
    normed = (features * inv_rms * gain_ref[...]).astype(jnp.bfloat16)
    normed_ref[...] = normed

    def place(send, stream, columns):
        for core, target in enumerate((keep_ref, give_ref)):
            for chip in range(order.chips):
                rows = order.rows(2 * chip + stream)
                target[rows, columns] = send[order.rows(core * order.chips + chip)]

    place(rounded(first_send, normed), 0, slice(None))
    copies[4].wait()
    gate_pre = dot(normed, gate_ref[...])
    sigma = jax.nn.sigmoid(gate_pre)
    mix_factor_ref[...] = gate_pre * sigma
    slope_ref[...] = sigma * (1.0 + gate_pre * (1.0 - sigma))

    @pl.when(active)
    def _():
        copies[5].wait()
        for columns, copy in zip(parts, copies[6:]):
            copy.wait()
            hidden = dot_rows(incoming_ref[...], out_ref[columns])
            hidden_ref[:, columns] = hidden
            mix = (hidden * mix_factor_ref[:, columns]).astype(jnp.bfloat16)
            place(rounded(second_send_ref[...], mix), 1, columns)

    @pl.when(jnp.logical_not(active))
    def _():
        hidden_ref[...] = jnp.zeros(hidden_ref.shape, hidden_ref.dtype)
        place(jnp.zeros(normed_ref.shape, normed_ref.dtype), 1, slice(None))


def begin(order, *operands):
    row_count, width = operands[0].shape
    square = array_of((row_count, row_count), jnp.bfloat16)
    short = array_of((row_count, width), jnp.bfloat16)
    full = array_of((row_count, width), jnp.float32)
    column = array_of((row_count, 1), jnp.float32)
    outs = [short, column, square, square, square, full, full, full, short, short]
    return pl.pallas_call(
        functools.partial(begin_kernel, order),
        in_specs=[ANYWHERE] * len(operands),
        out_specs=[WHOLE] * len(outs),
        out_shape=outs,
        scratch_shapes=[pltpu.VMEM(o.shape, o.dtype) for o in operands]
        + [pltpu.SemaphoreType.DMA((9,))],
        compiler_params=granted(13),
        name="begin",
    )(*[in_hbm(o) for o in operands])


def transpose_kernel(weight_hbm, after_ref, turned_ref, held, sems):
    parts = chunks(held.shape[0], sems.shape[0])
    copies = [
        pltpu.make_async_copy(weight_hbm.at[rows], held.at[rows], sems.at[i])
        for i, rows in enumerate(parts)
    ]
    for copy in copies:
        copy.start()
    for rows, copy in zip(parts, copies):
        copy.wait()
        turned_ref[:, rows] = held[rows].T


def transposed(weight, after):
    return pl.pallas_call(
        transpose_kernel,
        in_specs=[ANYWHERE, ANYWHERE],
        out_specs=WHOLE,
        out_shape=pltpu.VMEM(weight.shape[::-1], jnp.bfloat16),
        scratch_shapes=[pltpu.VMEM(weight.shape, weight.dtype), pltpu.SemaphoreType.DMA((6,))],
        compiler_params=granted(6),
        name="transposed",
    )(in_hbm(weight), after)


def outgoing_of(gate_back, first_back, gain, inputs, inv_rms, incoming):
    delta_norm = (first_back + gate_back) * gain
    unit_rows = inputs.astype(jnp.float32) * inv_rms
    centred = delta_norm - unit_rows * jnp.mean(delta_norm * unit_rows, axis=-1, keepdims=True)
    return (incoming.astype(jnp.float32) + inv_rms * centred).astype(jnp.bfloat16)


def finish_kernel(order, *refs):
    arrived, refs = refs[: order.chips], refs[order.chips :]
    (
        second_recv_ref, first_recv_ref, slope_ref, hidden_ref, gate_ref, gain_ref, x_ref, inv_ref,
        incoming_ref, moved_ref, mid_ref, gate_factor_ref, outgoing_ref,
    ) = refs
    for chip, message in enumerate(arrived):
        for core in range(2):
            for stream, target in enumerate((moved_ref, mid_ref)):
                target[order.rows(2 * chip + core)] = message[order.rows(2 * core + stream)]
    gate_factor = dot(second_recv_ref[...], moved_ref[...]) * slope_ref[...]
    gate_factor_ref[...] = gate_factor
    delta_gate = (hidden_ref[...] * gate_factor).astype(jnp.bfloat16)
    gate_back = dot(delta_gate, gate_ref[...])
    first_back = dot(first_recv_ref[...], mid_ref[...])
    outgoing_ref[...] = outgoing_of(
        gate_back, first_back, gain_ref[...], x_ref[...], inv_ref[...], incoming_ref[...]
    )


def finish(order, *operands):
    row_count, width = operands[-1].shape
    short = array_of((row_count, width), jnp.bfloat16)
    full = array_of((row_count, width), jnp.float32)
    return pl.pallas_call(
        functools.partial(finish_kernel, order),
        in_specs=[WHOLE] * len(operands),
        out_specs=[WHOLE] * 4,
        out_shape=[short, short, full, short],
        compiler_params=granted(4),
        name="finish",
    )(*operands)


def advance_kernel(
    mid_ref, first_recv_ref, gate_back_ref, gain_ref, x_ref, inv_ref, incoming_ref, outgoing_ref
):
    first_back = dot(first_recv_ref[...], mid_ref[...])
    outgoing_ref[...] = outgoing_of(
        gate_back_ref[...], first_back, gain_ref[...], x_ref[...], inv_ref[...], incoming_ref[...]
    )


def advance(*operands):
    return pl.pallas_call(
        advance_kernel,
        in_specs=[WHOLE] * len(operands),
        out_specs=WHOLE,
        out_shape=array_of(operands[0].shape, jnp.bfloat16),
        compiler_params=granted(4),
        name="advance",
    )(*operands)


def keep_kernel(
    section, outgoing_ref, mid_ref, mix_ref, normed_ref, moved_ref, *refs
):
    kept, new = refs[:3], refs[3:]
    active = lax.axis_index("pipe") == section

    @pl.when(active)
    def _():
        new[0][...] = outgoing_ref[...]
        new[1][...] = dot_rows(mid_ref[...], normed_ref[...])
        new[2][...] = dot_rows(mix_ref[...], moved_ref[...])

    @pl.when(jnp.logical_not(active))
    def _():
        for old_ref, new_ref in zip(kept, new):
            new_ref[...] = old_ref[...]


def keep(section, kept, *operands):
    count = len(operands)
    return pl.pallas_call(
        functools.partial(keep_kernel, section),
        in_specs=[WHOLE] * (count + 3),
        out_specs=[WHOLE] * 3,
        out_shape=[array_of(k.shape, k.dtype) for k in kept],
        input_output_aliases={count + i: i for i in range(3)},
        compiler_params=granted(2),
        name="keep",
    )(*operands, *kept)


def close_kernel(
    order, mid_ref, mix_ref, moved_ref, first_recv_ref, gate_back_ref, gain_ref, x_ref, inv_ref, incoming_ref, normed_ref,
    outgoing_kept_ref, first_kept_ref, second_kept_ref, outgoing_ref, first_ref, second_ref,
):
    active = lax.axis_index("pipe") == 0
    first_back = dot(first_recv_ref[...], mid_ref[...])
    outgoing = outgoing_of(
        gate_back_ref[...], first_back, gain_ref[...], x_ref[...], inv_ref[...], incoming_ref[...]
    )
    outgoing_ref[...] = jnp.where(active, outgoing, outgoing_kept_ref[...])
    first = jnp.where(active, dot_rows(mid_ref[...], normed_ref[...]), first_kept_ref[...])
    second = jnp.where(active, dot_rows(mix_ref[...], moved_ref[...]), second_kept_ref[...])
    me = lax.axis_index("seq")
    down, across = positions(order)

    def exact(left, right):
        return jnp.dot(
            left, right, precision=lax.Precision.HIGHEST, preferred_element_type=jnp.float32
        )

    to_first = order.first_rows(me, order.received(across), across) == down
    to_second = order.second_rows(me, order.received(down), down) == across
    first = exact(one_hot(to_first, jnp.float32), first)
    second = exact(second, one_hot(to_second, jnp.float32))
    for k, rows in enumerate(chunks(order.row_count, order.local_blocks)):
        first_ref[k] = first[rows, rows]
        second_ref[k] = second[rows, rows]


def close(order, *operands):
    row_count, width = operands[0].shape
    blocks = array_of((order.local_blocks, order.block_rows, order.block_rows), jnp.float32)
    return pl.pallas_call(
        functools.partial(close_kernel, order),
        in_specs=[WHOLE] * len(operands),
        out_specs=[WHOLE] * 3,
        out_shape=[array_of((row_count, width), jnp.bfloat16), blocks, blocks],
        compiler_params=granted(4),
        name="close",
    )(*operands)


def per_device(section_inputs, cotangent, gain, w_gate, w_out, mix_first, mix_second):
    inputs = section_inputs[0]
    local_blocks, block_rows = mix_first.shape[1:3]
    section_count = lax.axis_size("pipe")
    order = Order(inputs.shape[0], local_blocks, block_rows, lax.axis_size("seq"))

    (
        normed, inv_rms, first_recv, second_send, second_recv,
        mix_factor, slope, delta_hidden, kept, give,
    ) = begin(
        order, inputs, gain, mix_first[0], mix_second[0], w_gate[0], cotangent, w_out[0]
    )
    arrived = order.exchange(kept, give, streams=2)
    gate_turned = transposed(w_gate[0], arrived[0])
    moved, delta_mid, gate_factor, outgoing = finish(
        order, *arrived, second_recv, first_recv, slope, delta_hidden, gate_turned, gain,
        inputs, inv_rms, cotangent,
    )
    out_turned = transposed(w_out[0], outgoing)

    delta_mix = (delta_hidden * mix_factor).astype(jnp.bfloat16)
    kept = (outgoing, dot_rows(delta_mid, normed), dot_rows(delta_mix, moved))
    for sender in reversed(range(section_count - 1)):
        incoming = lax.ppermute(outgoing, "pipe", [(sender + 1, sender)])
        delta_hidden = dot(incoming, out_turned)
        delta_mix = (delta_hidden * mix_factor).astype(jnp.bfloat16)
        send = rounded(second_send, delta_mix)
        delta_mid = jnp.concatenate(order.exchange(*jnp.split(send, 2)))
        delta_gate = (delta_hidden * gate_factor).astype(jnp.bfloat16)
        gate_back = dot(delta_gate, gate_turned)
        if sender > 0:
            outgoing = advance(delta_mid, first_recv, gate_back, gain, inputs, inv_rms, incoming)
            kept = keep(sender, kept, outgoing, delta_mid, delta_mix, normed, moved)
    grad_inputs, grad_first, grad_second = close(
        order, delta_mid, delta_mix, moved, first_recv, gate_back, gain, inputs, inv_rms, incoming,
        normed, *kept,
    )
    return (grad_inputs[None], grad_first[None], grad_second[None])


def solution(mesh):
    placed = (
        P("pipe", "seq", None),
        P("seq", None),
        P("pipe", None),
        P("pipe", None, None),
        P("pipe", None, None),
        P("pipe", "seq", None, None),
        P("pipe", "seq", None, None),
    )
    return jax.shard_map(
        per_device,
        mesh=mesh,
        in_specs=placed,
        out_specs=(
            P("pipe", "seq", None),
            P("pipe", "seq", None, None),
            P("pipe", "seq", None, None),
        ),
        check_vma=False,
    )
```

time: 113 us -> 91.2 us (0.81)
  matrix products: 28.3 us -> 6.1 us
  Pallas kernels: 0 us -> 13.2 us
  other arithmetic: 8.77 us -> 0.14 us
  waiting for transfers between devices: 44.7 us -> 51.3 us
  local copies, waits for them, and re-layouts: 6.71 us -> 0.27 us
  starting transfers between devices: 22.5 us -> 19 us
    dot_general x16 -> x2, matrix products: 18.1 us -> 0.53 us  [dot_rows(): lax.dot_general(left, right, ROWS_BY_ROWS, preferred_element_type=jnp.flo...]
    pallas_call x0 -> x9, Pallas kernels: none -> 13.2 us  [the longest x2 5.54 us: transposed(): pl.pallas_call(transpose_kernel, in_specs=[ANYWHERE, ANYWHERE], out_specs...]
    ppermute x20 -> x16, waiting for transfers between devices: 14.5 us -> 22.8 us  [swap(): return lax.ppermute(block, 'seq', [(i, i ^ offset) for i in range(count)])]
    dot_general x13 -> x9, matrix products: 9.63 us -> 5.57 us  [dot(): return jnp.dot(left, right, preferred_element_type=jnp.float32)]
    ppermute x20 -> x16, starting transfers between devices: 19.6 us -> 16.3 us  [swap(): return lax.ppermute(block, 'seq', [(i, i ^ offset) for i in range(count)])]
    concatenate x15 -> x13, other arithmetic: 2.84 us -> 0.14 us  [exchange(): message = jnp.concatenate([kept[rows], got[rows]])]
    slice x15 -> x8, local copies, waits for them, and re-layouts: 2.77 us -> 0.14 us  [exchange(): message = jnp.concatenate([kept[rows], got[rows]])]
    broadcast_in_dim x3 -> x0, other arithmetic: 2.47 us -> none  [per_device(): return (outgoing_kept[None], grad_first[None], grad_second[None])]
  transfers between devices with their start and end apart: 23 -> 19, of which waited for: 10 -> 15; matrix products, arithmetic and copies ran while one was open for 22% -> 3% of each run, Pallas kernels for 0% -> 6%
where the time goes in v4:
time: 91.2 us; the launch traced here: 91.1 us
  waiting for transfers between devices  51.3 us (56%)
  starting transfers between devices  19 us (21%)
  Pallas kernels  13.2 us (14%)
  matrix products  6.1 us (7%)
  between operations  1.04 us (1%)
    ppermute x3, waiting for transfers between devices, per_device(): incoming = lax.ppermute(outgoing, 'pipe', [(sender + 1, sender)])  28.5 us
    ppermute x16, waiting for transfers between devices, swap(): return lax.ppermute(block, 'seq', [(i, i ^ offset) for i in range(count)])  22.8 us
    ppermute x16, starting transfers between devices, swap(): return lax.ppermute(block, 'seq', [(i, i ^ offset) for i in range(count)])  16.3 us
    dot_general x9, matrix products, dot(): return jnp.dot(left, right, preferred_element_type=jnp.float32)  5.57 us
    pallas_call x2, Pallas kernels, transposed(): pl.pallas_call(transpose_kernel, in_specs=[ANYWHERE, ANYWHERE], out_specs...  5.54 us
    pallas_call x1, Pallas kernels, begin(): pl.pallas_call(functools.partial(begin_kernel, order), in_specs=[ANYWHERE...  3.53 us
    ppermute x3, starting transfers between devices, per_device(): incoming = lax.ppermute(outgoing, 'pipe', [(sender + 1, sender)])  2.66 us
  transfers between devices with their start and end apart: 19, of which 15 were waited for; matrix products, arithmetic and copies ran while one was open for 3% of the time, Pallas kernels for 6%

profile of v4, /device:TPU:0, one launch (start us, length us, event | category | flops | bytes accessed | tf_op | source)
XLA Modules:
  0.0 91.1 jit_solution(16924281873378652594)
XLA Ops:
  0.6 3.5 %begin.1 = (bf16[128,1536]{1,0:T(8,128)(2,1)S(1)}, f32[128,1]{1,0:T(8,128)S(1)}, bf16[128,128]{1,0:T(8,128)(2,1)S(1)}, bf16[128,128]{1,0:T(8,128)(2,1)S(1)}, bf1...) custom-call(bf16[128,1536]{1,0:T(8,128)(2,1)} %bitcast.26, ...), custom_call_target="tpu_custom_call" | custom-call | tf_op jit(solution)/shard_map/begin/pallas_call | solution.py:194
  4.2 0.5 collective-permute-start
  4.7 1.3 %collective-permute-done = bf16[128,1536]{1,0:T(8,128)(2,1)S(1)} collective-permute-done((bf16[128,1536]{1,0:T(8,128)(2,1)S(1)}, bf16[128,1536]{1,0:T(8,128)(2,1)S(1)}, u32[]{:S(2)}, u32[]{:S(2)}) %collective-permute-start) | collective-permute-done | bytes 393248 | tf_op jit(solution)/shard_map/ppermute | solution.py:37
  6.1 2.9 %collective-permute-start.1 = (bf16[64,1536]{1,0:T(8,128)(2,1)S(1)}, bf16[64,1536]{1,0:T(8,128)(2,1)S(1)}, u32[]{:S(2)}, u32[]{:S(2)}) collective-permute-start(bf16[64,1536]{1,0:T(8,128)(2,1)S(1)} %pad_maximum_fusion.1), channel_id=1, source_target_pairs={{0,8},{4,12},{8,0},{12,4},{16,24},{20,28},{24,16},{28,20},{1,9},{5... | collective-permute-start | bytes 589832 | tf_op jit(solution)/shard_map/ppermute | solution.py:37
  9.0 1.6 %collective-permute-start.2 = (bf16[64,1536]{1,0:T(8,128)(2,1)S(1)}, bf16[64,1536]{1,0:T(8,128)(2,1)S(1)}, u32[]{:S(2)}, u32[]{:S(2)}) collective-permute-start(bf16[64,1536]{1,0:T(8,128)(2,1)S(1)} %pad_maximum_fusion.2), channel_id=1, source_target_pairs={{0,16},{4,20},{8,24},{12,28},{16,0},{20,4},{24,8},{28,12},{1,17},{... | collective-permute-start | bytes 589832 | tf_op jit(solution)/shard_map/ppermute | solution.py:37
  10.6 0.1 collective-permute-start.3
  10.7 0.0 copy-start
  10.8 0.0 copy-start.1
  10.8 0.0 copy-start.2
  10.8 2.8 %transposed.2.refs_8_ = bf16[1536,1536]{1,0:T(8,128)(2,1)S(1)} custom-call(bf16[1536,1536]{1,0:T(8,128)(2,1)} %bitcast.32, bf16[64,1536]{1,0:T(8,128)(2,1)S(1)} %pad_maximum_fusion.after_ref.refs_0_), custom_call_target="tpu_custom_call" | custom-call | tf_op jit(solution)/shard_map/transposed/pallas_call | solution.py:220
  13.6 1.1 %collective-permute-done.1.refs_1_ = bf16[64,1536]{1,0:T(8,128)(2,1)S(1)} collective-permute-done((bf16[64,1536]{1,0:T(8,128)(2,1)S(1)}, bf16[64,1536]{1,0:T(8,128)(2,1)S(1)}, u32[]{:S(2)}, u32[]{:S(2)}) %collective-permute-start.1) | collective-permute-done | bytes 196640 | tf_op jit(solution)/shard_map/ppermute | solution.py:37
  14.7 5.3 %collective-permute-done.2.refs_2_ = bf16[64,1536]{1,0:T(8,128)(2,1)S(1)} collective-permute-done((bf16[64,1536]{1,0:T(8,128)(2,1)S(1)}, bf16[64,1536]{1,0:T(8,128)(2,1)S(1)}, u32[]{:S(2)}, u32[]{:S(2)}) %collective-permute-start.2) | collective-permute-done | bytes 196640 | tf_op jit(solution)/shard_map/ppermute | solution.py:37
  20.0 0.0 collective-permute-done.3.refs_3_
  20.0 0.0 copy-done
  20.0 0.0 copy-done.1
  20.0 0.0 copy-done.2
  20.0 1.3 %finish.1 = (bf16[128,1536]{1,0:T(8,128)(2,1)S(1)}, bf16[128,1536]{1,0:T(8,128)(2,1)S(1)}, f32[128,1536]{1,0:T(8,128)S(1)}, bf16[128,1536]{1,0:T(8,128)(2,1)S(1)}) custom-call(bf16[64,1536]{1,0:T(8,128)(2,1)S(1)} %pad_maximum_fusion.after_ref.refs_0_, bf16[64,1536]{1,0:T(8,128)(2,1)S(1)} %collective-permute-done.1.refs_1_, ...), custom_call_target="tpu_custom_call" | custom-call | tf_op jit(solution)/shard_map/finish/pallas_call | solution.py:262
  21.3 0.7 collective-permute-start.4
  22.0 2.7 %transposed.3 = bf16[1536,1536]{1,0:T(8,128)(2,1)S(1)} custom-call(bf16[1536,1536]{1,0:T(8,128)(2,1)} %bitcast.34, bf16[128,1536]{1,0:T(8,128)(2,1)S(1)} %get-tuple-element.34.after_ref.refs_0_), custom_call_target="tpu_custom_call" | custom-call | tf_op jit(solution)/shard_map/transposed/pallas_call | solution.py:220
  24.7 0.0 collective-permute-done.4.incoming_ref
  24.7 0.8 multiply_convert_fusion.6
  25.5 0.2 convolution_convert_fusion.2
  25.8 0.1 collective-permute-start.5
  25.9 0.8 fusion.gate_back_ref
  26.7 0.6 collective-permute-done.5
  27.3 1.2 %collective-permute-start.6 = (bf16[32,1536]{1,0:T(8,128)(2,1)S(1)}, bf16[32,1536]{1,0:T(8,128)(2,1)S(1)}, u32[]{:S(2)}, u32[]{:S(2)}) collective-permute-start(bf16[32,1536]{1,0:T(8,128)(2,1)S(1)} %pad_maximum_fusion.4), channel_id=1, source_target_pairs={{0,8},{4,12},{8,0},{12,4},{16,24},{20,28},{24,16},{28,20},{1,9},{5... | collective-permute-start | bytes 294920 | tf_op jit(solution)/shard_map/ppermute | solution.py:37
  28.6 1.0 %collective-permute-start.7 = (bf16[32,1536]{1,0:T(8,128)(2,1)S(1)}, bf16[32,1536]{1,0:T(8,128)(2,1)S(1)}, u32[]{:S(2)}, u32[]{:S(2)}) collective-permute-start(bf16[32,1536]{1,0:T(8,128)(2,1)S(1)} %pad_maximum_fusion.5), channel_id=1, source_target_pairs={{0,16},{4,20},{8,24},{12,28},{16,0},{20,4},{24,8},{28,12},{1,17},{... | collective-permute-start | bytes 294920 | tf_op jit(solution)/shard_map/ppermute | solution.py:37
  29.5 1.5 %collective-permute-start.8 = (bf16[32,1536]{1,0:T(8,128)(2,1)S(1)}, bf16[32,1536]{1,0:T(8,128)(2,1)S(1)}, u32[]{:S(2)}, u32[]{:S(2)}) collective-permute-start(bf16[32,1536]{1,0:T(8,128)(2,1)S(1)} %pad_maximum_fusion.6), channel_id=1, source_target_pairs={{0,24},{4,28},{8,16},{12,20},{16,8},{20,12},{24,0},{28,4},{1,25},{... | collective-permute-start | bytes 294920 | tf_op jit(solution)/shard_map/ppermute | solution.py:37
  31.0 1.2 %collective-permute-done.6 = bf16[32,1536]{1,0:T(8,128)(2,1)S(1)} collective-permute-done((bf16[32,1536]{1,0:T(8,128)(2,1)S(1)}, bf16[32,1536]{1,0:T(8,128)(2,1)S(1)}, u32[]{:S(2)}, u32[]{:S(2)}) %collective-permute-start.6) | collective-permute-done | bytes 98336 | tf_op jit(solution)/shard_map/ppermute | solution.py:37
  32.3 1.7 %collective-permute-done.7 = bf16[32,1536]{1,0:T(8,128)(2,1)S(1)} collective-permute-done((bf16[32,1536]{1,0:T(8,128)(2,1)S(1)}, bf16[32,1536]{1,0:T(8,128)(2,1)S(1)}, u32[]{:S(2)}, u32[]{:S(2)}) %collective-permute-start.7) | collective-permute-done | bytes 98336 | tf_op jit(solution)/shard_map/ppermute | solution.py:37
  34.0 1.3 %collective-permute-done.8 = bf16[32,1536]{1,0:T(8,128)(2,1)S(1)} collective-permute-done((bf16[32,1536]{1,0:T(8,128)(2,1)S(1)}, bf16[32,1536]{1,0:T(8,128)(2,1)S(1)}, u32[]{:S(2)}, u32[]{:S(2)}) %collective-permute-start.8) | collective-permute-done | bytes 98336 | tf_op jit(solution)/shard_map/ppermute | solution.py:37
  35.3 0.5 advance.2.outgoing_ref
  35.8 0.7 collective-permute-start.9
  36.5 0.0 collective-permute-done.9.incoming_ref
  36.5 0.8 multiply_convert_fusion.4
  37.3 0.2 convolution_convert_fusion.1
  37.6 0.1 collective-permute-start.10
  37.7 0.8 fusion.1.gate_back_ref
  38.5 0.6 collective-permute-done.10
  39.2 1.3 %collective-permute-start.11 = (bf16[32,1536]{1,0:T(8,128)(2,1)S(1)}, bf16[32,1536]{1,0:T(8,128)(2,1)S(1)}, u32[]{:S(2)}, u32[]{:S(2)}) collective-permute-start(bf16[32,1536]{1,0:T(8,128)(2,1)S(1)} %pad_maximum_fusion.7), channel_id=1, source_target_pairs={{0,8},{4,12},{8,0},{12,4},{16,24},{20,28},{24,16},{28,20},{1,9},{5... | collective-permute-start | bytes 294920 | tf_op jit(solution)/shard_map/ppermute | solution.py:37
  40.5 1.2 %collective-permute-start.12 = (bf16[32,1536]{1,0:T(8,128)(2,1)S(1)}, bf16[32,1536]{1,0:T(8,128)(2,1)S(1)}, u32[]{:S(2)}, u32[]{:S(2)}) collective-permute-start(bf16[32,1536]{1,0:T(8,128)(2,1)S(1)} %pad_maximum_fusion.8), channel_id=1, source_target_pairs={{0,16},{4,20},{8,24},{12,28},{16,0},{20,4},{24,8},{28,12},{1,17},{... | collective-permute-start | bytes 294920 | tf_op jit(solution)/shard_map/ppermute | solution.py:37
  41.8 1.1 %collective-permute-start.13 = (bf16[32,1536]{1,0:T(8,128)(2,1)S(1)}, bf16[32,1536]{1,0:T(8,128)(2,1)S(1)}, u32[]{:S(2)}, u32[]{:S(2)}) collective-permute-start(bf16[32,1536]{1,0:T(8,128)(2,1)S(1)} %pad_maximum_fusion.9), channel_id=1, source_target_pairs={{0,24},{4,28},{8,16},{12,20},{16,8},{20,12},{24,0},{28,4},{1,25},{... | collective-permute-start | bytes 294920 | tf_op jit(solution)/shard_map/ppermute | solution.py:37
  42.9 1.2 %collective-permute-done.11 = bf16[32,1536]{1,0:T(8,128)(2,1)S(1)} collective-permute-done((bf16[32,1536]{1,0:T(8,128)(2,1)S(1)}, bf16[32,1536]{1,0:T(8,128)(2,1)S(1)}, u32[]{:S(2)}, u32[]{:S(2)}) %collective-permute-start.11) | collective-permute-done | bytes 98336 | tf_op jit(solution)/shard_map/ppermute | solution.py:37
  44.1 2.2 %collective-permute-done.12 = bf16[32,1536]{1,0:T(8,128)(2,1)S(1)} collective-permute-done((bf16[32,1536]{1,0:T(8,128)(2,1)S(1)}, bf16[32,1536]{1,0:T(8,128)(2,1)S(1)}, u32[]{:S(2)}, u32[]{:S(2)}) %collective-permute-start.12) | collective-permute-done | bytes 98336 | tf_op jit(solution)/shard_map/ppermute | solution.py:37
  46.3 1.1 %collective-permute-done.13 = bf16[32,1536]{1,0:T(8,128)(2,1)S(1)} collective-permute-done((bf16[32,1536]{1,0:T(8,128)(2,1)S(1)}, bf16[32,1536]{1,0:T(8,128)(2,1)S(1)}, u32[]{:S(2)}, u32[]{:S(2)}) %collective-permute-start.13) | collective-permute-done | bytes 98336 | tf_op jit(solution)/shard_map/ppermute | solution.py:37
  47.3 0.5 advance.3.outgoing_ref
  47.8 1.3 %collective-permute-start.14 = (bf16[128,1536]{1,0:T(8,128)(2,1)S(1)}, bf16[128,1536]{1,0:T(8,128)(2,1)S(1)}, u32[]{:S(2)}, u32[]{:S(2)}) collective-permute-start(bf16[128,1536]{1,0:T(8,128)(2,1)S(1)} %advance.3.outgoing_ref), channel_id=1, source_target_pairs={{1,0},{5,4},{9,8},{13,12},{17,16},{21,20},{25,24},{29,28}} | collective-permute-start | bytes 1179656 | tf_op jit(solution)/shard_map/ppermute | solution.py:388
  49.1 0.3 fusion.12.refs_1_
  49.4 0.3 fusion.3.refs_2_
  49.7 0.1 keep.2
  49.8 0.3 keep.3
  50.0 28.5 %collective-permute-done.14.incoming_ref = bf16[128,1536]{1,0:T(8,128)(2,1)S(1)} collective-permute-done((bf16[128,1536]{1,0:T(8,128)(2,1)S(1)}, bf16[128,1536]{1,0:T(8,128)(2,1)S(1)}, u32[]{:S(2)}, u32[]{:S(2)}) %collective-permute-start.14) | collective-permute-done | bytes 393248 | tf_op jit(solution)/shard_map/ppermute | solution.py:388
  78.5 0.8 multiply_convert_fusion.2
  79.3 0.2 convolution_convert_fusion
  79.6 0.1 collective-permute-start.15
  79.7 0.8 fusion.2.gate_back_ref
  80.5 0.6 collective-permute-done.15
  81.2 1.4 %collective-permute-start.16 = (bf16[32,1536]{1,0:T(8,128)(2,1)S(1)}, bf16[32,1536]{1,0:T(8,128)(2,1)S(1)}, u32[]{:S(2)}, u32[]{:S(2)}) collective-permute-start(bf16[32,1536]{1,0:T(8,128)(2,1)S(1)} %pad_maximum_fusion.10), channel_id=1, source_target_pairs={{0,8},{4,12},{8,0},{12,4},{16,24},{20,28},{24,16},{28,20},{1,9},{5... | collective-permute-start | bytes 294920 | tf_op jit(solution)/shard_map/ppermute | solution.py:37
  82.6 0.7 collective-permute-start.17
  83.4 1.5 %collective-permute-start.18 = (bf16[32,1536]{1,0:T(8,128)(2,1)S(1)}, bf16[32,1536]{1,0:T(8,128)(2,1)S(1)}, u32[]{:S(2)}, u32[]{:S(2)}) collective-permute-start(bf16[32,1536]{1,0:T(8,128)(2,1)S(1)} %pad_maximum_fusion.12), channel_id=1, source_target_pairs={{0,24},{4,28},{8,16},{12,20},{16,8},{20,12},{24,0},{28,4},{1,25},{... | collective-permute-start | bytes 294920 | tf_op jit(solution)/shard_map/ppermute | solution.py:37
  84.9 1.2 %collective-permute-done.16 = bf16[32,1536]{1,0:T(8,128)(2,1)S(1)} collective-permute-done((bf16[32,1536]{1,0:T(8,128)(2,1)S(1)}, bf16[32,1536]{1,0:T(8,128)(2,1)S(1)}, u32[]{:S(2)}, u32[]{:S(2)}) %collective-permute-start.16) | collective-permute-done | bytes 98336 | tf_op jit(solution)/shard_map/ppermute | solution.py:37
  86.1 3.3 %collective-permute-done.17 = bf16[32,1536]{1,0:T(8,128)(2,1)S(1)} collective-permute-done((bf16[32,1536]{1,0:T(8,128)(2,1)S(1)}, bf16[32,1536]{1,0:T(8,128)(2,1)S(1)}, u32[]{:S(2)}, u32[]{:S(2)}) %collective-permute-start.17) | collective-permute-done | bytes 98336 | tf_op jit(solution)/shard_map/ppermute | solution.py:37
  89.4 0.0 collective-permute-done.18
  89.5 1.6 %close.1 = (bf16[128,1536]{1,0:T(8,128)(2,1)}, f32[2,64,64]{2,1,0:T(8,128)}, f32[2,64,64]{2,1,0:T(8,128)}) custom-call(bf16[128,1536]{1,0:T(8,128)(2,1)S(1)} %constant_dynamic-update-slice_fusion.6.mid_ref, bf16[128,1536]{1,0:T(8,128)(2,1)S(1)} %get-tuple-element.85.mix_ref, bf16[128,1536]{1,0:T(8,128)(2,1)S(1)} %get-tuple-element.37.moved_ref, ...), custom_call_target="tpu_custom_call" | custom-call | tf_op jit(solution)/shard_map/close/pallas_call | solution.py:355
  (33 shorter events, 0.4 us)
Async XLA Ops:
  4.2 1.9 %collective-permute-start = (bf16[128,1536]{1,0:T(8,128)(2,1)S(1)}, bf16[128,1536]{1,0:T(8,128)(2,1)S(1)}, u32[]{:S(2)}, u32[]{:S(2)}) collective-permute-start(bf16[128,1536]{1,0:T(8,128)(2,1)S(1)} %get-tuple-element.28), channel_id=1, source_target_pairs={{0,4},{4,0},{8,12},{12,8},{16,20},{20,16},{24,28},{28,24},{1,5},{5... | collective-permute-start | bytes 1179656 | tf_op jit(solution)/shard_map/ppermute | solution.py:37
  6.1 8.6 %collective-permute-start.1 = (bf16[64,1536]{1,0:T(8,128)(2,1)S(1)}, bf16[64,1536]{1,0:T(8,128)(2,1)S(1)}, u32[]{:S(2)}, u32[]{:S(2)}) collective-permute-start(bf16[64,1536]{1,0:T(8,128)(2,1)S(1)} %pad_maximum_fusion.1), channel_id=1, source_target_pairs={{0,8},{4,12},{8,0},{12,4},{16,24},{20,28},{24,16},{28,20},{1,9},{5... | collective-permute-start | bytes 589832 | tf_op jit(solution)/shard_map/ppermute | solution.py:37
  9.0 10.9 %collective-permute-start.2 = (bf16[64,1536]{1,0:T(8,128)(2,1)S(1)}, bf16[64,1536]{1,0:T(8,128)(2,1)S(1)}, u32[]{:S(2)}, u32[]{:S(2)}) collective-permute-start(bf16[64,1536]{1,0:T(8,128)(2,1)S(1)} %pad_maximum_fusion.2), channel_id=1, source_target_pairs={{0,16},{4,20},{8,24},{12,28},{16,0},{20,4},{24,8},{28,12},{1,17},{... | collective-permute-start | bytes 589832 | tf_op jit(solution)/shard_map/ppermute | solution.py:37
  10.6 9.3 %collective-permute-start.3 = (bf16[64,1536]{1,0:T(8,128)(2,1)S(1)}, bf16[64,1536]{1,0:T(8,128)(2,1)S(1)}, u32[]{:S(2)}, u32[]{:S(2)}) collective-permute-start(bf16[64,1536]{1,0:T(8,128)(2,1)S(1)} %pad_maximum_fusion.3), channel_id=1, source_target_pairs={{0,24},{4,28},{8,16},{12,20},{16,8},{20,12},{24,0},{28,4},{1,25},{... | collective-permute-start | bytes 589832 | tf_op jit(solution)/shard_map/ppermute | solution.py:37
  10.7 9.2 %copy-start = (bf16[1,128,1536]{2,1,0:T(8,128)(2,1)S(1)}, bf16[1,128,1536]{2,1,0:T(8,128)(2,1)}, u32[]{:S(2)}) copy-start(bf16[1,128,1536]{2,1,0:T(8,128)(2,1)} %param.7) | copy-start | bytes 1179652
  10.8 9.2 %copy-start.1 = (bf16[128,1536]{1,0:T(8,128)(2,1)S(1)}, bf16[128,1536]{1,0:T(8,128)(2,1)}, u32[]{:S(2)}) copy-start(bf16[128,1536]{1,0:T(8,128)(2,1)} %refs_12_.1) | copy-start | bytes 1179652
  10.8 9.2 %copy-start.2 = (f32[1,1536]{1,0:T(1,128)S(1)}, f32[1,1536]{1,0:T(1,128)}, u32[]{:S(2)}) copy-start(f32[1,1536]{1,0:T(1,128)} %gain_ref.5) | copy-start | bytes 18436
  21.3 3.4 %collective-permute-start.4 = (bf16[128,1536]{1,0:T(8,128)(2,1)S(1)}, bf16[128,1536]{1,0:T(8,128)(2,1)S(1)}, u32[]{:S(2)}, u32[]{:S(2)}) collective-permute-start(bf16[128,1536]{1,0:T(8,128)(2,1)S(1)} %get-tuple-element.34.after_ref.refs_0_), channel_id=1, source_target_pairs={{3,2},{7,6},{11,10},{15,14},{19,18},{23,22},{27,26},{31,30}} | collective-permute-start | bytes 1179656 | tf_op jit(solution)/shard_map/ppermute | solution.py:388
  25.8 1.5 %collective-permute-start.5 = (bf16[64,1536]{1,0:T(8,128)(2,1)S(1)}, bf16[64,1536]{1,0:T(8,128)(2,1)S(1)}, u32[]{:S(2)}, u32[]{:S(2)}) collective-permute-start(bf16[64,1536]{1,0:T(8,128)(2,1)S(1)} %split.15), channel_id=1, source_target_pairs={{0,4},{4,0},{8,12},{12,8},{16,20},{20,16},{24,28},{28,24},{1,5},{5... | collective-permute-start | bytes 589832 | tf_op jit(solution)/shard_map/ppermute | solution.py:37
  27.3 4.9 %collective-permute-start.6 = (bf16[32,1536]{1,0:T(8,128)(2,1)S(1)}, bf16[32,1536]{1,0:T(8,128)(2,1)S(1)}, u32[]{:S(2)}, u32[]{:S(2)}) collective-permute-start(bf16[32,1536]{1,0:T(8,128)(2,1)S(1)} %pad_maximum_fusion.4), channel_id=1, source_target_pairs={{0,8},{4,12},{8,0},{12,4},{16,24},{20,28},{24,16},{28,20},{1,9},{5... | collective-permute-start | bytes 294920 | tf_op jit(solution)/shard_map/ppermute | solution.py:37
  28.6 5.4 %collective-permute-start.7 = (bf16[32,1536]{1,0:T(8,128)(2,1)S(1)}, bf16[32,1536]{1,0:T(8,128)(2,1)S(1)}, u32[]{:S(2)}, u32[]{:S(2)}) collective-permute-start(bf16[32,1536]{1,0:T(8,128)(2,1)S(1)} %pad_maximum_fusion.5), channel_id=1, source_target_pairs={{0,16},{4,20},{8,24},{12,28},{16,0},{20,4},{24,8},{28,12},{1,17},{... | collective-permute-start | bytes 294920 | tf_op jit(solution)/shard_map/ppermute | solution.py:37
  29.5 5.8 %collective-permute-start.8 = (bf16[32,1536]{1,0:T(8,128)(2,1)S(1)}, bf16[32,1536]{1,0:T(8,128)(2,1)S(1)}, u32[]{:S(2)}, u32[]{:S(2)}) collective-permute-start(bf16[32,1536]{1,0:T(8,128)(2,1)S(1)} %pad_maximum_fusion.6), channel_id=1, source_target_pairs={{0,24},{4,28},{8,16},{12,20},{16,8},{20,12},{24,0},{28,4},{1,25},{... | collective-permute-start | bytes 294920 | tf_op jit(solution)/shard_map/ppermute | solution.py:37
  35.8 0.7 collective-permute-start.9
  37.6 1.5 %collective-permute-start.10 = (bf16[64,1536]{1,0:T(8,128)(2,1)S(1)}, bf16[64,1536]{1,0:T(8,128)(2,1)S(1)}, u32[]{:S(2)}, u32[]{:S(2)}) collective-permute-start(bf16[64,1536]{1,0:T(8,128)(2,1)S(1)} %split.16), channel_id=1, source_target_pairs={{0,4},{4,0},{8,12},{12,8},{16,20},{20,16},{24,28},{28,24},{1,5},{5... | collective-permute-start | bytes 589832 | tf_op jit(solution)/shard_map/ppermute | solution.py:37
  39.2 4.9 %collective-permute-start.11 = (bf16[32,1536]{1,0:T(8,128)(2,1)S(1)}, bf16[32,1536]{1,0:T(8,128)(2,1)S(1)}, u32[]{:S(2)}, u32[]{:S(2)}) collective-permute-start(bf16[32,1536]{1,0:T(8,128)(2,1)S(1)} %pad_maximum_fusion.7), channel_id=1, source_target_pairs={{0,8},{4,12},{8,0},{12,4},{16,24},{20,28},{24,16},{28,20},{1,9},{5... | collective-permute-start | bytes 294920 | tf_op jit(solution)/shard_map/ppermute | solution.py:37
  40.5 5.7 %collective-permute-start.12 = (bf16[32,1536]{1,0:T(8,128)(2,1)S(1)}, bf16[32,1536]{1,0:T(8,128)(2,1)S(1)}, u32[]{:S(2)}, u32[]{:S(2)}) collective-permute-start(bf16[32,1536]{1,0:T(8,128)(2,1)S(1)} %pad_maximum_fusion.8), channel_id=1, source_target_pairs={{0,16},{4,20},{8,24},{12,28},{16,0},{20,4},{24,8},{28,12},{1,17},{... | collective-permute-start | bytes 294920 | tf_op jit(solution)/shard_map/ppermute | solution.py:37
  41.8 5.6 %collective-permute-start.13 = (bf16[32,1536]{1,0:T(8,128)(2,1)S(1)}, bf16[32,1536]{1,0:T(8,128)(2,1)S(1)}, u32[]{:S(2)}, u32[]{:S(2)}) collective-permute-start(bf16[32,1536]{1,0:T(8,128)(2,1)S(1)} %pad_maximum_fusion.9), channel_id=1, source_target_pairs={{0,24},{4,28},{8,16},{12,20},{16,8},{20,12},{24,0},{28,4},{1,25},{... | collective-permute-start | bytes 294920 | tf_op jit(solution)/shard_map/ppermute | solution.py:37
  47.8 30.7 %collective-permute-start.14 = (bf16[128,1536]{1,0:T(8,128)(2,1)S(1)}, bf16[128,1536]{1,0:T(8,128)(2,1)S(1)}, u32[]{:S(2)}, u32[]{:S(2)}) collective-permute-start(bf16[128,1536]{1,0:T(8,128)(2,1)S(1)} %advance.3.outgoing_ref), channel_id=1, source_target_pairs={{1,0},{5,4},{9,8},{13,12},{17,16},{21,20},{25,24},{29,28}} | collective-permute-start | bytes 1179656 | tf_op jit(solution)/shard_map/ppermute | solution.py:388
  79.6 1.5 %collective-permute-start.15 = (bf16[64,1536]{1,0:T(8,128)(2,1)S(1)}, bf16[64,1536]{1,0:T(8,128)(2,1)S(1)}, u32[]{:S(2)}, u32[]{:S(2)}) collective-permute-start(bf16[64,1536]{1,0:T(8,128)(2,1)S(1)} %split.17), channel_id=1, source_target_pairs={{0,4},{4,0},{8,12},{12,8},{16,20},{20,16},{24,28},{28,24},{1,5},{5... | collective-permute-start | bytes 589832 | tf_op jit(solution)/shard_map/ppermute | solution.py:37
  81.2 4.9 %collective-permute-start.16 = (bf16[32,1536]{1,0:T(8,128)(2,1)S(1)}, bf16[32,1536]{1,0:T(8,128)(2,1)S(1)}, u32[]{:S(2)}, u32[]{:S(2)}) collective-permute-start(bf16[32,1536]{1,0:T(8,128)(2,1)S(1)} %pad_maximum_fusion.10), channel_id=1, source_target_pairs={{0,8},{4,12},{8,0},{12,4},{16,24},{20,28},{24,16},{28,20},{1,9},{5... | collective-permute-start | bytes 294920 | tf_op jit(solution)/shard_map/ppermute | solution.py:37
  82.6 6.8 %collective-permute-start.17 = (bf16[32,1536]{1,0:T(8,128)(2,1)S(1)}, bf16[32,1536]{1,0:T(8,128)(2,1)S(1)}, u32[]{:S(2)}, u32[]{:S(2)}) collective-permute-start(bf16[32,1536]{1,0:T(8,128)(2,1)S(1)} %pad_maximum_fusion.11), channel_id=1, source_target_pairs={{0,16},{4,20},{8,24},{12,28},{16,0},{20,4},{24,8},{28,12},{1,17},{... | collective-permute-start | bytes 294920 | tf_op jit(solution)/shard_map/ppermute | solution.py:37
  83.4 6.0 %collective-permute-start.18 = (bf16[32,1536]{1,0:T(8,128)(2,1)S(1)}, bf16[32,1536]{1,0:T(8,128)(2,1)S(1)}, u32[]{:S(2)}, u32[]{:S(2)}) collective-permute-start(bf16[32,1536]{1,0:T(8,128)(2,1)S(1)} %pad_maximum_fusion.12), channel_id=1, source_target_pairs={{0,24},{4,28},{8,16},{12,20},{16,8},{20,12},{24,0},{28,4},{1,25},{... | collective-permute-start | bytes 294920 | tf_op jit(solution)/shard_map/ppermute | solution.py:37

commit v5 on v4

--- a/solution.py
+++ b/solution.py
@@ -35,6 +35,14 @@
 def swap(block, offset):
     count = lax.axis_size("seq")
     return lax.ppermute(block, "seq", [(i, i ^ offset) for i in range(count)])
+
+
+def passed_down(block, sender):
+    count = lax.axis_size("pipe")
+    pairs = [(sender, sender - 1)]
+    if count % 2 == 0 and sender % 2 == 1:
+        pairs = [(i, i ^ 1) for i in range(count)]
+    return lax.ppermute(block, "pipe", pairs)
 
 
 def chunks(size, count):
@@ -385,7 +393,7 @@
     delta_mix = (delta_hidden * mix_factor).astype(jnp.bfloat16)
     kept = (outgoing, dot_rows(delta_mid, normed), dot_rows(delta_mix, moved))
     for sender in reversed(range(section_count - 1)):
-        incoming = lax.ppermute(outgoing, "pipe", [(sender + 1, sender)])
+        incoming = passed_down(outgoing, sender + 1)
         delta_hidden = dot(incoming, out_turned)
         delta_mix = (delta_hidden * mix_factor).astype(jnp.bfloat16)
         send = rounded(second_send, delta_mix)

time: 91.2 us -> 88.9 us (0.975)
  waiting for transfers between devices: 51.3 us -> 35.4 us
  starting transfers between devices: 19 us -> 32.6 us
    ppermute x3, waiting for transfers between devices: 28.5 us -> 12.5 us  [passed_down(): return lax.ppermute(block, 'pipe', pairs)]
    ppermute x3, starting transfers between devices: 2.66 us -> 16.3 us  [passed_down(): return lax.ppermute(block, 'pipe', pairs)]
  transfers between devices with their start and end apart: 19 -> 19, of which waited for: 15 -> 15; matrix products, arithmetic and copies ran while one was open for 3% -> 4% of each run, Pallas kernels for 6% -> 7%
where the time goes in v5:
time: 88.9 us; the launch traced here: 88.7 us
  waiting for transfers between devices  35.4 us (40%)
  starting transfers between devices  32.6 us (37%)
  Pallas kernels  13.2 us (15%)
  matrix products  6.08 us (7%)
  between operations  1.03 us (1%)
    ppermute x16, waiting for transfers between devices, swap(): return lax.ppermute(block, 'seq', [(i, i ^ offset) for i in range(count)])  22.8 us
    ppermute x16, starting transfers between devices, swap(): return lax.ppermute(block, 'seq', [(i, i ^ offset) for i in range(count)])  16.3 us
    ppermute x3, starting transfers between devices, passed_down(): return lax.ppermute(block, 'pipe', pairs)  16.3 us
    ppermute x3, waiting for transfers between devices, passed_down(): return lax.ppermute(block, 'pipe', pairs)  12.5 us
    dot_general x9, matrix products, dot(): return jnp.dot(left, right, preferred_element_type=jnp.float32)  5.55 us
    pallas_call x2, Pallas kernels, transposed(): pl.pallas_call(transpose_kernel, in_specs=[ANYWHERE, ANYWHERE], out_specs...  5.53 us
    pallas_call x1, Pallas kernels, begin(): pl.pallas_call(functools.partial(begin_kernel, order), in_specs=[ANYWHERE...  3.53 us
  transfers between devices with their start and end apart: 19, of which 15 were waited for; matrix products, arithmetic and copies ran while one was open for 4% of the time, Pallas kernels for 7%

profile of v5, /device:TPU:0, one launch (start us, length us, event | category | flops | bytes accessed | tf_op | source)
XLA Modules:
  0.0 88.7 jit_solution(8684377367056228769)
XLA Ops:
  0.6 3.5 %begin.1 = (bf16[128,1536]{1,0:T(8,128)(2,1)S(1)}, f32[128,1]{1,0:T(8,128)S(1)}, bf16[128,128]{1,0:T(8,128)(2,1)S(1)}, bf16[128,128]{1,0:T(8,128)(2,1)S(1)}, bf1...) custom-call(bf16[128,1536]{1,0:T(8,128)(2,1)} %bitcast.26, ...), custom_call_target="tpu_custom_call" | custom-call | tf_op jit(solution)/shard_map/begin/pallas_call | solution.py:202
  4.2 0.5 collective-permute-start
  4.7 1.3 %collective-permute-done = bf16[128,1536]{1,0:T(8,128)(2,1)S(1)} collective-permute-done((bf16[128,1536]{1,0:T(8,128)(2,1)S(1)}, bf16[128,1536]{1,0:T(8,128)(2,1)S(1)}, u32[]{:S(2)}, u32[]{:S(2)}) %collective-permute-start) | collective-permute-done | bytes 393248 | tf_op jit(solution)/shard_map/ppermute | solution.py:37
  6.1 2.9 %collective-permute-start.1 = (bf16[64,1536]{1,0:T(8,128)(2,1)S(1)}, bf16[64,1536]{1,0:T(8,128)(2,1)S(1)}, u32[]{:S(2)}, u32[]{:S(2)}) collective-permute-start(bf16[64,1536]{1,0:T(8,128)(2,1)S(1)} %pad_maximum_fusion.1), channel_id=1, source_target_pairs={{0,8},{4,12},{8,0},{12,4},{16,24},{20,28},{24,16},{28,20},{1,9},{5... | collective-permute-start | bytes 589832 | tf_op jit(solution)/shard_map/ppermute | solution.py:37
  9.0 1.6 %collective-permute-start.2 = (bf16[64,1536]{1,0:T(8,128)(2,1)S(1)}, bf16[64,1536]{1,0:T(8,128)(2,1)S(1)}, u32[]{:S(2)}, u32[]{:S(2)}) collective-permute-start(bf16[64,1536]{1,0:T(8,128)(2,1)S(1)} %pad_maximum_fusion.2), channel_id=1, source_target_pairs={{0,16},{4,20},{8,24},{12,28},{16,0},{20,4},{24,8},{28,12},{1,17},{... | collective-permute-start | bytes 589832 | tf_op jit(solution)/shard_map/ppermute | solution.py:37
  10.6 0.1 collective-permute-start.3
  10.7 0.0 copy-start
  10.8 0.0 copy-start.1
  10.8 0.0 copy-start.2
  10.8 2.8 %transposed.2.refs_8_ = bf16[1536,1536]{1,0:T(8,128)(2,1)S(1)} custom-call(bf16[1536,1536]{1,0:T(8,128)(2,1)} %bitcast.32, bf16[64,1536]{1,0:T(8,128)(2,1)S(1)} %pad_maximum_fusion.after_ref.refs_0_), custom_call_target="tpu_custom_call" | custom-call | tf_op jit(solution)/shard_map/transposed/pallas_call | solution.py:228
  13.6 1.1 %collective-permute-done.1.refs_1_ = bf16[64,1536]{1,0:T(8,128)(2,1)S(1)} collective-permute-done((bf16[64,1536]{1,0:T(8,128)(2,1)S(1)}, bf16[64,1536]{1,0:T(8,128)(2,1)S(1)}, u32[]{:S(2)}, u32[]{:S(2)}) %collective-permute-start.1) | collective-permute-done | bytes 196640 | tf_op jit(solution)/shard_map/ppermute | solution.py:37
  14.7 5.3 %collective-permute-done.2.refs_2_ = bf16[64,1536]{1,0:T(8,128)(2,1)S(1)} collective-permute-done((bf16[64,1536]{1,0:T(8,128)(2,1)S(1)}, bf16[64,1536]{1,0:T(8,128)(2,1)S(1)}, u32[]{:S(2)}, u32[]{:S(2)}) %collective-permute-start.2) | collective-permute-done | bytes 196640 | tf_op jit(solution)/shard_map/ppermute | solution.py:37
  20.0 0.0 collective-permute-done.3.refs_3_
  20.0 0.0 copy-done
  20.0 0.0 copy-done.1
  20.0 0.0 copy-done.2
  20.0 1.3 %finish.1 = (bf16[128,1536]{1,0:T(8,128)(2,1)S(1)}, bf16[128,1536]{1,0:T(8,128)(2,1)S(1)}, f32[128,1536]{1,0:T(8,128)S(1)}, bf16[128,1536]{1,0:T(8,128)(2,1)S(1)}) custom-call(bf16[64,1536]{1,0:T(8,128)(2,1)S(1)} %pad_maximum_fusion.after_ref.refs_0_, bf16[64,1536]{1,0:T(8,128)(2,1)S(1)} %collective-permute-done.1.refs_1_, ...), custom_call_target="tpu_custom_call" | custom-call | tf_op jit(solution)/shard_map/finish/pallas_call | solution.py:270
  21.3 1.6 %collective-permute-start.4 = (bf16[128,1536]{1,0:T(8,128)(2,1)S(1)}, bf16[128,1536]{1,0:T(8,128)(2,1)S(1)}, u32[]{:S(2)}, u32[]{:S(2)}) collective-permute-start(bf16[128,1536]{1,0:T(8,128)(2,1)S(1)} %get-tuple-element.34.after_ref.refs_0_), channel_id=1, source_target_pairs={{0,1},{1,0},{2,3},{3,2},{4,5},{5,4},{6,7},{7,6},{8,9},{9,8},{10,11... | collective-permute-start | bytes 1179656 | tf_op jit(solution)/shard_map/ppermute | solution.py:45
  22.9 2.7 %transposed.3 = bf16[1536,1536]{1,0:T(8,128)(2,1)S(1)} custom-call(bf16[1536,1536]{1,0:T(8,128)(2,1)} %bitcast.34, bf16[128,1536]{1,0:T(8,128)(2,1)S(1)} %get-tuple-element.34.after_ref.refs_0_), custom_call_target="tpu_custom_call" | custom-call | tf_op jit(solution)/shard_map/transposed/pallas_call | solution.py:228
  25.6 5.7 %collective-permute-done.4.incoming_ref = bf16[128,1536]{1,0:T(8,128)(2,1)S(1)} collective-permute-done((bf16[128,1536]{1,0:T(8,128)(2,1)S(1)}, bf16[128,1536]{1,0:T(8,128)(2,1)S(1)}, u32[]{:S(2)}, u32[]{:S(2)}) %collective-permute-start.4) | collective-permute-done | bytes 393248 | tf_op jit(solution)/shard_map/ppermute | solution.py:45
  31.3 0.8 multiply_convert_fusion.6
  32.1 0.2 convolution_convert_fusion.2
  32.4 0.1 collective-permute-start.5
  32.5 0.8 fusion.gate_back_ref
  33.4 0.6 collective-permute-done.5
  34.0 1.5 %collective-permute-start.6 = (bf16[32,1536]{1,0:T(8,128)(2,1)S(1)}, bf16[32,1536]{1,0:T(8,128)(2,1)S(1)}, u32[]{:S(2)}, u32[]{:S(2)}) collective-permute-start(bf16[32,1536]{1,0:T(8,128)(2,1)S(1)} %pad_maximum_fusion.4), channel_id=1, source_target_pairs={{0,8},{4,12},{8,0},{12,4},{16,24},{20,28},{24,16},{28,20},{1,9},{5... | collective-permute-start | bytes 294920 | tf_op jit(solution)/shard_map/ppermute | solution.py:37
  35.5 0.6 collective-permute-start.7
  36.1 1.5 %collective-permute-start.8 = (bf16[32,1536]{1,0:T(8,128)(2,1)S(1)}, bf16[32,1536]{1,0:T(8,128)(2,1)S(1)}, u32[]{:S(2)}, u32[]{:S(2)}) collective-permute-start(bf16[32,1536]{1,0:T(8,128)(2,1)S(1)} %pad_maximum_fusion.6), channel_id=1, source_target_pairs={{0,24},{4,28},{8,16},{12,20},{16,8},{20,12},{24,0},{28,4},{1,25},{... | collective-permute-start | bytes 294920 | tf_op jit(solution)/shard_map/ppermute | solution.py:37
  37.7 1.2 %collective-permute-done.6 = bf16[32,1536]{1,0:T(8,128)(2,1)S(1)} collective-permute-done((bf16[32,1536]{1,0:T(8,128)(2,1)S(1)}, bf16[32,1536]{1,0:T(8,128)(2,1)S(1)}, u32[]{:S(2)}, u32[]{:S(2)}) %collective-permute-start.6) | collective-permute-done | bytes 98336 | tf_op jit(solution)/shard_map/ppermute | solution.py:37
  38.9 3.4 %collective-permute-done.7 = bf16[32,1536]{1,0:T(8,128)(2,1)S(1)} collective-permute-done((bf16[32,1536]{1,0:T(8,128)(2,1)S(1)}, bf16[32,1536]{1,0:T(8,128)(2,1)S(1)}, u32[]{:S(2)}, u32[]{:S(2)}) %collective-permute-start.7) | collective-permute-done | bytes 98336 | tf_op jit(solution)/shard_map/ppermute | solution.py:37
  42.3 0.0 collective-permute-done.8
  42.3 0.5 advance.2.outgoing_ref
  42.8 0.7 collective-permute-start.9
  43.5 0.0 collective-permute-done.9.incoming_ref
  43.5 0.8 multiply_convert_fusion.4
  44.3 0.2 convolution_convert_fusion.1
  44.6 0.1 collective-permute-start.10
  44.7 0.8 fusion.1.gate_back_ref
  45.5 0.6 collective-permute-done.10
  46.2 1.0 %collective-permute-start.11 = (bf16[32,1536]{1,0:T(8,128)(2,1)S(1)}, bf16[32,1536]{1,0:T(8,128)(2,1)S(1)}, u32[]{:S(2)}, u32[]{:S(2)}) collective-permute-start(bf16[32,1536]{1,0:T(8,128)(2,1)S(1)} %pad_maximum_fusion.7), channel_id=1, source_target_pairs={{0,8},{4,12},{8,0},{12,4},{16,24},{20,28},{24,16},{28,20},{1,9},{5... | collective-permute-start | bytes 294920 | tf_op jit(solution)/shard_map/ppermute | solution.py:37
  47.1 1.2 %collective-permute-start.12 = (bf16[32,1536]{1,0:T(8,128)(2,1)S(1)}, bf16[32,1536]{1,0:T(8,128)(2,1)S(1)}, u32[]{:S(2)}, u32[]{:S(2)}) collective-permute-start(bf16[32,1536]{1,0:T(8,128)(2,1)S(1)} %pad_maximum_fusion.8), channel_id=1, source_target_pairs={{0,16},{4,20},{8,24},{12,28},{16,0},{20,4},{24,8},{28,12},{1,17},{... | collective-permute-start | bytes 294920 | tf_op jit(solution)/shard_map/ppermute | solution.py:37
  48.4 1.5 %collective-permute-start.13 = (bf16[32,1536]{1,0:T(8,128)(2,1)S(1)}, bf16[32,1536]{1,0:T(8,128)(2,1)S(1)}, u32[]{:S(2)}, u32[]{:S(2)}) collective-permute-start(bf16[32,1536]{1,0:T(8,128)(2,1)S(1)} %pad_maximum_fusion.9), channel_id=1, source_target_pairs={{0,24},{4,28},{8,16},{12,20},{16,8},{20,12},{24,0},{28,4},{1,25},{... | collective-permute-start | bytes 294920 | tf_op jit(solution)/shard_map/ppermute | solution.py:37
  49.8 1.3 %collective-permute-done.11 = bf16[32,1536]{1,0:T(8,128)(2,1)S(1)} collective-permute-done((bf16[32,1536]{1,0:T(8,128)(2,1)S(1)}, bf16[32,1536]{1,0:T(8,128)(2,1)S(1)}, u32[]{:S(2)}, u32[]{:S(2)}) %collective-permute-start.11) | collective-permute-done | bytes 98336 | tf_op jit(solution)/shard_map/ppermute | solution.py:37
  51.2 1.7 %collective-permute-done.12 = bf16[32,1536]{1,0:T(8,128)(2,1)S(1)} collective-permute-done((bf16[32,1536]{1,0:T(8,128)(2,1)S(1)}, bf16[32,1536]{1,0:T(8,128)(2,1)S(1)}, u32[]{:S(2)}, u32[]{:S(2)}) %collective-permute-start.12) | collective-permute-done | bytes 98336 | tf_op jit(solution)/shard_map/ppermute | solution.py:37
  52.9 1.1 %collective-permute-done.13 = bf16[32,1536]{1,0:T(8,128)(2,1)S(1)} collective-permute-done((bf16[32,1536]{1,0:T(8,128)(2,1)S(1)}, bf16[32,1536]{1,0:T(8,128)(2,1)S(1)}, u32[]{:S(2)}, u32[]{:S(2)}) %collective-permute-start.13) | collective-permute-done | bytes 98336 | tf_op jit(solution)/shard_map/ppermute | solution.py:37
  54.0 0.5 advance.3.outgoing_ref
  54.5 13.9 %collective-permute-start.14 = (bf16[128,1536]{1,0:T(8,128)(2,1)S(1)}, bf16[128,1536]{1,0:T(8,128)(2,1)S(1)}, u32[]{:S(2)}, u32[]{:S(2)}) collective-permute-start(bf16[128,1536]{1,0:T(8,128)(2,1)S(1)} %advance.3.outgoing_ref), channel_id=1, source_target_pairs={{0,1},{1,0},{2,3},{3,2},{4,5},{5,4},{6,7},{7,6},{8,9},{9,8},{10,11... | collective-permute-start | bytes 1179656 | tf_op jit(solution)/shard_map/ppermute | solution.py:45
  68.4 0.3 fusion.12.refs_1_
  68.7 0.3 fusion.3.refs_2_
  68.9 0.1 keep.2
  69.0 0.3 keep.3
  69.3 6.8 %collective-permute-done.14.incoming_ref = bf16[128,1536]{1,0:T(8,128)(2,1)S(1)} collective-permute-done((bf16[128,1536]{1,0:T(8,128)(2,1)S(1)}, bf16[128,1536]{1,0:T(8,128)(2,1)S(1)}, u32[]{:S(2)}, u32[]{:S(2)}) %collective-permute-start.14) | collective-permute-done | bytes 393248 | tf_op jit(solution)/shard_map/ppermute | solution.py:45
  76.1 0.8 multiply_convert_fusion.2
  76.9 0.2 convolution_convert_fusion
  77.2 0.1 collective-permute-start.15
  77.3 0.8 fusion.2.gate_back_ref
  78.1 0.6 collective-permute-done.15
  78.8 1.5 %collective-permute-start.16 = (bf16[32,1536]{1,0:T(8,128)(2,1)S(1)}, bf16[32,1536]{1,0:T(8,128)(2,1)S(1)}, u32[]{:S(2)}, u32[]{:S(2)}) collective-permute-start(bf16[32,1536]{1,0:T(8,128)(2,1)S(1)} %pad_maximum_fusion.10), channel_id=1, source_target_pairs={{0,8},{4,12},{8,0},{12,4},{16,24},{20,28},{24,16},{28,20},{1,9},{5... | collective-permute-start | bytes 294920 | tf_op jit(solution)/shard_map/ppermute | solution.py:37
  80.3 0.7 collective-permute-start.17
  81.0 1.5 %collective-permute-start.18 = (bf16[32,1536]{1,0:T(8,128)(2,1)S(1)}, bf16[32,1536]{1,0:T(8,128)(2,1)S(1)}, u32[]{:S(2)}, u32[]{:S(2)}) collective-permute-start(bf16[32,1536]{1,0:T(8,128)(2,1)S(1)} %pad_maximum_fusion.12), channel_id=1, source_target_pairs={{0,24},{4,28},{8,16},{12,20},{16,8},{20,12},{24,0},{28,4},{1,25},{... | collective-permute-start | bytes 294920 | tf_op jit(solution)/shard_map/ppermute | solution.py:37
  82.4 1.2 %collective-permute-done.16 = bf16[32,1536]{1,0:T(8,128)(2,1)S(1)} collective-permute-done((bf16[32,1536]{1,0:T(8,128)(2,1)S(1)}, bf16[32,1536]{1,0:T(8,128)(2,1)S(1)}, u32[]{:S(2)}, u32[]{:S(2)}) %collective-permute-start.16) | collective-permute-done | bytes 98336 | tf_op jit(solution)/shard_map/ppermute | solution.py:37
  83.7 3.4 %collective-permute-done.17 = bf16[32,1536]{1,0:T(8,128)(2,1)S(1)} collective-permute-done((bf16[32,1536]{1,0:T(8,128)(2,1)S(1)}, bf16[32,1536]{1,0:T(8,128)(2,1)S(1)}, u32[]{:S(2)}, u32[]{:S(2)}) %collective-permute-start.17) | collective-permute-done | bytes 98336 | tf_op jit(solution)/shard_map/ppermute | solution.py:37
  87.1 0.0 collective-permute-done.18
  87.1 1.6 %close.1 = (bf16[128,1536]{1,0:T(8,128)(2,1)}, f32[2,64,64]{2,1,0:T(8,128)}, f32[2,64,64]{2,1,0:T(8,128)}) custom-call(bf16[128,1536]{1,0:T(8,128)(2,1)S(1)} %constant_dynamic-update-slice_fusion.6.mid_ref, bf16[128,1536]{1,0:T(8,128)(2,1)S(1)} %get-tuple-element.85.mix_ref, bf16[128,1536]{1,0:T(8,128)(2,1)S(1)} %get-tuple-element.37.moved_ref, ...), custom_call_target="tpu_custom_call" | custom-call | tf_op jit(solution)/shard_map/close/pallas_call | solution.py:363
  (33 shorter events, 0.4 us)
Async XLA Ops:
  4.2 1.9 %collective-permute-start = (bf16[128,1536]{1,0:T(8,128)(2,1)S(1)}, bf16[128,1536]{1,0:T(8,128)(2,1)S(1)}, u32[]{:S(2)}, u32[]{:S(2)}) collective-permute-start(bf16[128,1536]{1,0:T(8,128)(2,1)S(1)} %get-tuple-element.28), channel_id=1, source_target_pairs={{0,4},{4,0},{8,12},{12,8},{16,20},{20,16},{24,28},{28,24},{1,5},{5... | collective-permute-start | bytes 1179656 | tf_op jit(solution)/shard_map/ppermute | solution.py:37
  6.1 8.6 %collective-permute-start.1 = (bf16[64,1536]{1,0:T(8,128)(2,1)S(1)}, bf16[64,1536]{1,0:T(8,128)(2,1)S(1)}, u32[]{:S(2)}, u32[]{:S(2)}) collective-permute-start(bf16[64,1536]{1,0:T(8,128)(2,1)S(1)} %pad_maximum_fusion.1), channel_id=1, source_target_pairs={{0,8},{4,12},{8,0},{12,4},{16,24},{20,28},{24,16},{28,20},{1,9},{5... | collective-permute-start | bytes 589832 | tf_op jit(solution)/shard_map/ppermute | solution.py:37
  9.0 10.9 %collective-permute-start.2 = (bf16[64,1536]{1,0:T(8,128)(2,1)S(1)}, bf16[64,1536]{1,0:T(8,128)(2,1)S(1)}, u32[]{:S(2)}, u32[]{:S(2)}) collective-permute-start(bf16[64,1536]{1,0:T(8,128)(2,1)S(1)} %pad_maximum_fusion.2), channel_id=1, source_target_pairs={{0,16},{4,20},{8,24},{12,28},{16,0},{20,4},{24,8},{28,12},{1,17},{... | collective-permute-start | bytes 589832 | tf_op jit(solution)/shard_map/ppermute | solution.py:37
  10.6 9.3 %collective-permute-start.3 = (bf16[64,1536]{1,0:T(8,128)(2,1)S(1)}, bf16[64,1536]{1,0:T(8,128)(2,1)S(1)}, u32[]{:S(2)}, u32[]{:S(2)}) collective-permute-start(bf16[64,1536]{1,0:T(8,128)(2,1)S(1)} %pad_maximum_fusion.3), channel_id=1, source_target_pairs={{0,24},{4,28},{8,16},{12,20},{16,8},{20,12},{24,0},{28,4},{1,25},{... | collective-permute-start | bytes 589832 | tf_op jit(solution)/shard_map/ppermute | solution.py:37
  10.7 9.2 %copy-start = (bf16[1,128,1536]{2,1,0:T(8,128)(2,1)S(1)}, bf16[1,128,1536]{2,1,0:T(8,128)(2,1)}, u32[]{:S(2)}) copy-start(bf16[1,128,1536]{2,1,0:T(8,128)(2,1)} %param.7) | copy-start | bytes 1179652
  10.8 9.2 %copy-start.1 = (bf16[128,1536]{1,0:T(8,128)(2,1)S(1)}, bf16[128,1536]{1,0:T(8,128)(2,1)}, u32[]{:S(2)}) copy-start(bf16[128,1536]{1,0:T(8,128)(2,1)} %refs_12_.1) | copy-start | bytes 1179652
  10.8 9.2 %copy-start.2 = (f32[1,1536]{1,0:T(1,128)S(1)}, f32[1,1536]{1,0:T(1,128)}, u32[]{:S(2)}) copy-start(f32[1,1536]{1,0:T(1,128)} %gain_ref.5) | copy-start | bytes 18436
  21.3 10.1 %collective-permute-start.4 = (bf16[128,1536]{1,0:T(8,128)(2,1)S(1)}, bf16[128,1536]{1,0:T(8,128)(2,1)S(1)}, u32[]{:S(2)}, u32[]{:S(2)}) collective-permute-start(bf16[128,1536]{1,0:T(8,128)(2,1)S(1)} %get-tuple-element.34.after_ref.refs_0_), channel_id=1, source_target_pairs={{0,1},{1,0},{2,3},{3,2},{4,5},{5,4},{6,7},{7,6},{8,9},{9,8},{10,11... | collective-permute-start | bytes 1179656 | tf_op jit(solution)/shard_map/ppermute | solution.py:45
  32.4 1.5 %collective-permute-start.5 = (bf16[64,1536]{1,0:T(8,128)(2,1)S(1)}, bf16[64,1536]{1,0:T(8,128)(2,1)S(1)}, u32[]{:S(2)}, u32[]{:S(2)}) collective-permute-start(bf16[64,1536]{1,0:T(8,128)(2,1)S(1)} %split.15), channel_id=1, source_target_pairs={{0,4},{4,0},{8,12},{12,8},{16,20},{20,16},{24,28},{28,24},{1,5},{5... | collective-permute-start | bytes 589832 | tf_op jit(solution)/shard_map/ppermute | solution.py:37
  34.0 4.9 %collective-permute-start.6 = (bf16[32,1536]{1,0:T(8,128)(2,1)S(1)}, bf16[32,1536]{1,0:T(8,128)(2,1)S(1)}, u32[]{:S(2)}, u32[]{:S(2)}) collective-permute-start(bf16[32,1536]{1,0:T(8,128)(2,1)S(1)} %pad_maximum_fusion.4), channel_id=1, source_target_pairs={{0,8},{4,12},{8,0},{12,4},{16,24},{20,28},{24,16},{28,20},{1,9},{5... | collective-permute-start | bytes 294920 | tf_op jit(solution)/shard_map/ppermute | solution.py:37
  35.5 6.8 %collective-permute-start.7 = (bf16[32,1536]{1,0:T(8,128)(2,1)S(1)}, bf16[32,1536]{1,0:T(8,128)(2,1)S(1)}, u32[]{:S(2)}, u32[]{:S(2)}) collective-permute-start(bf16[32,1536]{1,0:T(8,128)(2,1)S(1)} %pad_maximum_fusion.5), channel_id=1, source_target_pairs={{0,16},{4,20},{8,24},{12,28},{16,0},{20,4},{24,8},{28,12},{1,17},{... | collective-permute-start | bytes 294920 | tf_op jit(solution)/shard_map/ppermute | solution.py:37
  36.1 6.2 %collective-permute-start.8 = (bf16[32,1536]{1,0:T(8,128)(2,1)S(1)}, bf16[32,1536]{1,0:T(8,128)(2,1)S(1)}, u32[]{:S(2)}, u32[]{:S(2)}) collective-permute-start(bf16[32,1536]{1,0:T(8,128)(2,1)S(1)} %pad_maximum_fusion.6), channel_id=1, source_target_pairs={{0,24},{4,28},{8,16},{12,20},{16,8},{20,12},{24,0},{28,4},{1,25},{... | collective-permute-start | bytes 294920 | tf_op jit(solution)/shard_map/ppermute | solution.py:37
  42.8 0.7 collective-permute-start.9
  44.6 1.5 %collective-permute-start.10 = (bf16[64,1536]{1,0:T(8,128)(2,1)S(1)}, bf16[64,1536]{1,0:T(8,128)(2,1)S(1)}, u32[]{:S(2)}, u32[]{:S(2)}) collective-permute-start(bf16[64,1536]{1,0:T(8,128)(2,1)S(1)} %split.16), channel_id=1, source_target_pairs={{0,4},{4,0},{8,12},{12,8},{16,20},{20,16},{24,28},{28,24},{1,5},{5... | collective-permute-start | bytes 589832 | tf_op jit(solution)/shard_map/ppermute | solution.py:37
  46.2 5.0 %collective-permute-start.11 = (bf16[32,1536]{1,0:T(8,128)(2,1)S(1)}, bf16[32,1536]{1,0:T(8,128)(2,1)S(1)}, u32[]{:S(2)}, u32[]{:S(2)}) collective-permute-start(bf16[32,1536]{1,0:T(8,128)(2,1)S(1)} %pad_maximum_fusion.7), channel_id=1, source_target_pairs={{0,8},{4,12},{8,0},{12,4},{16,24},{20,28},{24,16},{28,20},{1,9},{5... | collective-permute-start | bytes 294920 | tf_op jit(solution)/shard_map/ppermute | solution.py:37
  47.1 5.7 %collective-permute-start.12 = (bf16[32,1536]{1,0:T(8,128)(2,1)S(1)}, bf16[32,1536]{1,0:T(8,128)(2,1)S(1)}, u32[]{:S(2)}, u32[]{:S(2)}) collective-permute-start(bf16[32,1536]{1,0:T(8,128)(2,1)S(1)} %pad_maximum_fusion.8), channel_id=1, source_target_pairs={{0,16},{4,20},{8,24},{12,28},{16,0},{20,4},{24,8},{28,12},{1,17},{... | collective-permute-start | bytes 294920 | tf_op jit(solution)/shard_map/ppermute | solution.py:37
  48.4 5.6 %collective-permute-start.13 = (bf16[32,1536]{1,0:T(8,128)(2,1)S(1)}, bf16[32,1536]{1,0:T(8,128)(2,1)S(1)}, u32[]{:S(2)}, u32[]{:S(2)}) collective-permute-start(bf16[32,1536]{1,0:T(8,128)(2,1)S(1)} %pad_maximum_fusion.9), channel_id=1, source_target_pairs={{0,24},{4,28},{8,16},{12,20},{16,8},{20,12},{24,0},{28,4},{1,25},{... | collective-permute-start | bytes 294920 | tf_op jit(solution)/shard_map/ppermute | solution.py:37
  54.5 21.7 %collective-permute-start.14 = (bf16[128,1536]{1,0:T(8,128)(2,1)S(1)}, bf16[128,1536]{1,0:T(8,128)(2,1)S(1)}, u32[]{:S(2)}, u32[]{:S(2)}) collective-permute-start(bf16[128,1536]{1,0:T(8,128)(2,1)S(1)} %advance.3.outgoing_ref), channel_id=1, source_target_pairs={{0,1},{1,0},{2,3},{3,2},{4,5},{5,4},{6,7},{7,6},{8,9},{9,8},{10,11... | collective-permute-start | bytes 1179656 | tf_op jit(solution)/shard_map/ppermute | solution.py:45
  77.2 1.5 %collective-permute-start.15 = (bf16[64,1536]{1,0:T(8,128)(2,1)S(1)}, bf16[64,1536]{1,0:T(8,128)(2,1)S(1)}, u32[]{:S(2)}, u32[]{:S(2)}) collective-permute-start(bf16[64,1536]{1,0:T(8,128)(2,1)S(1)} %split.17), channel_id=1, source_target_pairs={{0,4},{4,0},{8,12},{12,8},{16,20},{20,16},{24,28},{28,24},{1,5},{5... | collective-permute-start | bytes 589832 | tf_op jit(solution)/shard_map/ppermute | solution.py:37
  78.8 4.9 %collective-permute-start.16 = (bf16[32,1536]{1,0:T(8,128)(2,1)S(1)}, bf16[32,1536]{1,0:T(8,128)(2,1)S(1)}, u32[]{:S(2)}, u32[]{:S(2)}) collective-permute-start(bf16[32,1536]{1,0:T(8,128)(2,1)S(1)} %pad_maximum_fusion.10), channel_id=1, source_target_pairs={{0,8},{4,12},{8,0},{12,4},{16,24},{20,28},{24,16},{28,20},{1,9},{5... | collective-permute-start | bytes 294920 | tf_op jit(solution)/shard_map/ppermute | solution.py:37
  80.3 6.8 %collective-permute-start.17 = (bf16[32,1536]{1,0:T(8,128)(2,1)S(1)}, bf16[32,1536]{1,0:T(8,128)(2,1)S(1)}, u32[]{:S(2)}, u32[]{:S(2)}) collective-permute-start(bf16[32,1536]{1,0:T(8,128)(2,1)S(1)} %pad_maximum_fusion.11), channel_id=1, source_target_pairs={{0,16},{4,20},{8,24},{12,28},{16,0},{20,4},{24,8},{28,12},{1,17},{... | collective-permute-start | bytes 294920 | tf_op jit(solution)/shard_map/ppermute | solution.py:37
  81.0 6.1 %collective-permute-start.18 = (bf16[32,1536]{1,0:T(8,128)(2,1)S(1)}, bf16[32,1536]{1,0:T(8,128)(2,1)S(1)}, u32[]{:S(2)}, u32[]{:S(2)}) collective-permute-start(bf16[32,1536]{1,0:T(8,128)(2,1)S(1)} %pad_maximum_fusion.12), channel_id=1, source_target_pairs={{0,24},{4,28},{8,16},{12,20},{16,8},{20,12},{24,0},{28,4},{1,25},{... | collective-permute-start | bytes 294920 | tf_op jit(solution)/shard_map/ppermute | solution.py:37

commit v6 on v5

--- a/solution.py
+++ b/solution.py
@@ -10,6 +10,7 @@
 ROWS_BY_ROWS = (((1,), (1,)), ((), ()))
 WHOLE = pl.BlockSpec(memory_space=pltpu.VMEM)
 ANYWHERE = pl.BlockSpec(memory_space=pl.ANY)
+HALVES = 2
 
 
 def granted(mebibytes):
@@ -211,29 +212,46 @@
     )(*[in_hbm(o) for o in operands])
 
 
-def transpose_kernel(weight_hbm, after_ref, turned_ref, held, sems):
-    parts = chunks(held.shape[0], sems.shape[0])
-    copies = [
-        pltpu.make_async_copy(weight_hbm.at[rows], held.at[rows], sems.at[i])
-        for i, rows in enumerate(parts)
-    ]
-    for copy in copies:
-        copy.start()
-    for rows, copy in zip(parts, copies):
+def transpose_kernel(gate_hbm, out_hbm, after_ref, gate_turned_ref, *refs):
+    out_turned_refs, (gate_held, out_held, sems) = refs[:-3], refs[-3:]
+    parts = chunks(gate_held.shape[0], sems.shape[1])
+    work = []
+    for i, (source, held) in enumerate(((gate_hbm, gate_held), (out_hbm, out_held))):
+        for j, rows in enumerate(parts):
+            copy = pltpu.make_async_copy(source.at[rows], held.at[rows], sems.at[i, j])
+            copy.start()
+            work.append((copy, held, rows, [gate_turned_ref] if i == 0 else out_turned_refs))
+    for copy, held, rows, targets in work:
         copy.wait()
-        turned_ref[:, rows] = held[rows].T
-
-
-def transposed(weight, after):
+        for target, columns in zip(targets, chunks(held.shape[1], len(targets))):
+            target[:, rows] = held[rows, columns].T
+
+
+def transposed(weight_gate, weight_out, after):
+    height, width = weight_out.shape
+    half = pltpu.VMEM((width // HALVES, height), jnp.bfloat16)
     return pl.pallas_call(
         transpose_kernel,
-        in_specs=[ANYWHERE, ANYWHERE],
-        out_specs=WHOLE,
-        out_shape=pltpu.VMEM(weight.shape[::-1], jnp.bfloat16),
-        scratch_shapes=[pltpu.VMEM(weight.shape, weight.dtype), pltpu.SemaphoreType.DMA((6,))],
-        compiler_params=granted(6),
+        in_specs=[ANYWHERE] * 3,
+        out_specs=[WHOLE] * (1 + HALVES),
+        out_shape=[pltpu.VMEM(weight_gate.shape[::-1], jnp.bfloat16)] + [half] * HALVES,
+        scratch_shapes=[
+            pltpu.VMEM(weight_gate.shape, weight_gate.dtype),
+            pltpu.VMEM(weight_out.shape, weight_out.dtype),
+            pltpu.SemaphoreType.DMA((2, 6)),
+        ],
+        compiler_params=granted(11),
         name="transposed",
-    )(in_hbm(weight), after)
+    )(in_hbm(weight_gate), in_hbm(weight_out), after)
+
+
+def joined(refs):
+    return jnp.concatenate([ref[...] for ref in refs], axis=1)
+
+
+def store_halves(refs, value):
+    for ref, columns in zip(refs, chunks(value.shape[1], len(refs))):
+        ref[...] = value[:, columns]
 
 
 def outgoing_of(gate_back, first_back, gain, inputs, inv_rms, incoming):
@@ -247,7 +265,7 @@
     arrived, refs = refs[: order.chips], refs[order.chips :]
     (
         second_recv_ref, first_recv_ref, slope_ref, hidden_ref, gate_ref, gain_ref, x_ref, inv_ref,
-        incoming_ref, moved_ref, mid_ref, gate_factor_ref, outgoing_ref,
+        incoming_ref, moved_ref, mid_ref, gate_factor_ref, *outgoing_refs,
     ) = refs
     for chip, message in enumerate(arrived):
         for core in range(2):
@@ -258,115 +276,113 @@
     delta_gate = (hidden_ref[...] * gate_factor).astype(jnp.bfloat16)
     gate_back = dot(delta_gate, gate_ref[...])
     first_back = dot(first_recv_ref[...], mid_ref[...])
-    outgoing_ref[...] = outgoing_of(
+    outgoing = outgoing_of(
         gate_back, first_back, gain_ref[...], x_ref[...], inv_ref[...], incoming_ref[...]
     )
+    store_halves(outgoing_refs, outgoing)
 
 
 def finish(order, *operands):
     row_count, width = operands[-1].shape
     short = array_of((row_count, width), jnp.bfloat16)
     full = array_of((row_count, width), jnp.float32)
+    part = array_of((row_count, width // HALVES), jnp.bfloat16)
     return pl.pallas_call(
         functools.partial(finish_kernel, order),
         in_specs=[WHOLE] * len(operands),
-        out_specs=[WHOLE] * 4,
-        out_shape=[short, short, full, short],
+        out_specs=[WHOLE] * (3 + HALVES),
+        out_shape=[short, short, full] + [part] * HALVES,
         compiler_params=granted(4),
         name="finish",
     )(*operands)
 
 
 def advance_kernel(
-    mid_ref, first_recv_ref, gate_back_ref, gain_ref, x_ref, inv_ref, incoming_ref, outgoing_ref
+    after_ref, mid_ref, first_recv_ref, gate_back_ref, gain_ref, x_ref, inv_ref, *refs
 ):
+    incoming_refs, outgoing_refs = refs[:HALVES], refs[HALVES:]
     first_back = dot(first_recv_ref[...], mid_ref[...])
-    outgoing_ref[...] = outgoing_of(
-        gate_back_ref[...], first_back, gain_ref[...], x_ref[...], inv_ref[...], incoming_ref[...]
-    )
-
-
-def advance(*operands):
+    outgoing = outgoing_of(
+        gate_back_ref[...], first_back, gain_ref[...], x_ref[...], inv_ref[...],
+        joined(incoming_refs),
+    )
+    store_halves(outgoing_refs, outgoing)
+
+
+def advance(incoming, *operands):
     return pl.pallas_call(
         advance_kernel,
-        in_specs=[WHOLE] * len(operands),
-        out_specs=WHOLE,
-        out_shape=array_of(operands[0].shape, jnp.bfloat16),
+        in_specs=[WHOLE] * (len(operands) + HALVES),
+        out_specs=[WHOLE] * HALVES,
+        out_shape=[array_of(part.shape, part.dtype) for part in incoming],
         compiler_params=granted(4),
         name="advance",
-    )(*operands)
-
-
-def keep_kernel(
-    section, outgoing_ref, mid_ref, mix_ref, normed_ref, moved_ref, *refs
+    )(*operands, *incoming)
+
+
+def exact(left, right):
+    return jnp.dot(
+        left, right, precision=lax.Precision.HIGHEST, preferred_element_type=jnp.float32
+    )
+
+
+def keep_kernel(order, section, after_ref, normed_ref, moved_ref, mid_ref, mix_ref, *refs):
+    outgoing_refs, kept, new = refs[:HALVES], refs[HALVES : HALVES + 3], refs[HALVES + 3 :]
+    index = lax.axis_index("pipe")
+    new[0][...] = jnp.where(index == section + 1, joined(outgoing_refs), kept[0][...])
+    first = dot_rows(mid_ref[...], normed_ref[...])
+    new[1][...] = jnp.where(index == section + 1, first, kept[1][...])
+    second = dot_rows(mix_ref[...], moved_ref[...])
+    second = jnp.where(index == section, second, kept[2][...])
+    if section > 0:
+        new[2][...] = second
+        return
+    down, across = positions(order)
+    rows_of = order.second_rows(lax.axis_index("seq"), order.received(down), down)
+    second = exact(second, one_hot(rows_of == across, jnp.float32))
+    for k, rows in enumerate(chunks(order.row_count, order.local_blocks)):
+        new[2][k] = second[rows, rows]
+
+
+def keep_first_kernel(
+    order, section, after_ref, normed_ref, moved_ref, mid_ref, mix_ref, hidden_ref, mix_factor_ref, *refs
 ):
-    kept, new = refs[:3], refs[3:]
-    active = lax.axis_index("pipe") == section
-
-    @pl.when(active)
-    def _():
-        new[0][...] = outgoing_ref[...]
-        new[1][...] = dot_rows(mid_ref[...], normed_ref[...])
-        new[2][...] = dot_rows(mix_ref[...], moved_ref[...])
-
-    @pl.when(jnp.logical_not(active))
-    def _():
-        for old_ref, new_ref in zip(kept, new):
-            new_ref[...] = old_ref[...]
-
-
-def keep(section, kept, *operands):
-    count = len(operands)
-    return pl.pallas_call(
-        functools.partial(keep_kernel, section),
-        in_specs=[WHOLE] * (count + 3),
-        out_specs=[WHOLE] * 3,
-        out_shape=[array_of(k.shape, k.dtype) for k in kept],
-        input_output_aliases={count + i: i for i in range(3)},
-        compiler_params=granted(2),
-        name="keep",
-    )(*operands, *kept)
+    outgoing_refs, new = refs[:HALVES], refs[HALVES:]
+    new[0][...] = joined(outgoing_refs)
+    new[1][...] = dot_rows(mid_ref[...], normed_ref[...])
+    before = (hidden_ref[...] * mix_factor_ref[...]).astype(jnp.bfloat16)
+    mix = jnp.where(lax.axis_index("pipe") == section, mix_ref[...], before)
+    new[2][...] = dot_rows(mix, moved_ref[...])
 
 
 def close_kernel(
-    order, mid_ref, mix_ref, moved_ref, first_recv_ref, gate_back_ref, gain_ref, x_ref, inv_ref, incoming_ref, normed_ref,
-    outgoing_kept_ref, first_kept_ref, second_kept_ref, outgoing_ref, first_ref, second_ref,
+    order, mid_ref, first_recv_ref, gate_back_ref, gain_ref, x_ref, inv_ref, normed_ref, *refs
 ):
+    incoming_refs, refs = refs[:HALVES], refs[HALVES:]
+    outgoing_kept_ref, first_kept_ref, outgoing_ref, first_ref = refs
     active = lax.axis_index("pipe") == 0
     first_back = dot(first_recv_ref[...], mid_ref[...])
     outgoing = outgoing_of(
-        gate_back_ref[...], first_back, gain_ref[...], x_ref[...], inv_ref[...], incoming_ref[...]
+        gate_back_ref[...], first_back, gain_ref[...], x_ref[...], inv_ref[...],
+        joined(incoming_refs),
     )
     outgoing_ref[...] = jnp.where(active, outgoing, outgoing_kept_ref[...])
     first = jnp.where(active, dot_rows(mid_ref[...], normed_ref[...]), first_kept_ref[...])
-    second = jnp.where(active, dot_rows(mix_ref[...], moved_ref[...]), second_kept_ref[...])
-    me = lax.axis_index("seq")
     down, across = positions(order)
-
-    def exact(left, right):
-        return jnp.dot(
-            left, right, precision=lax.Precision.HIGHEST, preferred_element_type=jnp.float32
-        )
-
-    to_first = order.first_rows(me, order.received(across), across) == down
-    to_second = order.second_rows(me, order.received(down), down) == across
-    first = exact(one_hot(to_first, jnp.float32), first)
-    second = exact(second, one_hot(to_second, jnp.float32))
+    rows_of = order.first_rows(lax.axis_index("seq"), order.received(across), across)
+    first = exact(one_hot(rows_of == down, jnp.float32), first)
     for k, rows in enumerate(chunks(order.row_count, order.local_blocks)):
         first_ref[k] = first[rows, rows]
-        second_ref[k] = second[rows, rows]
-
-
-def close(order, *operands):
-    row_count, width = operands[0].shape
-    blocks = array_of((order.local_blocks, order.block_rows, order.block_rows), jnp.float32)
+
+
+def call(kernel, name, outs, operands):
     return pl.pallas_call(
-        functools.partial(close_kernel, order),
+        kernel,
         in_specs=[WHOLE] * len(operands),
-        out_specs=[WHOLE] * 3,
-        out_shape=[array_of((row_count, width), jnp.bfloat16), blocks, blocks],
+        out_specs=[WHOLE] * len(outs),
+        out_shape=outs,
         compiler_params=granted(4),
-        name="close",
+        name=name,
     )(*operands)
 
 
@@ -383,29 +399,48 @@
         order, inputs, gain, mix_first[0], mix_second[0], w_gate[0], cotangent, w_out[0]
     )
     arrived = order.exchange(kept, give, streams=2)
-    gate_turned = transposed(w_gate[0], arrived[0])
-    moved, delta_mid, gate_factor, outgoing = finish(
+    gate_turned, *out_turned = transposed(w_gate[0], w_out[0], arrived[0])
+    moved, delta_mid, gate_factor, *outgoing = finish(
         order, *arrived, second_recv, first_recv, slope, delta_hidden, gate_turned, gain,
         inputs, inv_rms, cotangent,
     )
-    out_turned = transposed(w_out[0], outgoing)
-
-    delta_mix = (delta_hidden * mix_factor).astype(jnp.bfloat16)
-    kept = (outgoing, dot_rows(delta_mid, normed), dot_rows(delta_mix, moved))
+
+    row_count, width = inputs.shape
+    short = array_of((row_count, width), jnp.bfloat16)
+    square = array_of((row_count, row_count), jnp.float32)
+    blocks = array_of((local_blocks, block_rows, block_rows), jnp.float32)
+    kept = (delta_hidden, mix_factor)
     for sender in reversed(range(section_count - 1)):
-        incoming = passed_down(outgoing, sender + 1)
-        delta_hidden = dot(incoming, out_turned)
+        before = (delta_mid, *outgoing)
+        incoming = [passed_down(part, sender + 1) for part in outgoing]
+        delta_hidden = sum(dot(part, weight) for part, weight in zip(incoming, out_turned))
         delta_mix = (delta_hidden * mix_factor).astype(jnp.bfloat16)
         send = rounded(second_send, delta_mix)
-        delta_mid = jnp.concatenate(order.exchange(*jnp.split(send, 2)))
+        arrived = order.exchange(*jnp.split(send, 2))
+        before_mid, *before_outgoing = before
+        if sender + 2 == section_count:
+            kept = call(
+                functools.partial(keep_first_kernel, order, sender), "keep", [short, square, square],
+                (arrived[0], normed, moved, before_mid, delta_mix, *kept, *before_outgoing),
+            )
+        else:
+            kept = call(
+                functools.partial(keep_kernel, order, sender), "keep",
+                [short, square, square if sender else blocks],
+                (arrived[0], normed, moved, before_mid, delta_mix, *before_outgoing, *kept),
+            )
+        delta_mid = jnp.concatenate(arrived)
         delta_gate = (delta_hidden * gate_factor).astype(jnp.bfloat16)
         gate_back = dot(delta_gate, gate_turned)
         if sender > 0:
-            outgoing = advance(delta_mid, first_recv, gate_back, gain, inputs, inv_rms, incoming)
-            kept = keep(sender, kept, outgoing, delta_mid, delta_mix, normed, moved)
-    grad_inputs, grad_first, grad_second = close(
-        order, delta_mid, delta_mix, moved, first_recv, gate_back, gain, inputs, inv_rms, incoming,
-        normed, *kept,
+            outgoing = advance(incoming, kept[1], delta_mid, first_recv, gate_back, gain, inputs, inv_rms)
+    outgoing_kept, first_kept, grad_second = kept
+    grad_inputs, grad_first = call(
+        functools.partial(close_kernel, order), "close", [short, blocks],
+        (
+            delta_mid, first_recv, gate_back, gain, inputs, inv_rms, normed, *incoming,
+            outgoing_kept, first_kept,
+        ),
     )
     return (grad_inputs[None], grad_first[None], grad_second[None])
 

time: 88.9 us -> 87.9 us (0.989)
  waiting for transfers between devices: 35.4 us -> 33.7 us
    ppermute x16, waiting for transfers between devices: 22.8 us -> 19 us  [swap(): return lax.ppermute(block, 'seq', [(i, i ^ offset) for i in range(count)])]
    ppermute x3 -> x6, waiting for transfers between devices: 12.5 us -> 14.7 us  [passed_down(): return lax.ppermute(block, 'pipe', pairs)]
    dot_general x9 -> x12, matrix products: 5.55 us -> 6.18 us  [dot(): return jnp.dot(left, right, preferred_element_type=jnp.float32)]
    ppermute x3 -> x6, starting transfers between devices: 16.3 us -> 16.3 us  [passed_down(): return lax.ppermute(block, 'pipe', pairs)]
  transfers between devices with their start and end apart: 19 -> 22, of which waited for: 15 -> 15; matrix products, arithmetic and copies ran while one was open for 4% -> 5% of each run, Pallas kernels for 7% -> 7%
where the time goes in v6:
time: 87.9 us; the launch traced here: 87.7 us
  waiting for transfers between devices  33.7 us (38%)
  starting transfers between devices  32.6 us (37%)
  Pallas kernels  13.7 us (16%)
  matrix products  6.18 us (7%)
  between operations  1.06 us (1%)
    ppermute x16, waiting for transfers between devices, swap(): return lax.ppermute(block, 'seq', [(i, i ^ offset) for i in range(count)])  19 us
    ppermute x16, starting transfers between devices, swap(): return lax.ppermute(block, 'seq', [(i, i ^ offset) for i in range(count)])  16.3 us
    ppermute x6, starting transfers between devices, passed_down(): return lax.ppermute(block, 'pipe', pairs)  16.3 us
    ppermute x6, waiting for transfers between devices, passed_down(): return lax.ppermute(block, 'pipe', pairs)  14.7 us
    dot_general x12, matrix products, dot(): return jnp.dot(left, right, preferred_element_type=jnp.float32)  6.18 us
    pallas_call x1, Pallas kernels, transposed(): pl.pallas_call(transpose_kernel, in_specs=[ANYWHERE] * 3, out_specs=[WHOL...  4.41 us
    pallas_call x4, Pallas kernels, call(): pl.pallas_call(kernel, in_specs=[WHOLE] * len(operands), out_specs=[WHOLE...  3.64 us
    pallas_call x1, Pallas kernels, begin(): pl.pallas_call(functools.partial(begin_kernel, order), in_specs=[ANYWHERE...  3.53 us
  transfers between devices with their start and end apart: 22, of which 15 were waited for; matrix products, arithmetic and copies ran while one was open for 5% of the time, Pallas kernels for 7%

profile of v6, /device:TPU:0, one launch (start us, length us, event | category | flops | bytes accessed | tf_op | source)
XLA Modules:
  0.0 87.7 jit_solution(4351842643089373400)
XLA Ops:
  0.6 3.5 %begin.1 = (bf16[128,1536]{1,0:T(8,128)(2,1)S(1)}, f32[128,1]{1,0:T(8,128)S(1)}, bf16[128,128]{1,0:T(8,128)(2,1)S(1)}, bf16[128,128]{1,0:T(8,128)(2,1)S(1)}, bf1...) custom-call(bf16[128,1536]{1,0:T(8,128)(2,1)} %bitcast.29, ...), custom_call_target="tpu_custom_call" | custom-call | tf_op jit(solution)/shard_map/begin/pallas_call | solution.py:203
  4.2 0.5 collective-permute-start
  4.7 1.3 %collective-permute-done = bf16[128,1536]{1,0:T(8,128)(2,1)S(1)} collective-permute-done((bf16[128,1536]{1,0:T(8,128)(2,1)S(1)}, bf16[128,1536]{1,0:T(8,128)(2,1)S(1)}, u32[]{:S(2)}, u32[]{:S(2)}) %collective-permute-start) | collective-permute-done | bytes 393248 | tf_op jit(solution)/shard_map/ppermute | solution.py:38
  6.1 2.9 %collective-permute-start.1 = (bf16[64,1536]{1,0:T(8,128)(2,1)S(1)}, bf16[64,1536]{1,0:T(8,128)(2,1)S(1)}, u32[]{:S(2)}, u32[]{:S(2)}) collective-permute-start(bf16[64,1536]{1,0:T(8,128)(2,1)S(1)} %pad_maximum_fusion.1), channel_id=1, source_target_pairs={{0,8},{4,12},{8,0},{12,4},{16,24},{20,28},{24,16},{28,20},{1,9},{5... | collective-permute-start | bytes 589832 | tf_op jit(solution)/shard_map/ppermute | solution.py:38
  9.0 1.6 %collective-permute-start.2 = (bf16[64,1536]{1,0:T(8,128)(2,1)S(1)}, bf16[64,1536]{1,0:T(8,128)(2,1)S(1)}, u32[]{:S(2)}, u32[]{:S(2)}) collective-permute-start(bf16[64,1536]{1,0:T(8,128)(2,1)S(1)} %pad_maximum_fusion.2), channel_id=1, source_target_pairs={{0,16},{4,20},{8,24},{12,28},{16,0},{20,4},{24,8},{28,12},{1,17},{... | collective-permute-start | bytes 589832 | tf_op jit(solution)/shard_map/ppermute | solution.py:38
  10.6 0.1 collective-permute-start.3
  10.7 0.0 copy-start
  10.8 0.0 copy-start.1
  10.8 0.0 copy-start.2
  10.8 4.4 %transposed.1 = (bf16[1536,1536]{1,0:T(8,128)(2,1)S(1)}, bf16[768,1536]{1,0:T(8,128)(2,1)S(1)}, bf16[768,1536]{1,0:T(8,128)(2,1)S(1)}) custom-call(bf16[1536,1536]{1,0:T(8,128)(2,1)} %bitcast.35, bf16[1536,1536]{1,0:T(8,128)(2,1)} %bitcast.37, bf16[64,1536]{1,0:T(8,128)(2,1)S(1)} %pad_maximum_fusion.after_ref.refs_0_), custom_call_target="tpu_custom_call" | custom-call | tf_op jit(solution)/shard_map/transposed/pallas_call | solution.py:233
  15.2 0.0 collective-permute-done.1.refs_1_
  15.2 4.8 %collective-permute-done.2.refs_2_ = bf16[64,1536]{1,0:T(8,128)(2,1)S(1)} collective-permute-done((bf16[64,1536]{1,0:T(8,128)(2,1)S(1)}, bf16[64,1536]{1,0:T(8,128)(2,1)S(1)}, u32[]{:S(2)}, u32[]{:S(2)}) %collective-permute-start.2) | collective-permute-done | bytes 196640 | tf_op jit(solution)/shard_map/ppermute | solution.py:38
  20.0 0.0 collective-permute-done.3.refs_3_
  20.0 1.2 %finish.1 = (bf16[128,1536]{1,0:T(8,128)(2,1)S(1)}, bf16[128,1536]{1,0:T(8,128)(2,1)S(1)}, f32[128,1536]{1,0:T(8,128)S(1)}, bf16[128,768]{1,0:T(8,128)(2,1)S(1)}, bf16[128,768]{1,0:T(8,128)(2,1)S(1)}) custom-call(bf16[64,1536]{1,0:T(8,128)(2,1)S(1)} %pad_maximum_fusion.after_ref.refs_0_, bf16[64,1536]{1,0:T(8,128)(2,1)S(1)} %collective-permute-done.1.refs_1_, ...), custom_call_target="tpu_custom_call" | custom-call | tf_op jit(solution)/shard_map/finish/pallas_call | solution.py:290
  21.2 1.6 %collective-permute-start.5 = (bf16[128,768]{1,0:T(8,128)(2,1)S(1)}, bf16[128,768]{1,0:T(8,128)(2,1)S(1)}, u32[]{:S(2)}, u32[]{:S(2)}) collective-permute-start(bf16[128,768]{1,0:T(8,128)(2,1)S(1)} %get-tuple-element.47.refs_1_), channel_id=1, source_target_pairs={{0,1},{1,0},{2,3},{3,2},{4,5},{5,4},{6,7},{7,6},{8,9},{9,8},{10,11... | collective-permute-start | bytes 589832 | tf_op jit(solution)/shard_map/ppermute | solution.py:46
  22.8 0.5 collective-permute-start.4
  23.3 5.8 %collective-permute-done.5.refs_1_ = bf16[128,768]{1,0:T(8,128)(2,1)S(1)} collective-permute-done((bf16[128,768]{1,0:T(8,128)(2,1)S(1)}, bf16[128,768]{1,0:T(8,128)(2,1)S(1)}, u32[]{:S(2)}, u32[]{:S(2)}) %collective-permute-start.5) | collective-permute-done | bytes 196640 | tf_op jit(solution)/shard_map/ppermute | solution.py:46
  29.1 0.5 fusion.11
  29.6 1.7 %collective-permute-done.4.refs_0_ = bf16[128,768]{1,0:T(8,128)(2,1)S(1)} collective-permute-done((bf16[128,768]{1,0:T(8,128)(2,1)S(1)}, bf16[128,768]{1,0:T(8,128)(2,1)S(1)}, u32[]{:S(2)}, u32[]{:S(2)}) %collective-permute-start.4) | collective-permute-done | bytes 196640 | tf_op jit(solution)/shard_map/ppermute | solution.py:46
  31.3 0.5 multiply_convert_fusion.5
  31.8 0.2 convolution_convert_fusion.2
  32.1 0.1 collective-permute-start.6
  32.2 0.8 fusion.gate_back_ref
  33.0 0.6 collective-permute-done.6
  33.7 1.5 %collective-permute-start.7 = (bf16[32,1536]{1,0:T(8,128)(2,1)S(1)}, bf16[32,1536]{1,0:T(8,128)(2,1)S(1)}, u32[]{:S(2)}, u32[]{:S(2)}) collective-permute-start(bf16[32,1536]{1,0:T(8,128)(2,1)S(1)} %pad_maximum_fusion.5), channel_id=1, source_target_pairs={{0,8},{4,12},{8,0},{12,4},{16,24},{20,28},{24,16},{28,20},{1,9},{5... | collective-permute-start | bytes 294920 | tf_op jit(solution)/shard_map/ppermute | solution.py:38
  35.2 0.6 collective-permute-start.8
  35.8 1.6 %collective-permute-start.9 = (bf16[32,1536]{1,0:T(8,128)(2,1)S(1)}, bf16[32,1536]{1,0:T(8,128)(2,1)S(1)}, u32[]{:S(2)}, u32[]{:S(2)}) collective-permute-start(bf16[32,1536]{1,0:T(8,128)(2,1)S(1)} %pad_maximum_fusion.7), channel_id=1, source_target_pairs={{0,24},{4,28},{8,16},{12,20},{16,8},{20,12},{24,0},{28,4},{1,25},{... | collective-permute-start | bytes 294920 | tf_op jit(solution)/shard_map/ppermute | solution.py:38
  37.4 0.4 keep.3
  37.8 0.8 collective-permute-done.7
  38.6 3.4 %collective-permute-done.8 = bf16[32,1536]{1,0:T(8,128)(2,1)S(1)} collective-permute-done((bf16[32,1536]{1,0:T(8,128)(2,1)S(1)}, bf16[32,1536]{1,0:T(8,128)(2,1)S(1)}, u32[]{:S(2)}, u32[]{:S(2)}) %collective-permute-start.8) | collective-permute-done | bytes 98336 | tf_op jit(solution)/shard_map/ppermute | solution.py:38
  42.0 0.0 collective-permute-done.9
  42.0 0.5 advance.2
  42.5 0.7 collective-permute-start.11
  43.2 0.9 collective-permute-start.10
  44.0 0.5 fusion.12
  44.5 0.5 multiply_convert_fusion.3
  45.1 0.2 convolution_convert_fusion.1
  45.4 0.1 collective-permute-start.12
  45.4 0.8 fusion.1.gate_back_ref
  46.3 0.6 collective-permute-done.12
  46.9 1.0 %collective-permute-start.13 = (bf16[32,1536]{1,0:T(8,128)(2,1)S(1)}, bf16[32,1536]{1,0:T(8,128)(2,1)S(1)}, u32[]{:S(2)}, u32[]{:S(2)}) collective-permute-start(bf16[32,1536]{1,0:T(8,128)(2,1)S(1)} %pad_maximum_fusion.9), channel_id=1, source_target_pairs={{0,8},{4,12},{8,0},{12,4},{16,24},{20,28},{24,16},{28,20},{1,9},{5... | collective-permute-start | bytes 294920 | tf_op jit(solution)/shard_map/ppermute | solution.py:38
  47.9 1.2 %collective-permute-start.14 = (bf16[32,1536]{1,0:T(8,128)(2,1)S(1)}, bf16[32,1536]{1,0:T(8,128)(2,1)S(1)}, u32[]{:S(2)}, u32[]{:S(2)}) collective-permute-start(bf16[32,1536]{1,0:T(8,128)(2,1)S(1)} %pad_maximum_fusion.10), channel_id=1, source_target_pairs={{0,16},{4,20},{8,24},{12,28},{16,0},{20,4},{24,8},{28,12},{1,17},{... | collective-permute-start | bytes 294920 | tf_op jit(solution)/shard_map/ppermute | solution.py:38
  49.1 1.5 %collective-permute-start.15 = (bf16[32,1536]{1,0:T(8,128)(2,1)S(1)}, bf16[32,1536]{1,0:T(8,128)(2,1)S(1)}, u32[]{:S(2)}, u32[]{:S(2)}) collective-permute-start(bf16[32,1536]{1,0:T(8,128)(2,1)S(1)} %pad_maximum_fusion.11), channel_id=1, source_target_pairs={{0,24},{4,28},{8,16},{12,20},{16,8},{20,12},{24,0},{28,4},{1,25},{... | collective-permute-start | bytes 294920 | tf_op jit(solution)/shard_map/ppermute | solution.py:38
  50.6 0.4 keep.4
  51.0 1.0 %collective-permute-done.13 = bf16[32,1536]{1,0:T(8,128)(2,1)S(1)} collective-permute-done((bf16[32,1536]{1,0:T(8,128)(2,1)S(1)}, bf16[32,1536]{1,0:T(8,128)(2,1)S(1)}, u32[]{:S(2)}, u32[]{:S(2)}) %collective-permute-start.13) | collective-permute-done | bytes 98336 | tf_op jit(solution)/shard_map/ppermute | solution.py:38
  51.9 1.7 %collective-permute-done.14 = bf16[32,1536]{1,0:T(8,128)(2,1)S(1)} collective-permute-done((bf16[32,1536]{1,0:T(8,128)(2,1)S(1)}, bf16[32,1536]{1,0:T(8,128)(2,1)S(1)}, u32[]{:S(2)}, u32[]{:S(2)}) %collective-permute-start.14) | collective-permute-done | bytes 98336 | tf_op jit(solution)/shard_map/ppermute | solution.py:38
  53.6 1.1 %collective-permute-done.15 = bf16[32,1536]{1,0:T(8,128)(2,1)S(1)} collective-permute-done((bf16[32,1536]{1,0:T(8,128)(2,1)S(1)}, bf16[32,1536]{1,0:T(8,128)(2,1)S(1)}, u32[]{:S(2)}, u32[]{:S(2)}) %collective-permute-start.15) | collective-permute-done | bytes 98336 | tf_op jit(solution)/shard_map/ppermute | solution.py:38
  54.7 0.5 advance.3
  55.2 12.6 %collective-permute-start.17 = (bf16[128,768]{1,0:T(8,128)(2,1)S(1)}, bf16[128,768]{1,0:T(8,128)(2,1)S(1)}, u32[]{:S(2)}, u32[]{:S(2)}) collective-permute-start(bf16[128,768]{1,0:T(8,128)(2,1)S(1)} %get-tuple-element.61.refs_1_), channel_id=1, source_target_pairs={{0,1},{1,0},{2,3},{3,2},{4,5},{5,4},{6,7},{7,6},{8,9},{9,8},{10,11... | collective-permute-start | bytes 589832 | tf_op jit(solution)/shard_map/ppermute | solution.py:46
  67.8 0.1 collective-permute-start.16
  67.8 5.6 %collective-permute-done.17.refs_1_ = bf16[128,768]{1,0:T(8,128)(2,1)S(1)} collective-permute-done((bf16[128,768]{1,0:T(8,128)(2,1)S(1)}, bf16[128,768]{1,0:T(8,128)(2,1)S(1)}, u32[]{:S(2)}, u32[]{:S(2)}) %collective-permute-start.17) | collective-permute-done | bytes 196640 | tf_op jit(solution)/shard_map/ppermute | solution.py:46
  73.4 0.5 fusion.13
  73.9 1.6 %collective-permute-done.16.refs_0_ = bf16[128,768]{1,0:T(8,128)(2,1)S(1)} collective-permute-done((bf16[128,768]{1,0:T(8,128)(2,1)S(1)}, bf16[128,768]{1,0:T(8,128)(2,1)S(1)}, u32[]{:S(2)}, u32[]{:S(2)}) %collective-permute-start.16) | collective-permute-done | bytes 196640 | tf_op jit(solution)/shard_map/ppermute | solution.py:46
  75.5 0.5 multiply_convert_fusion.1
  76.1 0.2 convolution_convert_fusion
  76.4 0.1 collective-permute-start.18
  76.5 0.8 fusion.2.gate_back_ref
  77.3 0.6 collective-permute-done.18
  77.9 1.4 %collective-permute-start.19 = (bf16[32,1536]{1,0:T(8,128)(2,1)S(1)}, bf16[32,1536]{1,0:T(8,128)(2,1)S(1)}, u32[]{:S(2)}, u32[]{:S(2)}) collective-permute-start(bf16[32,1536]{1,0:T(8,128)(2,1)S(1)} %pad_maximum_fusion.12), channel_id=1, source_target_pairs={{0,8},{4,12},{8,0},{12,4},{16,24},{20,28},{24,16},{28,20},{1,9},{5... | collective-permute-start | bytes 294920 | tf_op jit(solution)/shard_map/ppermute | solution.py:38
  79.4 0.8 collective-permute-start.20
  80.1 1.5 %collective-permute-start.21 = (bf16[32,1536]{1,0:T(8,128)(2,1)S(1)}, bf16[32,1536]{1,0:T(8,128)(2,1)S(1)}, u32[]{:S(2)}, u32[]{:S(2)}) collective-permute-start(bf16[32,1536]{1,0:T(8,128)(2,1)S(1)} %pad_maximum_fusion.14), channel_id=1, source_target_pairs={{0,24},{4,28},{8,16},{12,20},{16,8},{20,12},{24,0},{28,4},{1,25},{... | collective-permute-start | bytes 294920 | tf_op jit(solution)/shard_map/ppermute | solution.py:38
  81.6 1.3 %keep.5 = (bf16[128,1536]{1,0:T(8,128)(2,1)S(1)}, f32[128,128]{1,0:T(8,128)S(1)}, f32[2,64,64]{2,1,0:T(8,128)}) custom-call(bf16[32,1536]{1,0:T(8,128)(2,1)S(1)} %pad_maximum_fusion.15.after_ref, bf16[128,1536]{1,0:T(8,128)(2,1)S(1)} %get-tuple-element.50.normed_ref, bf16[128,1536]{1,0:T(8,128)(2,1)S(1)} %get-tuple-element.51.moved_ref, ...), custom_call_target="tpu_custom_call" | custom-call | tf_op jit(solution)/shard_map/keep/pallas_call | solution.py:379
  82.9 3.2 %collective-permute-done.20 = bf16[32,1536]{1,0:T(8,128)(2,1)S(1)} collective-permute-done((bf16[32,1536]{1,0:T(8,128)(2,1)S(1)}, bf16[32,1536]{1,0:T(8,128)(2,1)S(1)}, u32[]{:S(2)}, u32[]{:S(2)}) %collective-permute-start.20) | collective-permute-done | bytes 98336 | tf_op jit(solution)/shard_map/ppermute | solution.py:38
  86.2 1.6 %close.1 = (bf16[128,1536]{1,0:T(8,128)(2,1)}, f32[2,64,64]{2,1,0:T(8,128)}) custom-call(bf16[128,1536]{1,0:T(8,128)(2,1)S(1)} %constant_dynamic-update-slice_fusion.10.mid_ref, bf16[128,128]{1,0:T(8,128)(2,1)S(1)} %get-tuple-element.40.refs_5_.first_recv_ref, f32[128,1536]{1,0:T(8,128)S(1)} %fusion.2.gate_back_ref, f32[1,1536]{1,0:T(1,128)S(1)} %copy-done.2, ...), custom_call_target="tpu_custom_call" | custom-call | tf_op jit(solution)/shard_map/close/pallas_call | solution.py:379
  (43 shorter events, 0.4 us)
Async XLA Ops:
  4.2 1.9 %collective-permute-start = (bf16[128,1536]{1,0:T(8,128)(2,1)S(1)}, bf16[128,1536]{1,0:T(8,128)(2,1)S(1)}, u32[]{:S(2)}, u32[]{:S(2)}) collective-permute-start(bf16[128,1536]{1,0:T(8,128)(2,1)S(1)} %get-tuple-element.38), channel_id=1, source_target_pairs={{0,4},{4,0},{8,12},{12,8},{16,20},{20,16},{24,28},{28,24},{1,5},{5... | collective-permute-start | bytes 1179656 | tf_op jit(solution)/shard_map/ppermute | solution.py:38
  6.1 9.1 %collective-permute-start.1 = (bf16[64,1536]{1,0:T(8,128)(2,1)S(1)}, bf16[64,1536]{1,0:T(8,128)(2,1)S(1)}, u32[]{:S(2)}, u32[]{:S(2)}) collective-permute-start(bf16[64,1536]{1,0:T(8,128)(2,1)S(1)} %pad_maximum_fusion.1), channel_id=1, source_target_pairs={{0,8},{4,12},{8,0},{12,4},{16,24},{20,28},{24,16},{28,20},{1,9},{5... | collective-permute-start | bytes 589832 | tf_op jit(solution)/shard_map/ppermute | solution.py:38
  9.0 10.9 %collective-permute-start.2 = (bf16[64,1536]{1,0:T(8,128)(2,1)S(1)}, bf16[64,1536]{1,0:T(8,128)(2,1)S(1)}, u32[]{:S(2)}, u32[]{:S(2)}) collective-permute-start(bf16[64,1536]{1,0:T(8,128)(2,1)S(1)} %pad_maximum_fusion.2), channel_id=1, source_target_pairs={{0,16},{4,20},{8,24},{12,28},{16,0},{20,4},{24,8},{28,12},{1,17},{... | collective-permute-start | bytes 589832 | tf_op jit(solution)/shard_map/ppermute | solution.py:38
  10.6 9.3 %collective-permute-start.3 = (bf16[64,1536]{1,0:T(8,128)(2,1)S(1)}, bf16[64,1536]{1,0:T(8,128)(2,1)S(1)}, u32[]{:S(2)}, u32[]{:S(2)}) collective-permute-start(bf16[64,1536]{1,0:T(8,128)(2,1)S(1)} %pad_maximum_fusion.3), channel_id=1, source_target_pairs={{0,24},{4,28},{8,16},{12,20},{16,8},{20,12},{24,0},{28,4},{1,25},{... | collective-permute-start | bytes 589832 | tf_op jit(solution)/shard_map/ppermute | solution.py:38
  10.7 9.2 %copy-start = (bf16[1,128,1536]{2,1,0:T(8,128)(2,1)S(1)}, bf16[1,128,1536]{2,1,0:T(8,128)(2,1)}, u32[]{:S(2)}) copy-start(bf16[1,128,1536]{2,1,0:T(8,128)(2,1)} %param.7) | copy-start | bytes 1179652
  10.8 9.2 %copy-start.1 = (bf16[128,1536]{1,0:T(8,128)(2,1)S(1)}, bf16[128,1536]{1,0:T(8,128)(2,1)}, u32[]{:S(2)}) copy-start(bf16[128,1536]{1,0:T(8,128)(2,1)} %refs_12_.1) | copy-start | bytes 1179652
  10.8 9.2 %copy-start.2 = (f32[1,1536]{1,0:T(1,128)S(1)}, f32[1,1536]{1,0:T(1,128)}, u32[]{:S(2)}) copy-start(f32[1,1536]{1,0:T(1,128)} %gain_ref.5) | copy-start | bytes 18436
  21.2 7.9 %collective-permute-start.5 = (bf16[128,768]{1,0:T(8,128)(2,1)S(1)}, bf16[128,768]{1,0:T(8,128)(2,1)S(1)}, u32[]{:S(2)}, u32[]{:S(2)}) collective-permute-start(bf16[128,768]{1,0:T(8,128)(2,1)S(1)} %get-tuple-element.47.refs_1_), channel_id=1, source_target_pairs={{0,1},{1,0},{2,3},{3,2},{4,5},{5,4},{6,7},{7,6},{8,9},{9,8},{10,11... | collective-permute-start | bytes 589832 | tf_op jit(solution)/shard_map/ppermute | solution.py:46
  22.8 8.5 %collective-permute-start.4 = (bf16[128,768]{1,0:T(8,128)(2,1)S(1)}, bf16[128,768]{1,0:T(8,128)(2,1)S(1)}, u32[]{:S(2)}, u32[]{:S(2)}) collective-permute-start(bf16[128,768]{1,0:T(8,128)(2,1)S(1)} %get-tuple-element.45.refs_0_), channel_id=1, source_target_pairs={{0,1},{1,0},{2,3},{3,2},{4,5},{5,4},{6,7},{7,6},{8,9},{9,8},{10,11... | collective-permute-start | bytes 589832 | tf_op jit(solution)/shard_map/ppermute | solution.py:46
  32.1 1.5 %collective-permute-start.6 = (bf16[64,1536]{1,0:T(8,128)(2,1)S(1)}, bf16[64,1536]{1,0:T(8,128)(2,1)S(1)}, u32[]{:S(2)}, u32[]{:S(2)}) collective-permute-start(bf16[64,1536]{1,0:T(8,128)(2,1)S(1)} %split.15), channel_id=1, source_target_pairs={{0,4},{4,0},{8,12},{12,8},{16,20},{20,16},{24,28},{28,24},{1,5},{5... | collective-permute-start | bytes 589832 | tf_op jit(solution)/shard_map/ppermute | solution.py:38
  33.7 4.9 %collective-permute-start.7 = (bf16[32,1536]{1,0:T(8,128)(2,1)S(1)}, bf16[32,1536]{1,0:T(8,128)(2,1)S(1)}, u32[]{:S(2)}, u32[]{:S(2)}) collective-permute-start(bf16[32,1536]{1,0:T(8,128)(2,1)S(1)} %pad_maximum_fusion.5), channel_id=1, source_target_pairs={{0,8},{4,12},{8,0},{12,4},{16,24},{20,28},{24,16},{28,20},{1,9},{5... | collective-permute-start | bytes 294920 | tf_op jit(solution)/shard_map/ppermute | solution.py:38
  35.2 6.8 %collective-permute-start.8 = (bf16[32,1536]{1,0:T(8,128)(2,1)S(1)}, bf16[32,1536]{1,0:T(8,128)(2,1)S(1)}, u32[]{:S(2)}, u32[]{:S(2)}) collective-permute-start(bf16[32,1536]{1,0:T(8,128)(2,1)S(1)} %pad_maximum_fusion.6), channel_id=1, source_target_pairs={{0,16},{4,20},{8,24},{12,28},{16,0},{20,4},{24,8},{28,12},{1,17},{... | collective-permute-start | bytes 294920 | tf_op jit(solution)/shard_map/ppermute | solution.py:38
  35.8 6.2 %collective-permute-start.9 = (bf16[32,1536]{1,0:T(8,128)(2,1)S(1)}, bf16[32,1536]{1,0:T(8,128)(2,1)S(1)}, u32[]{:S(2)}, u32[]{:S(2)}) collective-permute-start(bf16[32,1536]{1,0:T(8,128)(2,1)S(1)} %pad_maximum_fusion.7), channel_id=1, source_target_pairs={{0,24},{4,28},{8,16},{12,20},{16,8},{20,12},{24,0},{28,4},{1,25},{... | collective-permute-start | bytes 294920 | tf_op jit(solution)/shard_map/ppermute | solution.py:38
  42.5 1.5 %collective-permute-start.11 = (bf16[128,768]{1,0:T(8,128)(2,1)S(1)}, bf16[128,768]{1,0:T(8,128)(2,1)S(1)}, u32[]{:S(2)}, u32[]{:S(2)}) collective-permute-start(bf16[128,768]{1,0:T(8,128)(2,1)S(1)} %get-tuple-element.56.refs_1_), channel_id=1, source_target_pairs={{2,1},{6,5},{10,9},{14,13},{18,17},{22,21},{26,25},{30,29}} | collective-permute-start | bytes 589832 | tf_op jit(solution)/shard_map/ppermute | solution.py:46
  43.2 1.4 %collective-permute-start.10 = (bf16[128,768]{1,0:T(8,128)(2,1)S(1)}, bf16[128,768]{1,0:T(8,128)(2,1)S(1)}, u32[]{:S(2)}, u32[]{:S(2)}) collective-permute-start(bf16[128,768]{1,0:T(8,128)(2,1)S(1)} %get-tuple-element.55.refs_0_), channel_id=1, source_target_pairs={{2,1},{6,5},{10,9},{14,13},{18,17},{22,21},{26,25},{30,29}} | collective-permute-start | bytes 589832 | tf_op jit(solution)/shard_map/ppermute | solution.py:46
  45.4 1.5 %collective-permute-start.12 = (bf16[64,1536]{1,0:T(8,128)(2,1)S(1)}, bf16[64,1536]{1,0:T(8,128)(2,1)S(1)}, u32[]{:S(2)}, u32[]{:S(2)}) collective-permute-start(bf16[64,1536]{1,0:T(8,128)(2,1)S(1)} %split.16), channel_id=1, source_target_pairs={{0,4},{4,0},{8,12},{12,8},{16,20},{20,16},{24,28},{28,24},{1,5},{5... | collective-permute-start | bytes 589832 | tf_op jit(solution)/shard_map/ppermute | solution.py:38
  46.9 5.0 %collective-permute-start.13 = (bf16[32,1536]{1,0:T(8,128)(2,1)S(1)}, bf16[32,1536]{1,0:T(8,128)(2,1)S(1)}, u32[]{:S(2)}, u32[]{:S(2)}) collective-permute-start(bf16[32,1536]{1,0:T(8,128)(2,1)S(1)} %pad_maximum_fusion.9), channel_id=1, source_target_pairs={{0,8},{4,12},{8,0},{12,4},{16,24},{20,28},{24,16},{28,20},{1,9},{5... | collective-permute-start | bytes 294920 | tf_op jit(solution)/shard_map/ppermute | solution.py:38
  47.9 5.7 %collective-permute-start.14 = (bf16[32,1536]{1,0:T(8,128)(2,1)S(1)}, bf16[32,1536]{1,0:T(8,128)(2,1)S(1)}, u32[]{:S(2)}, u32[]{:S(2)}) collective-permute-start(bf16[32,1536]{1,0:T(8,128)(2,1)S(1)} %pad_maximum_fusion.10), channel_id=1, source_target_pairs={{0,16},{4,20},{8,24},{12,28},{16,0},{20,4},{24,8},{28,12},{1,17},{... | collective-permute-start | bytes 294920 | tf_op jit(solution)/shard_map/ppermute | solution.py:38
  49.1 5.6 %collective-permute-start.15 = (bf16[32,1536]{1,0:T(8,128)(2,1)S(1)}, bf16[32,1536]{1,0:T(8,128)(2,1)S(1)}, u32[]{:S(2)}, u32[]{:S(2)}) collective-permute-start(bf16[32,1536]{1,0:T(8,128)(2,1)S(1)} %pad_maximum_fusion.11), channel_id=1, source_target_pairs={{0,24},{4,28},{8,16},{12,20},{16,8},{20,12},{24,0},{28,4},{1,25},{... | collective-permute-start | bytes 294920 | tf_op jit(solution)/shard_map/ppermute | solution.py:38
  55.2 18.2 %collective-permute-start.17 = (bf16[128,768]{1,0:T(8,128)(2,1)S(1)}, bf16[128,768]{1,0:T(8,128)(2,1)S(1)}, u32[]{:S(2)}, u32[]{:S(2)}) collective-permute-start(bf16[128,768]{1,0:T(8,128)(2,1)S(1)} %get-tuple-element.61.refs_1_), channel_id=1, source_target_pairs={{0,1},{1,0},{2,3},{3,2},{4,5},{5,4},{6,7},{7,6},{8,9},{9,8},{10,11... | collective-permute-start | bytes 589832 | tf_op jit(solution)/shard_map/ppermute | solution.py:46
  67.8 7.8 %collective-permute-start.16 = (bf16[128,768]{1,0:T(8,128)(2,1)S(1)}, bf16[128,768]{1,0:T(8,128)(2,1)S(1)}, u32[]{:S(2)}, u32[]{:S(2)}) collective-permute-start(bf16[128,768]{1,0:T(8,128)(2,1)S(1)} %get-tuple-element.60.refs_0_), channel_id=1, source_target_pairs={{0,1},{1,0},{2,3},{3,2},{4,5},{5,4},{6,7},{7,6},{8,9},{9,8},{10,11... | collective-permute-start | bytes 589832 | tf_op jit(solution)/shard_map/ppermute | solution.py:46
  76.4 1.5 %collective-permute-start.18 = (bf16[64,1536]{1,0:T(8,128)(2,1)S(1)}, bf16[64,1536]{1,0:T(8,128)(2,1)S(1)}, u32[]{:S(2)}, u32[]{:S(2)}) collective-permute-start(bf16[64,1536]{1,0:T(8,128)(2,1)S(1)} %split.17), channel_id=1, source_target_pairs={{0,4},{4,0},{8,12},{12,8},{16,20},{20,16},{24,28},{28,24},{1,5},{5... | collective-permute-start | bytes 589832 | tf_op jit(solution)/shard_map/ppermute | solution.py:38
  77.9 5.0 %collective-permute-start.19 = (bf16[32,1536]{1,0:T(8,128)(2,1)S(1)}, bf16[32,1536]{1,0:T(8,128)(2,1)S(1)}, u32[]{:S(2)}, u32[]{:S(2)}) collective-permute-start(bf16[32,1536]{1,0:T(8,128)(2,1)S(1)} %pad_maximum_fusion.12), channel_id=1, source_target_pairs={{0,8},{4,12},{8,0},{12,4},{16,24},{20,28},{24,16},{28,20},{1,9},{5... | collective-permute-start | bytes 294920 | tf_op jit(solution)/shard_map/ppermute | solution.py:38
  79.4 6.8 %collective-permute-start.20 = (bf16[32,1536]{1,0:T(8,128)(2,1)S(1)}, bf16[32,1536]{1,0:T(8,128)(2,1)S(1)}, u32[]{:S(2)}, u32[]{:S(2)}) collective-permute-start(bf16[32,1536]{1,0:T(8,128)(2,1)S(1)} %pad_maximum_fusion.13), channel_id=1, source_target_pairs={{0,16},{4,20},{8,24},{12,28},{16,0},{20,4},{24,8},{28,12},{1,17},{... | collective-permute-start | bytes 294920 | tf_op jit(solution)/shard_map/ppermute | solution.py:38
  80.1 6.0 %collective-permute-start.21 = (bf16[32,1536]{1,0:T(8,128)(2,1)S(1)}, bf16[32,1536]{1,0:T(8,128)(2,1)S(1)}, u32[]{:S(2)}, u32[]{:S(2)}) collective-permute-start(bf16[32,1536]{1,0:T(8,128)(2,1)S(1)} %pad_maximum_fusion.14), channel_id=1, source_target_pairs={{0,24},{4,28},{8,16},{12,20},{16,8},{20,12},{24,0},{28,4},{1,25},{... | collective-permute-start | bytes 294920 | tf_op jit(solution)/shard_map/ppermute | solution.py:38

commit v7 on v6

--- a/solution.py
+++ b/solution.py
@@ -39,11 +39,15 @@
 
 
 def passed_down(block, sender):
-    count = lax.axis_size("pipe")
-    pairs = [(sender, sender - 1)]
-    if count % 2 == 0 and sender % 2 == 1:
-        pairs = [(i, i ^ 1) for i in range(count)]
-    return lax.ppermute(block, "pipe", pairs)
+    sections = lax.axis_size("pipe")
+    pairs = []
+    for device in range(lax.axis_size("seq")):
+        for section in range(sections):
+            target = (device ^ 1, section)
+            if section in (sender, sender - 1):
+                target = (device, 2 * sender - 1 - section)
+            pairs.append((device * sections + section, target[0] * sections + target[1]))
+    return lax.ppermute(block, ("seq", "pipe"), pairs)
 
 
 def chunks(size, count):

time: 87.9 us -> 86.7 us (0.986)
  waiting for transfers between devices: 33.7 us -> 27.9 us
  starting transfers between devices: 32.6 us -> 37.3 us
    ppermute x6, waiting for transfers between devices: 14.7 us -> 9.1 us  [passed_down(): return lax.ppermute(block, ('seq', 'pipe'), pairs)]
    ppermute x6, starting transfers between devices: 16.3 us -> 20.7 us  [passed_down(): return lax.ppermute(block, ('seq', 'pipe'), pairs)]
  transfers between devices with their start and end apart: 22 -> 22, of which waited for: 15 -> 16; matrix products, arithmetic and copies ran while one was open for 5% -> 5% of each run, Pallas kernels for 7% -> 8%
where the time goes in v7:
time: 86.7 us; the launch traced here: 86.5 us
  starting transfers between devices  37.3 us (43%)
  waiting for transfers between devices  27.9 us (32%)
  Pallas kernels  13.7 us (16%)
  matrix products  6.19 us (7%)
  between operations  1.03 us (1%)
    ppermute x6, starting transfers between devices, passed_down(): return lax.ppermute(block, ('seq', 'pipe'), pairs)  20.7 us
    ppermute x16, waiting for transfers between devices, swap(): return lax.ppermute(block, 'seq', [(i, i ^ offset) for i in range(count)])  18.8 us
    ppermute x16, starting transfers between devices, swap(): return lax.ppermute(block, 'seq', [(i, i ^ offset) for i in range(count)])  16.6 us
    ppermute x6, waiting for transfers between devices, passed_down(): return lax.ppermute(block, ('seq', 'pipe'), pairs)  9.1 us
    dot_general x12, matrix products, dot(): return jnp.dot(left, right, preferred_element_type=jnp.float32)  6.19 us
    pallas_call x1, Pallas kernels, transposed(): pl.pallas_call(transpose_kernel, in_specs=[ANYWHERE] * 3, out_specs=[WHOL...  4.41 us
    pallas_call x4, Pallas kernels, call(): pl.pallas_call(kernel, in_specs=[WHOLE] * len(operands), out_specs=[WHOLE...  3.64 us
    pallas_call x1, Pallas kernels, begin(): pl.pallas_call(functools.partial(begin_kernel, order), in_specs=[ANYWHERE...  3.53 us
  transfers between devices with their start and end apart: 22, of which 16 were waited for; matrix products, arithmetic and copies ran while one was open for 5% of the time, Pallas kernels for 8%

profile of v7, /device:TPU:0, one launch (start us, length us, event | category | flops | bytes accessed | tf_op | source)
XLA Modules:
  0.0 86.5 jit_solution(16614933773269374695)
XLA Ops:
  0.6 3.5 %begin.1 = (bf16[128,1536]{1,0:T(8,128)(2,1)S(1)}, f32[128,1]{1,0:T(8,128)S(1)}, bf16[128,128]{1,0:T(8,128)(2,1)S(1)}, bf16[128,128]{1,0:T(8,128)(2,1)S(1)}, bf1...) custom-call(bf16[128,1536]{1,0:T(8,128)(2,1)} %bitcast.29, ...), custom_call_target="tpu_custom_call" | custom-call | tf_op jit(solution)/shard_map/begin/pallas_call | solution.py:207
  4.2 0.5 collective-permute-start
  4.7 1.3 %collective-permute-done = bf16[128,1536]{1,0:T(8,128)(2,1)S(1)} collective-permute-done((bf16[128,1536]{1,0:T(8,128)(2,1)S(1)}, bf16[128,1536]{1,0:T(8,128)(2,1)S(1)}, u32[]{:S(2)}, u32[]{:S(2)}) %collective-permute-start) | collective-permute-done | bytes 393248 | tf_op jit(solution)/shard_map/ppermute | solution.py:38
  6.1 2.9 %collective-permute-start.1 = (bf16[64,1536]{1,0:T(8,128)(2,1)S(1)}, bf16[64,1536]{1,0:T(8,128)(2,1)S(1)}, u32[]{:S(2)}, u32[]{:S(2)}) collective-permute-start(bf16[64,1536]{1,0:T(8,128)(2,1)S(1)} %pad_maximum_fusion.1), channel_id=1, source_target_pairs={{0,8},{4,12},{8,0},{12,4},{16,24},{20,28},{24,16},{28,20},{1,9},{5... | collective-permute-start | bytes 589832 | tf_op jit(solution)/shard_map/ppermute | solution.py:38
  9.0 1.6 %collective-permute-start.2 = (bf16[64,1536]{1,0:T(8,128)(2,1)S(1)}, bf16[64,1536]{1,0:T(8,128)(2,1)S(1)}, u32[]{:S(2)}, u32[]{:S(2)}) collective-permute-start(bf16[64,1536]{1,0:T(8,128)(2,1)S(1)} %pad_maximum_fusion.2), channel_id=1, source_target_pairs={{0,16},{4,20},{8,24},{12,28},{16,0},{20,4},{24,8},{28,12},{1,17},{... | collective-permute-start | bytes 589832 | tf_op jit(solution)/shard_map/ppermute | solution.py:38
  10.6 0.1 collective-permute-start.3
  10.7 0.0 copy-start
  10.7 0.0 copy-start.1
  10.8 0.0 copy-start.2
  10.8 4.4 %transposed.1 = (bf16[1536,1536]{1,0:T(8,128)(2,1)S(1)}, bf16[768,1536]{1,0:T(8,128)(2,1)S(1)}, bf16[768,1536]{1,0:T(8,128)(2,1)S(1)}) custom-call(bf16[1536,1536]{1,0:T(8,128)(2,1)} %bitcast.35, bf16[1536,1536]{1,0:T(8,128)(2,1)} %bitcast.37, bf16[64,1536]{1,0:T(8,128)(2,1)S(1)} %pad_maximum_fusion.after_ref.refs_0_), custom_call_target="tpu_custom_call" | custom-call | tf_op jit(solution)/shard_map/transposed/pallas_call | solution.py:237
  15.2 0.0 collective-permute-done.1.refs_1_
  15.2 4.8 %collective-permute-done.2.refs_2_ = bf16[64,1536]{1,0:T(8,128)(2,1)S(1)} collective-permute-done((bf16[64,1536]{1,0:T(8,128)(2,1)S(1)}, bf16[64,1536]{1,0:T(8,128)(2,1)S(1)}, u32[]{:S(2)}, u32[]{:S(2)}) %collective-permute-start.2) | collective-permute-done | bytes 196640 | tf_op jit(solution)/shard_map/ppermute | solution.py:38
  20.0 0.0 collective-permute-done.3.refs_3_
  20.0 1.2 %finish.1 = (bf16[128,1536]{1,0:T(8,128)(2,1)S(1)}, bf16[128,1536]{1,0:T(8,128)(2,1)S(1)}, f32[128,1536]{1,0:T(8,128)S(1)}, bf16[128,768]{1,0:T(8,128)(2,1)S(1)}, bf16[128,768]{1,0:T(8,128)(2,1)S(1)}) custom-call(bf16[64,1536]{1,0:T(8,128)(2,1)S(1)} %pad_maximum_fusion.after_ref.refs_0_, bf16[64,1536]{1,0:T(8,128)(2,1)S(1)} %collective-permute-done.1.refs_1_, ...), custom_call_target="tpu_custom_call" | custom-call | tf_op jit(solution)/shard_map/finish/pallas_call | solution.py:294
  21.2 0.1 collective-permute-start.5
  21.3 0.5 collective-permute-start.4
  21.8 0.9 %collective-permute-done.5.refs_1_ = bf16[128,768]{1,0:T(8,128)(2,1)S(1)} collective-permute-done((bf16[128,768]{1,0:T(8,128)(2,1)S(1)}, bf16[128,768]{1,0:T(8,128)(2,1)S(1)}, u32[]{:S(2)}, u32[]{:S(2)}) %collective-permute-start.5) | collective-permute-done | bytes 196640 | tf_op jit(solution)/shard_map/ppermute | solution.py:50
  22.7 0.5 fusion.11
  23.2 0.5 multiply_convert_fusion.5
  23.7 0.3 convolution_convert_fusion.2
  24.0 0.2 collective-permute-start.6
  24.2 0.8 fusion.gate_back_ref
  25.1 0.5 collective-permute-done.6
  25.6 1.2 %collective-permute-start.7 = (bf16[32,1536]{1,0:T(8,128)(2,1)S(1)}, bf16[32,1536]{1,0:T(8,128)(2,1)S(1)}, u32[]{:S(2)}, u32[]{:S(2)}) collective-permute-start(bf16[32,1536]{1,0:T(8,128)(2,1)S(1)} %pad_maximum_fusion.5), channel_id=1, source_target_pairs={{0,8},{4,12},{8,0},{12,4},{16,24},{20,28},{24,16},{28,20},{1,9},{5... | collective-permute-start | bytes 294920 | tf_op jit(solution)/shard_map/ppermute | solution.py:38
  26.8 1.0 %collective-permute-start.8 = (bf16[32,1536]{1,0:T(8,128)(2,1)S(1)}, bf16[32,1536]{1,0:T(8,128)(2,1)S(1)}, u32[]{:S(2)}, u32[]{:S(2)}) collective-permute-start(bf16[32,1536]{1,0:T(8,128)(2,1)S(1)} %pad_maximum_fusion.6), channel_id=1, source_target_pairs={{0,16},{4,20},{8,24},{12,28},{16,0},{20,4},{24,8},{28,12},{1,17},{... | collective-permute-start | bytes 294920 | tf_op jit(solution)/shard_map/ppermute | solution.py:38
  27.8 1.5 %collective-permute-start.9 = (bf16[32,1536]{1,0:T(8,128)(2,1)S(1)}, bf16[32,1536]{1,0:T(8,128)(2,1)S(1)}, u32[]{:S(2)}, u32[]{:S(2)}) collective-permute-start(bf16[32,1536]{1,0:T(8,128)(2,1)S(1)} %pad_maximum_fusion.7), channel_id=1, source_target_pairs={{0,24},{4,28},{8,16},{12,20},{16,8},{20,12},{24,0},{28,4},{1,25},{... | collective-permute-start | bytes 294920 | tf_op jit(solution)/shard_map/ppermute | solution.py:38
  29.3 0.4 keep.3
  29.7 0.8 collective-permute-done.7
  30.5 1.8 %collective-permute-done.8 = bf16[32,1536]{1,0:T(8,128)(2,1)S(1)} collective-permute-done((bf16[32,1536]{1,0:T(8,128)(2,1)S(1)}, bf16[32,1536]{1,0:T(8,128)(2,1)S(1)}, u32[]{:S(2)}, u32[]{:S(2)}) %collective-permute-start.8) | collective-permute-done | bytes 98336 | tf_op jit(solution)/shard_map/ppermute | solution.py:38
  32.3 1.3 %collective-permute-done.9 = bf16[32,1536]{1,0:T(8,128)(2,1)S(1)} collective-permute-done((bf16[32,1536]{1,0:T(8,128)(2,1)S(1)}, bf16[32,1536]{1,0:T(8,128)(2,1)S(1)}, u32[]{:S(2)}, u32[]{:S(2)}) %collective-permute-start.9) | collective-permute-done | bytes 98336 | tf_op jit(solution)/shard_map/ppermute | solution.py:38
  33.6 0.5 advance.2
  34.1 0.1 collective-permute-start.11
  34.1 0.5 collective-permute-start.10
  34.6 0.9 %collective-permute-done.11.refs_1_ = bf16[128,768]{1,0:T(8,128)(2,1)S(1)} collective-permute-done((bf16[128,768]{1,0:T(8,128)(2,1)S(1)}, bf16[128,768]{1,0:T(8,128)(2,1)S(1)}, u32[]{:S(2)}, u32[]{:S(2)}) %collective-permute-start.11) | collective-permute-done | bytes 196640 | tf_op jit(solution)/shard_map/ppermute | solution.py:50
  35.6 0.5 fusion.12
  36.1 0.5 multiply_convert_fusion.3
  36.6 0.3 convolution_convert_fusion.1
  36.9 0.2 collective-permute-start.12
  37.1 0.8 fusion.1.gate_back_ref
  37.9 0.5 collective-permute-done.12
  38.4 1.3 %collective-permute-start.13 = (bf16[32,1536]{1,0:T(8,128)(2,1)S(1)}, bf16[32,1536]{1,0:T(8,128)(2,1)S(1)}, u32[]{:S(2)}, u32[]{:S(2)}) collective-permute-start(bf16[32,1536]{1,0:T(8,128)(2,1)S(1)} %pad_maximum_fusion.9), channel_id=1, source_target_pairs={{0,8},{4,12},{8,0},{12,4},{16,24},{20,28},{24,16},{28,20},{1,9},{5... | collective-permute-start | bytes 294920 | tf_op jit(solution)/shard_map/ppermute | solution.py:38
  39.8 1.2 %collective-permute-start.14 = (bf16[32,1536]{1,0:T(8,128)(2,1)S(1)}, bf16[32,1536]{1,0:T(8,128)(2,1)S(1)}, u32[]{:S(2)}, u32[]{:S(2)}) collective-permute-start(bf16[32,1536]{1,0:T(8,128)(2,1)S(1)} %pad_maximum_fusion.10), channel_id=1, source_target_pairs={{0,16},{4,20},{8,24},{12,28},{16,0},{20,4},{24,8},{28,12},{1,17},{... | collective-permute-start | bytes 294920 | tf_op jit(solution)/shard_map/ppermute | solution.py:38
  41.0 1.1 %collective-permute-start.15 = (bf16[32,1536]{1,0:T(8,128)(2,1)S(1)}, bf16[32,1536]{1,0:T(8,128)(2,1)S(1)}, u32[]{:S(2)}, u32[]{:S(2)}) collective-permute-start(bf16[32,1536]{1,0:T(8,128)(2,1)S(1)} %pad_maximum_fusion.11), channel_id=1, source_target_pairs={{0,24},{4,28},{8,16},{12,20},{16,8},{20,12},{24,0},{28,4},{1,25},{... | collective-permute-start | bytes 294920 | tf_op jit(solution)/shard_map/ppermute | solution.py:38
  42.1 0.4 keep.4
  42.5 0.8 collective-permute-done.13
  43.4 2.1 %collective-permute-done.14 = bf16[32,1536]{1,0:T(8,128)(2,1)S(1)} collective-permute-done((bf16[32,1536]{1,0:T(8,128)(2,1)S(1)}, bf16[32,1536]{1,0:T(8,128)(2,1)S(1)}, u32[]{:S(2)}, u32[]{:S(2)}) %collective-permute-start.14) | collective-permute-done | bytes 98336 | tf_op jit(solution)/shard_map/ppermute | solution.py:38
  45.5 1.1 %collective-permute-done.15 = bf16[32,1536]{1,0:T(8,128)(2,1)S(1)} collective-permute-done((bf16[32,1536]{1,0:T(8,128)(2,1)S(1)}, bf16[32,1536]{1,0:T(8,128)(2,1)S(1)}, u32[]{:S(2)}, u32[]{:S(2)}) %collective-permute-start.15) | collective-permute-done | bytes 98336 | tf_op jit(solution)/shard_map/ppermute | solution.py:38
  46.6 0.5 advance.3
  47.1 19.5 %collective-permute-start.17 = (bf16[128,768]{1,0:T(8,128)(2,1)S(1)}, bf16[128,768]{1,0:T(8,128)(2,1)S(1)}, u32[]{:S(2)}, u32[]{:S(2)}) collective-permute-start(bf16[128,768]{1,0:T(8,128)(2,1)S(1)} %get-tuple-element.61.refs_1_), channel_id=1, source_target_pairs={{0,1},{1,0},{2,6},{3,7},{4,5},{5,4},{6,2},{7,3},{8,9},{9,8},{10,14... | collective-permute-start | bytes 589832 | tf_op jit(solution)/shard_map/ppermute | solution.py:50
  66.6 0.1 collective-permute-start.16
  66.6 5.6 %collective-permute-done.17.refs_1_ = bf16[128,768]{1,0:T(8,128)(2,1)S(1)} collective-permute-done((bf16[128,768]{1,0:T(8,128)(2,1)S(1)}, bf16[128,768]{1,0:T(8,128)(2,1)S(1)}, u32[]{:S(2)}, u32[]{:S(2)}) %collective-permute-start.17) | collective-permute-done | bytes 196640 | tf_op jit(solution)/shard_map/ppermute | solution.py:50
  72.2 0.5 fusion.13
  72.7 1.6 %collective-permute-done.16.refs_0_ = bf16[128,768]{1,0:T(8,128)(2,1)S(1)} collective-permute-done((bf16[128,768]{1,0:T(8,128)(2,1)S(1)}, bf16[128,768]{1,0:T(8,128)(2,1)S(1)}, u32[]{:S(2)}, u32[]{:S(2)}) %collective-permute-start.16) | collective-permute-done | bytes 196640 | tf_op jit(solution)/shard_map/ppermute | solution.py:50
  74.3 0.5 multiply_convert_fusion.1
  74.9 0.3 convolution_convert_fusion
  75.2 0.1 collective-permute-start.18
  75.3 0.8 fusion.2.gate_back_ref
  76.1 0.6 collective-permute-done.18
  76.7 1.4 %collective-permute-start.19 = (bf16[32,1536]{1,0:T(8,128)(2,1)S(1)}, bf16[32,1536]{1,0:T(8,128)(2,1)S(1)}, u32[]{:S(2)}, u32[]{:S(2)}) collective-permute-start(bf16[32,1536]{1,0:T(8,128)(2,1)S(1)} %pad_maximum_fusion.12), channel_id=1, source_target_pairs={{0,8},{4,12},{8,0},{12,4},{16,24},{20,28},{24,16},{28,20},{1,9},{5... | collective-permute-start | bytes 294920 | tf_op jit(solution)/shard_map/ppermute | solution.py:38
  78.2 0.8 collective-permute-start.20
  78.9 1.5 %collective-permute-start.21 = (bf16[32,1536]{1,0:T(8,128)(2,1)S(1)}, bf16[32,1536]{1,0:T(8,128)(2,1)S(1)}, u32[]{:S(2)}, u32[]{:S(2)}) collective-permute-start(bf16[32,1536]{1,0:T(8,128)(2,1)S(1)} %pad_maximum_fusion.14), channel_id=1, source_target_pairs={{0,24},{4,28},{8,16},{12,20},{16,8},{20,12},{24,0},{28,4},{1,25},{... | collective-permute-start | bytes 294920 | tf_op jit(solution)/shard_map/ppermute | solution.py:38
  80.4 1.3 %keep.5 = (bf16[128,1536]{1,0:T(8,128)(2,1)S(1)}, f32[128,128]{1,0:T(8,128)S(1)}, f32[2,64,64]{2,1,0:T(8,128)}) custom-call(bf16[32,1536]{1,0:T(8,128)(2,1)S(1)} %pad_maximum_fusion.15.after_ref, bf16[128,1536]{1,0:T(8,128)(2,1)S(1)} %get-tuple-element.50.normed_ref, bf16[128,1536]{1,0:T(8,128)(2,1)S(1)} %get-tuple-element.51.moved_ref, ...), custom_call_target="tpu_custom_call" | custom-call | tf_op jit(solution)/shard_map/keep/pallas_call | solution.py:383
  81.7 3.2 %collective-permute-done.20 = bf16[32,1536]{1,0:T(8,128)(2,1)S(1)} collective-permute-done((bf16[32,1536]{1,0:T(8,128)(2,1)S(1)}, bf16[32,1536]{1,0:T(8,128)(2,1)S(1)}, u32[]{:S(2)}, u32[]{:S(2)}) %collective-permute-start.20) | collective-permute-done | bytes 98336 | tf_op jit(solution)/shard_map/ppermute | solution.py:38
  85.0 1.6 %close.1 = (bf16[128,1536]{1,0:T(8,128)(2,1)}, f32[2,64,64]{2,1,0:T(8,128)}) custom-call(bf16[128,1536]{1,0:T(8,128)(2,1)S(1)} %constant_dynamic-update-slice_fusion.10.mid_ref, bf16[128,128]{1,0:T(8,128)(2,1)S(1)} %get-tuple-element.40.refs_5_.first_recv_ref, f32[128,1536]{1,0:T(8,128)S(1)} %fusion.2.gate_back_ref, f32[1,1536]{1,0:T(1,128)S(1)} %copy-done.2, ...), custom_call_target="tpu_custom_call" | custom-call | tf_op jit(solution)/shard_map/close/pallas_call | solution.py:383
  (43 shorter events, 0.4 us)
Async XLA Ops:
  4.2 1.9 %collective-permute-start = (bf16[128,1536]{1,0:T(8,128)(2,1)S(1)}, bf16[128,1536]{1,0:T(8,128)(2,1)S(1)}, u32[]{:S(2)}, u32[]{:S(2)}) collective-permute-start(bf16[128,1536]{1,0:T(8,128)(2,1)S(1)} %get-tuple-element.38), channel_id=1, source_target_pairs={{0,4},{4,0},{8,12},{12,8},{16,20},{20,16},{24,28},{28,24},{1,5},{5... | collective-permute-start | bytes 1179656 | tf_op jit(solution)/shard_map/ppermute | solution.py:38
  6.1 9.1 %collective-permute-start.1 = (bf16[64,1536]{1,0:T(8,128)(2,1)S(1)}, bf16[64,1536]{1,0:T(8,128)(2,1)S(1)}, u32[]{:S(2)}, u32[]{:S(2)}) collective-permute-start(bf16[64,1536]{1,0:T(8,128)(2,1)S(1)} %pad_maximum_fusion.1), channel_id=1, source_target_pairs={{0,8},{4,12},{8,0},{12,4},{16,24},{20,28},{24,16},{28,20},{1,9},{5... | collective-permute-start | bytes 589832 | tf_op jit(solution)/shard_map/ppermute | solution.py:38
  9.0 10.9 %collective-permute-start.2 = (bf16[64,1536]{1,0:T(8,128)(2,1)S(1)}, bf16[64,1536]{1,0:T(8,128)(2,1)S(1)}, u32[]{:S(2)}, u32[]{:S(2)}) collective-permute-start(bf16[64,1536]{1,0:T(8,128)(2,1)S(1)} %pad_maximum_fusion.2), channel_id=1, source_target_pairs={{0,16},{4,20},{8,24},{12,28},{16,0},{20,4},{24,8},{28,12},{1,17},{... | collective-permute-start | bytes 589832 | tf_op jit(solution)/shard_map/ppermute | solution.py:38
  10.6 9.4 %collective-permute-start.3 = (bf16[64,1536]{1,0:T(8,128)(2,1)S(1)}, bf16[64,1536]{1,0:T(8,128)(2,1)S(1)}, u32[]{:S(2)}, u32[]{:S(2)}) collective-permute-start(bf16[64,1536]{1,0:T(8,128)(2,1)S(1)} %pad_maximum_fusion.3), channel_id=1, source_target_pairs={{0,24},{4,28},{8,16},{12,20},{16,8},{20,12},{24,0},{28,4},{1,25},{... | collective-permute-start | bytes 589832 | tf_op jit(solution)/shard_map/ppermute | solution.py:38
  10.7 9.3 %copy-start = (bf16[1,128,1536]{2,1,0:T(8,128)(2,1)S(1)}, bf16[1,128,1536]{2,1,0:T(8,128)(2,1)}, u32[]{:S(2)}) copy-start(bf16[1,128,1536]{2,1,0:T(8,128)(2,1)} %param.7) | copy-start | bytes 1179652
  10.7 9.2 %copy-start.1 = (bf16[128,1536]{1,0:T(8,128)(2,1)S(1)}, bf16[128,1536]{1,0:T(8,128)(2,1)}, u32[]{:S(2)}) copy-start(bf16[128,1536]{1,0:T(8,128)(2,1)} %refs_12_.1) | copy-start | bytes 1179652
  10.8 9.2 %copy-start.2 = (f32[1,1536]{1,0:T(1,128)S(1)}, f32[1,1536]{1,0:T(1,128)}, u32[]{:S(2)}) copy-start(f32[1,1536]{1,0:T(1,128)} %gain_ref.5) | copy-start | bytes 18436
  21.2 1.5 %collective-permute-start.5 = (bf16[128,768]{1,0:T(8,128)(2,1)S(1)}, bf16[128,768]{1,0:T(8,128)(2,1)S(1)}, u32[]{:S(2)}, u32[]{:S(2)}) collective-permute-start(bf16[128,768]{1,0:T(8,128)(2,1)S(1)} %get-tuple-element.47.refs_1_), channel_id=1, source_target_pairs={{0,4},{1,5},{2,3},{3,2},{4,0},{5,1},{6,7},{7,6},{8,12},{9,13},{10,... | collective-permute-start | bytes 589832 | tf_op jit(solution)/shard_map/ppermute | solution.py:50
  21.3 1.9 %collective-permute-start.4 = (bf16[128,768]{1,0:T(8,128)(2,1)S(1)}, bf16[128,768]{1,0:T(8,128)(2,1)S(1)}, u32[]{:S(2)}, u32[]{:S(2)}) collective-permute-start(bf16[128,768]{1,0:T(8,128)(2,1)S(1)} %get-tuple-element.45.refs_0_), channel_id=1, source_target_pairs={{0,4},{1,5},{2,3},{3,2},{4,0},{5,1},{6,7},{7,6},{8,12},{9,13},{10,... | collective-permute-start | bytes 589832 | tf_op jit(solution)/shard_map/ppermute | solution.py:50
  24.0 1.5 %collective-permute-start.6 = (bf16[64,1536]{1,0:T(8,128)(2,1)S(1)}, bf16[64,1536]{1,0:T(8,128)(2,1)S(1)}, u32[]{:S(2)}, u32[]{:S(2)}) collective-permute-start(bf16[64,1536]{1,0:T(8,128)(2,1)S(1)} %split.15), channel_id=1, source_target_pairs={{0,4},{4,0},{8,12},{12,8},{16,20},{20,16},{24,28},{28,24},{1,5},{5... | collective-permute-start | bytes 589832 | tf_op jit(solution)/shard_map/ppermute | solution.py:38
  25.6 4.9 %collective-permute-start.7 = (bf16[32,1536]{1,0:T(8,128)(2,1)S(1)}, bf16[32,1536]{1,0:T(8,128)(2,1)S(1)}, u32[]{:S(2)}, u32[]{:S(2)}) collective-permute-start(bf16[32,1536]{1,0:T(8,128)(2,1)S(1)} %pad_maximum_fusion.5), channel_id=1, source_target_pairs={{0,8},{4,12},{8,0},{12,4},{16,24},{20,28},{24,16},{28,20},{1,9},{5... | collective-permute-start | bytes 294920 | tf_op jit(solution)/shard_map/ppermute | solution.py:38
  26.8 5.5 %collective-permute-start.8 = (bf16[32,1536]{1,0:T(8,128)(2,1)S(1)}, bf16[32,1536]{1,0:T(8,128)(2,1)S(1)}, u32[]{:S(2)}, u32[]{:S(2)}) collective-permute-start(bf16[32,1536]{1,0:T(8,128)(2,1)S(1)} %pad_maximum_fusion.6), channel_id=1, source_target_pairs={{0,16},{4,20},{8,24},{12,28},{16,0},{20,4},{24,8},{28,12},{1,17},{... | collective-permute-start | bytes 294920 | tf_op jit(solution)/shard_map/ppermute | solution.py:38
  27.8 5.8 %collective-permute-start.9 = (bf16[32,1536]{1,0:T(8,128)(2,1)S(1)}, bf16[32,1536]{1,0:T(8,128)(2,1)S(1)}, u32[]{:S(2)}, u32[]{:S(2)}) collective-permute-start(bf16[32,1536]{1,0:T(8,128)(2,1)S(1)} %pad_maximum_fusion.7), channel_id=1, source_target_pairs={{0,24},{4,28},{8,16},{12,20},{16,8},{20,12},{24,0},{28,4},{1,25},{... | collective-permute-start | bytes 294920 | tf_op jit(solution)/shard_map/ppermute | solution.py:38
  34.1 1.5 %collective-permute-start.11 = (bf16[128,768]{1,0:T(8,128)(2,1)S(1)}, bf16[128,768]{1,0:T(8,128)(2,1)S(1)}, u32[]{:S(2)}, u32[]{:S(2)}) collective-permute-start(bf16[128,768]{1,0:T(8,128)(2,1)S(1)} %get-tuple-element.56.refs_1_), channel_id=1, source_target_pairs={{0,4},{1,2},{2,1},{3,7},{4,0},{5,6},{6,5},{7,3},{8,12},{9,10},{10,... | collective-permute-start | bytes 589832 | tf_op jit(solution)/shard_map/ppermute | solution.py:50
  34.1 1.9 %collective-permute-start.10 = (bf16[128,768]{1,0:T(8,128)(2,1)S(1)}, bf16[128,768]{1,0:T(8,128)(2,1)S(1)}, u32[]{:S(2)}, u32[]{:S(2)}) collective-permute-start(bf16[128,768]{1,0:T(8,128)(2,1)S(1)} %get-tuple-element.55.refs_0_), channel_id=1, source_target_pairs={{0,4},{1,2},{2,1},{3,7},{4,0},{5,6},{6,5},{7,3},{8,12},{9,10},{10,... | collective-permute-start | bytes 589832 | tf_op jit(solution)/shard_map/ppermute | solution.py:50
  36.9 1.5 %collective-permute-start.12 = (bf16[64,1536]{1,0:T(8,128)(2,1)S(1)}, bf16[64,1536]{1,0:T(8,128)(2,1)S(1)}, u32[]{:S(2)}, u32[]{:S(2)}) collective-permute-start(bf16[64,1536]{1,0:T(8,128)(2,1)S(1)} %split.16), channel_id=1, source_target_pairs={{0,4},{4,0},{8,12},{12,8},{16,20},{20,16},{24,28},{28,24},{1,5},{5... | collective-permute-start | bytes 589832 | tf_op jit(solution)/shard_map/ppermute | solution.py:38
  38.4 4.9 %collective-permute-start.13 = (bf16[32,1536]{1,0:T(8,128)(2,1)S(1)}, bf16[32,1536]{1,0:T(8,128)(2,1)S(1)}, u32[]{:S(2)}, u32[]{:S(2)}) collective-permute-start(bf16[32,1536]{1,0:T(8,128)(2,1)S(1)} %pad_maximum_fusion.9), channel_id=1, source_target_pairs={{0,8},{4,12},{8,0},{12,4},{16,24},{20,28},{24,16},{28,20},{1,9},{5... | collective-permute-start | bytes 294920 | tf_op jit(solution)/shard_map/ppermute | solution.py:38
  39.8 5.7 %collective-permute-start.14 = (bf16[32,1536]{1,0:T(8,128)(2,1)S(1)}, bf16[32,1536]{1,0:T(8,128)(2,1)S(1)}, u32[]{:S(2)}, u32[]{:S(2)}) collective-permute-start(bf16[32,1536]{1,0:T(8,128)(2,1)S(1)} %pad_maximum_fusion.10), channel_id=1, source_target_pairs={{0,16},{4,20},{8,24},{12,28},{16,0},{20,4},{24,8},{28,12},{1,17},{... | collective-permute-start | bytes 294920 | tf_op jit(solution)/shard_map/ppermute | solution.py:38
  41.0 5.6 %collective-permute-start.15 = (bf16[32,1536]{1,0:T(8,128)(2,1)S(1)}, bf16[32,1536]{1,0:T(8,128)(2,1)S(1)}, u32[]{:S(2)}, u32[]{:S(2)}) collective-permute-start(bf16[32,1536]{1,0:T(8,128)(2,1)S(1)} %pad_maximum_fusion.11), channel_id=1, source_target_pairs={{0,24},{4,28},{8,16},{12,20},{16,8},{20,12},{24,0},{28,4},{1,25},{... | collective-permute-start | bytes 294920 | tf_op jit(solution)/shard_map/ppermute | solution.py:38
  47.1 25.2 %collective-permute-start.17 = (bf16[128,768]{1,0:T(8,128)(2,1)S(1)}, bf16[128,768]{1,0:T(8,128)(2,1)S(1)}, u32[]{:S(2)}, u32[]{:S(2)}) collective-permute-start(bf16[128,768]{1,0:T(8,128)(2,1)S(1)} %get-tuple-element.61.refs_1_), channel_id=1, source_target_pairs={{0,1},{1,0},{2,6},{3,7},{4,5},{5,4},{6,2},{7,3},{8,9},{9,8},{10,14... | collective-permute-start | bytes 589832 | tf_op jit(solution)/shard_map/ppermute | solution.py:50
  66.6 7.8 %collective-permute-start.16 = (bf16[128,768]{1,0:T(8,128)(2,1)S(1)}, bf16[128,768]{1,0:T(8,128)(2,1)S(1)}, u32[]{:S(2)}, u32[]{:S(2)}) collective-permute-start(bf16[128,768]{1,0:T(8,128)(2,1)S(1)} %get-tuple-element.60.refs_0_), channel_id=1, source_target_pairs={{0,1},{1,0},{2,6},{3,7},{4,5},{5,4},{6,2},{7,3},{8,9},{9,8},{10,14... | collective-permute-start | bytes 589832 | tf_op jit(solution)/shard_map/ppermute | solution.py:50
  75.2 1.5 %collective-permute-start.18 = (bf16[64,1536]{1,0:T(8,128)(2,1)S(1)}, bf16[64,1536]{1,0:T(8,128)(2,1)S(1)}, u32[]{:S(2)}, u32[]{:S(2)}) collective-permute-start(bf16[64,1536]{1,0:T(8,128)(2,1)S(1)} %split.17), channel_id=1, source_target_pairs={{0,4},{4,0},{8,12},{12,8},{16,20},{20,16},{24,28},{28,24},{1,5},{5... | collective-permute-start | bytes 589832 | tf_op jit(solution)/shard_map/ppermute | solution.py:38
  76.7 5.0 %collective-permute-start.19 = (bf16[32,1536]{1,0:T(8,128)(2,1)S(1)}, bf16[32,1536]{1,0:T(8,128)(2,1)S(1)}, u32[]{:S(2)}, u32[]{:S(2)}) collective-permute-start(bf16[32,1536]{1,0:T(8,128)(2,1)S(1)} %pad_maximum_fusion.12), channel_id=1, source_target_pairs={{0,8},{4,12},{8,0},{12,4},{16,24},{20,28},{24,16},{28,20},{1,9},{5... | collective-permute-start | bytes 294920 | tf_op jit(solution)/shard_map/ppermute | solution.py:38
  78.2 6.8 %collective-permute-start.20 = (bf16[32,1536]{1,0:T(8,128)(2,1)S(1)}, bf16[32,1536]{1,0:T(8,128)(2,1)S(1)}, u32[]{:S(2)}, u32[]{:S(2)}) collective-permute-start(bf16[32,1536]{1,0:T(8,128)(2,1)S(1)} %pad_maximum_fusion.13), channel_id=1, source_target_pairs={{0,16},{4,20},{8,24},{12,28},{16,0},{20,4},{24,8},{28,12},{1,17},{... | collective-permute-start | bytes 294920 | tf_op jit(solution)/shard_map/ppermute | solution.py:38
  78.9 6.0 %collective-permute-start.21 = (bf16[32,1536]{1,0:T(8,128)(2,1)S(1)}, bf16[32,1536]{1,0:T(8,128)(2,1)S(1)}, u32[]{:S(2)}, u32[]{:S(2)}) collective-permute-start(bf16[32,1536]{1,0:T(8,128)(2,1)S(1)} %pad_maximum_fusion.14), channel_id=1, source_target_pairs={{0,24},{4,28},{8,16},{12,20},{16,8},{20,12},{24,0},{28,4},{1,25},{... | collective-permute-start | bytes 294920 | tf_op jit(solution)/shard_map/ppermute | solution.py:38

commit v8 on v7

--- a/solution.py
+++ b/solution.py
@@ -52,6 +52,11 @@
 
 def chunks(size, count):
     return [slice(i * size // count, (i + 1) * size // count) for i in range(count)]
+
+
+def column_parts(width):
+    cut = width // 3 // 128 * 128
+    return [slice(0, cut), slice(cut, width)]
 
 
 def log2(size):
@@ -186,10 +191,9 @@
         copies[5].wait()
         for columns, copy in zip(parts, copies[6:]):
             copy.wait()
-            hidden = dot_rows(incoming_ref[...], out_ref[columns])
-            hidden_ref[:, columns] = hidden
-            mix = (hidden * mix_factor_ref[:, columns]).astype(jnp.bfloat16)
-            place(rounded(second_send_ref[...], mix), 1, columns)
+            hidden_ref[:, columns] = dot_rows(incoming_ref[...], out_ref[columns])
+        mix = (hidden_ref[...] * mix_factor_ref[...]).astype(jnp.bfloat16)
+        place(rounded(second_send_ref[...], mix), 1, slice(None))
 
     @pl.when(jnp.logical_not(active))
     def _():
@@ -227,18 +231,20 @@
             work.append((copy, held, rows, [gate_turned_ref] if i == 0 else out_turned_refs))
     for copy, held, rows, targets in work:
         copy.wait()
-        for target, columns in zip(targets, chunks(held.shape[1], len(targets))):
+        width = held.shape[1]
+        columns_of = column_parts(width) if len(targets) > 1 else [slice(0, width)]
+        for target, columns in zip(targets, columns_of):
             target[:, rows] = held[rows, columns].T
 
 
 def transposed(weight_gate, weight_out, after):
     height, width = weight_out.shape
-    half = pltpu.VMEM((width // HALVES, height), jnp.bfloat16)
+    parts = [pltpu.VMEM((c.stop - c.start, height), jnp.bfloat16) for c in column_parts(width)]
     return pl.pallas_call(
         transpose_kernel,
         in_specs=[ANYWHERE] * 3,
         out_specs=[WHOLE] * (1 + HALVES),
-        out_shape=[pltpu.VMEM(weight_gate.shape[::-1], jnp.bfloat16)] + [half] * HALVES,
+        out_shape=[pltpu.VMEM(weight_gate.shape[::-1], jnp.bfloat16)] + parts,
         scratch_shapes=[
             pltpu.VMEM(weight_gate.shape, weight_gate.dtype),
             pltpu.VMEM(weight_out.shape, weight_out.dtype),
@@ -254,7 +260,7 @@
 
 
 def store_halves(refs, value):
-    for ref, columns in zip(refs, chunks(value.shape[1], len(refs))):
+    for ref, columns in zip(refs, column_parts(value.shape[1])):
         ref[...] = value[:, columns]
 
 
@@ -290,12 +296,12 @@
     row_count, width = operands[-1].shape
     short = array_of((row_count, width), jnp.bfloat16)
     full = array_of((row_count, width), jnp.float32)
-    part = array_of((row_count, width // HALVES), jnp.bfloat16)
+    parts = [array_of((row_count, c.stop - c.start), jnp.bfloat16) for c in column_parts(width)]
     return pl.pallas_call(
         functools.partial(finish_kernel, order),
         in_specs=[WHOLE] * len(operands),
         out_specs=[WHOLE] * (3 + HALVES),
-        out_shape=[short, short, full] + [part] * HALVES,
+        out_shape=[short, short, full] + parts,
         compiler_params=granted(4),
         name="finish",
     )(*operands)

time: 86.7 us -> 86 us (level)
  no operation moved by 1% of the time
where the time goes in v8:
time: 86 us; the launch traced here: 85.9 us
  starting transfers between devices  36.6 us (43%)
  waiting for transfers between devices  28 us (33%)
  Pallas kernels  13.7 us (16%)
  matrix products  6.09 us (7%)
  between operations  1.04 us (1%)
    ppermute x6, starting transfers between devices, passed_down(): return lax.ppermute(block, ('seq', 'pipe'), pairs)  20 us
    ppermute x16, waiting for transfers between devices, swap(): return lax.ppermute(block, 'seq', [(i, i ^ offset) for i in range(count)])  18.8 us
    ppermute x16, starting transfers between devices, swap(): return lax.ppermute(block, 'seq', [(i, i ^ offset) for i in range(count)])  16.6 us
    ppermute x6, waiting for transfers between devices, passed_down(): return lax.ppermute(block, ('seq', 'pipe'), pairs)  9.19 us
    dot_general x12, matrix products, dot(): return jnp.dot(left, right, preferred_element_type=jnp.float32)  6.09 us
    pallas_call x1, Pallas kernels, transposed(): pl.pallas_call(transpose_kernel, in_specs=[ANYWHERE] * 3, out_specs=[WHOL...  4.41 us
    pallas_call x4, Pallas kernels, call(): pl.pallas_call(kernel, in_specs=[WHOLE] * len(operands), out_specs=[WHOLE...  3.63 us
    pallas_call x1, Pallas kernels, begin(): pl.pallas_call(functools.partial(begin_kernel, order), in_specs=[ANYWHERE...  3.53 us
  transfers between devices with their start and end apart: 22, of which 16 were waited for; matrix products, arithmetic and copies ran while one was open for 5% of the time, Pallas kernels for 8%

profile of v8, /device:TPU:0, one launch (start us, length us, event | category | flops | bytes accessed | tf_op | source)
XLA Modules:
  0.0 85.9 jit_solution(13507150650877810704)
XLA Ops:
  0.6 3.5 %begin.1 = (bf16[128,1536]{1,0:T(8,128)(2,1)S(1)}, f32[128,1]{1,0:T(8,128)S(1)}, bf16[128,128]{1,0:T(8,128)(2,1)S(1)}, bf16[128,128]{1,0:T(8,128)(2,1)S(1)}, bf1...) custom-call(bf16[128,1536]{1,0:T(8,128)(2,1)} %bitcast.29, ...), custom_call_target="tpu_custom_call" | custom-call | tf_op jit(solution)/shard_map/begin/pallas_call | solution.py:211
  4.2 0.5 collective-permute-start
  4.7 1.3 %collective-permute-done = bf16[128,1536]{1,0:T(8,128)(2,1)S(1)} collective-permute-done((bf16[128,1536]{1,0:T(8,128)(2,1)S(1)}, bf16[128,1536]{1,0:T(8,128)(2,1)S(1)}, u32[]{:S(2)}, u32[]{:S(2)}) %collective-permute-start) | collective-permute-done | bytes 393248 | tf_op jit(solution)/shard_map/ppermute | solution.py:38
  6.1 2.9 %collective-permute-start.1 = (bf16[64,1536]{1,0:T(8,128)(2,1)S(1)}, bf16[64,1536]{1,0:T(8,128)(2,1)S(1)}, u32[]{:S(2)}, u32[]{:S(2)}) collective-permute-start(bf16[64,1536]{1,0:T(8,128)(2,1)S(1)} %pad_maximum_fusion.1), channel_id=1, source_target_pairs={{0,8},{4,12},{8,0},{12,4},{16,24},{20,28},{24,16},{28,20},{1,9},{5... | collective-permute-start | bytes 589832 | tf_op jit(solution)/shard_map/ppermute | solution.py:38
  9.0 1.6 %collective-permute-start.2 = (bf16[64,1536]{1,0:T(8,128)(2,1)S(1)}, bf16[64,1536]{1,0:T(8,128)(2,1)S(1)}, u32[]{:S(2)}, u32[]{:S(2)}) collective-permute-start(bf16[64,1536]{1,0:T(8,128)(2,1)S(1)} %pad_maximum_fusion.2), channel_id=1, source_target_pairs={{0,16},{4,20},{8,24},{12,28},{16,0},{20,4},{24,8},{28,12},{1,17},{... | collective-permute-start | bytes 589832 | tf_op jit(solution)/shard_map/ppermute | solution.py:38
  10.6 0.1 collective-permute-start.3
  10.7 0.0 copy-start
  10.7 0.0 copy-start.1
  10.8 0.0 copy-start.2
  10.8 4.4 %transposed.1 = (bf16[1536,1536]{1,0:T(8,128)(2,1)S(1)}, bf16[512,1536]{1,0:T(8,128)(2,1)S(1)}, bf16[1024,1536]{1,0:T(8,128)(2,1)S(1)}) custom-call(bf16[1536,1536]{1,0:T(8,128)(2,1)} %bitcast.35, bf16[1536,1536]{1,0:T(8,128)(2,1)} %bitcast.37, bf16[64,1536]{1,0:T(8,128)(2,1)S(1)} %pad_maximum_fusion.after_ref.refs_0_), custom_call_target="tpu_custom_call" | custom-call | tf_op jit(solution)/shard_map/transposed/pallas_call | solution.py:243
  15.2 0.0 collective-permute-done.1.refs_1_
  15.2 4.8 %collective-permute-done.2.refs_2_ = bf16[64,1536]{1,0:T(8,128)(2,1)S(1)} collective-permute-done((bf16[64,1536]{1,0:T(8,128)(2,1)S(1)}, bf16[64,1536]{1,0:T(8,128)(2,1)S(1)}, u32[]{:S(2)}, u32[]{:S(2)}) %collective-permute-start.2) | collective-permute-done | bytes 196640 | tf_op jit(solution)/shard_map/ppermute | solution.py:38
  20.0 0.0 collective-permute-done.3.refs_3_
  20.0 1.2 %finish.1 = (bf16[128,1536]{1,0:T(8,128)(2,1)S(1)}, bf16[128,1536]{1,0:T(8,128)(2,1)S(1)}, f32[128,1536]{1,0:T(8,128)S(1)}, bf16[128,512]{1,0:T(8,128)(2,1)S(1)}, bf16[128,1024]{1,0:T(8,128)(2,1)S(1)}) custom-call(bf16[64,1536]{1,0:T(8,128)(2,1)S(1)} %pad_maximum_fusion.after_ref.refs_0_, bf16[64,1536]{1,0:T(8,128)(2,1)S(1)} %collective-permute-done.1.refs_1_, ...), custom_call_target="tpu_custom_call" | custom-call | tf_op jit(solution)/shard_map/finish/pallas_call | solution.py:300
  21.2 0.1 collective-permute-start.5
  21.3 0.5 collective-permute-start.4
  21.8 1.0 %collective-permute-done.5.refs_1_ = bf16[128,1024]{1,0:T(8,128)(2,1)S(1)} collective-permute-done((bf16[128,1024]{1,0:T(8,128)(2,1)S(1)}, bf16[128,1024]{1,0:T(8,128)(2,1)S(1)}, u32[]{:S(2)}, u32[]{:S(2)}) %collective-permute-start.5) | collective-permute-done | bytes 262176 | tf_op jit(solution)/shard_map/ppermute | solution.py:50
  22.8 0.6 fusion.11
  23.4 0.4 multiply_convert_fusion.5
  23.8 0.2 convolution_convert_fusion.2
  24.1 0.2 collective-permute-start.6
  24.3 0.8 fusion.gate_back_ref
  25.1 0.5 collective-permute-done.6
  25.7 1.2 %collective-permute-start.7 = (bf16[32,1536]{1,0:T(8,128)(2,1)S(1)}, bf16[32,1536]{1,0:T(8,128)(2,1)S(1)}, u32[]{:S(2)}, u32[]{:S(2)}) collective-permute-start(bf16[32,1536]{1,0:T(8,128)(2,1)S(1)} %pad_maximum_fusion.5), channel_id=1, source_target_pairs={{0,8},{4,12},{8,0},{12,4},{16,24},{20,28},{24,16},{28,20},{1,9},{5... | collective-permute-start | bytes 294920 | tf_op jit(solution)/shard_map/ppermute | solution.py:38
  26.9 1.0 %collective-permute-start.8 = (bf16[32,1536]{1,0:T(8,128)(2,1)S(1)}, bf16[32,1536]{1,0:T(8,128)(2,1)S(1)}, u32[]{:S(2)}, u32[]{:S(2)}) collective-permute-start(bf16[32,1536]{1,0:T(8,128)(2,1)S(1)} %pad_maximum_fusion.6), channel_id=1, source_target_pairs={{0,16},{4,20},{8,24},{12,28},{16,0},{20,4},{24,8},{28,12},{1,17},{... | collective-permute-start | bytes 294920 | tf_op jit(solution)/shard_map/ppermute | solution.py:38
  27.9 1.5 %collective-permute-start.9 = (bf16[32,1536]{1,0:T(8,128)(2,1)S(1)}, bf16[32,1536]{1,0:T(8,128)(2,1)S(1)}, u32[]{:S(2)}, u32[]{:S(2)}) collective-permute-start(bf16[32,1536]{1,0:T(8,128)(2,1)S(1)} %pad_maximum_fusion.7), channel_id=1, source_target_pairs={{0,24},{4,28},{8,16},{12,20},{16,8},{20,12},{24,0},{28,4},{1,25},{... | collective-permute-start | bytes 294920 | tf_op jit(solution)/shard_map/ppermute | solution.py:38
  29.4 0.4 keep.3
  29.8 0.8 collective-permute-done.7
  30.6 1.7 %collective-permute-done.8 = bf16[32,1536]{1,0:T(8,128)(2,1)S(1)} collective-permute-done((bf16[32,1536]{1,0:T(8,128)(2,1)S(1)}, bf16[32,1536]{1,0:T(8,128)(2,1)S(1)}, u32[]{:S(2)}, u32[]{:S(2)}) %collective-permute-start.8) | collective-permute-done | bytes 98336 | tf_op jit(solution)/shard_map/ppermute | solution.py:38
  32.3 1.3 %collective-permute-done.9 = bf16[32,1536]{1,0:T(8,128)(2,1)S(1)} collective-permute-done((bf16[32,1536]{1,0:T(8,128)(2,1)S(1)}, bf16[32,1536]{1,0:T(8,128)(2,1)S(1)}, u32[]{:S(2)}, u32[]{:S(2)}) %collective-permute-start.9) | collective-permute-done | bytes 98336 | tf_op jit(solution)/shard_map/ppermute | solution.py:38
  33.7 0.5 advance.2
  34.1 0.1 collective-permute-start.11
  34.2 0.5 collective-permute-start.10
  34.7 1.0 %collective-permute-done.11.refs_1_ = bf16[128,1024]{1,0:T(8,128)(2,1)S(1)} collective-permute-done((bf16[128,1024]{1,0:T(8,128)(2,1)S(1)}, bf16[128,1024]{1,0:T(8,128)(2,1)S(1)}, u32[]{:S(2)}, u32[]{:S(2)}) %collective-permute-start.11) | collective-permute-done | bytes 262176 | tf_op jit(solution)/shard_map/ppermute | solution.py:50
  35.8 0.6 fusion.12
  36.3 0.4 multiply_convert_fusion.3
  36.8 0.2 convolution_convert_fusion.1
  37.1 0.2 collective-permute-start.12
  37.3 0.8 fusion.1.gate_back_ref
  38.1 0.5 collective-permute-done.12
  38.6 1.3 %collective-permute-start.13 = (bf16[32,1536]{1,0:T(8,128)(2,1)S(1)}, bf16[32,1536]{1,0:T(8,128)(2,1)S(1)}, u32[]{:S(2)}, u32[]{:S(2)}) collective-permute-start(bf16[32,1536]{1,0:T(8,128)(2,1)S(1)} %pad_maximum_fusion.9), channel_id=1, source_target_pairs={{0,8},{4,12},{8,0},{12,4},{16,24},{20,28},{24,16},{28,20},{1,9},{5... | collective-permute-start | bytes 294920 | tf_op jit(solution)/shard_map/ppermute | solution.py:38
  40.0 1.2 %collective-permute-start.14 = (bf16[32,1536]{1,0:T(8,128)(2,1)S(1)}, bf16[32,1536]{1,0:T(8,128)(2,1)S(1)}, u32[]{:S(2)}, u32[]{:S(2)}) collective-permute-start(bf16[32,1536]{1,0:T(8,128)(2,1)S(1)} %pad_maximum_fusion.10), channel_id=1, source_target_pairs={{0,16},{4,20},{8,24},{12,28},{16,0},{20,4},{24,8},{28,12},{1,17},{... | collective-permute-start | bytes 294920 | tf_op jit(solution)/shard_map/ppermute | solution.py:38
  41.2 1.1 %collective-permute-start.15 = (bf16[32,1536]{1,0:T(8,128)(2,1)S(1)}, bf16[32,1536]{1,0:T(8,128)(2,1)S(1)}, u32[]{:S(2)}, u32[]{:S(2)}) collective-permute-start(bf16[32,1536]{1,0:T(8,128)(2,1)S(1)} %pad_maximum_fusion.11), channel_id=1, source_target_pairs={{0,24},{4,28},{8,16},{12,20},{16,8},{20,12},{24,0},{28,4},{1,25},{... | collective-permute-start | bytes 294920 | tf_op jit(solution)/shard_map/ppermute | solution.py:38
  42.3 0.4 keep.4
  42.7 0.8 collective-permute-done.13
  43.5 2.2 %collective-permute-done.14 = bf16[32,1536]{1,0:T(8,128)(2,1)S(1)} collective-permute-done((bf16[32,1536]{1,0:T(8,128)(2,1)S(1)}, bf16[32,1536]{1,0:T(8,128)(2,1)S(1)}, u32[]{:S(2)}, u32[]{:S(2)}) %collective-permute-start.14) | collective-permute-done | bytes 98336 | tf_op jit(solution)/shard_map/ppermute | solution.py:38
  45.7 1.1 %collective-permute-done.15 = bf16[32,1536]{1,0:T(8,128)(2,1)S(1)} collective-permute-done((bf16[32,1536]{1,0:T(8,128)(2,1)S(1)}, bf16[32,1536]{1,0:T(8,128)(2,1)S(1)}, u32[]{:S(2)}, u32[]{:S(2)}) %collective-permute-start.15) | collective-permute-done | bytes 98336 | tf_op jit(solution)/shard_map/ppermute | solution.py:38
  46.8 0.5 advance.3
  47.2 18.8 %collective-permute-start.17 = (bf16[128,1024]{1,0:T(8,128)(2,1)S(1)}, bf16[128,1024]{1,0:T(8,128)(2,1)S(1)}, u32[]{:S(2)}, u32[]{:S(2)}) collective-permute-start(bf16[128,1024]{1,0:T(8,128)(2,1)S(1)} %get-tuple-element.61.refs_1_), channel_id=1, source_target_pairs={{0,1},{1,0},{2,6},{3,7},{4,5},{5,4},{6,2},{7,3},{8,9},{9,8},{10,14... | collective-permute-start | bytes 786440 | tf_op jit(solution)/shard_map/ppermute | solution.py:50
  66.0 0.1 collective-permute-start.16
  66.1 6.3 %collective-permute-done.17.refs_1_ = bf16[128,1024]{1,0:T(8,128)(2,1)S(1)} collective-permute-done((bf16[128,1024]{1,0:T(8,128)(2,1)S(1)}, bf16[128,1024]{1,0:T(8,128)(2,1)S(1)}, u32[]{:S(2)}, u32[]{:S(2)}) %collective-permute-start.17) | collective-permute-done | bytes 262176 | tf_op jit(solution)/shard_map/ppermute | solution.py:50
  72.4 0.6 fusion.13
  73.0 0.8 collective-permute-done.16.refs_0_
  73.8 0.4 multiply_convert_fusion.1
  74.2 0.2 convolution_convert_fusion
  74.5 0.1 collective-permute-start.18
  74.6 0.8 fusion.2.gate_back_ref
  75.4 0.6 collective-permute-done.18
  76.1 1.4 %collective-permute-start.19 = (bf16[32,1536]{1,0:T(8,128)(2,1)S(1)}, bf16[32,1536]{1,0:T(8,128)(2,1)S(1)}, u32[]{:S(2)}, u32[]{:S(2)}) collective-permute-start(bf16[32,1536]{1,0:T(8,128)(2,1)S(1)} %pad_maximum_fusion.12), channel_id=1, source_target_pairs={{0,8},{4,12},{8,0},{12,4},{16,24},{20,28},{24,16},{28,20},{1,9},{5... | collective-permute-start | bytes 294920 | tf_op jit(solution)/shard_map/ppermute | solution.py:38
  77.5 0.8 collective-permute-start.20
  78.3 1.5 %collective-permute-start.21 = (bf16[32,1536]{1,0:T(8,128)(2,1)S(1)}, bf16[32,1536]{1,0:T(8,128)(2,1)S(1)}, u32[]{:S(2)}, u32[]{:S(2)}) collective-permute-start(bf16[32,1536]{1,0:T(8,128)(2,1)S(1)} %pad_maximum_fusion.14), channel_id=1, source_target_pairs={{0,24},{4,28},{8,16},{12,20},{16,8},{20,12},{24,0},{28,4},{1,25},{... | collective-permute-start | bytes 294920 | tf_op jit(solution)/shard_map/ppermute | solution.py:38
  79.8 1.3 %keep.5 = (bf16[128,1536]{1,0:T(8,128)(2,1)S(1)}, f32[128,128]{1,0:T(8,128)S(1)}, f32[2,64,64]{2,1,0:T(8,128)}) custom-call(bf16[32,1536]{1,0:T(8,128)(2,1)S(1)} %pad_maximum_fusion.15.after_ref, bf16[128,1536]{1,0:T(8,128)(2,1)S(1)} %get-tuple-element.50.normed_ref, bf16[128,1536]{1,0:T(8,128)(2,1)S(1)} %get-tuple-element.51.moved_ref, ...), custom_call_target="tpu_custom_call" | custom-call | tf_op jit(solution)/shard_map/keep/pallas_call | solution.py:389
  81.1 3.2 %collective-permute-done.20 = bf16[32,1536]{1,0:T(8,128)(2,1)S(1)} collective-permute-done((bf16[32,1536]{1,0:T(8,128)(2,1)S(1)}, bf16[32,1536]{1,0:T(8,128)(2,1)S(1)}, u32[]{:S(2)}, u32[]{:S(2)}) %collective-permute-start.20) | collective-permute-done | bytes 98336 | tf_op jit(solution)/shard_map/ppermute | solution.py:38
  84.3 1.6 %close.1 = (bf16[128,1536]{1,0:T(8,128)(2,1)}, f32[2,64,64]{2,1,0:T(8,128)}) custom-call(bf16[128,1536]{1,0:T(8,128)(2,1)S(1)} %constant_dynamic-update-slice_fusion.10.mid_ref, bf16[128,128]{1,0:T(8,128)(2,1)S(1)} %get-tuple-element.40.refs_5_.first_recv_ref, f32[128,1536]{1,0:T(8,128)S(1)} %fusion.2.gate_back_ref, f32[1,1536]{1,0:T(1,128)S(1)} %copy-done.2, ...), custom_call_target="tpu_custom_call" | custom-call | tf_op jit(solution)/shard_map/close/pallas_call | solution.py:389
  (43 shorter events, 0.4 us)
Async XLA Ops:
  4.2 1.9 %collective-permute-start = (bf16[128,1536]{1,0:T(8,128)(2,1)S(1)}, bf16[128,1536]{1,0:T(8,128)(2,1)S(1)}, u32[]{:S(2)}, u32[]{:S(2)}) collective-permute-start(bf16[128,1536]{1,0:T(8,128)(2,1)S(1)} %get-tuple-element.38), channel_id=1, source_target_pairs={{0,4},{4,0},{8,12},{12,8},{16,20},{20,16},{24,28},{28,24},{1,5},{5... | collective-permute-start | bytes 1179656 | tf_op jit(solution)/shard_map/ppermute | solution.py:38
  6.1 9.1 %collective-permute-start.1 = (bf16[64,1536]{1,0:T(8,128)(2,1)S(1)}, bf16[64,1536]{1,0:T(8,128)(2,1)S(1)}, u32[]{:S(2)}, u32[]{:S(2)}) collective-permute-start(bf16[64,1536]{1,0:T(8,128)(2,1)S(1)} %pad_maximum_fusion.1), channel_id=1, source_target_pairs={{0,8},{4,12},{8,0},{12,4},{16,24},{20,28},{24,16},{28,20},{1,9},{5... | collective-permute-start | bytes 589832 | tf_op jit(solution)/shard_map/ppermute | solution.py:38
  9.0 10.9 %collective-permute-start.2 = (bf16[64,1536]{1,0:T(8,128)(2,1)S(1)}, bf16[64,1536]{1,0:T(8,128)(2,1)S(1)}, u32[]{:S(2)}, u32[]{:S(2)}) collective-permute-start(bf16[64,1536]{1,0:T(8,128)(2,1)S(1)} %pad_maximum_fusion.2), channel_id=1, source_target_pairs={{0,16},{4,20},{8,24},{12,28},{16,0},{20,4},{24,8},{28,12},{1,17},{... | collective-permute-start | bytes 589832 | tf_op jit(solution)/shard_map/ppermute | solution.py:38
  10.6 9.4 %collective-permute-start.3 = (bf16[64,1536]{1,0:T(8,128)(2,1)S(1)}, bf16[64,1536]{1,0:T(8,128)(2,1)S(1)}, u32[]{:S(2)}, u32[]{:S(2)}) collective-permute-start(bf16[64,1536]{1,0:T(8,128)(2,1)S(1)} %pad_maximum_fusion.3), channel_id=1, source_target_pairs={{0,24},{4,28},{8,16},{12,20},{16,8},{20,12},{24,0},{28,4},{1,25},{... | collective-permute-start | bytes 589832 | tf_op jit(solution)/shard_map/ppermute | solution.py:38
  10.7 9.3 %copy-start = (bf16[1,128,1536]{2,1,0:T(8,128)(2,1)S(1)}, bf16[1,128,1536]{2,1,0:T(8,128)(2,1)}, u32[]{:S(2)}) copy-start(bf16[1,128,1536]{2,1,0:T(8,128)(2,1)} %param.7) | copy-start | bytes 1179652
  10.7 9.2 %copy-start.1 = (bf16[128,1536]{1,0:T(8,128)(2,1)S(1)}, bf16[128,1536]{1,0:T(8,128)(2,1)}, u32[]{:S(2)}) copy-start(bf16[128,1536]{1,0:T(8,128)(2,1)} %refs_12_.1) | copy-start | bytes 1179652
  10.8 9.2 %copy-start.2 = (f32[1,1536]{1,0:T(1,128)S(1)}, f32[1,1536]{1,0:T(1,128)}, u32[]{:S(2)}) copy-start(f32[1,1536]{1,0:T(1,128)} %gain_ref.5) | copy-start | bytes 18436
  21.2 1.6 %collective-permute-start.5 = (bf16[128,1024]{1,0:T(8,128)(2,1)S(1)}, bf16[128,1024]{1,0:T(8,128)(2,1)S(1)}, u32[]{:S(2)}, u32[]{:S(2)}) collective-permute-start(bf16[128,1024]{1,0:T(8,128)(2,1)S(1)} %get-tuple-element.47.refs_1_), channel_id=1, source_target_pairs={{0,4},{1,5},{2,3},{3,2},{4,0},{5,1},{6,7},{7,6},{8,12},{9,13},{10,... | collective-permute-start | bytes 786440 | tf_op jit(solution)/shard_map/ppermute | solution.py:50
  21.3 2.1 %collective-permute-start.4 = (bf16[128,512]{1,0:T(8,128)(2,1)S(1)}, bf16[128,512]{1,0:T(8,128)(2,1)S(1)}, u32[]{:S(2)}, u32[]{:S(2)}) collective-permute-start(bf16[128,512]{1,0:T(8,128)(2,1)S(1)} %get-tuple-element.45.refs_0_), channel_id=1, source_target_pairs={{0,4},{1,5},{2,3},{3,2},{4,0},{5,1},{6,7},{7,6},{8,12},{9,13},{10,... | collective-permute-start | bytes 393224 | tf_op jit(solution)/shard_map/ppermute | solution.py:50
  24.1 1.5 %collective-permute-start.6 = (bf16[64,1536]{1,0:T(8,128)(2,1)S(1)}, bf16[64,1536]{1,0:T(8,128)(2,1)S(1)}, u32[]{:S(2)}, u32[]{:S(2)}) collective-permute-start(bf16[64,1536]{1,0:T(8,128)(2,1)S(1)} %split.15), channel_id=1, source_target_pairs={{0,4},{4,0},{8,12},{12,8},{16,20},{20,16},{24,28},{28,24},{1,5},{5... | collective-permute-start | bytes 589832 | tf_op jit(solution)/shard_map/ppermute | solution.py:38
  25.7 4.9 %collective-permute-start.7 = (bf16[32,1536]{1,0:T(8,128)(2,1)S(1)}, bf16[32,1536]{1,0:T(8,128)(2,1)S(1)}, u32[]{:S(2)}, u32[]{:S(2)}) collective-permute-start(bf16[32,1536]{1,0:T(8,128)(2,1)S(1)} %pad_maximum_fusion.5), channel_id=1, source_target_pairs={{0,8},{4,12},{8,0},{12,4},{16,24},{20,28},{24,16},{28,20},{1,9},{5... | collective-permute-start | bytes 294920 | tf_op jit(solution)/shard_map/ppermute | solution.py:38
  26.9 5.4 %collective-permute-start.8 = (bf16[32,1536]{1,0:T(8,128)(2,1)S(1)}, bf16[32,1536]{1,0:T(8,128)(2,1)S(1)}, u32[]{:S(2)}, u32[]{:S(2)}) collective-permute-start(bf16[32,1536]{1,0:T(8,128)(2,1)S(1)} %pad_maximum_fusion.6), channel_id=1, source_target_pairs={{0,16},{4,20},{8,24},{12,28},{16,0},{20,4},{24,8},{28,12},{1,17},{... | collective-permute-start | bytes 294920 | tf_op jit(solution)/shard_map/ppermute | solution.py:38
  27.9 5.8 %collective-permute-start.9 = (bf16[32,1536]{1,0:T(8,128)(2,1)S(1)}, bf16[32,1536]{1,0:T(8,128)(2,1)S(1)}, u32[]{:S(2)}, u32[]{:S(2)}) collective-permute-start(bf16[32,1536]{1,0:T(8,128)(2,1)S(1)} %pad_maximum_fusion.7), channel_id=1, source_target_pairs={{0,24},{4,28},{8,16},{12,20},{16,8},{20,12},{24,0},{28,4},{1,25},{... | collective-permute-start | bytes 294920 | tf_op jit(solution)/shard_map/ppermute | solution.py:38
  34.1 1.6 %collective-permute-start.11 = (bf16[128,1024]{1,0:T(8,128)(2,1)S(1)}, bf16[128,1024]{1,0:T(8,128)(2,1)S(1)}, u32[]{:S(2)}, u32[]{:S(2)}) collective-permute-start(bf16[128,1024]{1,0:T(8,128)(2,1)S(1)} %get-tuple-element.56.refs_1_), channel_id=1, source_target_pairs={{0,4},{1,2},{2,1},{3,7},{4,0},{5,6},{6,5},{7,3},{8,12},{9,10},{10,... | collective-permute-start | bytes 786440 | tf_op jit(solution)/shard_map/ppermute | solution.py:50
  34.2 2.1 %collective-permute-start.10 = (bf16[128,512]{1,0:T(8,128)(2,1)S(1)}, bf16[128,512]{1,0:T(8,128)(2,1)S(1)}, u32[]{:S(2)}, u32[]{:S(2)}) collective-permute-start(bf16[128,512]{1,0:T(8,128)(2,1)S(1)} %get-tuple-element.55.refs_0_), channel_id=1, source_target_pairs={{0,4},{1,2},{2,1},{3,7},{4,0},{5,6},{6,5},{7,3},{8,12},{9,10},{10,... | collective-permute-start | bytes 393224 | tf_op jit(solution)/shard_map/ppermute | solution.py:50
  37.1 1.5 %collective-permute-start.12 = (bf16[64,1536]{1,0:T(8,128)(2,1)S(1)}, bf16[64,1536]{1,0:T(8,128)(2,1)S(1)}, u32[]{:S(2)}, u32[]{:S(2)}) collective-permute-start(bf16[64,1536]{1,0:T(8,128)(2,1)S(1)} %split.16), channel_id=1, source_target_pairs={{0,4},{4,0},{8,12},{12,8},{16,20},{20,16},{24,28},{28,24},{1,5},{5... | collective-permute-start | bytes 589832 | tf_op jit(solution)/shard_map/ppermute | solution.py:38
  38.6 4.9 %collective-permute-start.13 = (bf16[32,1536]{1,0:T(8,128)(2,1)S(1)}, bf16[32,1536]{1,0:T(8,128)(2,1)S(1)}, u32[]{:S(2)}, u32[]{:S(2)}) collective-permute-start(bf16[32,1536]{1,0:T(8,128)(2,1)S(1)} %pad_maximum_fusion.9), channel_id=1, source_target_pairs={{0,8},{4,12},{8,0},{12,4},{16,24},{20,28},{24,16},{28,20},{1,9},{5... | collective-permute-start | bytes 294920 | tf_op jit(solution)/shard_map/ppermute | solution.py:38
  40.0 5.7 %collective-permute-start.14 = (bf16[32,1536]{1,0:T(8,128)(2,1)S(1)}, bf16[32,1536]{1,0:T(8,128)(2,1)S(1)}, u32[]{:S(2)}, u32[]{:S(2)}) collective-permute-start(bf16[32,1536]{1,0:T(8,128)(2,1)S(1)} %pad_maximum_fusion.10), channel_id=1, source_target_pairs={{0,16},{4,20},{8,24},{12,28},{16,0},{20,4},{24,8},{28,12},{1,17},{... | collective-permute-start | bytes 294920 | tf_op jit(solution)/shard_map/ppermute | solution.py:38
  41.2 5.6 %collective-permute-start.15 = (bf16[32,1536]{1,0:T(8,128)(2,1)S(1)}, bf16[32,1536]{1,0:T(8,128)(2,1)S(1)}, u32[]{:S(2)}, u32[]{:S(2)}) collective-permute-start(bf16[32,1536]{1,0:T(8,128)(2,1)S(1)} %pad_maximum_fusion.11), channel_id=1, source_target_pairs={{0,24},{4,28},{8,16},{12,20},{16,8},{20,12},{24,0},{28,4},{1,25},{... | collective-permute-start | bytes 294920 | tf_op jit(solution)/shard_map/ppermute | solution.py:38
  47.2 25.2 %collective-permute-start.17 = (bf16[128,1024]{1,0:T(8,128)(2,1)S(1)}, bf16[128,1024]{1,0:T(8,128)(2,1)S(1)}, u32[]{:S(2)}, u32[]{:S(2)}) collective-permute-start(bf16[128,1024]{1,0:T(8,128)(2,1)S(1)} %get-tuple-element.61.refs_1_), channel_id=1, source_target_pairs={{0,1},{1,0},{2,6},{3,7},{4,5},{5,4},{6,2},{7,3},{8,9},{9,8},{10,14... | collective-permute-start | bytes 786440 | tf_op jit(solution)/shard_map/ppermute | solution.py:50
  66.0 7.8 %collective-permute-start.16 = (bf16[128,512]{1,0:T(8,128)(2,1)S(1)}, bf16[128,512]{1,0:T(8,128)(2,1)S(1)}, u32[]{:S(2)}, u32[]{:S(2)}) collective-permute-start(bf16[128,512]{1,0:T(8,128)(2,1)S(1)} %get-tuple-element.60.refs_0_), channel_id=1, source_target_pairs={{0,1},{1,0},{2,6},{3,7},{4,5},{5,4},{6,2},{7,3},{8,9},{9,8},{10,14... | collective-permute-start | bytes 393224 | tf_op jit(solution)/shard_map/ppermute | solution.py:50
  74.5 1.5 %collective-permute-start.18 = (bf16[64,1536]{1,0:T(8,128)(2,1)S(1)}, bf16[64,1536]{1,0:T(8,128)(2,1)S(1)}, u32[]{:S(2)}, u32[]{:S(2)}) collective-permute-start(bf16[64,1536]{1,0:T(8,128)(2,1)S(1)} %split.17), channel_id=1, source_target_pairs={{0,4},{4,0},{8,12},{12,8},{16,20},{20,16},{24,28},{28,24},{1,5},{5... | collective-permute-start | bytes 589832 | tf_op jit(solution)/shard_map/ppermute | solution.py:38
  76.1 5.0 %collective-permute-start.19 = (bf16[32,1536]{1,0:T(8,128)(2,1)S(1)}, bf16[32,1536]{1,0:T(8,128)(2,1)S(1)}, u32[]{:S(2)}, u32[]{:S(2)}) collective-permute-start(bf16[32,1536]{1,0:T(8,128)(2,1)S(1)} %pad_maximum_fusion.12), channel_id=1, source_target_pairs={{0,8},{4,12},{8,0},{12,4},{16,24},{20,28},{24,16},{28,20},{1,9},{5... | collective-permute-start | bytes 294920 | tf_op jit(solution)/shard_map/ppermute | solution.py:38
  77.5 6.8 %collective-permute-start.20 = (bf16[32,1536]{1,0:T(8,128)(2,1)S(1)}, bf16[32,1536]{1,0:T(8,128)(2,1)S(1)}, u32[]{:S(2)}, u32[]{:S(2)}) collective-permute-start(bf16[32,1536]{1,0:T(8,128)(2,1)S(1)} %pad_maximum_fusion.13), channel_id=1, source_target_pairs={{0,16},{4,20},{8,24},{12,28},{16,0},{20,4},{24,8},{28,12},{1,17},{... | collective-permute-start | bytes 294920 | tf_op jit(solution)/shard_map/ppermute | solution.py:38
  78.3 6.0 %collective-permute-start.21 = (bf16[32,1536]{1,0:T(8,128)(2,1)S(1)}, bf16[32,1536]{1,0:T(8,128)(2,1)S(1)}, u32[]{:S(2)}, u32[]{:S(2)}) collective-permute-start(bf16[32,1536]{1,0:T(8,128)(2,1)S(1)} %pad_maximum_fusion.14), channel_id=1, source_target_pairs={{0,24},{4,28},{8,16},{12,20},{16,8},{20,12},{24,0},{28,4},{1,25},{... | collective-permute-start | bytes 294920 | tf_op jit(solution)/shard_map/ppermute | solution.py:38

commit v9 on v8

--- a/solution.py
+++ b/solution.py
@@ -135,7 +135,7 @@
     x_ref, gain_ref, first_ref, second_ref, gate_ref, incoming_ref, out_ref, sems,
 ):
     parts = chunks(out_hbm.shape[0], sems.shape[0] - 6)
-    pairs = [(x_hbm, x_ref), (first_hbm, first_ref), (second_hbm, second_ref), (gain_hbm, gain_ref)]
+    pairs = [(first_hbm, first_ref), (second_hbm, second_ref), (x_hbm, x_ref), (gain_hbm, gain_ref)]
     pairs += [(gate_hbm, gate_ref), (incoming_hbm, incoming_ref)]
     pairs += [(out_hbm.at[rows], out_ref.at[rows]) for rows in parts]
     copies = [pltpu.make_async_copy(*pair, sems.at[i]) for i, pair in enumerate(pairs)]
@@ -150,23 +150,21 @@
 
     me = lax.axis_index("seq")
     down, across = positions(order)
-    for copy in copies[:4]:
+    sent, received = order.sent(down), order.received(across)
+    first_sent = one_hot(order.first_rows(me, sent, down) == across)
+    second_sent = one_hot(order.second_rows(me, sent, down) == across)
+    first_received = one_hot(order.first_rows(me, received, across) == down)
+    second_received = one_hot(order.second_rows(me, received, across) == down)
+    for copy in copies[:2]:
         copy.wait()
     first = block_diagonal([first_ref[k].astype(jnp.float32) for k in range(order.local_blocks)])
     second = block_diagonal([second_ref[k].astype(jnp.float32) for k in range(order.local_blocks)])
-    sent, received = order.sent(down), order.received(across)
-    first_send = rounded(
-        one_hot(order.first_rows(me, sent, down) == across), first.astype(jnp.bfloat16)
-    )
-    second_send_ref[...] = rounded(
-        one_hot(order.second_rows(me, sent, down) == across), second.T.astype(jnp.bfloat16)
-    )
-    first_recv_ref[...] = rounded(
-        first.T.astype(jnp.bfloat16), one_hot(order.first_rows(me, received, across) == down)
-    )
-    second_recv_ref[...] = rounded(
-        second.astype(jnp.bfloat16), one_hot(order.second_rows(me, received, across) == down)
-    )
+    first_send = rounded(first_sent, first.astype(jnp.bfloat16))
+    second_send_ref[...] = rounded(second_sent, second.T.astype(jnp.bfloat16))
+    first_recv_ref[...] = rounded(first.T.astype(jnp.bfloat16), first_received)
+    second_recv_ref[...] = rounded(second.astype(jnp.bfloat16), second_received)
+    for copy in copies[2:4]:
+        copy.wait()
     features = x_ref[...].astype(jnp.float32)
     inv_rms = lax.rsqrt(jnp.mean(features * features, axis=-1, keepdims=True) + 1e-06)
     inv_ref[...] = inv_rms
@@ -307,6 +305,20 @@
     )(*operands)
 
 
+def mix_kernel(
+    partial_ref, last_ref, weight_ref, mix_factor_ref, gate_factor_ref, second_send_ref,
+    mix_ref, gate_ref, keep_ref, give_ref,
+):
+    hidden = partial_ref[...] + dot(last_ref[...], weight_ref[...])
+    mix = (hidden * mix_factor_ref[...]).astype(jnp.bfloat16)
+    mix_ref[...] = mix
+    send = rounded(second_send_ref[...], mix)
+    half = keep_ref.shape[0]
+    keep_ref[...] = send[:half]
+    give_ref[...] = send[half:]
+    gate_ref[...] = (hidden * gate_factor_ref[...]).astype(jnp.bfloat16)
+
+
 def advance_kernel(
     after_ref, mid_ref, first_recv_ref, gate_back_ref, gain_ref, x_ref, inv_ref, *refs
 ):
@@ -417,16 +429,20 @@
 
     row_count, width = inputs.shape
     short = array_of((row_count, width), jnp.bfloat16)
+    half = array_of((row_count // 2, width), jnp.bfloat16)
     square = array_of((row_count, row_count), jnp.float32)
     blocks = array_of((local_blocks, block_rows, block_rows), jnp.float32)
     kept = (delta_hidden, mix_factor)
     for sender in reversed(range(section_count - 1)):
         before = (delta_mid, *outgoing)
         incoming = [passed_down(part, sender + 1) for part in outgoing]
-        delta_hidden = sum(dot(part, weight) for part, weight in zip(incoming, out_turned))
-        delta_mix = (delta_hidden * mix_factor).astype(jnp.bfloat16)
-        send = rounded(second_send, delta_mix)
-        arrived = order.exchange(*jnp.split(send, 2))
+        last, *first = zip(incoming, out_turned)
+        partial = sum(dot(part, weight) for part, weight in first)
+        delta_mix, delta_gate, kept_pieces, give = call(
+            mix_kernel, "mix", [short, short, half, half],
+            (partial, *last, mix_factor, gate_factor, second_send),
+        )
+        arrived = order.exchange(kept_pieces, give)
         before_mid, *before_outgoing = before
         if sender + 2 == section_count:
             kept = call(
@@ -440,7 +456,6 @@
                 (arrived[0], normed, moved, before_mid, delta_mix, *before_outgoing, *kept),
             )
         delta_mid = jnp.concatenate(arrived)
-        delta_gate = (delta_hidden * gate_factor).astype(jnp.bfloat16)
         gate_back = dot(delta_gate, gate_turned)
         if sender > 0:
             outgoing = advance(incoming, kept[1], delta_mid, first_recv, gate_back, gain, inputs, inv_rms)

time: 86 us -> 85.5 us (level)
  matrix products: 6.09 us -> 4.08 us
  Pallas kernels: 13.7 us -> 15.4 us
    dot_general x12 -> x6, matrix products: 6.09 us -> 4.08 us  [dot(): return jnp.dot(left, right, preferred_element_type=jnp.float32)]
    pallas_call x4 -> x7, Pallas kernels: 3.63 us -> 5.31 us  [call(): pl.pallas_call(kernel, in_specs=[WHOLE] * len(operands), out_specs=[WHOLE...]
where the time goes in v9:
time: 85.5 us; the launch traced here: 85.4 us
  starting transfers between devices  36.5 us (43%)
  waiting for transfers between devices  28 us (33%)
  Pallas kernels  15.4 us (18%)
  matrix products  4.08 us (5%)
  between operations  0.99 us (1%)
    ppermute x6, starting transfers between devices, passed_down(): return lax.ppermute(block, ('seq', 'pipe'), pairs)  19.9 us
    ppermute x16, waiting for transfers between devices, swap(): return lax.ppermute(block, 'seq', [(i, i ^ offset) for i in range(count)])  18.8 us
    ppermute x16, starting transfers between devices, swap(): return lax.ppermute(block, 'seq', [(i, i ^ offset) for i in range(count)])  16.6 us
    ppermute x6, waiting for transfers between devices, passed_down(): return lax.ppermute(block, ('seq', 'pipe'), pairs)  9.19 us
    pallas_call x7, Pallas kernels, call(): pl.pallas_call(kernel, in_specs=[WHOLE] * len(operands), out_specs=[WHOLE...  5.31 us
    pallas_call x1, Pallas kernels, transposed(): pl.pallas_call(transpose_kernel, in_specs=[ANYWHERE] * 3, out_specs=[WHOL...  4.41 us
    dot_general x6, matrix products, dot(): return jnp.dot(left, right, preferred_element_type=jnp.float32)  4.08 us
    pallas_call x1, Pallas kernels, begin(): pl.pallas_call(functools.partial(begin_kernel, order), in_specs=[ANYWHERE...  3.53 us
  transfers between devices with their start and end apart: 22, of which 16 were waited for; matrix products, arithmetic and copies ran while one was open for 5% of the time, Pallas kernels for 8%

profile of v9, /device:TPU:0, one launch (start us, length us, event | category | flops | bytes accessed | tf_op | source)
XLA Modules:
  0.0 85.4 jit_solution(17101125834783021502)
XLA Ops:
  0.6 3.5 %begin.1 = (bf16[128,1536]{1,0:T(8,128)(2,1)S(1)}, f32[128,1]{1,0:T(8,128)S(1)}, bf16[128,128]{1,0:T(8,128)(2,1)S(1)}, bf16[128,128]{1,0:T(8,128)(2,1)S(1)}, bf1...) custom-call(bf16[128,1536]{1,0:T(8,128)(2,1)} %bitcast.20, ...), custom_call_target="tpu_custom_call" | custom-call | tf_op jit(solution)/shard_map/begin/pallas_call | solution.py:209
  4.2 0.5 collective-permute-start
  4.7 1.3 %collective-permute-done = bf16[128,1536]{1,0:T(8,128)(2,1)S(1)} collective-permute-done((bf16[128,1536]{1,0:T(8,128)(2,1)S(1)}, bf16[128,1536]{1,0:T(8,128)(2,1)S(1)}, u32[]{:S(2)}, u32[]{:S(2)}) %collective-permute-start) | collective-permute-done | bytes 393248 | tf_op jit(solution)/shard_map/ppermute | solution.py:38
  6.1 2.9 %collective-permute-start.1 = (bf16[64,1536]{1,0:T(8,128)(2,1)S(1)}, bf16[64,1536]{1,0:T(8,128)(2,1)S(1)}, u32[]{:S(2)}, u32[]{:S(2)}) collective-permute-start(bf16[64,1536]{1,0:T(8,128)(2,1)S(1)} %pad_maximum_fusion.1), channel_id=1, source_target_pairs={{0,8},{4,12},{8,0},{12,4},{16,24},{20,28},{24,16},{28,20},{1,9},{5... | collective-permute-start | bytes 589832 | tf_op jit(solution)/shard_map/ppermute | solution.py:38
  9.0 1.6 %collective-permute-start.2 = (bf16[64,1536]{1,0:T(8,128)(2,1)S(1)}, bf16[64,1536]{1,0:T(8,128)(2,1)S(1)}, u32[]{:S(2)}, u32[]{:S(2)}) collective-permute-start(bf16[64,1536]{1,0:T(8,128)(2,1)S(1)} %pad_maximum_fusion.2), channel_id=1, source_target_pairs={{0,16},{4,20},{8,24},{12,28},{16,0},{20,4},{24,8},{28,12},{1,17},{... | collective-permute-start | bytes 589832 | tf_op jit(solution)/shard_map/ppermute | solution.py:38
  10.6 0.1 collective-permute-start.3
  10.7 0.0 copy-start
  10.7 0.0 copy-start.1
  10.8 0.0 copy-start.2
  10.8 4.4 %transposed.1 = (bf16[1536,1536]{1,0:T(8,128)(2,1)S(1)}, bf16[512,1536]{1,0:T(8,128)(2,1)S(1)}, bf16[1024,1536]{1,0:T(8,128)(2,1)S(1)}) custom-call(bf16[1536,1536]{1,0:T(8,128)(2,1)} %bitcast.26, bf16[1536,1536]{1,0:T(8,128)(2,1)} %bitcast.28, bf16[64,1536]{1,0:T(8,128)(2,1)S(1)} %pad_maximum_fusion.after_ref.refs_0_), custom_call_target="tpu_custom_call" | custom-call | tf_op jit(solution)/shard_map/transposed/pallas_call | solution.py:241
  15.2 0.0 collective-permute-done.1.refs_1_
  15.2 4.8 %collective-permute-done.2.refs_2_ = bf16[64,1536]{1,0:T(8,128)(2,1)S(1)} collective-permute-done((bf16[64,1536]{1,0:T(8,128)(2,1)S(1)}, bf16[64,1536]{1,0:T(8,128)(2,1)S(1)}, u32[]{:S(2)}, u32[]{:S(2)}) %collective-permute-start.2) | collective-permute-done | bytes 196640 | tf_op jit(solution)/shard_map/ppermute | solution.py:38
  20.0 0.0 collective-permute-done.3.refs_3_
  20.0 1.2 %finish.1 = (bf16[128,1536]{1,0:T(8,128)(2,1)S(1)}, bf16[128,1536]{1,0:T(8,128)(2,1)S(1)}, f32[128,1536]{1,0:T(8,128)S(1)}, bf16[128,512]{1,0:T(8,128)(2,1)S(1)}, bf16[128,1024]{1,0:T(8,128)(2,1)S(1)}) custom-call(bf16[64,1536]{1,0:T(8,128)(2,1)S(1)} %pad_maximum_fusion.after_ref.refs_0_, bf16[64,1536]{1,0:T(8,128)(2,1)S(1)} %collective-permute-done.1.refs_1_, ...), custom_call_target="tpu_custom_call" | custom-call | tf_op jit(solution)/shard_map/finish/pallas_call | solution.py:298
  21.2 0.1 collective-permute-start.4
  21.3 0.5 collective-permute-start.5
  21.8 1.0 %collective-permute-done.4.refs_1_ = bf16[128,1024]{1,0:T(8,128)(2,1)S(1)} collective-permute-done((bf16[128,1024]{1,0:T(8,128)(2,1)S(1)}, bf16[128,1024]{1,0:T(8,128)(2,1)S(1)}, u32[]{:S(2)}, u32[]{:S(2)}) %collective-permute-start.4) | collective-permute-done | bytes 262176 | tf_op jit(solution)/shard_map/ppermute | solution.py:50
  22.8 0.6 fusion.8.partial_ref
  23.4 0.0 collective-permute-done.5.last_ref.refs_0_
  23.4 0.6 mix.3
  24.0 0.2 collective-permute-start.6
  24.2 0.8 fusion.9.gate_back_ref
  25.0 0.5 collective-permute-done.6
  25.5 1.2 %collective-permute-start.7 = (bf16[32,1536]{1,0:T(8,128)(2,1)S(1)}, bf16[32,1536]{1,0:T(8,128)(2,1)S(1)}, u32[]{:S(2)}, u32[]{:S(2)}) collective-permute-start(bf16[32,1536]{1,0:T(8,128)(2,1)S(1)} %pad_maximum_fusion.5), channel_id=1, source_target_pairs={{0,8},{4,12},{8,0},{12,4},{16,24},{20,28},{24,16},{28,20},{1,9},{5... | collective-permute-start | bytes 294920 | tf_op jit(solution)/shard_map/ppermute | solution.py:38
  26.7 1.0 %collective-permute-start.8 = (bf16[32,1536]{1,0:T(8,128)(2,1)S(1)}, bf16[32,1536]{1,0:T(8,128)(2,1)S(1)}, u32[]{:S(2)}, u32[]{:S(2)}) collective-permute-start(bf16[32,1536]{1,0:T(8,128)(2,1)S(1)} %pad_maximum_fusion.6), channel_id=1, source_target_pairs={{0,16},{4,20},{8,24},{12,28},{16,0},{20,4},{24,8},{28,12},{1,17},{... | collective-permute-start | bytes 294920 | tf_op jit(solution)/shard_map/ppermute | solution.py:38
  27.7 1.5 %collective-permute-start.9 = (bf16[32,1536]{1,0:T(8,128)(2,1)S(1)}, bf16[32,1536]{1,0:T(8,128)(2,1)S(1)}, u32[]{:S(2)}, u32[]{:S(2)}) collective-permute-start(bf16[32,1536]{1,0:T(8,128)(2,1)S(1)} %pad_maximum_fusion.7), channel_id=1, source_target_pairs={{0,24},{4,28},{8,16},{12,20},{16,8},{20,12},{24,0},{28,4},{1,25},{... | collective-permute-start | bytes 294920 | tf_op jit(solution)/shard_map/ppermute | solution.py:38
  29.2 0.4 keep.3
  29.6 0.8 collective-permute-done.7
  30.4 1.9 %collective-permute-done.8 = bf16[32,1536]{1,0:T(8,128)(2,1)S(1)} collective-permute-done((bf16[32,1536]{1,0:T(8,128)(2,1)S(1)}, bf16[32,1536]{1,0:T(8,128)(2,1)S(1)}, u32[]{:S(2)}, u32[]{:S(2)}) %collective-permute-start.8) | collective-permute-done | bytes 98336 | tf_op jit(solution)/shard_map/ppermute | solution.py:38
  32.4 1.1 %collective-permute-done.9 = bf16[32,1536]{1,0:T(8,128)(2,1)S(1)} collective-permute-done((bf16[32,1536]{1,0:T(8,128)(2,1)S(1)}, bf16[32,1536]{1,0:T(8,128)(2,1)S(1)}, u32[]{:S(2)}, u32[]{:S(2)}) %collective-permute-start.9) | collective-permute-done | bytes 98336 | tf_op jit(solution)/shard_map/ppermute | solution.py:38
  33.5 0.5 advance.2
  34.0 0.1 collective-permute-start.10
  34.1 0.5 collective-permute-start.11
  34.6 1.0 %collective-permute-done.10.refs_1_ = bf16[128,1024]{1,0:T(8,128)(2,1)S(1)} collective-permute-done((bf16[128,1024]{1,0:T(8,128)(2,1)S(1)}, bf16[128,1024]{1,0:T(8,128)(2,1)S(1)}, u32[]{:S(2)}, u32[]{:S(2)}) %collective-permute-start.10) | collective-permute-done | bytes 262176 | tf_op jit(solution)/shard_map/ppermute | solution.py:50
  35.6 0.6 fusion.10.partial_ref
  36.2 0.6 mix.4
  36.8 0.2 collective-permute-start.12
  37.0 0.8 fusion.11.gate_back_ref
  37.8 0.5 collective-permute-done.12
  38.3 1.3 %collective-permute-start.13 = (bf16[32,1536]{1,0:T(8,128)(2,1)S(1)}, bf16[32,1536]{1,0:T(8,128)(2,1)S(1)}, u32[]{:S(2)}, u32[]{:S(2)}) collective-permute-start(bf16[32,1536]{1,0:T(8,128)(2,1)S(1)} %pad_maximum_fusion.9), channel_id=1, source_target_pairs={{0,8},{4,12},{8,0},{12,4},{16,24},{20,28},{24,16},{28,20},{1,9},{5... | collective-permute-start | bytes 294920 | tf_op jit(solution)/shard_map/ppermute | solution.py:38
  39.7 1.2 %collective-permute-start.14 = (bf16[32,1536]{1,0:T(8,128)(2,1)S(1)}, bf16[32,1536]{1,0:T(8,128)(2,1)S(1)}, u32[]{:S(2)}, u32[]{:S(2)}) collective-permute-start(bf16[32,1536]{1,0:T(8,128)(2,1)S(1)} %pad_maximum_fusion.10), channel_id=1, source_target_pairs={{0,16},{4,20},{8,24},{12,28},{16,0},{20,4},{24,8},{28,12},{1,17},{... | collective-permute-start | bytes 294920 | tf_op jit(solution)/shard_map/ppermute | solution.py:38
  40.9 1.1 %collective-permute-start.15 = (bf16[32,1536]{1,0:T(8,128)(2,1)S(1)}, bf16[32,1536]{1,0:T(8,128)(2,1)S(1)}, u32[]{:S(2)}, u32[]{:S(2)}) collective-permute-start(bf16[32,1536]{1,0:T(8,128)(2,1)S(1)} %pad_maximum_fusion.11), channel_id=1, source_target_pairs={{0,24},{4,28},{8,16},{12,20},{16,8},{20,12},{24,0},{28,4},{1,25},{... | collective-permute-start | bytes 294920 | tf_op jit(solution)/shard_map/ppermute | solution.py:38
  42.0 0.4 keep.4
  42.4 0.8 collective-permute-done.13
  43.3 2.1 %collective-permute-done.14 = bf16[32,1536]{1,0:T(8,128)(2,1)S(1)} collective-permute-done((bf16[32,1536]{1,0:T(8,128)(2,1)S(1)}, bf16[32,1536]{1,0:T(8,128)(2,1)S(1)}, u32[]{:S(2)}, u32[]{:S(2)}) %collective-permute-start.14) | collective-permute-done | bytes 98336 | tf_op jit(solution)/shard_map/ppermute | solution.py:38
  45.4 1.1 %collective-permute-done.15 = bf16[32,1536]{1,0:T(8,128)(2,1)S(1)} collective-permute-done((bf16[32,1536]{1,0:T(8,128)(2,1)S(1)}, bf16[32,1536]{1,0:T(8,128)(2,1)S(1)}, u32[]{:S(2)}, u32[]{:S(2)}) %collective-permute-start.15) | collective-permute-done | bytes 98336 | tf_op jit(solution)/shard_map/ppermute | solution.py:38
  46.5 0.5 advance.3
  47.0 18.7 %collective-permute-start.16 = (bf16[128,1024]{1,0:T(8,128)(2,1)S(1)}, bf16[128,1024]{1,0:T(8,128)(2,1)S(1)}, u32[]{:S(2)}, u32[]{:S(2)}) collective-permute-start(bf16[128,1024]{1,0:T(8,128)(2,1)S(1)} %get-tuple-element.80.refs_1_), channel_id=1, source_target_pairs={{0,1},{1,0},{2,6},{3,7},{4,5},{5,4},{6,2},{7,3},{8,9},{9,8},{10,14... | collective-permute-start | bytes 786440 | tf_op jit(solution)/shard_map/ppermute | solution.py:50
  65.7 0.1 collective-permute-start.17
  65.8 6.3 %collective-permute-done.16.refs_1_ = bf16[128,1024]{1,0:T(8,128)(2,1)S(1)} collective-permute-done((bf16[128,1024]{1,0:T(8,128)(2,1)S(1)}, bf16[128,1024]{1,0:T(8,128)(2,1)S(1)}, u32[]{:S(2)}, u32[]{:S(2)}) %collective-permute-start.16) | collective-permute-done | bytes 262176 | tf_op jit(solution)/shard_map/ppermute | solution.py:50
  72.1 0.6 fusion.12.partial_ref
  72.7 0.8 collective-permute-done.17.last_ref.refs_0_
  73.5 0.6 mix.5
  74.1 0.1 collective-permute-start.18
  74.2 0.8 fusion.13.gate_back_ref
  75.0 0.6 collective-permute-done.18
  75.6 1.4 %collective-permute-start.19 = (bf16[32,1536]{1,0:T(8,128)(2,1)S(1)}, bf16[32,1536]{1,0:T(8,128)(2,1)S(1)}, u32[]{:S(2)}, u32[]{:S(2)}) collective-permute-start(bf16[32,1536]{1,0:T(8,128)(2,1)S(1)} %pad_maximum_fusion.12), channel_id=1, source_target_pairs={{0,8},{4,12},{8,0},{12,4},{16,24},{20,28},{24,16},{28,20},{1,9},{5... | collective-permute-start | bytes 294920 | tf_op jit(solution)/shard_map/ppermute | solution.py:38
  77.0 0.8 collective-permute-start.20
  77.8 1.5 %collective-permute-start.21 = (bf16[32,1536]{1,0:T(8,128)(2,1)S(1)}, bf16[32,1536]{1,0:T(8,128)(2,1)S(1)}, u32[]{:S(2)}, u32[]{:S(2)}) collective-permute-start(bf16[32,1536]{1,0:T(8,128)(2,1)S(1)} %pad_maximum_fusion.14), channel_id=1, source_target_pairs={{0,24},{4,28},{8,16},{12,20},{16,8},{20,12},{24,0},{28,4},{1,25},{... | collective-permute-start | bytes 294920 | tf_op jit(solution)/shard_map/ppermute | solution.py:38
  79.3 1.3 %keep.5 = (bf16[128,1536]{1,0:T(8,128)(2,1)S(1)}, f32[128,128]{1,0:T(8,128)S(1)}, f32[2,64,64]{2,1,0:T(8,128)}) custom-call(bf16[32,1536]{1,0:T(8,128)(2,1)S(1)} %pad_maximum_fusion.15.after_ref, bf16[128,1536]{1,0:T(8,128)(2,1)S(1)} %get-tuple-element.65.normed_ref, bf16[128,1536]{1,0:T(8,128)(2,1)S(1)} %get-tuple-element.66.moved_ref, ...), custom_call_target="tpu_custom_call" | custom-call | tf_op jit(solution)/shard_map/keep/pallas_call | solution.py:401
  80.6 0.0 collective-permute-done.19
  80.6 3.1 %collective-permute-done.20 = bf16[32,1536]{1,0:T(8,128)(2,1)S(1)} collective-permute-done((bf16[32,1536]{1,0:T(8,128)(2,1)S(1)}, bf16[32,1536]{1,0:T(8,128)(2,1)S(1)}, u32[]{:S(2)}, u32[]{:S(2)}) %collective-permute-start.20) | collective-permute-done | bytes 98336 | tf_op jit(solution)/shard_map/ppermute | solution.py:38
  83.8 0.0 collective-permute-done.21
  83.8 1.5 %close.1 = (bf16[128,1536]{1,0:T(8,128)(2,1)}, f32[2,64,64]{2,1,0:T(8,128)}) custom-call(bf16[128,1536]{1,0:T(8,128)(2,1)S(1)} %constant_dynamic-update-slice_fusion.10.mid_ref, bf16[128,128]{1,0:T(8,128)(2,1)S(1)} %get-tuple-element.51.refs_5_.first_recv_ref, f32[128,1536]{1,0:T(8,128)S(1)} %fusion.13.gate_back_ref, f32[1,1536]{1,0:T(1,128)S(1)} %copy-done.2, ...), custom_call_target="tpu_custom_call" | custom-call | tf_op jit(solution)/shard_map/close/pallas_call | solution.py:401
  (37 shorter events, 0.4 us)
Async XLA Ops:
  4.2 1.9 %collective-permute-start = (bf16[128,1536]{1,0:T(8,128)(2,1)S(1)}, bf16[128,1536]{1,0:T(8,128)(2,1)S(1)}, u32[]{:S(2)}, u32[]{:S(2)}) collective-permute-start(bf16[128,1536]{1,0:T(8,128)(2,1)S(1)} %get-tuple-element.49), channel_id=1, source_target_pairs={{0,4},{4,0},{8,12},{12,8},{16,20},{20,16},{24,28},{28,24},{1,5},{5... | collective-permute-start | bytes 1179656 | tf_op jit(solution)/shard_map/ppermute | solution.py:38
  6.1 9.1 %collective-permute-start.1 = (bf16[64,1536]{1,0:T(8,128)(2,1)S(1)}, bf16[64,1536]{1,0:T(8,128)(2,1)S(1)}, u32[]{:S(2)}, u32[]{:S(2)}) collective-permute-start(bf16[64,1536]{1,0:T(8,128)(2,1)S(1)} %pad_maximum_fusion.1), channel_id=1, source_target_pairs={{0,8},{4,12},{8,0},{12,4},{16,24},{20,28},{24,16},{28,20},{1,9},{5... | collective-permute-start | bytes 589832 | tf_op jit(solution)/shard_map/ppermute | solution.py:38
  9.0 10.9 %collective-permute-start.2 = (bf16[64,1536]{1,0:T(8,128)(2,1)S(1)}, bf16[64,1536]{1,0:T(8,128)(2,1)S(1)}, u32[]{:S(2)}, u32[]{:S(2)}) collective-permute-start(bf16[64,1536]{1,0:T(8,128)(2,1)S(1)} %pad_maximum_fusion.2), channel_id=1, source_target_pairs={{0,16},{4,20},{8,24},{12,28},{16,0},{20,4},{24,8},{28,12},{1,17},{... | collective-permute-start | bytes 589832 | tf_op jit(solution)/shard_map/ppermute | solution.py:38
  10.6 9.3 %collective-permute-start.3 = (bf16[64,1536]{1,0:T(8,128)(2,1)S(1)}, bf16[64,1536]{1,0:T(8,128)(2,1)S(1)}, u32[]{:S(2)}, u32[]{:S(2)}) collective-permute-start(bf16[64,1536]{1,0:T(8,128)(2,1)S(1)} %pad_maximum_fusion.3), channel_id=1, source_target_pairs={{0,24},{4,28},{8,16},{12,20},{16,8},{20,12},{24,0},{28,4},{1,25},{... | collective-permute-start | bytes 589832 | tf_op jit(solution)/shard_map/ppermute | solution.py:38
  10.7 9.2 %copy-start = (bf16[1,128,1536]{2,1,0:T(8,128)(2,1)S(1)}, bf16[1,128,1536]{2,1,0:T(8,128)(2,1)}, u32[]{:S(2)}) copy-start(bf16[1,128,1536]{2,1,0:T(8,128)(2,1)} %param.7) | copy-start | bytes 1179652
  10.7 9.2 %copy-start.1 = (bf16[128,1536]{1,0:T(8,128)(2,1)S(1)}, bf16[128,1536]{1,0:T(8,128)(2,1)}, u32[]{:S(2)}) copy-start(bf16[128,1536]{1,0:T(8,128)(2,1)} %refs_12_.1) | copy-start | bytes 1179652
  10.8 9.2 %copy-start.2 = (f32[1,1536]{1,0:T(1,128)S(1)}, f32[1,1536]{1,0:T(1,128)}, u32[]{:S(2)}) copy-start(f32[1,1536]{1,0:T(1,128)} %gain_ref.5) | copy-start | bytes 18436
  21.2 1.6 %collective-permute-start.4 = (bf16[128,1024]{1,0:T(8,128)(2,1)S(1)}, bf16[128,1024]{1,0:T(8,128)(2,1)S(1)}, u32[]{:S(2)}, u32[]{:S(2)}) collective-permute-start(bf16[128,1024]{1,0:T(8,128)(2,1)S(1)} %get-tuple-element.56.refs_1_), channel_id=1, source_target_pairs={{0,4},{1,5},{2,3},{3,2},{4,0},{5,1},{6,7},{7,6},{8,12},{9,13},{10,... | collective-permute-start | bytes 786440 | tf_op jit(solution)/shard_map/ppermute | solution.py:50
  21.3 2.1 %collective-permute-start.5 = (bf16[128,512]{1,0:T(8,128)(2,1)S(1)}, bf16[128,512]{1,0:T(8,128)(2,1)S(1)}, u32[]{:S(2)}, u32[]{:S(2)}) collective-permute-start(bf16[128,512]{1,0:T(8,128)(2,1)S(1)} %get-tuple-element.58.refs_0_), channel_id=1, source_target_pairs={{0,4},{1,5},{2,3},{3,2},{4,0},{5,1},{6,7},{7,6},{8,12},{9,13},{10,... | collective-permute-start | bytes 393224 | tf_op jit(solution)/shard_map/ppermute | solution.py:50
  24.0 1.5 %collective-permute-start.6 = (bf16[64,1536]{1,0:T(8,128)(2,1)S(1)}, bf16[64,1536]{1,0:T(8,128)(2,1)S(1)}, u32[]{:S(2)}, u32[]{:S(2)}) collective-permute-start(bf16[64,1536]{1,0:T(8,128)(2,1)S(1)} %get-tuple-element.64), channel_id=1, source_target_pairs={{0,4},{4,0},{8,12},{12,8},{16,20},{20,16},{24,28},{28,24},{1,5},{5... | collective-permute-start | bytes 589832 | tf_op jit(solution)/shard_map/ppermute | solution.py:38
  25.5 4.9 %collective-permute-start.7 = (bf16[32,1536]{1,0:T(8,128)(2,1)S(1)}, bf16[32,1536]{1,0:T(8,128)(2,1)S(1)}, u32[]{:S(2)}, u32[]{:S(2)}) collective-permute-start(bf16[32,1536]{1,0:T(8,128)(2,1)S(1)} %pad_maximum_fusion.5), channel_id=1, source_target_pairs={{0,8},{4,12},{8,0},{12,4},{16,24},{20,28},{24,16},{28,20},{1,9},{5... | collective-permute-start | bytes 294920 | tf_op jit(solution)/shard_map/ppermute | solution.py:38
  26.7 5.6 %collective-permute-start.8 = (bf16[32,1536]{1,0:T(8,128)(2,1)S(1)}, bf16[32,1536]{1,0:T(8,128)(2,1)S(1)}, u32[]{:S(2)}, u32[]{:S(2)}) collective-permute-start(bf16[32,1536]{1,0:T(8,128)(2,1)S(1)} %pad_maximum_fusion.6), channel_id=1, source_target_pairs={{0,16},{4,20},{8,24},{12,28},{16,0},{20,4},{24,8},{28,12},{1,17},{... | collective-permute-start | bytes 294920 | tf_op jit(solution)/shard_map/ppermute | solution.py:38
  27.7 5.8 %collective-permute-start.9 = (bf16[32,1536]{1,0:T(8,128)(2,1)S(1)}, bf16[32,1536]{1,0:T(8,128)(2,1)S(1)}, u32[]{:S(2)}, u32[]{:S(2)}) collective-permute-start(bf16[32,1536]{1,0:T(8,128)(2,1)S(1)} %pad_maximum_fusion.7), channel_id=1, source_target_pairs={{0,24},{4,28},{8,16},{12,20},{16,8},{20,12},{24,0},{28,4},{1,25},{... | collective-permute-start | bytes 294920 | tf_op jit(solution)/shard_map/ppermute | solution.py:38
  34.0 1.6 %collective-permute-start.10 = (bf16[128,1024]{1,0:T(8,128)(2,1)S(1)}, bf16[128,1024]{1,0:T(8,128)(2,1)S(1)}, u32[]{:S(2)}, u32[]{:S(2)}) collective-permute-start(bf16[128,1024]{1,0:T(8,128)(2,1)S(1)} %get-tuple-element.71.refs_1_), channel_id=1, source_target_pairs={{0,4},{1,2},{2,1},{3,7},{4,0},{5,6},{6,5},{7,3},{8,12},{9,10},{10,... | collective-permute-start | bytes 786440 | tf_op jit(solution)/shard_map/ppermute | solution.py:50
  34.1 2.1 %collective-permute-start.11 = (bf16[128,512]{1,0:T(8,128)(2,1)S(1)}, bf16[128,512]{1,0:T(8,128)(2,1)S(1)}, u32[]{:S(2)}, u32[]{:S(2)}) collective-permute-start(bf16[128,512]{1,0:T(8,128)(2,1)S(1)} %get-tuple-element.72.refs_0_), channel_id=1, source_target_pairs={{0,4},{1,2},{2,1},{3,7},{4,0},{5,6},{6,5},{7,3},{8,12},{9,10},{10,... | collective-permute-start | bytes 393224 | tf_op jit(solution)/shard_map/ppermute | solution.py:50
  36.8 1.5 %collective-permute-start.12 = (bf16[64,1536]{1,0:T(8,128)(2,1)S(1)}, bf16[64,1536]{1,0:T(8,128)(2,1)S(1)}, u32[]{:S(2)}, u32[]{:S(2)}) collective-permute-start(bf16[64,1536]{1,0:T(8,128)(2,1)S(1)} %get-tuple-element.74), channel_id=1, source_target_pairs={{0,4},{4,0},{8,12},{12,8},{16,20},{20,16},{24,28},{28,24},{1,5},{5... | collective-permute-start | bytes 589832 | tf_op jit(solution)/shard_map/ppermute | solution.py:38
  38.3 4.9 %collective-permute-start.13 = (bf16[32,1536]{1,0:T(8,128)(2,1)S(1)}, bf16[32,1536]{1,0:T(8,128)(2,1)S(1)}, u32[]{:S(2)}, u32[]{:S(2)}) collective-permute-start(bf16[32,1536]{1,0:T(8,128)(2,1)S(1)} %pad_maximum_fusion.9), channel_id=1, source_target_pairs={{0,8},{4,12},{8,0},{12,4},{16,24},{20,28},{24,16},{28,20},{1,9},{5... | collective-permute-start | bytes 294920 | tf_op jit(solution)/shard_map/ppermute | solution.py:38
  39.7 5.7 %collective-permute-start.14 = (bf16[32,1536]{1,0:T(8,128)(2,1)S(1)}, bf16[32,1536]{1,0:T(8,128)(2,1)S(1)}, u32[]{:S(2)}, u32[]{:S(2)}) collective-permute-start(bf16[32,1536]{1,0:T(8,128)(2,1)S(1)} %pad_maximum_fusion.10), channel_id=1, source_target_pairs={{0,16},{4,20},{8,24},{12,28},{16,0},{20,4},{24,8},{28,12},{1,17},{... | collective-permute-start | bytes 294920 | tf_op jit(solution)/shard_map/ppermute | solution.py:38
  40.9 5.6 %collective-permute-start.15 = (bf16[32,1536]{1,0:T(8,128)(2,1)S(1)}, bf16[32,1536]{1,0:T(8,128)(2,1)S(1)}, u32[]{:S(2)}, u32[]{:S(2)}) collective-permute-start(bf16[32,1536]{1,0:T(8,128)(2,1)S(1)} %pad_maximum_fusion.11), channel_id=1, source_target_pairs={{0,24},{4,28},{8,16},{12,20},{16,8},{20,12},{24,0},{28,4},{1,25},{... | collective-permute-start | bytes 294920 | tf_op jit(solution)/shard_map/ppermute | solution.py:38
  47.0 25.1 %collective-permute-start.16 = (bf16[128,1024]{1,0:T(8,128)(2,1)S(1)}, bf16[128,1024]{1,0:T(8,128)(2,1)S(1)}, u32[]{:S(2)}, u32[]{:S(2)}) collective-permute-start(bf16[128,1024]{1,0:T(8,128)(2,1)S(1)} %get-tuple-element.80.refs_1_), channel_id=1, source_target_pairs={{0,1},{1,0},{2,6},{3,7},{4,5},{5,4},{6,2},{7,3},{8,9},{9,8},{10,14... | collective-permute-start | bytes 786440 | tf_op jit(solution)/shard_map/ppermute | solution.py:50
  65.7 7.8 %collective-permute-start.17 = (bf16[128,512]{1,0:T(8,128)(2,1)S(1)}, bf16[128,512]{1,0:T(8,128)(2,1)S(1)}, u32[]{:S(2)}, u32[]{:S(2)}) collective-permute-start(bf16[128,512]{1,0:T(8,128)(2,1)S(1)} %get-tuple-element.81.refs_0_), channel_id=1, source_target_pairs={{0,1},{1,0},{2,6},{3,7},{4,5},{5,4},{6,2},{7,3},{8,9},{9,8},{10,14... | collective-permute-start | bytes 393224 | tf_op jit(solution)/shard_map/ppermute | solution.py:50
  74.1 1.5 %collective-permute-start.18 = (bf16[64,1536]{1,0:T(8,128)(2,1)S(1)}, bf16[64,1536]{1,0:T(8,128)(2,1)S(1)}, u32[]{:S(2)}, u32[]{:S(2)}) collective-permute-start(bf16[64,1536]{1,0:T(8,128)(2,1)S(1)} %get-tuple-element.83), channel_id=1, source_target_pairs={{0,4},{4,0},{8,12},{12,8},{16,20},{20,16},{24,28},{28,24},{1,5},{5... | collective-permute-start | bytes 589832 | tf_op jit(solution)/shard_map/ppermute | solution.py:38
  75.6 5.0 %collective-permute-start.19 = (bf16[32,1536]{1,0:T(8,128)(2,1)S(1)}, bf16[32,1536]{1,0:T(8,128)(2,1)S(1)}, u32[]{:S(2)}, u32[]{:S(2)}) collective-permute-start(bf16[32,1536]{1,0:T(8,128)(2,1)S(1)} %pad_maximum_fusion.12), channel_id=1, source_target_pairs={{0,8},{4,12},{8,0},{12,4},{16,24},{20,28},{24,16},{28,20},{1,9},{5... | collective-permute-start | bytes 294920 | tf_op jit(solution)/shard_map/ppermute | solution.py:38
  77.0 6.8 %collective-permute-start.20 = (bf16[32,1536]{1,0:T(8,128)(2,1)S(1)}, bf16[32,1536]{1,0:T(8,128)(2,1)S(1)}, u32[]{:S(2)}, u32[]{:S(2)}) collective-permute-start(bf16[32,1536]{1,0:T(8,128)(2,1)S(1)} %pad_maximum_fusion.13), channel_id=1, source_target_pairs={{0,16},{4,20},{8,24},{12,28},{16,0},{20,4},{24,8},{28,12},{1,17},{... | collective-permute-start | bytes 294920 | tf_op jit(solution)/shard_map/ppermute | solution.py:38
  77.8 6.0 %collective-permute-start.21 = (bf16[32,1536]{1,0:T(8,128)(2,1)S(1)}, bf16[32,1536]{1,0:T(8,128)(2,1)S(1)}, u32[]{:S(2)}, u32[]{:S(2)}) collective-permute-start(bf16[32,1536]{1,0:T(8,128)(2,1)S(1)} %pad_maximum_fusion.14), channel_id=1, source_target_pairs={{0,24},{4,28},{8,16},{12,20},{16,8},{20,12},{24,0},{28,4},{1,25},{... | collective-permute-start | bytes 294920 | tf_op jit(solution)/shard_map/ppermute | solution.py:38

commit v10 on v9

--- a/solution.py
+++ b/solution.py
@@ -94,12 +94,16 @@
         step = position & (self.steps - 1)
         return (step * self.seq_count + (me ^ partner)) * self.local_blocks + block
 
+    def given(self, chip):
+        return (0, 0) if chip == 1 else (1, max(chip - 1, 0))
+
     def exchange(self, kept, give, streams=1):
-        got = swap(give, 1)
+        got = [swap(part, 1) for part in give]
         arrived = []
         for chip in range(self.chips):
-            rows = self.rows(chip * streams, streams)
-            message = jnp.concatenate([kept[rows], got[rows]])
+            part, index = self.given(chip)
+            own = kept[self.rows(chip * streams, streams)]
+            message = jnp.concatenate([own, got[part][self.rows(index * streams, streams)]])
             arrived.append(swap(message, 2 * chip) if chip else message)
         return arrived
 
@@ -131,7 +135,7 @@
 def begin_kernel(
     order, x_hbm, gain_hbm, first_hbm, second_hbm, gate_hbm, incoming_hbm, out_hbm,
     normed_ref, inv_ref, first_recv_ref, second_send_ref, second_recv_ref,
-    mix_factor_ref, slope_ref, hidden_ref, keep_ref, give_ref,
+    mix_factor_ref, slope_ref, hidden_ref, keep_ref, give_first_ref, give_rest_ref,
     x_ref, gain_ref, first_ref, second_ref, gate_ref, incoming_ref, out_ref, sems,
 ):
     parts = chunks(out_hbm.shape[0], sems.shape[0] - 6)
@@ -172,10 +176,11 @@
     normed_ref[...] = normed
 
     def place(send, stream, columns):
-        for core, target in enumerate((keep_ref, give_ref)):
-            for chip in range(order.chips):
-                rows = order.rows(2 * chip + stream)
-                target[rows, columns] = send[order.rows(core * order.chips + chip)]
+        for chip in range(order.chips):
+            keep_ref[order.rows(2 * chip + stream), columns] = send[order.rows(chip)]
+            part, index = order.given(chip)
+            target = (give_first_ref, give_rest_ref)[part]
+            target[order.rows(2 * index + stream), columns] = send[order.rows(order.chips + chip)]
 
     place(rounded(first_send, normed), 0, slice(None))
     copies[4].wait()
@@ -205,7 +210,8 @@
     short = array_of((row_count, width), jnp.bfloat16)
     full = array_of((row_count, width), jnp.float32)
     column = array_of((row_count, 1), jnp.float32)
-    outs = [short, column, square, square, square, full, full, full, short, short]
+    give = [array_of((2 * order.piece * n, width), jnp.bfloat16) for n in (1, order.chips - 1)]
+    outs = [short, column, square, square, square, full, full, full, short, *give]
     return pl.pallas_call(
         functools.partial(begin_kernel, order),
         in_specs=[ANYWHERE] * len(operands),
@@ -306,17 +312,22 @@
 
 
 def mix_kernel(
-    partial_ref, last_ref, weight_ref, mix_factor_ref, gate_factor_ref, second_send_ref,
-    mix_ref, gate_ref, keep_ref, give_ref,
+    order, partial_ref, last_ref, weight_ref, mix_factor_ref, gate_factor_ref, second_send_ref,
+    mix_ref, gate_ref, keep_ref, *give_refs,
 ):
     hidden = partial_ref[...] + dot(last_ref[...], weight_ref[...])
     mix = (hidden * mix_factor_ref[...]).astype(jnp.bfloat16)
     mix_ref[...] = mix
     send = rounded(second_send_ref[...], mix)
-    half = keep_ref.shape[0]
-    keep_ref[...] = send[:half]
-    give_ref[...] = send[half:]
+    keep_ref[...] = send[: keep_ref.shape[0]]
+    for chip in range(order.chips):
+        part, index = order.given(chip)
+        give_refs[part][order.rows(index)] = send[order.rows(order.chips + chip)]
     gate_ref[...] = (hidden * gate_factor_ref[...]).astype(jnp.bfloat16)
+
+
+def gate_kernel(after_ref, gate_ref, weight_ref, out_ref):
+    out_ref[...] = dot(gate_ref[...], weight_ref[...])
 
 
 def advance_kernel(
@@ -416,7 +427,7 @@
 
     (
         normed, inv_rms, first_recv, second_send, second_recv,
-        mix_factor, slope, delta_hidden, kept, give,
+        mix_factor, slope, delta_hidden, kept, *give,
     ) = begin(
         order, inputs, gain, mix_first[0], mix_second[0], w_gate[0], cotangent, w_out[0]
     )
@@ -429,7 +440,9 @@
 
     row_count, width = inputs.shape
     short = array_of((row_count, width), jnp.bfloat16)
+    full = array_of((row_count, width), jnp.float32)
     half = array_of((row_count // 2, width), jnp.bfloat16)
+    pieces = [array_of((order.piece * n, width), jnp.bfloat16) for n in (1, order.chips - 1)]
     square = array_of((row_count, row_count), jnp.float32)
     blocks = array_of((local_blocks, block_rows, block_rows), jnp.float32)
     kept = (delta_hidden, mix_factor)
@@ -438,8 +451,8 @@
         incoming = [passed_down(part, sender + 1) for part in outgoing]
         last, *first = zip(incoming, out_turned)
         partial = sum(dot(part, weight) for part, weight in first)
-        delta_mix, delta_gate, kept_pieces, give = call(
-            mix_kernel, "mix", [short, short, half, half],
+        delta_mix, delta_gate, kept_pieces, *give = call(
+            functools.partial(mix_kernel, order), "mix", [short, short, half, *pieces],
             (partial, *last, mix_factor, gate_factor, second_send),
         )
         arrived = order.exchange(kept_pieces, give)
@@ -456,7 +469,7 @@
                 (arrived[0], normed, moved, before_mid, delta_mix, *before_outgoing, *kept),
             )
         delta_mid = jnp.concatenate(arrived)
-        gate_back = dot(delta_gate, gate_turned)
+        (gate_back,) = call(gate_kernel, "gate", [full], (arrived[0], delta_gate, gate_turned))
         if sender > 0:
             outgoing = advance(incoming, kept[1], delta_mid, first_recv, gate_back, gain, inputs, inv_rms)
     outgoing_kept, first_kept, grad_second = kept

time: 85.5 us -> 84.1 us (0.984)
  waiting for transfers between devices: 28 us -> 25 us
  Pallas kernels: 15.4 us -> 17.8 us
  matrix products: 4.08 us -> 1.74 us
  starting transfers between devices: 36.5 us -> 38 us
    ppermute x16 -> x20, waiting for transfers between devices: 18.8 us -> 15.8 us  [swap(): return lax.ppermute(block, 'seq', [(i, i ^ offset) for i in range(count)])]
    pallas_call x7 -> x10, Pallas kernels: 5.31 us -> 7.66 us  [call(): pl.pallas_call(kernel, in_specs=[WHOLE] * len(operands), out_specs=[WHOLE...]
    dot_general x6 -> x3, matrix products: 4.08 us -> 1.74 us  [dot(): return jnp.dot(left, right, preferred_element_type=jnp.float32)]
    ppermute x16 -> x20, starting transfers between devices: 16.6 us -> 18.2 us  [swap(): return lax.ppermute(block, 'seq', [(i, i ^ offset) for i in range(count)])]
  transfers between devices with their start and end apart: 22 -> 26, of which waited for: 16 -> 15; matrix products, arithmetic and copies ran while one was open for 5% -> 2% of each run, Pallas kernels for 8% -> 11%
where the time goes in v10:
time: 84.1 us; the launch traced here: 83.9 us
  starting transfers between devices  38 us (45%)
  waiting for transfers between devices  25 us (30%)
  Pallas kernels  17.8 us (21%)
  matrix products  1.74 us (2%)
  between operations  0.99 us (1%)
    ppermute x6, starting transfers between devices, passed_down(): return lax.ppermute(block, ('seq', 'pipe'), pairs)  19.8 us
    ppermute x20, starting transfers between devices, swap(): return lax.ppermute(block, 'seq', [(i, i ^ offset) for i in range(count)])  18.2 us
    ppermute x20, waiting for transfers between devices, swap(): return lax.ppermute(block, 'seq', [(i, i ^ offset) for i in range(count)])  15.8 us
    ppermute x6, waiting for transfers between devices, passed_down(): return lax.ppermute(block, ('seq', 'pipe'), pairs)  9.18 us
    pallas_call x10, Pallas kernels, call(): pl.pallas_call(kernel, in_specs=[WHOLE] * len(operands), out_specs=[WHOLE...  7.66 us
    pallas_call x1, Pallas kernels, transposed(): pl.pallas_call(transpose_kernel, in_specs=[ANYWHERE] * 3, out_specs=[WHOL...  4.41 us
    pallas_call x1, Pallas kernels, begin(): pl.pallas_call(functools.partial(begin_kernel, order), in_specs=[ANYWHERE...  3.52 us
    dot_general x3, matrix products, dot(): return jnp.dot(left, right, preferred_element_type=jnp.float32)  1.74 us
  transfers between devices with their start and end apart: 26, of which 15 were waited for; matrix products, arithmetic and copies ran while one was open for 2% of the time, Pallas kernels for 11%

profile of v10, /device:TPU:0, one launch (start us, length us, event | category | flops | bytes accessed | tf_op | source)
XLA Modules:
  0.0 83.9 jit_solution(1620046724769127138)
XLA Ops:
  0.6 3.5 %begin.1 = (bf16[128,1536]{1,0:T(8,128)(2,1)S(1)}, f32[128,1]{1,0:T(8,128)S(1)}, bf16[128,128]{1,0:T(8,128)(2,1)S(1)}, bf16[128,128]{1,0:T(8,128)(2,1)S(1)}, bf1...) custom-call(bf16[128,1536]{1,0:T(8,128)(2,1)} %bitcast.14, ...), custom_call_target="tpu_custom_call" | custom-call | tf_op jit(solution)/shard_map/begin/pallas_call | solution.py:215
  4.2 0.5 collective-permute-start.1
  4.7 0.1 collective-permute-start
  4.8 0.8 collective-permute-done.1
  5.6 2.9 %collective-permute-start.2 = (bf16[64,1536]{1,0:T(8,128)(2,1)S(1)}, bf16[64,1536]{1,0:T(8,128)(2,1)S(1)}, u32[]{:S(2)}, u32[]{:S(2)}) collective-permute-start(bf16[64,1536]{1,0:T(8,128)(2,1)S(1)} %pad_maximum_fusion.1), channel_id=1, source_target_pairs={{0,8},{4,12},{8,0},{12,4},{16,24},{20,28},{24,16},{28,20},{1,9},{5... | collective-permute-start | bytes 589832 | tf_op jit(solution)/shard_map/ppermute | solution.py:38
  8.6 1.6 %collective-permute-start.3 = (bf16[64,1536]{1,0:T(8,128)(2,1)S(1)}, bf16[64,1536]{1,0:T(8,128)(2,1)S(1)}, u32[]{:S(2)}, u32[]{:S(2)}) collective-permute-start(bf16[64,1536]{1,0:T(8,128)(2,1)S(1)} %pad_maximum_fusion.2), channel_id=1, source_target_pairs={{0,16},{4,20},{8,24},{12,28},{16,0},{20,4},{24,8},{28,12},{1,17},{... | collective-permute-start | bytes 589832 | tf_op jit(solution)/shard_map/ppermute | solution.py:38
  10.2 0.4 collective-permute-start.4
  10.6 0.0 copy-start
  10.6 0.0 copy-start.1
  10.6 0.0 copy-start.2
  10.6 4.4 %transposed.1 = (bf16[1536,1536]{1,0:T(8,128)(2,1)S(1)}, bf16[512,1536]{1,0:T(8,128)(2,1)S(1)}, bf16[1024,1536]{1,0:T(8,128)(2,1)S(1)}) custom-call(bf16[1536,1536]{1,0:T(8,128)(2,1)} %bitcast.20, bf16[1536,1536]{1,0:T(8,128)(2,1)} %bitcast.22, bf16[64,1536]{1,0:T(8,128)(2,1)S(1)} %pad_maximum_fusion.after_ref.refs_0_), custom_call_target="tpu_custom_call" | custom-call | tf_op jit(solution)/shard_map/transposed/pallas_call | solution.py:247
  15.0 0.0 collective-permute-done.2.refs_1_
  15.0 4.5 %collective-permute-done.3.refs_2_ = bf16[64,1536]{1,0:T(8,128)(2,1)S(1)} collective-permute-done((bf16[64,1536]{1,0:T(8,128)(2,1)S(1)}, bf16[64,1536]{1,0:T(8,128)(2,1)S(1)}, u32[]{:S(2)}, u32[]{:S(2)}) %collective-permute-start.3) | collective-permute-done | bytes 196640 | tf_op jit(solution)/shard_map/ppermute | solution.py:38
  19.6 1.2 %finish.1 = (bf16[128,1536]{1,0:T(8,128)(2,1)S(1)}, bf16[128,1536]{1,0:T(8,128)(2,1)S(1)}, f32[128,1536]{1,0:T(8,128)S(1)}, bf16[128,512]{1,0:T(8,128)(2,1)S(1)}, bf16[128,1024]{1,0:T(8,128)(2,1)S(1)}) custom-call(bf16[64,1536]{1,0:T(8,128)(2,1)S(1)} %pad_maximum_fusion.after_ref.refs_0_, bf16[64,1536]{1,0:T(8,128)(2,1)S(1)} %collective-permute-done.2.refs_1_, ...), custom_call_target="tpu_custom_call" | custom-call | tf_op jit(solution)/shard_map/finish/pallas_call | solution.py:304
  20.8 0.1 collective-permute-start.5
  20.9 0.5 collective-permute-start.6
  21.4 1.0 %collective-permute-done.5.refs_1_ = bf16[128,1024]{1,0:T(8,128)(2,1)S(1)} collective-permute-done((bf16[128,1024]{1,0:T(8,128)(2,1)S(1)}, bf16[128,1024]{1,0:T(8,128)(2,1)S(1)}, u32[]{:S(2)}, u32[]{:S(2)}) %collective-permute-start.5) | collective-permute-done | bytes 262176 | tf_op jit(solution)/shard_map/ppermute | solution.py:50
  22.4 0.6 fusion.8.partial_ref
  23.0 0.0 collective-permute-done.6.last_ref.refs_0_
  23.0 0.6 mix.3
  23.6 0.2 collective-permute-start.8
  23.8 0.4 collective-permute-start.7
  24.2 0.7 collective-permute-done.8
  24.9 1.2 %collective-permute-start.9 = (bf16[32,1536]{1,0:T(8,128)(2,1)S(1)}, bf16[32,1536]{1,0:T(8,128)(2,1)S(1)}, u32[]{:S(2)}, u32[]{:S(2)}) collective-permute-start(bf16[32,1536]{1,0:T(8,128)(2,1)S(1)} %pad_maximum_fusion.5), channel_id=1, source_target_pairs={{0,8},{4,12},{8,0},{12,4},{16,24},{20,28},{24,16},{28,20},{1,9},{5... | collective-permute-start | bytes 294920 | tf_op jit(solution)/shard_map/ppermute | solution.py:38
  26.1 1.3 %collective-permute-start.10 = (bf16[32,1536]{1,0:T(8,128)(2,1)S(1)}, bf16[32,1536]{1,0:T(8,128)(2,1)S(1)}, u32[]{:S(2)}, u32[]{:S(2)}) collective-permute-start(bf16[32,1536]{1,0:T(8,128)(2,1)S(1)} %pad_maximum_fusion.6), channel_id=1, source_target_pairs={{0,16},{4,20},{8,24},{12,28},{16,0},{20,4},{24,8},{28,12},{1,17},{... | collective-permute-start | bytes 294920 | tf_op jit(solution)/shard_map/ppermute | solution.py:38
  27.4 1.2 %collective-permute-start.11 = (bf16[32,1536]{1,0:T(8,128)(2,1)S(1)}, bf16[32,1536]{1,0:T(8,128)(2,1)S(1)}, u32[]{:S(2)}, u32[]{:S(2)}) collective-permute-start(bf16[32,1536]{1,0:T(8,128)(2,1)S(1)} %pad_maximum_fusion.7), channel_id=1, source_target_pairs={{0,24},{4,28},{8,16},{12,20},{16,8},{20,12},{24,0},{28,4},{1,25},{... | collective-permute-start | bytes 294920 | tf_op jit(solution)/shard_map/ppermute | solution.py:38
  28.6 0.8 gate.3.gate_back_ref
  29.4 0.4 keep.3
  29.8 1.8 %collective-permute-done.10 = bf16[32,1536]{1,0:T(8,128)(2,1)S(1)} collective-permute-done((bf16[32,1536]{1,0:T(8,128)(2,1)S(1)}, bf16[32,1536]{1,0:T(8,128)(2,1)S(1)}, u32[]{:S(2)}, u32[]{:S(2)}) %collective-permute-start.10) | collective-permute-done | bytes 98336 | tf_op jit(solution)/shard_map/ppermute | solution.py:38
  31.7 1.3 %collective-permute-done.11 = bf16[32,1536]{1,0:T(8,128)(2,1)S(1)} collective-permute-done((bf16[32,1536]{1,0:T(8,128)(2,1)S(1)}, bf16[32,1536]{1,0:T(8,128)(2,1)S(1)}, u32[]{:S(2)}, u32[]{:S(2)}) %collective-permute-start.11) | collective-permute-done | bytes 98336 | tf_op jit(solution)/shard_map/ppermute | solution.py:38
  33.0 0.5 advance.2
  33.5 0.1 collective-permute-start.12
  33.5 0.5 collective-permute-start.13
  34.0 1.0 %collective-permute-done.12.refs_1_ = bf16[128,1024]{1,0:T(8,128)(2,1)S(1)} collective-permute-done((bf16[128,1024]{1,0:T(8,128)(2,1)S(1)}, bf16[128,1024]{1,0:T(8,128)(2,1)S(1)}, u32[]{:S(2)}, u32[]{:S(2)}) %collective-permute-start.12) | collective-permute-done | bytes 262176 | tf_op jit(solution)/shard_map/ppermute | solution.py:50
  35.1 0.6 fusion.9.partial_ref
  35.7 0.6 mix.4
  36.2 0.2 collective-permute-start.15
  36.4 0.4 collective-permute-start.14
  36.8 0.7 collective-permute-done.15
  37.5 1.3 %collective-permute-start.16 = (bf16[32,1536]{1,0:T(8,128)(2,1)S(1)}, bf16[32,1536]{1,0:T(8,128)(2,1)S(1)}, u32[]{:S(2)}, u32[]{:S(2)}) collective-permute-start(bf16[32,1536]{1,0:T(8,128)(2,1)S(1)} %pad_maximum_fusion.9), channel_id=1, source_target_pairs={{0,8},{4,12},{8,0},{12,4},{16,24},{20,28},{24,16},{28,20},{1,9},{5... | collective-permute-start | bytes 294920 | tf_op jit(solution)/shard_map/ppermute | solution.py:38
  38.8 1.2 %collective-permute-start.17 = (bf16[32,1536]{1,0:T(8,128)(2,1)S(1)}, bf16[32,1536]{1,0:T(8,128)(2,1)S(1)}, u32[]{:S(2)}, u32[]{:S(2)}) collective-permute-start(bf16[32,1536]{1,0:T(8,128)(2,1)S(1)} %pad_maximum_fusion.10), channel_id=1, source_target_pairs={{0,16},{4,20},{8,24},{12,28},{16,0},{20,4},{24,8},{28,12},{1,17},{... | collective-permute-start | bytes 294920 | tf_op jit(solution)/shard_map/ppermute | solution.py:38
  40.1 1.2 %collective-permute-start.18 = (bf16[32,1536]{1,0:T(8,128)(2,1)S(1)}, bf16[32,1536]{1,0:T(8,128)(2,1)S(1)}, u32[]{:S(2)}, u32[]{:S(2)}) collective-permute-start(bf16[32,1536]{1,0:T(8,128)(2,1)S(1)} %pad_maximum_fusion.11), channel_id=1, source_target_pairs={{0,24},{4,28},{8,16},{12,20},{16,8},{20,12},{24,0},{28,4},{1,25},{... | collective-permute-start | bytes 294920 | tf_op jit(solution)/shard_map/ppermute | solution.py:38
  41.3 0.8 gate.4.gate_back_ref
  42.1 0.4 keep.4
  42.5 2.1 %collective-permute-done.17 = bf16[32,1536]{1,0:T(8,128)(2,1)S(1)} collective-permute-done((bf16[32,1536]{1,0:T(8,128)(2,1)S(1)}, bf16[32,1536]{1,0:T(8,128)(2,1)S(1)}, u32[]{:S(2)}, u32[]{:S(2)}) %collective-permute-start.17) | collective-permute-done | bytes 98336 | tf_op jit(solution)/shard_map/ppermute | solution.py:38
  44.6 1.1 %collective-permute-done.18 = bf16[32,1536]{1,0:T(8,128)(2,1)S(1)} collective-permute-done((bf16[32,1536]{1,0:T(8,128)(2,1)S(1)}, bf16[32,1536]{1,0:T(8,128)(2,1)S(1)}, u32[]{:S(2)}, u32[]{:S(2)}) %collective-permute-start.18) | collective-permute-done | bytes 98336 | tf_op jit(solution)/shard_map/ppermute | solution.py:38
  45.7 0.5 advance.3
  46.2 18.6 %collective-permute-start.19 = (bf16[128,1024]{1,0:T(8,128)(2,1)S(1)}, bf16[128,1024]{1,0:T(8,128)(2,1)S(1)}, u32[]{:S(2)}, u32[]{:S(2)}) collective-permute-start(bf16[128,1024]{1,0:T(8,128)(2,1)S(1)} %get-tuple-element.87.refs_1_), channel_id=1, source_target_pairs={{0,1},{1,0},{2,6},{3,7},{4,5},{5,4},{6,2},{7,3},{8,9},{9,8},{10,14... | collective-permute-start | bytes 786440 | tf_op jit(solution)/shard_map/ppermute | solution.py:50
  64.8 0.1 collective-permute-start.20
  64.9 6.3 %collective-permute-done.19.refs_1_ = bf16[128,1024]{1,0:T(8,128)(2,1)S(1)} collective-permute-done((bf16[128,1024]{1,0:T(8,128)(2,1)S(1)}, bf16[128,1024]{1,0:T(8,128)(2,1)S(1)}, u32[]{:S(2)}, u32[]{:S(2)}) %collective-permute-start.19) | collective-permute-done | bytes 262176 | tf_op jit(solution)/shard_map/ppermute | solution.py:50
  71.2 0.6 fusion.10.partial_ref
  71.8 0.8 collective-permute-done.20.last_ref.refs_0_
  72.6 0.6 mix.5
  73.2 0.1 collective-permute-start.22
  73.2 0.5 collective-permute-start.21
  73.8 0.7 collective-permute-done.22
  74.5 1.0 %collective-permute-start.23 = (bf16[32,1536]{1,0:T(8,128)(2,1)S(1)}, bf16[32,1536]{1,0:T(8,128)(2,1)S(1)}, u32[]{:S(2)}, u32[]{:S(2)}) collective-permute-start(bf16[32,1536]{1,0:T(8,128)(2,1)S(1)} %pad_maximum_fusion.12), channel_id=1, source_target_pairs={{0,8},{4,12},{8,0},{12,4},{16,24},{20,28},{24,16},{28,20},{1,9},{5... | collective-permute-start | bytes 294920 | tf_op jit(solution)/shard_map/ppermute | solution.py:38
  75.5 1.2 %collective-permute-start.24 = (bf16[32,1536]{1,0:T(8,128)(2,1)S(1)}, bf16[32,1536]{1,0:T(8,128)(2,1)S(1)}, u32[]{:S(2)}, u32[]{:S(2)}) collective-permute-start(bf16[32,1536]{1,0:T(8,128)(2,1)S(1)} %pad_maximum_fusion.13), channel_id=1, source_target_pairs={{0,16},{4,20},{8,24},{12,28},{16,0},{20,4},{24,8},{28,12},{1,17},{... | collective-permute-start | bytes 294920 | tf_op jit(solution)/shard_map/ppermute | solution.py:38
  76.8 1.4 %collective-permute-start.25 = (bf16[32,1536]{1,0:T(8,128)(2,1)S(1)}, bf16[32,1536]{1,0:T(8,128)(2,1)S(1)}, u32[]{:S(2)}, u32[]{:S(2)}) collective-permute-start(bf16[32,1536]{1,0:T(8,128)(2,1)S(1)} %pad_maximum_fusion.14), channel_id=1, source_target_pairs={{0,24},{4,28},{8,16},{12,20},{16,8},{20,12},{24,0},{28,4},{1,25},{... | collective-permute-start | bytes 294920 | tf_op jit(solution)/shard_map/ppermute | solution.py:38
  78.2 1.2 %collective-permute-done.23 = bf16[32,1536]{1,0:T(8,128)(2,1)S(1)} collective-permute-done((bf16[32,1536]{1,0:T(8,128)(2,1)S(1)}, bf16[32,1536]{1,0:T(8,128)(2,1)S(1)}, u32[]{:S(2)}, u32[]{:S(2)}) %collective-permute-start.23) | collective-permute-done | bytes 98336 | tf_op jit(solution)/shard_map/ppermute | solution.py:38
  79.4 0.8 gate.5.gate_back_ref
  80.2 1.3 %keep.5 = (bf16[128,1536]{1,0:T(8,128)(2,1)S(1)}, f32[128,128]{1,0:T(8,128)S(1)}, f32[2,64,64]{2,1,0:T(8,128)}) custom-call(bf16[32,1536]{1,0:T(8,128)(2,1)S(1)} %pad_maximum_fusion.15.after_ref, bf16[128,1536]{1,0:T(8,128)(2,1)S(1)} %get-tuple-element.70.normed_ref, bf16[128,1536]{1,0:T(8,128)(2,1)S(1)} %get-tuple-element.71.moved_ref, ...), custom_call_target="tpu_custom_call" | custom-call | tf_op jit(solution)/shard_map/keep/pallas_call | solution.py:412
  81.5 0.9 %collective-permute-done.25 = bf16[32,1536]{1,0:T(8,128)(2,1)S(1)} collective-permute-done((bf16[32,1536]{1,0:T(8,128)(2,1)S(1)}, bf16[32,1536]{1,0:T(8,128)(2,1)S(1)}, u32[]{:S(2)}, u32[]{:S(2)}) %collective-permute-start.25) | collective-permute-done | bytes 98336 | tf_op jit(solution)/shard_map/ppermute | solution.py:38
  82.4 1.5 %close.1 = (bf16[128,1536]{1,0:T(8,128)(2,1)}, f32[2,64,64]{2,1,0:T(8,128)}) custom-call(bf16[128,1536]{1,0:T(8,128)(2,1)S(1)} %constant_dynamic-update-slice_fusion.10.mid_ref, bf16[128,128]{1,0:T(8,128)(2,1)S(1)} %get-tuple-element.56.refs_5_.first_recv_ref, f32[128,1536]{1,0:T(8,128)S(1)} %gate.5.gate_back_ref, f32[1,1536]{1,0:T(1,128)S(1)} %copy-done.2, ...), custom_call_target="tpu_custom_call" | custom-call | tf_op jit(solution)/shard_map/close/pallas_call | solution.py:412
  (45 shorter events, 0.4 us)
Async XLA Ops:
  4.2 1.5 %collective-permute-start.1 = (bf16[32,1536]{1,0:T(8,128)(2,1)S(1)}, bf16[32,1536]{1,0:T(8,128)(2,1)S(1)}, u32[]{:S(2)}, u32[]{:S(2)}) collective-permute-start(bf16[32,1536]{1,0:T(8,128)(2,1)S(1)} %get-tuple-element.54), channel_id=1, source_target_pairs={{0,4},{4,0},{8,12},{12,8},{16,20},{20,16},{24,28},{28,24},{1,5},{5... | collective-permute-start | bytes 294920 | tf_op jit(solution)/shard_map/ppermute | solution.py:38
  4.7 3.9 %collective-permute-start = (bf16[96,1536]{1,0:T(8,128)(2,1)S(1)}, bf16[96,1536]{1,0:T(8,128)(2,1)S(1)}, u32[]{:S(2)}, u32[]{:S(2)}) collective-permute-start(bf16[96,1536]{1,0:T(8,128)(2,1)S(1)} %get-tuple-element.53), channel_id=1, source_target_pairs={{0,4},{4,0},{8,12},{12,8},{16,20},{20,16},{24,28},{28,24},{1,5},{5... | collective-permute-start | bytes 884744 | tf_op jit(solution)/shard_map/ppermute | solution.py:38
  5.6 9.4 %collective-permute-start.2 = (bf16[64,1536]{1,0:T(8,128)(2,1)S(1)}, bf16[64,1536]{1,0:T(8,128)(2,1)S(1)}, u32[]{:S(2)}, u32[]{:S(2)}) collective-permute-start(bf16[64,1536]{1,0:T(8,128)(2,1)S(1)} %pad_maximum_fusion.1), channel_id=1, source_target_pairs={{0,8},{4,12},{8,0},{12,4},{16,24},{20,28},{24,16},{28,20},{1,9},{5... | collective-permute-start | bytes 589832 | tf_op jit(solution)/shard_map/ppermute | solution.py:38
  8.6 11.0 %collective-permute-start.3 = (bf16[64,1536]{1,0:T(8,128)(2,1)S(1)}, bf16[64,1536]{1,0:T(8,128)(2,1)S(1)}, u32[]{:S(2)}, u32[]{:S(2)}) collective-permute-start(bf16[64,1536]{1,0:T(8,128)(2,1)S(1)} %pad_maximum_fusion.2), channel_id=1, source_target_pairs={{0,16},{4,20},{8,24},{12,28},{16,0},{20,4},{24,8},{28,12},{1,17},{... | collective-permute-start | bytes 589832 | tf_op jit(solution)/shard_map/ppermute | solution.py:38
  10.2 9.4 %collective-permute-start.4 = (bf16[64,1536]{1,0:T(8,128)(2,1)S(1)}, bf16[64,1536]{1,0:T(8,128)(2,1)S(1)}, u32[]{:S(2)}, u32[]{:S(2)}) collective-permute-start(bf16[64,1536]{1,0:T(8,128)(2,1)S(1)} %pad_maximum_fusion.3), channel_id=1, source_target_pairs={{0,24},{4,28},{8,16},{12,20},{16,8},{20,12},{24,0},{28,4},{1,25},{... | collective-permute-start | bytes 589832 | tf_op jit(solution)/shard_map/ppermute | solution.py:38
  10.6 9.0 %copy-start = (bf16[1,128,1536]{2,1,0:T(8,128)(2,1)S(1)}, bf16[1,128,1536]{2,1,0:T(8,128)(2,1)}, u32[]{:S(2)}) copy-start(bf16[1,128,1536]{2,1,0:T(8,128)(2,1)} %param.7) | copy-start | bytes 1179652
  10.6 9.0 %copy-start.1 = (bf16[128,1536]{1,0:T(8,128)(2,1)S(1)}, bf16[128,1536]{1,0:T(8,128)(2,1)}, u32[]{:S(2)}) copy-start(bf16[128,1536]{1,0:T(8,128)(2,1)} %refs_12_.1) | copy-start | bytes 1179652
  10.6 9.0 %copy-start.2 = (f32[1,1536]{1,0:T(1,128)S(1)}, f32[1,1536]{1,0:T(1,128)}, u32[]{:S(2)}) copy-start(f32[1,1536]{1,0:T(1,128)} %gain_ref.5) | copy-start | bytes 18436
  20.8 1.6 %collective-permute-start.5 = (bf16[128,1024]{1,0:T(8,128)(2,1)S(1)}, bf16[128,1024]{1,0:T(8,128)(2,1)S(1)}, u32[]{:S(2)}, u32[]{:S(2)}) collective-permute-start(bf16[128,1024]{1,0:T(8,128)(2,1)S(1)} %get-tuple-element.61.refs_1_), channel_id=1, source_target_pairs={{0,4},{1,5},{2,3},{3,2},{4,0},{5,1},{6,7},{7,6},{8,12},{9,13},{10,... | collective-permute-start | bytes 786440 | tf_op jit(solution)/shard_map/ppermute | solution.py:50
  20.9 2.1 %collective-permute-start.6 = (bf16[128,512]{1,0:T(8,128)(2,1)S(1)}, bf16[128,512]{1,0:T(8,128)(2,1)S(1)}, u32[]{:S(2)}, u32[]{:S(2)}) collective-permute-start(bf16[128,512]{1,0:T(8,128)(2,1)S(1)} %get-tuple-element.63.refs_0_), channel_id=1, source_target_pairs={{0,4},{1,5},{2,3},{3,2},{4,0},{5,1},{6,7},{7,6},{8,12},{9,13},{10,... | collective-permute-start | bytes 393224 | tf_op jit(solution)/shard_map/ppermute | solution.py:50
  23.6 1.3 %collective-permute-start.8 = (bf16[16,1536]{1,0:T(8,128)(2,1)S(1)}, bf16[16,1536]{1,0:T(8,128)(2,1)S(1)}, u32[]{:S(2)}, u32[]{:S(2)}) collective-permute-start(bf16[16,1536]{1,0:T(8,128)(2,1)S(1)} %get-tuple-element.75), channel_id=1, source_target_pairs={{0,4},{4,0},{8,12},{12,8},{16,20},{20,16},{24,28},{28,24},{1,5},{5... | collective-permute-start | bytes 147464 | tf_op jit(solution)/shard_map/ppermute | solution.py:38
  23.8 2.3 %collective-permute-start.7 = (bf16[48,1536]{1,0:T(8,128)(2,1)S(1)}, bf16[48,1536]{1,0:T(8,128)(2,1)S(1)}, u32[]{:S(2)}, u32[]{:S(2)}) collective-permute-start(bf16[48,1536]{1,0:T(8,128)(2,1)S(1)} %get-tuple-element.69), channel_id=1, source_target_pairs={{0,4},{4,0},{8,12},{12,8},{16,20},{20,16},{24,28},{28,24},{1,5},{5... | collective-permute-start | bytes 442376 | tf_op jit(solution)/shard_map/ppermute | solution.py:38
  24.9 5.0 %collective-permute-start.9 = (bf16[32,1536]{1,0:T(8,128)(2,1)S(1)}, bf16[32,1536]{1,0:T(8,128)(2,1)S(1)}, u32[]{:S(2)}, u32[]{:S(2)}) collective-permute-start(bf16[32,1536]{1,0:T(8,128)(2,1)S(1)} %pad_maximum_fusion.5), channel_id=1, source_target_pairs={{0,8},{4,12},{8,0},{12,4},{16,24},{20,28},{24,16},{28,20},{1,9},{5... | collective-permute-start | bytes 294920 | tf_op jit(solution)/shard_map/ppermute | solution.py:38
  26.1 5.6 %collective-permute-start.10 = (bf16[32,1536]{1,0:T(8,128)(2,1)S(1)}, bf16[32,1536]{1,0:T(8,128)(2,1)S(1)}, u32[]{:S(2)}, u32[]{:S(2)}) collective-permute-start(bf16[32,1536]{1,0:T(8,128)(2,1)S(1)} %pad_maximum_fusion.6), channel_id=1, source_target_pairs={{0,16},{4,20},{8,24},{12,28},{16,0},{20,4},{24,8},{28,12},{1,17},{... | collective-permute-start | bytes 294920 | tf_op jit(solution)/shard_map/ppermute | solution.py:38
  27.4 5.6 %collective-permute-start.11 = (bf16[32,1536]{1,0:T(8,128)(2,1)S(1)}, bf16[32,1536]{1,0:T(8,128)(2,1)S(1)}, u32[]{:S(2)}, u32[]{:S(2)}) collective-permute-start(bf16[32,1536]{1,0:T(8,128)(2,1)S(1)} %pad_maximum_fusion.7), channel_id=1, source_target_pairs={{0,24},{4,28},{8,16},{12,20},{16,8},{20,12},{24,0},{28,4},{1,25},{... | collective-permute-start | bytes 294920 | tf_op jit(solution)/shard_map/ppermute | solution.py:38
  33.5 1.6 %collective-permute-start.12 = (bf16[128,1024]{1,0:T(8,128)(2,1)S(1)}, bf16[128,1024]{1,0:T(8,128)(2,1)S(1)}, u32[]{:S(2)}, u32[]{:S(2)}) collective-permute-start(bf16[128,1024]{1,0:T(8,128)(2,1)S(1)} %get-tuple-element.77.refs_1_), channel_id=1, source_target_pairs={{0,4},{1,2},{2,1},{3,7},{4,0},{5,6},{6,5},{7,3},{8,12},{9,10},{10,... | collective-permute-start | bytes 786440 | tf_op jit(solution)/shard_map/ppermute | solution.py:50
  33.5 2.1 %collective-permute-start.13 = (bf16[128,512]{1,0:T(8,128)(2,1)S(1)}, bf16[128,512]{1,0:T(8,128)(2,1)S(1)}, u32[]{:S(2)}, u32[]{:S(2)}) collective-permute-start(bf16[128,512]{1,0:T(8,128)(2,1)S(1)} %get-tuple-element.78.refs_0_), channel_id=1, source_target_pairs={{0,4},{1,2},{2,1},{3,7},{4,0},{5,6},{6,5},{7,3},{8,12},{9,10},{10,... | collective-permute-start | bytes 393224 | tf_op jit(solution)/shard_map/ppermute | solution.py:50
  36.2 1.3 %collective-permute-start.15 = (bf16[16,1536]{1,0:T(8,128)(2,1)S(1)}, bf16[16,1536]{1,0:T(8,128)(2,1)S(1)}, u32[]{:S(2)}, u32[]{:S(2)}) collective-permute-start(bf16[16,1536]{1,0:T(8,128)(2,1)S(1)} %get-tuple-element.85), channel_id=1, source_target_pairs={{0,4},{4,0},{8,12},{12,8},{16,20},{20,16},{24,28},{28,24},{1,5},{5... | collective-permute-start | bytes 147464 | tf_op jit(solution)/shard_map/ppermute | solution.py:38
  36.4 2.4 %collective-permute-start.14 = (bf16[48,1536]{1,0:T(8,128)(2,1)S(1)}, bf16[48,1536]{1,0:T(8,128)(2,1)S(1)}, u32[]{:S(2)}, u32[]{:S(2)}) collective-permute-start(bf16[48,1536]{1,0:T(8,128)(2,1)S(1)} %get-tuple-element.80), channel_id=1, source_target_pairs={{0,4},{4,0},{8,12},{12,8},{16,20},{20,16},{24,28},{28,24},{1,5},{5... | collective-permute-start | bytes 442376 | tf_op jit(solution)/shard_map/ppermute | solution.py:38
  37.5 4.9 %collective-permute-start.16 = (bf16[32,1536]{1,0:T(8,128)(2,1)S(1)}, bf16[32,1536]{1,0:T(8,128)(2,1)S(1)}, u32[]{:S(2)}, u32[]{:S(2)}) collective-permute-start(bf16[32,1536]{1,0:T(8,128)(2,1)S(1)} %pad_maximum_fusion.9), channel_id=1, source_target_pairs={{0,8},{4,12},{8,0},{12,4},{16,24},{20,28},{24,16},{28,20},{1,9},{5... | collective-permute-start | bytes 294920 | tf_op jit(solution)/shard_map/ppermute | solution.py:38
  38.8 5.7 %collective-permute-start.17 = (bf16[32,1536]{1,0:T(8,128)(2,1)S(1)}, bf16[32,1536]{1,0:T(8,128)(2,1)S(1)}, u32[]{:S(2)}, u32[]{:S(2)}) collective-permute-start(bf16[32,1536]{1,0:T(8,128)(2,1)S(1)} %pad_maximum_fusion.10), channel_id=1, source_target_pairs={{0,16},{4,20},{8,24},{12,28},{16,0},{20,4},{24,8},{28,12},{1,17},{... | collective-permute-start | bytes 294920 | tf_op jit(solution)/shard_map/ppermute | solution.py:38
  40.1 5.6 %collective-permute-start.18 = (bf16[32,1536]{1,0:T(8,128)(2,1)S(1)}, bf16[32,1536]{1,0:T(8,128)(2,1)S(1)}, u32[]{:S(2)}, u32[]{:S(2)}) collective-permute-start(bf16[32,1536]{1,0:T(8,128)(2,1)S(1)} %pad_maximum_fusion.11), channel_id=1, source_target_pairs={{0,24},{4,28},{8,16},{12,20},{16,8},{20,12},{24,0},{28,4},{1,25},{... | collective-permute-start | bytes 294920 | tf_op jit(solution)/shard_map/ppermute | solution.py:38
  46.2 25.0 %collective-permute-start.19 = (bf16[128,1024]{1,0:T(8,128)(2,1)S(1)}, bf16[128,1024]{1,0:T(8,128)(2,1)S(1)}, u32[]{:S(2)}, u32[]{:S(2)}) collective-permute-start(bf16[128,1024]{1,0:T(8,128)(2,1)S(1)} %get-tuple-element.87.refs_1_), channel_id=1, source_target_pairs={{0,1},{1,0},{2,6},{3,7},{4,5},{5,4},{6,2},{7,3},{8,9},{9,8},{10,14... | collective-permute-start | bytes 786440 | tf_op jit(solution)/shard_map/ppermute | solution.py:50
  64.8 7.8 %collective-permute-start.20 = (bf16[128,512]{1,0:T(8,128)(2,1)S(1)}, bf16[128,512]{1,0:T(8,128)(2,1)S(1)}, u32[]{:S(2)}, u32[]{:S(2)}) collective-permute-start(bf16[128,512]{1,0:T(8,128)(2,1)S(1)} %get-tuple-element.88.refs_0_), channel_id=1, source_target_pairs={{0,1},{1,0},{2,6},{3,7},{4,5},{5,4},{6,2},{7,3},{8,9},{9,8},{10,14... | collective-permute-start | bytes 393224 | tf_op jit(solution)/shard_map/ppermute | solution.py:50
  73.2 1.3 %collective-permute-start.22 = (bf16[16,1536]{1,0:T(8,128)(2,1)S(1)}, bf16[16,1536]{1,0:T(8,128)(2,1)S(1)}, u32[]{:S(2)}, u32[]{:S(2)}) collective-permute-start(bf16[16,1536]{1,0:T(8,128)(2,1)S(1)} %get-tuple-element.91), channel_id=1, source_target_pairs={{0,4},{4,0},{8,12},{12,8},{16,20},{20,16},{24,28},{28,24},{1,5},{5... | collective-permute-start | bytes 147464 | tf_op jit(solution)/shard_map/ppermute | solution.py:38
  73.2 2.3 %collective-permute-start.21 = (bf16[48,1536]{1,0:T(8,128)(2,1)S(1)}, bf16[48,1536]{1,0:T(8,128)(2,1)S(1)}, u32[]{:S(2)}, u32[]{:S(2)}) collective-permute-start(bf16[48,1536]{1,0:T(8,128)(2,1)S(1)} %get-tuple-element.90), channel_id=1, source_target_pairs={{0,4},{4,0},{8,12},{12,8},{16,20},{20,16},{24,28},{28,24},{1,5},{5... | collective-permute-start | bytes 442376 | tf_op jit(solution)/shard_map/ppermute | solution.py:38
  74.5 4.9 %collective-permute-start.23 = (bf16[32,1536]{1,0:T(8,128)(2,1)S(1)}, bf16[32,1536]{1,0:T(8,128)(2,1)S(1)}, u32[]{:S(2)}, u32[]{:S(2)}) collective-permute-start(bf16[32,1536]{1,0:T(8,128)(2,1)S(1)} %pad_maximum_fusion.12), channel_id=1, source_target_pairs={{0,8},{4,12},{8,0},{12,4},{16,24},{20,28},{24,16},{28,20},{1,9},{5... | collective-permute-start | bytes 294920 | tf_op jit(solution)/shard_map/ppermute | solution.py:38
  75.5 5.9 %collective-permute-start.24 = (bf16[32,1536]{1,0:T(8,128)(2,1)S(1)}, bf16[32,1536]{1,0:T(8,128)(2,1)S(1)}, u32[]{:S(2)}, u32[]{:S(2)}) collective-permute-start(bf16[32,1536]{1,0:T(8,128)(2,1)S(1)} %pad_maximum_fusion.13), channel_id=1, source_target_pairs={{0,16},{4,20},{8,24},{12,28},{16,0},{20,4},{24,8},{28,12},{1,17},{... | collective-permute-start | bytes 294920 | tf_op jit(solution)/shard_map/ppermute | solution.py:38
  76.8 5.6 %collective-permute-start.25 = (bf16[32,1536]{1,0:T(8,128)(2,1)S(1)}, bf16[32,1536]{1,0:T(8,128)(2,1)S(1)}, u32[]{:S(2)}, u32[]{:S(2)}) collective-permute-start(bf16[32,1536]{1,0:T(8,128)(2,1)S(1)} %pad_maximum_fusion.14), channel_id=1, source_target_pairs={{0,24},{4,28},{8,16},{12,20},{16,8},{20,12},{24,0},{28,4},{1,25},{... | collective-permute-start | bytes 294920 | tf_op jit(solution)/shard_map/ppermute | solution.py:38
